TPU v7x, 32 devices: a whole 2x2x4 slice. The times are simulated.
32 devices in a mesh: energy: 4 (over y, x), slab: 8 (over z, core).
Axes of the slice: x: 2, y: 2, z: 4, core: 2. Of those that a mesh axis runs over, the one named last changes fastest.
Arguments:
- greens: bfloat16 [2, 8, 32, 128, 256], P(None, 'energy', 'slab'), may hold values from -6 to 6
- coupling: bfloat16 [4, 3, 128, 128], replicated, may hold values from -0.15625 to 0.15625
- occupation: float32 [4], replicated, may hold values from 0.2 to 3
- offsets: int32 [4], replicated, may hold values from 1 to 2, as said below
- neighbours: int32 [32, 3], P('slab'), may hold values from -1 to 31, as said below
Outputs:
- sigma: bfloat16 [2, 8, 32, 128, 256], P(None, 'energy', 'slab')
Inputs may be any that keep to these rules, and one draw needn't show every extreme that they name: `offsets`: every offset is 1 to 2; one mode has offset 2 and one has offset 1. `neighbours`: an entry is -1 (padding) or an atom block that differs from the row's own block by at most 1. Block a with a % 4 == 0 and a > 0 lists a - 1 in slot 1; block a with a % 4 == 3 and a < 31 lists a + 1 in slot 2.
All inputs are finite; a program needn't handle non-finite values.
Results may differ from a plain program's by a relative error of at most 0.0058.
Values may be sent and summed in bfloat16 or wider, within the bound.
No kernel may reach another device: no remote copies, remote signals or barrier semaphores. Data moves between devices by JAX's collectives and lax.ppermute only.
A program may use at most 128 MiB of HBM per device.

v0:
```python
import jax
import jax.numpy as jnp
from jax import lax
from jax.sharding import PartitionSpec as P


def with_halo(shard, sides, width, wrap):
    for axis, dim in sides:
        size, length = (lax.axis_size(axis), shard.shape[dim])
        up = [(i, (i + 1) % size) for i in range(size if wrap else size - 1)]
        down = [(j, i) for i, j in up]
        last = lax.slice_in_dim(shard, length - width, length, axis=dim)
        first = lax.slice_in_dim(shard, 0, width, axis=dim)
        before = lax.ppermute(last, axis, up)
        after = lax.ppermute(first, axis, down)
        shard = jnp.concatenate([before, shard, after], axis=dim)
    return shard


def couple(blocks, matrix):
    half = jnp.einsum("pq,...qr->...pr", matrix, blocks, preferred_element_type=jnp.float32).astype(
        jnp.bfloat16
    )
    shaped = half.reshape(half.shape[:-1] + (2, half.shape[-1] // 2))
    result = jnp.einsum("...psq,rq->...psr", shaped, matrix, preferred_element_type=jnp.float32)
    return result.reshape(blocks.shape)


def mixture_of(widened, occupation, offsets, mode_at, count, width):
    filling = occupation[mode_at]
    ahead = lax.dynamic_slice_in_dim(widened, width + offsets[mode_at], count, 1).astype(
        jnp.float32
    )
    behind = lax.dynamic_slice_in_dim(widened, width - offsets[mode_at], count, 1).astype(
        jnp.float32
    )
    lesser = (filling + 1.0) * ahead[0] + filling * behind[0]
    greater = (filling + 1.0) * behind[1] + filling * ahead[1]
    return jnp.stack([lesser, greater]).astype(jnp.bfloat16)


def widen(greens, count):
    return with_halo(greens, (("energy", 1),), count, True)


def owner_terms(
    padded, coupling, occupation, offsets, neighbours, summed, count, owned, first_block
):
    for mode_at in range(coupling.shape[0]):
        mixture = mixture_of(padded, occupation, offsets, mode_at, count, count)
        for slot_at in range(coupling.shape[1]):
            listed = neighbours[:, slot_at]
            local_at = jnp.clip(listed - first_block + 1, 0, owned + 1)
            is_live = listed >= 0
            picked = jnp.take(mixture, local_at, axis=2)
            picked = jnp.where(
                is_live[None, None, :, None, None], picked, jnp.zeros((), jnp.bfloat16)
            )
            summed = summed + couple(picked, coupling[mode_at, slot_at])
    return summed


def on_device(greens, coupling, occupation, offsets, neighbours):
    count = greens.shape[1]
    owned = greens.shape[2]
    first_block = lax.axis_index("slab") * owned
    summed = jnp.zeros(greens.shape, jnp.float32)
    widened = widen(greens, count)
    padded = with_halo(widened, (("slab", 2),), 1, False)
    summed = owner_terms(
        padded, coupling, occupation, offsets, neighbours, summed, count, owned, first_block
    )
    return summed.astype(jnp.bfloat16)


def solution(mesh):
    in_specs = (P(None, "energy", "slab", None, None), P(), P(), P(), P("slab", None))
    out_specs = P(None, "energy", "slab", None, None)
    return jax.shard_map(
        on_device, mesh=mesh, in_specs=in_specs, out_specs=out_specs, check_vma=False
    )
```

profile of v0, /device:TPU:1, one launch (start us, length us, event | category | flops | bytes accessed | tf_op | source)
XLA Modules:
  0.0 139.1 jit_solution(5239435865183462590)
XLA Ops:
  0.0 2.0 %collective-permute-start = (bf16[2,2,4,128,256]{4,3,2,1,0:T(8,128)(2,1)}, bf16[2,2,4,128,256]{4,3,2,1,0:T(8,128)(2,1)}, u32[]{:S(2)}, u32[]{:S(2)}) collective-permute-start(bf16[2,2,4,128,256]{4,3,2,1,0:T(8,128)(2,1)} %param.7), channel_id=1, source_target_pairs={{0,8},{8,16},{16,24},{24,0},{1,9},{9,17},{17,25},{25,1},{2,10},{10... | collective-permute-start | bytes 3145736 | tf_op jit(solution)/shard_map/ppermute | solution.py:14
  3.0 1.5 %fusion.89 = (s32[1]{0:T(128)}, s32[1]{0:T(128)}, s32[1]{0:T(128)}, s32[1]{0:T(128)}) fusion(s32[4]{0:T(128)} %param.10), kind=kLoop, calls=%fused_computation.173 | loop fusion | bytes 32 | tf_op jit(solution)/shard_map/slice | solution.py:31
  15.7 1.5 %fusion.88 = (f32[1]{0:T(128)}, f32[1]{0:T(128)}, f32[1]{0:T(128)}, f32[1]{0:T(128)}) fusion(f32[4]{0:T(128)} %param.9), kind=kLoop, calls=%fused_computation.172 | loop fusion | bytes 32 | tf_op jit(solution)/shard_map/slice | solution.py:30
  17.2 9.0 %collective-permute-done = bf16[2,2,4,128,256]{4,3,2,1,0:T(8,128)(2,1)} collective-permute-done((bf16[2,2,4,128,256]{4,3,2,1,0:T(8,128)(2,1)}, bf16[2,2,4,128,256]{4,3,2,1,0:T(8,128)(2,1)}, u32[]{:S(2)}, u32[]{:S(2)}) %collective-permute-start) | collective-permute-done | bytes 1048608 | tf_op jit(solution)/shard_map/ppermute | solution.py:14
  26.2 1.3 constant_dynamic-update-slice_fusion.2
  27.6 21.0 %collective-permute-done.1 = bf16[2,2,4,128,256]{4,3,2,1,0:T(8,128)(2,1)} collective-permute-done((bf16[2,2,4,128,256]{4,3,2,1,0:T(8,128)(2,1)}, bf16[2,2,4,128,256]{4,3,2,1,0:T(8,128)(2,1)}, u32[]{:S(2)}, u32[]{:S(2)}) %collective-permute-start.1) | collective-permute-done | bytes 1048608 | tf_op jit(solution)/shard_map/ppermute | solution.py:15
  48.6 1.3 constant_dynamic-update-slice_fusion
  51.2 4.6 %collective-permute-start.2 = (bf16[2,6,1,128,256]{4,3,2,1,0:T(8,128)(2,1)}, bf16[2,6,1,128,256]{4,3,2,1,0:T(8,128)(2,1)}, u32[]{:S(2)}, u32[]{:S(2)}) collective-permute-start(bf16[2,6,1,128,256]{4,3,2,1,0:T(8,128)(2,1)} %get-tuple-element.28), channel_id=1, source_target_pairs={{0,1},{1,2},{2,3},{3,4},{4,5},{5,6},{6,7},{8,9},{9,10},{10,11},{11... | collective-permute-start | bytes 2359304 | tf_op jit(solution)/shard_map/ppermute | solution.py:14
  55.8 1.9 %collective-permute-start.3 = (bf16[2,6,1,128,256]{4,3,2,1,0:T(8,128)(2,1)}, bf16[2,6,1,128,256]{4,3,2,1,0:T(8,128)(2,1)}, u32[]{:S(2)}, u32[]{:S(2)}) collective-permute-start(bf16[2,6,1,128,256]{4,3,2,1,0:T(8,128)(2,1)} %get-tuple-element.29), channel_id=1, source_target_pairs={{1,0},{2,1},{3,2},{4,3},{5,4},{6,5},{7,6},{9,8},{10,9},{11,10},{12... | collective-permute-start | bytes 2359304 | tf_op jit(solution)/shard_map/ppermute | solution.py:15
  60.5 4.5 %collective-permute-done.2 = bf16[2,6,1,128,256]{4,3,2,1,0:T(8,128)(2,1)} collective-permute-done((bf16[2,6,1,128,256]{4,3,2,1,0:T(8,128)(2,1)}, bf16[2,6,1,128,256]{4,3,2,1,0:T(8,128)(2,1)}, u32[]{:S(2)}, u32[]{:S(2)}) %collective-permute-start.2) | collective-permute-done | bytes 786464 | tf_op jit(solution)/shard_map/ppermute | solution.py:14
  65.0 4.4 %collective-permute-done.3 = bf16[2,6,1,128,256]{4,3,2,1,0:T(8,128)(2,1)} collective-permute-done((bf16[2,6,1,128,256]{4,3,2,1,0:T(8,128)(2,1)}, bf16[2,6,1,128,256]{4,3,2,1,0:T(8,128)(2,1)}, u32[]{:S(2)}, u32[]{:S(2)}) %collective-permute-start.3) | collective-permute-done | bytes 786464 | tf_op jit(solution)/shard_map/ppermute | solution.py:15
  69.4 1.7 %pad_maximum_fusion = bf16[2,6,6,128,256]{4,3,2,1,0:T(8,128)(2,1)S(1)} fusion(bf16[2,6,1,128,256]{4,3,2,1,0:T(8,128)(2,1)} %collective-permute-done.3, bf16[2,6,4,128,256]{4,3,2,1,0:T(8,128)(2,1)S(1)} %constant_dynamic-update-slice_fusion, bf16[2,6,1,128,256]{4,3,2,1,0:T(8,128)(2,1)} %collective-permute-done.2), kind=kLoop, calls=%fused_computation.12 | loop fusion | flops 4718592 | bytes 9437184 | tf_op jit(solution)/shard_map/concatenate | solution.py:16
  71.2 5.6 %dynamic-slice_convert_fusion.6 = (f32[2,2,6,128,256]{4,3,2,1,0:T(8,128)}, f32[2,2,6,128,256]{4,3,2,1,0:T(8,128)S(1)}, f32[2,2,6,128,256]{4,3,2,1,0:T(8,128)S(1)...) fusion(bf16[2,6,6,128,256]{4,3,2,1,0:T(8,128)(2,1)S(1)} %pad_ma, ...), kind=kLoop, calls=%fused_computation.56 | loop fusion | flops 6291456 | bytes 37748768 | tf_op jit(solution)/shard_map/convert_element_type | solution.py:34
  76.7 4.0 %fusion.3 = (bf16[1,2,6,128,256]{4,3,2,1,0:T(8,128)(2,1)S(1)}, bf16[1,2,6,128,256]{4,3,2,1,0:T(8,128)(2,1)S(1)}, bf16[1,2,6,128,256]{4,3,2,1,0:T(8,128)(2,1)}, bf16[1,2,6,128,256]{4,3,2,1,0:T(8,128)(2,1)}) fusion(f32[2,2,6,128,256]{4,3,2,1,0:T(8,128)S(1)} %get-tuple-element.21, f32[2,2,6,128,256]{4,3,2,1,0:T(8,128)S(1)} %get-tuple-element.22, f32[]{:T(128)} %bitcast.87, ...), kind=kLoop, calls=%fused_computation.20 | loop fusion | flops 6291456 | bytes 15728656 | tf_op jit(solution)/shard_map/convert
  80.9 1.6 %gather_fusion.11 = bf16[4,2,2,128,256]{4,3,2,1,0:T(8,128)(2,1)} fusion(bf16[2,2,6,128,256]{4,3,2,1,0:T(8,128)(2,1)S(1)} %pad_maximum_fusion.4, s32[1024]{0:T(1024)S(1)} %pad_clamp_fusion), kind=kCustom, calls=%fused_computation.11.clone | custom fusion | bytes 2097168 | tf_op jit(solution)/shard_map/jit(_take)/gather | solution.py:55
  82.5 1.5 %pad_maximum_fusion.3 = bf16[2,2,6,128,256]{4,3,2,1,0:T(8,128)(2,1)S(1)} fusion(bf16[1,2,6,128,256]{4,3,2,1,0:T(8,128)(2,1)} %get-tuple-element.54, bf16[1,2,6,128,256]{4,3,2,1,0:T(8,128)(2,1)} %get-tuple-element.55), kind=kLoop, calls=%fused_computation.48 | loop fusion | flops 786432 | bytes 3145728 | tf_op jit(solution)/shard_map/stack | solution.py:39
  84.0 1.6 %gather_fusion.8 = bf16[4,2,2,128,256]{4,3,2,1,0:T(8,128)(2,1)} fusion(bf16[2,2,6,128,256]{4,3,2,1,0:T(8,128)(2,1)S(1)} %pad_maximum_fusion.3, s32[1024]{0:T(1024)S(1)} %pad_clamp_fusion), kind=kCustom, calls=%fused_computation.8.clone | custom fusion | bytes 2097168 | tf_op jit(solution)/shard_map/jit(_take)/gather | solution.py:55
  85.6 1.6 %gather_fusion.9 = bf16[4,2,2,128,256]{4,3,2,1,0:T(8,128)(2,1)} fusion(bf16[2,2,6,128,256]{4,3,2,1,0:T(8,128)(2,1)S(1)} %pad_maximum_fusion.4, s32[1024]{0:T(1024)S(1)} %pad_clamp_fusion.2), kind=kCustom, calls=%fused_computation.9.clone | custom fusion | bytes 2097168 | tf_op jit(solution)/shard_map/jit(_take)/gather | solution.py:55
  87.1 1.7 %gather_fusion.6 = bf16[4,2,2,128,256]{4,3,2,1,0:T(8,128)(2,1)} fusion(bf16[2,2,6,128,256]{4,3,2,1,0:T(8,128)(2,1)S(1)} %pad_maximum_fusion.3, s32[1024]{0:T(1024)S(1)} %pad_clamp_fusion.2), kind=kCustom, calls=%fused_computation.6.clone | custom fusion | bytes 2097168 | tf_op jit(solution)/shard_map/jit(_take)/gather | solution.py:55
  88.8 8.5 %fusion.11 = (bf16[1,2,6,128,256]{4,3,2,1,0:T(8,128)(2,1)S(1)}, bf16[1,2,6,128,256]{4,3,2,1,0:T(8,128)(2,1)S(1)}, bf16[1,2,6,128,256]{4,3,2,1,0:T(8,128)(2,1)}, bf16[1,2,6,128,256]{4,3,2,1,0:T(8,128)(2,1)}) fusion(f32[2,2,6,128,256]{4,3,2,1,0:T(8,128)} %get-tuple-element.25, f32[2,2,6,128,256]{4,3,2,1,0:T(8,128)} %get-tuple-element.26, f32[]{:T(128)} %bitcast.29, ...), kind=kLoop, calls=%fused_computation.36 | loop fusion | flops 6291456 | bytes 15728656 | tf_op jit(solution)/shard_map/convert.4
  97.3 1.3 pad_maximum_fusion.2
  98.6 3.0 %gather_fusion.5 = bf16[4,2,2,128,256]{4,3,2,1,0:T(8,128)(2,1)} fusion(bf16[2,2,6,128,256]{4,3,2,1,0:T(8,128)(2,1)} %pad_maximum_fusion.2, s32[1024]{0:T(1024)S(1)} %pad_clamp_fusion), kind=kCustom, calls=%fused_computation.5.clone | custom fusion | bytes 2097168 | tf_op jit(solution)/shard_map/jit(_take)/gather | solution.py:55
  101.7 3.0 %gather_fusion.3 = bf16[4,2,2,128,256]{4,3,2,1,0:T(8,128)(2,1)} fusion(bf16[2,2,6,128,256]{4,3,2,1,0:T(8,128)(2,1)} %pad_maximum_fusion.2, s32[1024]{0:T(1024)S(1)} %pad_clamp_fusion.2), kind=kCustom, calls=%fused_computation.3.clone | custom fusion | bytes 2097168 | tf_op jit(solution)/shard_map/jit(_take)/gather | solution.py:55
  104.7 2.7 %pad_maximum_fusion.1 = bf16[2,2,6,128,256]{4,3,2,1,0:T(8,128)(2,1)} fusion(bf16[1,2,6,128,256]{4,3,2,1,0:T(8,128)(2,1)} %get-tuple-element.56, bf16[1,2,6,128,256]{4,3,2,1,0:T(8,128)(2,1)} %get-tuple-element.57), kind=kLoop, calls=%fused_computation.46 | loop fusion | flops 786432 | bytes 3145728 | tf_op jit(solution)/shard_map/stack | solution.py:39
  107.3 3.1 %gather_fusion.2 = bf16[4,2,2,128,256]{4,3,2,1,0:T(8,128)(2,1)} fusion(bf16[2,2,6,128,256]{4,3,2,1,0:T(8,128)(2,1)} %pad_maximum_fusion.1, s32[1024]{0:T(1024)S(1)} %pad_clamp_fusion), kind=kCustom, calls=%fused_computation.2.clone | custom fusion | bytes 2097168 | tf_op jit(solution)/shard_map/jit(_take)/gather | solution.py:55
  110.4 3.0 %gather_fusion = bf16[4,2,2,128,256]{4,3,2,1,0:T(8,128)(2,1)} fusion(bf16[2,2,6,128,256]{4,3,2,1,0:T(8,128)(2,1)} %pad_maximum_fusion.1, s32[1024]{0:T(1024)S(1)} %pad_clamp_fusion.2), kind=kCustom, calls=%fused_computation.clone | custom fusion | bytes 2097168 | tf_op jit(solution)/shard_map/jit(_take)/gather | solution.py:55
  113.5 1.6 %gather_fusion.10 = bf16[4,2,2,128,256]{4,3,2,1,0:T(8,128)(2,1)} fusion(bf16[2,2,6,128,256]{4,3,2,1,0:T(8,128)(2,1)S(1)} %pad_maximum_fusion.4, s32[1024]{0:T(1024)S(1)} %pad_clamp_fusion.1), kind=kCustom, calls=%fused_computation.10.clone | custom fusion | bytes 2097168 | tf_op jit(solution)/shard_map/jit(_take)/gather | solution.py:55
  115.1 1.6 %gather_fusion.7 = bf16[4,2,2,128,256]{4,3,2,1,0:T(8,128)(2,1)} fusion(bf16[2,2,6,128,256]{4,3,2,1,0:T(8,128)(2,1)S(1)} %pad_maximum_fusion.3, s32[1024]{0:T(1024)S(1)} %pad_clamp_fusion.1), kind=kCustom, calls=%fused_computation.7.clone | custom fusion | bytes 2097168 | tf_op jit(solution)/shard_map/jit(_take)/gather | solution.py:55
  116.7 1.6 %gather_fusion.4 = bf16[4,2,2,128,256]{4,3,2,1,0:T(8,128)(2,1)} fusion(bf16[2,2,6,128,256]{4,3,2,1,0:T(8,128)(2,1)S(1)} %copy-done, s32[1024]{0:T(1024)S(1)} %pad_clamp_fusion.1), kind=kCustom, calls=%fused_computation.4.clone | custom fusion | bytes 2097168 | tf_op jit(solution)/shard_map/jit(_take)/gather | solution.py:55
  118.9 2.7 %bitcast_select_fusion = (bf16[2,2,4,128,256]{4,3,1,0,2:T(8,128)(2,1)S(1)}, bf16[2,2,4,128,256]{4,3,1,0,2:T(8,128)(2,1)S(1)}, bf16[2,2,4,128,256]{4,3,1,0,2:T(8,128)(2,1)S(1)}, bf16[2,2,4,128,256]{4,3,1,0,2:T(8,128)(2,1)S(1)}) fusion(bf16[4,2,2,128,256]{4,3,2,1,0:T(8,128)(2,1)} %gather_fusion.11, pred[4]{0:T(512)(128)(4,1)S(1)} %get-tuple-element.52, ...), kind=kLoop, calls=%fused_computation.71 | loop fusion | flops 4194304 | bytes 8388616 | tf_op jit(solution)/shard_map/jit(_where)/select_n | solution.py:56
  136.0 1.7 %add_convert_fusion = bf16[2,2,4,128,2,128]{3,5,4,2,1,0:T(8,128)(2,1)S(1)} fusion(f32[2,2,4,128,2,128]{3,5,4,2,1,0:T(8,128)S(1)} %fusion.30, f32[2,2,4,128,2,128]{3,5,4,2,1,0:T(8,128)S(1)} %fusion.33, f32[2,2,4,128,2,128]{3,5,4,2,1,0:T(8,128)S(1)} %fusion.36, f32[2,2,4,128,2,128]{3,5,4,2,1,0:T(8,128)S(1)} %fusion.39, ...), kind=kOutput, calls=%fused_computation.13 | convolution fusion | flops 140509184 | bytes 25198592 | tf_op jit(solution)/shard_map/...psq,rq->...psr/dot_general | solution.py:25
  137.7 1.3 copy.30
  (63 shorter events, 18.5 us)
Async XLA Ops:
  0.0 26.2 %collective-permute-start = (bf16[2,2,4,128,256]{4,3,2,1,0:T(8,128)(2,1)}, bf16[2,2,4,128,256]{4,3,2,1,0:T(8,128)(2,1)}, u32[]{:S(2)}, u32[]{:S(2)}) collective-permute-start(bf16[2,2,4,128,256]{4,3,2,1,0:T(8,128)(2,1)} %param.7), channel_id=1, source_target_pairs={{0,8},{8,16},{16,24},{24,0},{1,9},{9,17},{17,25},{25,1},{2,10},{10... | collective-permute-start | bytes 3145736 | tf_op jit(solution)/shard_map/ppermute | solution.py:14
  2.0 46.6 %collective-permute-start.1 = (bf16[2,2,4,128,256]{4,3,2,1,0:T(8,128)(2,1)}, bf16[2,2,4,128,256]{4,3,2,1,0:T(8,128)(2,1)}, u32[]{:S(2)}, u32[]{:S(2)}) collective-permute-start(bf16[2,2,4,128,256]{4,3,2,1,0:T(8,128)(2,1)} %param.7), channel_id=1, source_target_pairs={{8,0},{16,8},{24,16},{0,24},{9,1},{17,9},{25,17},{1,25},{10,2},{18... | collective-permute-start | bytes 3145736 | tf_op jit(solution)/shard_map/ppermute | solution.py:15
  14.6 12.9 %copy-start.10 = (bf16[2,2,4,128,256]{4,3,2,1,0:T(8,128)(2,1)S(1)}, bf16[2,2,4,128,256]{4,3,2,1,0:T(8,128)(2,1)}, u32[]{:S(2)}) copy-start(bf16[2,2,4,128,256]{4,3,2,1,0:T(8,128)(2,1)} %param.7) | copy-start | bytes 3145732
  49.9 10.3 %copy-start.11 = (s32[4,3]{1,0:T(4,128)S(1)}, s32[4,3]{1,0:T(4,128)}, u32[]{:S(2)}) copy-start(s32[4,3]{1,0:T(4,128)} %param.11) | copy-start | bytes 148
  51.2 13.9 %collective-permute-start.2 = (bf16[2,6,1,128,256]{4,3,2,1,0:T(8,128)(2,1)}, bf16[2,6,1,128,256]{4,3,2,1,0:T(8,128)(2,1)}, u32[]{:S(2)}, u32[]{:S(2)}) collective-permute-start(bf16[2,6,1,128,256]{4,3,2,1,0:T(8,128)(2,1)} %get-tuple-element.28), channel_id=1, source_target_pairs={{0,1},{1,2},{2,3},{3,4},{4,5},{5,6},{6,7},{8,9},{9,10},{10,11},{11... | collective-permute-start | bytes 2359304 | tf_op jit(solution)/shard_map/ppermute | solution.py:14
  55.8 13.6 %collective-permute-start.3 = (bf16[2,6,1,128,256]{4,3,2,1,0:T(8,128)(2,1)}, bf16[2,6,1,128,256]{4,3,2,1,0:T(8,128)(2,1)}, u32[]{:S(2)}, u32[]{:S(2)}) collective-permute-start(bf16[2,6,1,128,256]{4,3,2,1,0:T(8,128)(2,1)} %get-tuple-element.29), channel_id=1, source_target_pairs={{1,0},{2,1},{3,2},{4,3},{5,4},{6,5},{7,6},{9,8},{10,9},{11,10},{12... | collective-permute-start | bytes 2359304 | tf_op jit(solution)/shard_map/ppermute | solution.py:15
  115.1 1.6 %copy-start = (bf16[2,2,6,128,256]{4,3,2,1,0:T(8,128)(2,1)S(1)}, bf16[2,2,6,128,256]{4,3,2,1,0:T(8,128)(2,1)}, u32[]{:S(2)}) copy-start(bf16[2,2,6,128,256]{4,3,2,1,0:T(8,128)(2,1)} %pad_maximum_fusion.2) | copy-start | bytes 4718596
  116.7 1.6 %copy-start.1 = (bf16[2,2,6,128,256]{4,3,2,1,0:T(8,128)(2,1)S(1)}, bf16[2,2,6,128,256]{4,3,2,1,0:T(8,128)(2,1)}, u32[]{:S(2)}) copy-start(bf16[2,2,6,128,256]{4,3,2,1,0:T(8,128)(2,1)} %pad_maximum_fusion.1) | copy-start | bytes 4718596
  118.9 2.8 %copy-start.9 = (bf16[4,3,128,128]{3,2,1,0:T(8,128)(2,1)S(1)}, bf16[4,3,128,128]{3,2,1,0:T(8,128)(2,1)}, u32[]{:S(2)}) copy-start(bf16[4,3,128,128]{3,2,1,0:T(8,128)(2,1)} %param.8) | copy-start | bytes 1179652
  123.9 1.2 copy-start.8
  124.3 1.3 copy-start.3
  124.4 1.6 %copy-start.4 = (bf16[4,2,2,128,256]{4,3,2,1,0:T(8,128)(2,1)S(1)}, bf16[4,2,2,128,256]{4,3,2,1,0:T(8,128)(2,1)}, u32[]{:S(2)}) copy-start(bf16[4,2,2,128,256]{4,3,2,1,0:T(8,128)(2,1)} %gather_fusion.6) | copy-start | bytes 3145732
  124.4 1.9 %copy-start.7 = (bf16[4,2,2,128,256]{4,3,2,1,0:T(8,128)(2,1)S(1)}, bf16[4,2,2,128,256]{4,3,2,1,0:T(8,128)(2,1)}, u32[]{:S(2)}) copy-start(bf16[4,2,2,128,256]{4,3,2,1,0:T(8,128)(2,1)} %gather_fusion.3) | copy-start | bytes 3145732
  130.0 1.2 copy-start.2
  130.0 1.5 %copy-start.5 = (bf16[4,2,2,128,256]{4,3,2,1,0:T(8,128)(2,1)S(1)}, bf16[4,2,2,128,256]{4,3,2,1,0:T(8,128)(2,1)}, u32[]{:S(2)}) copy-start(bf16[4,2,2,128,256]{4,3,2,1,0:T(8,128)(2,1)} %gather_fusion.7) | copy-start | bytes 3145732
  130.0 1.8 %copy-start.6 = (bf16[4,2,2,128,256]{4,3,2,1,0:T(8,128)(2,1)S(1)}, bf16[4,2,2,128,256]{4,3,2,1,0:T(8,128)(2,1)}, u32[]{:S(2)}) copy-start(bf16[4,2,2,128,256]{4,3,2,1,0:T(8,128)(2,1)} %gather_fusion.4) | copy-start | bytes 3145732
where the time goes:
time: 140 us; the launch traced here: 139 us
  waiting for transfers between devices  38.9 us (28%)
  local copies, waits for them, and re-layouts  35 us (25%)
  other arithmetic  30.5 us (22%)
  between operations  13.1 us (9%)
  matrix products  12 us (9%)
  starting transfers between devices  9.55 us (7%)
    ppermute x2, waiting for transfers between devices, with_halo(): after = lax.ppermute(first, axis, down)  25.4 us
    gather x12, local copies, waits for them, and re-layouts, owner_terms(): picked = jnp.take(mixture, local_at, axis=2)  24 us
    ppermute x2, waiting for transfers between devices, with_halo(): before = lax.ppermute(last, axis, up)  13.5 us
    another operation x2, other arithmetic  12.6 us
    ppermute x2, starting transfers between devices, with_halo(): before = lax.ppermute(last, axis, up)  6.67 us
    dot_general x12, matrix products, couple(): jnp.einsum('...psq,rq->...psr', shaped, matrix, preferred_element_type=jn...  6.36 us
    dot_general x12, matrix products, couple(): jnp.einsum('pq,...qr->...pr', matrix, blocks, preferred_element_type=jnp....  5.63 us
    another operation x4, other arithmetic, mixture_of(): return jnp.stack([lesser, greater]).astype(jnp.bfloat16)  5.61 us
  transfers between devices with their start and end apart: 4, of which 4 were waited for; matrix products, arithmetic and copies ran while one was open for 4% of the time, Pallas kernels for 0%

commit v1 on v0

v1 whole, which is shorter than its diff:
```python
import functools

import jax
import jax.numpy as jnp
from jax import lax
from jax.experimental import pallas as pl
from jax.experimental.pallas import tpu as pltpu
from jax.sharding import PartitionSpec as P


def partial_body(part, blocks, halo, *refs):
    if halo:
        occ, off, nbr, c_ref, g_ref, b_ref, a_ref = refs[:7]
    else:
        occ, off, nbr, c_ref, g_ref = refs[:5]
    far, near, mine, rows, cols, half, acc = refs[-7:]
    modes, slots, size = c_ref.shape[:3]
    count = g_ref.shape[1]
    owned = nbr.shape[0]
    first = lax.axis_index("slab") * owned
    odd = lax.rem(lax.axis_index("energy"), 2)
    for m in range(modes):
        for k in range(slots):
            c = c_ref[m, k]
            rows[k, m * size : (m + 1) * size, :] = c
            cols[m, :, k * size : (k + 1) * size] = c

    def per_block(i, carry):
        a = blocks[0] + (blocks[-1] - blocks[0]) * i
        acc[...] = jnp.zeros_like(acc)
        for e in range(count):
            for k in range(slots):
                v = nbr[a, k]
                at = v - first
                src = g_ref[0, e, jnp.clip(at, 0, owned - 1)]
                if halo:
                    src = jnp.where(at < 0, b_ref[0, e, 0], src)
                    src = jnp.where(at >= owned, a_ref[0, e, 0], src)
                src = jnp.where(v >= 0, src, jnp.zeros_like(src))
                r = jnp.dot(rows[k], src, preferred_element_type=jnp.float32)
                r = r.astype(jnp.bfloat16)
                for m in range(modes):
                    for s in range(2):
                        h = (e * 2 + s) * size
                        half[m, h : h + size, k * size : (k + 1) * size] = r[
                            m * size : (m + 1) * size, s * size : (s + 1) * size
                        ]
        for m in range(modes):
            y = lax.dot_general(
                half[m], cols[m], (((1,), (1,)), ((), ())), preferred_element_type=jnp.float32
            )
            o = off[m]
            n = occ[m]
            down, up = (n + 1.0, n) if part == 0 else (n, n + 1.0)
            for e in range(count):
                for s in range(2):
                    h = (e * 2 + s) * size
                    ys = y[h : h + size]
                    acc[e - o + count, :, s * size : (s + 1) * size] += down * ys
                    acc[e + o + count, :, s * size : (s + 1) * size] += up * ys
        for j in range(count):
            far[0, j, i] = acc[2 * count * odd + j].astype(jnp.bfloat16)
            near[0, j, i] = acc[2 * count * (1 - odd) + j]
            mine[0, j, i] = acc[count + j]
        return carry

    lax.fori_loop(0, len(blocks), per_block, 0)


def whole(shape):
    return pl.BlockSpec(shape, lambda i: (0,) * len(shape))


def partial(part, blocks, greens, coupling, occupation, offsets, neighbours, edges=()):
    specs = [pl.BlockSpec(memory_space=pltpu.SMEM)] * 3 + [whole(coupling.shape)]
    for array in (greens,) + tuple(edges):
        specs.append(pl.BlockSpec((1,) + array.shape[1:], lambda i: (part, 0, 0, 0, 0)))
    modes, slots, size = coupling.shape[:3]
    count = greens.shape[1]
    n = len(blocks)
    shape = (1, count, n) + greens.shape[3:]
    return pl.pallas_call(
        functools.partial(partial_body, part, blocks, len(edges) > 0),
        out_shape=[
            jax.ShapeDtypeStruct(shape, jnp.bfloat16),
            jax.ShapeDtypeStruct(shape, jnp.float32),
            jax.ShapeDtypeStruct(shape, jnp.float32),
        ],
        grid=(1,),
        in_specs=specs,
        out_specs=[whole(shape)] * 3,
        scratch_shapes=[
            pltpu.VMEM((slots, modes * size, size), jnp.bfloat16),
            pltpu.VMEM((modes, size, slots * size), jnp.bfloat16),
            pltpu.VMEM((modes, count * 2 * size, slots * size), jnp.bfloat16),
            pltpu.VMEM((3 * count, size, 2 * size), jnp.float32),
        ],
        compiler_params=pltpu.CompilerParams(vmem_limit_bytes=32 << 20),
        cost_estimate=pl.CostEstimate(
            flops=8 * count * n * modes * slots * size * size * size,
            bytes_accessed=4 << 20,
            transcendentals=0,
        ),
    )(occupation, offsets, neighbours, coupling, greens, *edges)


def finish_body(mine, received, *refs):
    out = refs[-1]
    out[...] = (mine[...] + received[...].astype(jnp.float32)).astype(jnp.bfloat16)


def finish(part, blocks, mine, received, shape, out):
    block = (1, mine.shape[1], 1) + mine.shape[3:]
    spec = pl.BlockSpec(block, lambda i: (0, 0, i, 0, 0))
    step = blocks[-1] - blocks[0]
    return pl.pallas_call(
        finish_body,
        out_shape=jax.ShapeDtypeStruct(shape, jnp.bfloat16),
        grid=(len(blocks),),
        in_specs=[spec, spec] + ([pl.BlockSpec(memory_space=pl.ANY)] if out is not None else []),
        out_specs=pl.BlockSpec(block, lambda i: (part, 0, blocks[0] + i * step, 0, 0)),
        input_output_aliases={2: 0} if out is not None else {},
        cost_estimate=pl.CostEstimate(flops=mine.size, bytes_accessed=8 * mine.size, transcendentals=0),
    )(mine, received, *([out] if out is not None else []))


def on_device(greens, coupling, occupation, offsets, neighbours):
    slabs = lax.axis_size("slab")
    owned = greens.shape[2]
    across = [(i, i ^ 1) for i in range(4)]
    along = [(i, i ^ 2) for i in range(4)]
    upward = [(i, i + 1) for i in range(slabs - 1)]
    downward = [(i + 1, i) for i in range(slabs - 1)]
    before = lax.ppermute(greens[:, :, owned - 1 :], "slab", upward)
    after = lax.ppermute(greens[:, :, :1], "slab", downward)
    inner, outer = tuple(range(1, owned - 1)), (0, owned - 1)
    chunks = [(1, inner), (0, inner), (1, outer), (0, outer)]
    args = (greens, coupling, occupation, offsets, neighbours)
    pieces = []
    for part, blocks in chunks:
        edges = (before, after) if blocks == outer else ()
        far, near, mine = partial(part, blocks, *args, edges)
        pieces.append((near, mine, lax.ppermute(far, "energy", along)))
    out = None
    for (part, blocks), (near, mine, relayed) in zip(chunks, pieces):
        both = (near + relayed.astype(jnp.float32)).astype(jnp.bfloat16)
        received = lax.ppermute(both, "energy", across)
        out = finish(part, blocks, mine, received, greens.shape, out)
    return out


def solution(mesh):
    in_specs = (P(None, "energy", "slab", None, None), P(), P(), P(), P("slab", None))
    out_specs = P(None, "energy", "slab", None, None)
    return jax.shard_map(
        on_device, mesh=mesh, in_specs=in_specs, out_specs=out_specs, check_vma=False
    )
```

time: 140 us -> 50.8 us (0.36)
  the two profiles are of different devices: /device:TPU:1 before, /device:TPU:8 now
where the time goes in v1:
time: 50.8 us; the launch traced here: 50.3 us
  Pallas kernels  18.8 us (37%)
  starting transfers between devices  13.2 us (26%)
  waiting for transfers between devices  10.1 us (20%)
  local copies, waits for them, and re-layouts  7.88 us (16%)
    pallas_call x4, Pallas kernels, partial(): pl.pallas_call(functools.partial(partial_body, part, blocks, len(edges) >...  11.6 us
    ppermute x4, waiting for transfers between devices, on_device(): pieces.append((near, mine, lax.ppermute(far, 'energy', along)))  8.21 us
    unnamed x26, local copies, waits for them, and re-layouts  7.85 us
    pallas_call x4, Pallas kernels, finish(): pl.pallas_call(finish_body, out_shape=jax.ShapeDtypeStruct(shape, jnp.bfl...  7.24 us
    ppermute x4, starting transfers between devices, on_device(): pieces.append((near, mine, lax.ppermute(far, 'energy', along)))  4.39 us
    ppermute x1, starting transfers between devices, on_device(): after = lax.ppermute(greens[:, :, :1], 'slab', downward)  3.64 us
    ppermute x4, starting transfers between devices, on_device(): received = lax.ppermute(both, 'energy', across)  3.23 us
    ppermute x1, starting transfers between devices, on_device(): before = lax.ppermute(greens[:, :, owned - 1:], 'slab', upward)  1.92 us
  transfers between devices with their start and end apart: 10, of which 3 were waited for; matrix products, arithmetic and copies ran while one was open for 1% of the time, Pallas kernels for 28%

profile of v1, /device:TPU:8, one launch (start us, length us, event | category | flops | bytes accessed | tf_op | source)
XLA Modules:
  0.0 50.3 jit_solution(8054059316409181049)
XLA Ops:
  0.0 1.2 %copy-done.4 = bf16[2,2,4,128,256]{4,3,2,1,0:T(8,128)(2,1)S(1)} copy-done((bf16[2,2,4,128,256]{4,3,2,1,0:T(8,128)(2,1)S(1)}, bf16[2,2,4,128,256]{4,3,2,1,0:T(8,128)(2,1)}, u32[]{:S(2)}) %copy-start.4) | copy-done | bytes 1048600
  1.2 1.0 %copy-done.5 = bf16[4,3,128,128]{3,2,1,0:T(8,128)(2,1)S(1)} copy-done((bf16[4,3,128,128]{3,2,1,0:T(8,128)(2,1)S(1)}, bf16[4,3,128,128]{3,2,1,0:T(8,128)(2,1)}, u32[]{:S(2)}) %copy-start.5) | copy-done | bytes 393240
  2.2 0.7 %copy-done.6 = s32[4,3]{1,0:T(4,128)S(1)} copy-done((s32[4,3]{1,0:T(4,128)S(1)}, s32[4,3]{1,0:T(4,128)}, u32[]{:S(2)}) %copy-start.6) | copy-done | bytes 72
  2.9 0.7 %copy-done.7 = f32[4]{0:T(128)S(1)} copy-done((f32[4]{0:T(128)S(1)}, f32[4]{0:T(128)}, u32[]{:S(2)}) %copy-start.7) | copy-done | bytes 40
  3.6 0.7 %copy-done.8 = s32[4]{0:T(128)S(1)} copy-done((s32[4]{0:T(128)S(1)}, s32[4]{0:T(128)}, u32[]{:S(2)}) %copy-start.8) | copy-done | bytes 40
  4.2 2.9 %shard_map.58 = (bf16[1,2,2,128,256]{4,3,2,1,0:T(8,128)(2,1)S(1)}, f32[1,2,2,128,256]{4,3,2,1,0:T(8,128)S(1)}, f32[1,2,2,128,256]{4,3,2,1,0:T(8,128)S(1)}) custom-call(f32[4]{0:T(128)S(1)} %copy-done.7, s32[4]{0:T(128)S(1)} %copy-done.8, s32[4,3]{1,0:T(4,128)S(1)} %copy-done.6, bf16[4,3,128,128]{3,2,1,0:T(8,128)(2,1)S(1)} %copy-done.5, ...), custom_call_target="tpu_custom_call" | custom-call | flops 805306368 | bytes 4194304 | tf_op jit(solution)/shard_map/pallas_call | solution.py:82
  7.1 1.6 %collective-permute-start.8 = (bf16[1,2,2,128,256]{4,3,2,1,0:T(8,128)(2,1)S(1)}, bf16[1,2,2,128,256]{4,3,2,1,0:T(8,128)(2,1)S(1)}, u32[]{:S(2)}, u32[]{:S(2)}) collective-permute-start(bf16[1,2,2,128,256]{4,3,2,1,0:T(8,128)(2,1)S(1)} %get-tuple-element.28), channel_id=1, source_target_pairs={{0,16},{8,24},{16,0},{24,8},{1,17},{9,25},{17,1},{25,9},{2,18},{10... | collective-permute-start | bytes 786440 | tf_op jit(solution)/shard_map/ppermute | solution.py:143
  8.8 1.9 %collective-permute-start = (bf16[2,2,1,128,256]{4,3,2,1,0:T(8,128)(2,1)S(1)}, bf16[2,2,1,128,256]{4,3,2,1,0:T(8,128)(2,1)S(1)}, u32[]{:S(2)}, u32[]{:S(2)}) collective-permute-start(bf16[2,2,1,128,256]{4,3,2,1,0:T(8,128)(2,1)S(1)} %get-tuple-element.30), channel_id=1, source_target_pairs={{0,1},{1,2},{2,3},{3,4},{4,5},{5,6},{6,7},{8,9},{9,10},{10,11},{11... | collective-permute-start | bytes 786440 | tf_op jit(solution)/shard_map/ppermute | solution.py:134
  10.7 3.6 %collective-permute-start.1 = (bf16[2,2,1,128,256]{4,3,2,1,0:T(8,128)(2,1)S(1)}, bf16[2,2,1,128,256]{4,3,2,1,0:T(8,128)(2,1)S(1)}, u32[]{:S(2)}, u32[]{:S(2)}) collective-permute-start(bf16[2,2,1,128,256]{4,3,2,1,0:T(8,128)(2,1)S(1)} %get-tuple-element.29), channel_id=1, source_target_pairs={{1,0},{2,1},{3,2},{4,3},{5,4},{6,5},{7,6},{9,8},{10,9},{11,10},{12... | collective-permute-start | bytes 786440 | tf_op jit(solution)/shard_map/ppermute | solution.py:135
  14.3 2.9 %shard_map.57 = (bf16[1,2,2,128,256]{4,3,2,1,0:T(8,128)(2,1)S(1)}, f32[1,2,2,128,256]{4,3,2,1,0:T(8,128)S(1)}, f32[1,2,2,128,256]{4,3,2,1,0:T(8,128)S(1)}) custom-call(f32[4]{0:T(128)S(1)} %copy-done.7, s32[4]{0:T(128)S(1)} %copy-done.8, s32[4,3]{1,0:T(4,128)S(1)} %copy-done.6, bf16[4,3,128,128]{3,2,1,0:T(8,128)(2,1)S(1)} %copy-done.5, ...), custom_call_target="tpu_custom_call" | custom-call | flops 805306368 | bytes 4194304 | tf_op jit(solution)/shard_map/pallas_call | solution.py:82
  17.3 0.7 %collective-permute-start.6 = (bf16[1,2,2,128,256]{4,3,2,1,0:T(8,128)(2,1)S(1)}, bf16[1,2,2,128,256]{4,3,2,1,0:T(8,128)(2,1)S(1)}, u32[]{:S(2)}, u32[]{:S(2)}) collective-permute-start(bf16[1,2,2,128,256]{4,3,2,1,0:T(8,128)(2,1)S(1)} %get-tuple-element.25), channel_id=1, source_target_pairs={{0,16},{8,24},{16,0},{24,8},{1,17},{9,25},{17,1},{25,9},{2,18},{10... | collective-permute-start | bytes 786440 | tf_op jit(solution)/shard_map/ppermute | solution.py:143
  18.0 1.6 %collective-permute-start.9 = (bf16[1,2,2,128,256]{4,3,2,1,0:T(8,128)(2,1)S(1)}, bf16[1,2,2,128,256]{4,3,2,1,0:T(8,128)(2,1)S(1)}, u32[]{:S(2)}, u32[]{:S(2)}) collective-permute-start(bf16[1,2,2,128,256]{4,3,2,1,0:T(8,128)(2,1)S(1)} %add_convert_fusion), channel_id=1, source_target_pairs={{0,8},{8,0},{16,24},{24,16},{1,9},{9,1},{17,25},{25,17},{2,10},{10... | collective-permute-start | bytes 786440 | tf_op jit(solution)/shard_map/ppermute | solution.py:147
  19.6 2.9 %shard_map.56 = (bf16[1,2,2,128,256]{4,3,2,1,0:T(8,128)(2,1)S(1)}, f32[1,2,2,128,256]{4,3,2,1,0:T(8,128)S(1)}, f32[1,2,2,128,256]{4,3,2,1,0:T(8,128)S(1)}) custom-call(f32[4]{0:T(128)S(1)} %copy-done.7, s32[4]{0:T(128)S(1)} %copy-done.8, s32[4,3]{1,0:T(4,128)S(1)} %copy-done.6, bf16[4,3,128,128]{3,2,1,0:T(8,128)(2,1)S(1)} %copy-done.5, ...), custom_call_target="tpu_custom_call" | custom-call | flops 805306368 | bytes 4194304 | tf_op jit(solution)/shard_map/pallas_call | solution.py:82
  22.5 0.8 %copy-done.3 = f32[1,2,2,128,256]{4,3,2,1,0:T(8,128)} copy-done((f32[1,2,2,128,256]{4,3,2,1,0:T(8,128)}, f32[1,2,2,128,256]{4,3,2,1,0:T(8,128)S(1)}, u32[]{:S(2)}) %copy-start.3) | copy-done | bytes 524312
  23.3 1.4 %collective-permute-start.4 = (bf16[1,2,2,128,256]{4,3,2,1,0:T(8,128)(2,1)S(1)}, bf16[1,2,2,128,256]{4,3,2,1,0:T(8,128)(2,1)S(1)}, u32[]{:S(2)}, u32[]{:S(2)}) collective-permute-start(bf16[1,2,2,128,256]{4,3,2,1,0:T(8,128)(2,1)S(1)} %get-tuple-element.22), channel_id=1, source_target_pairs={{0,16},{8,24},{16,0},{24,8},{1,17},{9,25},{17,1},{25,9},{2,18},{10... | collective-permute-start | bytes 786440 | tf_op jit(solution)/shard_map/ppermute | solution.py:143
  24.7 2.9 %shard_map.55 = (bf16[1,2,2,128,256]{4,3,2,1,0:T(8,128)(2,1)S(1)}, f32[1,2,2,128,256]{4,3,2,1,0:T(8,128)S(1)}, f32[1,2,2,128,256]{4,3,2,1,0:T(8,128)S(1)}) custom-call(f32[4]{0:T(128)S(1)} %copy-done.7, s32[4]{0:T(128)S(1)} %copy-done.8, s32[4,3]{1,0:T(4,128)S(1)} %copy-done.6, bf16[4,3,128,128]{3,2,1,0:T(8,128)(2,1)S(1)} %copy-done.5, ...), custom_call_target="tpu_custom_call" | custom-call | flops 805306368 | bytes 4194304 | tf_op jit(solution)/shard_map/pallas_call | solution.py:82
  27.6 0.7 %collective-permute-start.2 = (bf16[1,2,2,128,256]{4,3,2,1,0:T(8,128)(2,1)S(1)}, bf16[1,2,2,128,256]{4,3,2,1,0:T(8,128)(2,1)S(1)}, u32[]{:S(2)}, u32[]{:S(2)}) collective-permute-start(bf16[1,2,2,128,256]{4,3,2,1,0:T(8,128)(2,1)S(1)} %get-tuple-element.19), channel_id=1, source_target_pairs={{0,16},{8,24},{16,0},{24,8},{1,17},{9,25},{17,1},{25,9},{2,18},{10... | collective-permute-start | bytes 786440 | tf_op jit(solution)/shard_map/ppermute | solution.py:143
  28.4 0.6 %collective-permute-start.7 = (bf16[1,2,2,128,256]{4,3,2,1,0:T(8,128)(2,1)S(1)}, bf16[1,2,2,128,256]{4,3,2,1,0:T(8,128)(2,1)S(1)}, u32[]{:S(2)}, u32[]{:S(2)}) collective-permute-start(bf16[1,2,2,128,256]{4,3,2,1,0:T(8,128)(2,1)S(1)} %add_convert_fusion.1), channel_id=1, source_target_pairs={{0,8},{8,0},{16,24},{24,16},{1,9},{9,1},{17,25},{25,17},{2,10},{10... | collective-permute-start | bytes 786440 | tf_op jit(solution)/shard_map/ppermute | solution.py:147
  29.0 3.4 %collective-permute-done.4 = bf16[1,2,2,128,256]{4,3,2,1,0:T(8,128)(2,1)S(1)} collective-permute-done((bf16[1,2,2,128,256]{4,3,2,1,0:T(8,128)(2,1)S(1)}, bf16[1,2,2,128,256]{4,3,2,1,0:T(8,128)(2,1)S(1)}, u32[]{:S(2)}, u32[]{:S(2)}) %collective-permute-start.4) | collective-permute-done | bytes 262176 | tf_op jit(solution)/shard_map/ppermute | solution.py:143
  32.4 0.1 add_convert_fusion.2
  32.5 0.3 collective-permute-start.5
  32.8 4.8 %collective-permute-done.2 = bf16[1,2,2,128,256]{4,3,2,1,0:T(8,128)(2,1)S(1)} collective-permute-done((bf16[1,2,2,128,256]{4,3,2,1,0:T(8,128)(2,1)S(1)}, bf16[1,2,2,128,256]{4,3,2,1,0:T(8,128)(2,1)S(1)}, u32[]{:S(2)}, u32[]{:S(2)}) %collective-permute-start.2) | collective-permute-done | bytes 262176 | tf_op jit(solution)/shard_map/ppermute | solution.py:143
  37.7 0.8 %collective-permute-start.3 = (bf16[1,2,2,128,256]{4,3,2,1,0:T(8,128)(2,1)S(1)}, bf16[1,2,2,128,256]{4,3,2,1,0:T(8,128)(2,1)S(1)}, u32[]{:S(2)}, u32[]{:S(2)}) collective-permute-start(bf16[1,2,2,128,256]{4,3,2,1,0:T(8,128)(2,1)S(1)} %add_convert_fusion.3), channel_id=1, source_target_pairs={{0,8},{8,0},{16,24},{24,16},{1,9},{9,1},{17,25},{25,17},{2,10},{10... | collective-permute-start | bytes 786440 | tf_op jit(solution)/shard_map/ppermute | solution.py:147
  38.4 0.7 %copy-done.9 = bf16[1,2,2,128,256]{4,3,2,1,0:T(8,128)(2,1)} copy-done((bf16[1,2,2,128,256]{4,3,2,1,0:T(8,128)(2,1)}, bf16[1,2,2,128,256]{4,3,2,1,0:T(8,128)(2,1)S(1)}, u32[]{:S(2)}) %copy-start.9) | copy-done | bytes 262168
  39.1 1.8 %shard_map.59.refs_0_ = bf16[2,2,4,128,256]{4,3,2,1,0:T(8,128)(2,1)} custom-call(f32[1,2,2,128,256]{4,3,2,1,0:T(8,128)} %copy-done, bf16[1,2,2,128,256]{4,3,2,1,0:T(8,128)(2,1)} %copy-done.9), custom_call_target="tpu_custom_call" | custom-call | flops 131072 | bytes 1048576 | tf_op jit(solution)/shard_map/pallas_call | solution.py:116
  41.0 0.7 %copy-done.10 = bf16[1,2,2,128,256]{4,3,2,1,0:T(8,128)(2,1)} copy-done((bf16[1,2,2,128,256]{4,3,2,1,0:T(8,128)(2,1)}, bf16[1,2,2,128,256]{4,3,2,1,0:T(8,128)(2,1)S(1)}, u32[]{:S(2)}) %copy-start.10) | copy-done | bytes 262168
  41.7 1.8 %shard_map.60.refs_0_ = bf16[2,2,4,128,256]{4,3,2,1,0:T(8,128)(2,1)} custom-call(f32[1,2,2,128,256]{4,3,2,1,0:T(8,128)} %copy-done.1, bf16[1,2,2,128,256]{4,3,2,1,0:T(8,128)(2,1)} %copy-done.10, bf16[2,2,4,128,256]{4,3,2,1,0:T(8,128)(2,1)} %shard_map.59.refs_0_), custom_call_target="tpu_custom_call", output_to_operand_aliasing={{}: (2, {})} | custom-call | flops 131072 | bytes 1048576 | tf_op jit(solution)/shard_map/pallas_call | solution.py:116
  43.5 0.7 %copy-done.11 = bf16[1,2,2,128,256]{4,3,2,1,0:T(8,128)(2,1)} copy-done((bf16[1,2,2,128,256]{4,3,2,1,0:T(8,128)(2,1)}, bf16[1,2,2,128,256]{4,3,2,1,0:T(8,128)(2,1)S(1)}, u32[]{:S(2)}) %copy-start.11) | copy-done | bytes 262168
  44.2 1.8 %shard_map.61.refs_0_ = bf16[2,2,4,128,256]{4,3,2,1,0:T(8,128)(2,1)} custom-call(f32[1,2,2,128,256]{4,3,2,1,0:T(8,128)} %copy-done.3, bf16[1,2,2,128,256]{4,3,2,1,0:T(8,128)(2,1)} %copy-done.11, bf16[2,2,4,128,256]{4,3,2,1,0:T(8,128)(2,1)} %shard_map.60.refs_0_), custom_call_target="tpu_custom_call", output_to_operand_aliasing={{}: (2, {})} | custom-call | flops 131072 | bytes 1048576 | tf_op jit(solution)/shard_map/pallas_call | solution.py:116
  46.0 1.8 %collective-permute-done.3.received = bf16[1,2,2,128,256]{4,3,2,1,0:T(8,128)(2,1)S(1)} collective-permute-done((bf16[1,2,2,128,256]{4,3,2,1,0:T(8,128)(2,1)S(1)}, bf16[1,2,2,128,256]{4,3,2,1,0:T(8,128)(2,1)S(1)}, u32[]{:S(2)}, u32[]{:S(2)}) %collective-permute-start.3) | collective-permute-done | bytes 262176 | tf_op jit(solution)/shard_map/ppermute | solution.py:147
  47.8 0.7 %copy-done.12 = bf16[1,2,2,128,256]{4,3,2,1,0:T(8,128)(2,1)} copy-done((bf16[1,2,2,128,256]{4,3,2,1,0:T(8,128)(2,1)}, bf16[1,2,2,128,256]{4,3,2,1,0:T(8,128)(2,1)S(1)}, u32[]{:S(2)}) %copy-start.12) | copy-done | bytes 262168
  48.5 1.8 %shard_map.62 = bf16[2,2,4,128,256]{4,3,2,1,0:T(8,128)(2,1)} custom-call(f32[1,2,2,128,256]{4,3,2,1,0:T(8,128)} %copy-done.2, bf16[1,2,2,128,256]{4,3,2,1,0:T(8,128)(2,1)} %copy-done.12, bf16[2,2,4,128,256]{4,3,2,1,0:T(8,128)(2,1)} %shard_map.61.refs_0_), custom_call_target="tpu_custom_call", output_to_operand_aliasing={{}: (2, {})} | custom-call | flops 131072 | bytes 1048576 | tf_op jit(solution)/shard_map/pallas_call | solution.py:116
  (27 shorter events, 0.3 us)
Async XLA Ops:
  0.0 1.2 %copy-start.4 = (bf16[2,2,4,128,256]{4,3,2,1,0:T(8,128)(2,1)S(1)}, bf16[2,2,4,128,256]{4,3,2,1,0:T(8,128)(2,1)}, u32[]{:S(2)}) copy-start(bf16[2,2,4,128,256]{4,3,2,1,0:T(8,128)(2,1)} %refs_4_.7) | copy-start | bytes 3145732
  1.2 1.0 %copy-start.5 = (bf16[4,3,128,128]{3,2,1,0:T(8,128)(2,1)S(1)}, bf16[4,3,128,128]{3,2,1,0:T(8,128)(2,1)}, u32[]{:S(2)}) copy-start(bf16[4,3,128,128]{3,2,1,0:T(8,128)(2,1)} %refs_3_.7) | copy-start | bytes 1179652
  2.2 0.7 %copy-start.6 = (s32[4,3]{1,0:T(4,128)S(1)}, s32[4,3]{1,0:T(4,128)}, u32[]{:S(2)}) copy-start(s32[4,3]{1,0:T(4,128)} %refs_2_.7) | copy-start | bytes 148
  2.9 0.7 %copy-start.7 = (f32[4]{0:T(128)S(1)}, f32[4]{0:T(128)}, u32[]{:S(2)}) copy-start(f32[4]{0:T(128)} %refs_0_.7) | copy-start | bytes 52
  3.6 0.7 %copy-start.8 = (s32[4]{0:T(128)S(1)}, s32[4]{0:T(128)}, u32[]{:S(2)}) copy-start(s32[4]{0:T(128)} %refs_1_.7) | copy-start | bytes 52
  7.1 1.6 %copy-start = (f32[1,2,2,128,256]{4,3,2,1,0:T(8,128)}, f32[1,2,2,128,256]{4,3,2,1,0:T(8,128)S(1)}, u32[]{:S(2)}) copy-start(f32[1,2,2,128,256]{4,3,2,1,0:T(8,128)S(1)} %get-tuple-element.26.mine) | copy-start | bytes 1572868
  7.1 10.8 %collective-permute-start.8 = (bf16[1,2,2,128,256]{4,3,2,1,0:T(8,128)(2,1)S(1)}, bf16[1,2,2,128,256]{4,3,2,1,0:T(8,128)(2,1)S(1)}, u32[]{:S(2)}, u32[]{:S(2)}) collective-permute-start(bf16[1,2,2,128,256]{4,3,2,1,0:T(8,128)(2,1)S(1)} %get-tuple-element.28), channel_id=1, source_target_pairs={{0,16},{8,24},{16,0},{24,8},{1,17},{9,25},{17,1},{25,9},{2,18},{10... | collective-permute-start | bytes 786440 | tf_op jit(solution)/shard_map/ppermute | solution.py:143
  8.8 10.9 %collective-permute-start = (bf16[2,2,1,128,256]{4,3,2,1,0:T(8,128)(2,1)S(1)}, bf16[2,2,1,128,256]{4,3,2,1,0:T(8,128)(2,1)S(1)}, u32[]{:S(2)}, u32[]{:S(2)}) collective-permute-start(bf16[2,2,1,128,256]{4,3,2,1,0:T(8,128)(2,1)S(1)} %get-tuple-element.30), channel_id=1, source_target_pairs={{0,1},{1,2},{2,3},{3,4},{4,5},{5,6},{6,7},{8,9},{9,10},{10,11},{11... | collective-permute-start | bytes 786440 | tf_op jit(solution)/shard_map/ppermute | solution.py:134
  10.7 8.9 %collective-permute-start.1 = (bf16[2,2,1,128,256]{4,3,2,1,0:T(8,128)(2,1)S(1)}, bf16[2,2,1,128,256]{4,3,2,1,0:T(8,128)(2,1)S(1)}, u32[]{:S(2)}, u32[]{:S(2)}) collective-permute-start(bf16[2,2,1,128,256]{4,3,2,1,0:T(8,128)(2,1)S(1)} %get-tuple-element.29), channel_id=1, source_target_pairs={{1,0},{2,1},{3,2},{4,3},{5,4},{6,5},{7,6},{9,8},{10,9},{11,10},{12... | collective-permute-start | bytes 786440 | tf_op jit(solution)/shard_map/ppermute | solution.py:135
  17.2 0.8 %copy-start.1 = (f32[1,2,2,128,256]{4,3,2,1,0:T(8,128)}, f32[1,2,2,128,256]{4,3,2,1,0:T(8,128)S(1)}, u32[]{:S(2)}) copy-start(f32[1,2,2,128,256]{4,3,2,1,0:T(8,128)S(1)} %get-tuple-element.23.mine) | copy-start | bytes 1572868
  17.3 11.1 %collective-permute-start.6 = (bf16[1,2,2,128,256]{4,3,2,1,0:T(8,128)(2,1)S(1)}, bf16[1,2,2,128,256]{4,3,2,1,0:T(8,128)(2,1)S(1)}, u32[]{:S(2)}, u32[]{:S(2)}) collective-permute-start(bf16[1,2,2,128,256]{4,3,2,1,0:T(8,128)(2,1)S(1)} %get-tuple-element.25), channel_id=1, source_target_pairs={{0,16},{8,24},{16,0},{24,8},{1,17},{9,25},{17,1},{25,9},{2,18},{10... | collective-permute-start | bytes 786440 | tf_op jit(solution)/shard_map/ppermute | solution.py:143
  18.0 20.4 %collective-permute-start.9 = (bf16[1,2,2,128,256]{4,3,2,1,0:T(8,128)(2,1)S(1)}, bf16[1,2,2,128,256]{4,3,2,1,0:T(8,128)(2,1)S(1)}, u32[]{:S(2)}, u32[]{:S(2)}) collective-permute-start(bf16[1,2,2,128,256]{4,3,2,1,0:T(8,128)(2,1)S(1)} %add_convert_fusion), channel_id=1, source_target_pairs={{0,8},{8,0},{16,24},{24,16},{1,9},{9,1},{17,25},{25,17},{2,10},{10... | collective-permute-start | bytes 786440 | tf_op jit(solution)/shard_map/ppermute | solution.py:147
  22.5 0.8 %copy-start.3 = (f32[1,2,2,128,256]{4,3,2,1,0:T(8,128)}, f32[1,2,2,128,256]{4,3,2,1,0:T(8,128)S(1)}, u32[]{:S(2)}) copy-start(f32[1,2,2,128,256]{4,3,2,1,0:T(8,128)S(1)} %get-tuple-element.20.mine) | copy-start | bytes 1572868
  23.3 9.1 %collective-permute-start.4 = (bf16[1,2,2,128,256]{4,3,2,1,0:T(8,128)(2,1)S(1)}, bf16[1,2,2,128,256]{4,3,2,1,0:T(8,128)(2,1)S(1)}, u32[]{:S(2)}, u32[]{:S(2)}) collective-permute-start(bf16[1,2,2,128,256]{4,3,2,1,0:T(8,128)(2,1)S(1)} %get-tuple-element.22), channel_id=1, source_target_pairs={{0,16},{8,24},{16,0},{24,8},{1,17},{9,25},{17,1},{25,9},{2,18},{10... | collective-permute-start | bytes 786440 | tf_op jit(solution)/shard_map/ppermute | solution.py:143
  27.6 0.8 %copy-start.2 = (f32[1,2,2,128,256]{4,3,2,1,0:T(8,128)}, f32[1,2,2,128,256]{4,3,2,1,0:T(8,128)S(1)}, u32[]{:S(2)}) copy-start(f32[1,2,2,128,256]{4,3,2,1,0:T(8,128)S(1)} %get-tuple-element.17.mine) | copy-start | bytes 1572868
  27.6 10.0 %collective-permute-start.2 = (bf16[1,2,2,128,256]{4,3,2,1,0:T(8,128)(2,1)S(1)}, bf16[1,2,2,128,256]{4,3,2,1,0:T(8,128)(2,1)S(1)}, u32[]{:S(2)}, u32[]{:S(2)}) collective-permute-start(bf16[1,2,2,128,256]{4,3,2,1,0:T(8,128)(2,1)S(1)} %get-tuple-element.19), channel_id=1, source_target_pairs={{0,16},{8,24},{16,0},{24,8},{1,17},{9,25},{17,1},{25,9},{2,18},{10... | collective-permute-start | bytes 786440 | tf_op jit(solution)/shard_map/ppermute | solution.py:143
  28.4 12.5 %collective-permute-start.7 = (bf16[1,2,2,128,256]{4,3,2,1,0:T(8,128)(2,1)S(1)}, bf16[1,2,2,128,256]{4,3,2,1,0:T(8,128)(2,1)S(1)}, u32[]{:S(2)}, u32[]{:S(2)}) collective-permute-start(bf16[1,2,2,128,256]{4,3,2,1,0:T(8,128)(2,1)S(1)} %add_convert_fusion.1), channel_id=1, source_target_pairs={{0,8},{8,0},{16,24},{24,16},{1,9},{9,1},{17,25},{25,17},{2,10},{10... | collective-permute-start | bytes 786440 | tf_op jit(solution)/shard_map/ppermute | solution.py:147
  32.5 11.0 %collective-permute-start.5 = (bf16[1,2,2,128,256]{4,3,2,1,0:T(8,128)(2,1)S(1)}, bf16[1,2,2,128,256]{4,3,2,1,0:T(8,128)(2,1)S(1)}, u32[]{:S(2)}, u32[]{:S(2)}) collective-permute-start(bf16[1,2,2,128,256]{4,3,2,1,0:T(8,128)(2,1)S(1)} %add_convert_fusion.2), channel_id=1, source_target_pairs={{0,8},{8,0},{16,24},{24,16},{1,9},{9,1},{17,25},{25,17},{2,10},{10... | collective-permute-start | bytes 786440 | tf_op jit(solution)/shard_map/ppermute | solution.py:147
  37.7 10.1 %collective-permute-start.3 = (bf16[1,2,2,128,256]{4,3,2,1,0:T(8,128)(2,1)S(1)}, bf16[1,2,2,128,256]{4,3,2,1,0:T(8,128)(2,1)S(1)}, u32[]{:S(2)}, u32[]{:S(2)}) collective-permute-start(bf16[1,2,2,128,256]{4,3,2,1,0:T(8,128)(2,1)S(1)} %add_convert_fusion.3), channel_id=1, source_target_pairs={{0,8},{8,0},{16,24},{24,16},{1,9},{9,1},{17,25},{25,17},{2,10},{10... | collective-permute-start | bytes 786440 | tf_op jit(solution)/shard_map/ppermute | solution.py:147
  38.4 0.7 %copy-start.9 = (bf16[1,2,2,128,256]{4,3,2,1,0:T(8,128)(2,1)}, bf16[1,2,2,128,256]{4,3,2,1,0:T(8,128)(2,1)S(1)}, u32[]{:S(2)}) copy-start(bf16[1,2,2,128,256]{4,3,2,1,0:T(8,128)(2,1)S(1)} %collective-permute-done.9.received) | copy-start | bytes 786436
  40.9 0.7 %copy-start.10 = (bf16[1,2,2,128,256]{4,3,2,1,0:T(8,128)(2,1)}, bf16[1,2,2,128,256]{4,3,2,1,0:T(8,128)(2,1)S(1)}, u32[]{:S(2)}) copy-start(bf16[1,2,2,128,256]{4,3,2,1,0:T(8,128)(2,1)S(1)} %collective-permute-done.7.received) | copy-start | bytes 786436
  43.5 0.7 %copy-start.11 = (bf16[1,2,2,128,256]{4,3,2,1,0:T(8,128)(2,1)}, bf16[1,2,2,128,256]{4,3,2,1,0:T(8,128)(2,1)S(1)}, u32[]{:S(2)}) copy-start(bf16[1,2,2,128,256]{4,3,2,1,0:T(8,128)(2,1)S(1)} %collective-permute-done.5.received) | copy-start | bytes 786436
  47.8 0.7 %copy-start.12 = (bf16[1,2,2,128,256]{4,3,2,1,0:T(8,128)(2,1)}, bf16[1,2,2,128,256]{4,3,2,1,0:T(8,128)(2,1)S(1)}, u32[]{:S(2)}) copy-start(bf16[1,2,2,128,256]{4,3,2,1,0:T(8,128)(2,1)S(1)} %collective-permute-done.3.received) | copy-start | bytes 786436

commit v2 on v0

v2 whole, which is shorter than its diff:
```python
import functools

import jax
import jax.numpy as jnp
from jax import lax
from jax.experimental import pallas as pl
from jax.experimental.pallas import tpu as pltpu
from jax.sharding import PartitionSpec as P

BF16 = jnp.bfloat16
F32 = jnp.float32


def stack_coupling(c_ref, rows, cols):
    modes, slots, size = c_ref.shape[:3]
    for m in range(modes):
        for k in range(slots):
            c = c_ref[m, k]
            rows[k, m * size : (m + 1) * size, :] = c
            cols[m, :, k * size : (k + 1) * size] = c


def source_tile(nbr, first, owned, at, e, k, own, edges):
    listed = nbr[at, k]
    local = listed - first
    tile = own[e, jnp.clip(local, 0, owned - 1)]
    if edges:
        tile = jnp.where(local < 0, edges[0][e, 0], tile)
        tile = jnp.where(local >= owned, edges[1][e, 0], tile)
    return jnp.where(listed >= 0, tile, jnp.zeros_like(tile))


def terms(part, blocks, flip, occ, off, nbr, rows, cols, own, edges, outs, half, acc):
    far, near, mine = outs
    slots, wide, size = rows.shape
    modes = wide // size
    count, owned, _, lanes = own.shape
    per = 2 * size // lanes
    first = lax.axis_index("slab") * owned
    odd = lax.rem(lax.axis_index("energy") + flip, 2)
    step = blocks[1] - blocks[0]

    def group(i, carry):
        if per == 1:
            places = [(blocks[0] + step * i, i)]
        elif len(blocks) == 2:
            places = [(blocks[0], 0), (blocks[1], 1)]
        else:
            places = [(2 * i, 2 * i), (2 * i + 1, 2 * i + 1)]
        acc[...] = jnp.zeros_like(acc)
        for k in range(slots):
            for j in range(2):
                if per == 1:
                    src = source_tile(nbr, first, owned, places[0][0], j, k, own, edges)
                else:
                    src = jnp.concatenate(
                        [source_tile(nbr, first, owned, places[j][0], e, k, own, edges) for e in range(count)],
                        axis=1,
                    )
                r = jnp.dot(rows[k], src, preferred_element_type=F32).astype(BF16)
                for m in range(modes):
                    for h in range(2):
                        e, u = (j, h) if per == 1 else (h, j)
                        to = (e * 2 + u) * size
                        half[m, to : to + size, k * size : (k + 1) * size] = r[
                            m * size : (m + 1) * size, h * size : (h + 1) * size
                        ]

        def second(m):
            y = lax.dot_general(
                half[m], cols[m], (((1,), (1,)), ((), ())), preferred_element_type=F32
            )
            o = off[m]
            n = occ[m]
            down, up = (n + 1.0, n) if part == 0 else (n, n + 1.0)
            for e in range(count):
                for u in range(2):
                    to = (e * 2 + u) * size
                    ys = y[to : to + size]
                    acc[e - o + count, u] += down * ys
                    acc[e + o + count, u] += up * ys

        for m in range(modes):
            if far is None and near is None:
                pl.when(off[m] < count)(functools.partial(second, m))
            else:
                second(m)
        for j in range(count):
            for u in range(2):
                to, cut = (places[0][1], slice(u * size, (u + 1) * size)) if per == 1 else (places[u][1], slice(0, size))
                if far is not None:
                    far[0, j, to, :, cut] = acc[2 * count * odd + j, u].astype(BF16)
                if near is not None:
                    near[0, j, to, :, cut] = acc[2 * count * (1 - odd) + j, u]
                if mine is not None:
                    mine[0, j, to, :, cut] = acc[count + j, u]
        return carry

    groups = len(blocks) // per
    if groups == 1:
        group(0, 0)
    else:
        lax.fori_loop(0, groups, group, 0)


def scratch(modes, slots, size, count):
    return [
        pltpu.VMEM((modes, count * 2 * size, slots * size), BF16),
        pltpu.VMEM((3 * count, 2, size, size), F32),
    ]


def first_body(part, blocks, occ_h, off_h, nbr_h, c_h, g_h, far, near, mine, rows, cols, raw, last, head, occ, off, nbr, c_ref, own, sems, half, acc):
    size = c_h.shape[-1]
    owned = g_h.shape[2]
    copies = [
        pltpu.make_async_copy(src, dst, sems.at[i])
        for i, (src, dst) in enumerate(
            [
                (c_h, c_ref),
                (g_h.at[part], own),
                (occ_h, occ),
                (off_h, off),
                (nbr_h, nbr),
                (g_h.at[pl.ds(1 - part, 1), :, :, :, pl.ds(0, size)], raw),
                (g_h.at[:, :, pl.ds(owned - 1, 1)], last),
                (g_h.at[:, :, pl.ds(0, 1)], head),
            ]
        )
    ]
    for copy in copies:
        copy.start()
    copies[0].wait()
    stack_coupling(c_ref, rows, cols)
    for copy in copies[1:5]:
        copy.wait()
    terms(part, blocks, 0, occ, off, nbr, rows, cols, own, (), (far, near, mine), half, acc)
    for copy in copies[5:]:
        copy.wait()


def first_call(part, blocks, greens, coupling, occupation, offsets, neighbours):
    modes, slots, size = coupling.shape[:3]
    parts, count, owned = greens.shape[:3]
    shape = (1, count, len(blocks), size, 2 * size)
    edge = (parts, count, 1, size, 2 * size)
    anywhere = pl.BlockSpec(memory_space=pl.ANY)
    vmem = pl.BlockSpec(memory_space=pltpu.VMEM)
    return pl.pallas_call(
        functools.partial(first_body, part, blocks),
        out_shape=[
            jax.ShapeDtypeStruct(shape, BF16),
            jax.ShapeDtypeStruct(shape, F32),
            jax.ShapeDtypeStruct(shape, F32),
            jax.ShapeDtypeStruct((slots, modes * size, size), BF16),
            jax.ShapeDtypeStruct((modes, size, slots * size), BF16),
            jax.ShapeDtypeStruct((1, count, owned, size, size), BF16),
            jax.ShapeDtypeStruct(edge, BF16),
            jax.ShapeDtypeStruct(edge, BF16),
        ],
        in_specs=[anywhere] * 5,
        out_specs=[vmem] * 5 + [anywhere] * 3,
        scratch_shapes=[
            pltpu.SMEM(occupation.shape, F32),
            pltpu.SMEM(offsets.shape, jnp.int32),
            pltpu.SMEM(neighbours.shape, jnp.int32),
            pltpu.VMEM(coupling.shape, BF16),
            pltpu.VMEM(greens.shape[1:], BF16),
            pltpu.SemaphoreType.DMA((8,)),
        ]
        + scratch(modes, slots, size, count),
        compiler_params=pltpu.CompilerParams(vmem_limit_bytes=16 << 20),
        cost_estimate=cost(shape, modes, slots),
    )(occupation, offsets, neighbours, coupling, greens)


def cost(shape, modes, slots):
    size = shape[3]
    flops = 4 * shape[1] * shape[2] * size * size * shape[4] * modes * slots
    return pl.CostEstimate(flops=flops, bytes_accessed=1 << 20, transcendentals=0)


def next_body(part, blocks, flip, wanted, n_edges, *refs):
    occ, off, nbr, rows, cols, own = refs[:6]
    edges = tuple(ref.at[0] for ref in refs[6 : 6 + n_edges])
    outs = list(refs[6 + n_edges : -2])
    outs = [outs.pop(0) if want else None for want in wanted]
    terms(part, blocks, flip, occ, off, nbr, rows, cols, own.at[0], edges, outs, refs[-2], refs[-1])


def next_call(part, blocks, flip, wanted, scalars, stacked, own, edges):
    rows, cols = stacked
    slots, wide, size = rows.shape
    modes = wide // size
    count = own[0].shape[1]
    lanes = own[3]
    shape = (1, count, len(blocks), size, lanes)
    vmem = pl.BlockSpec(memory_space=pltpu.VMEM)

    def cut(array, lead, tail, lanes):
        return pl.BlockSpec(
            (1,) + array.shape[1:-1] + (lanes,), lambda i, lead=lead, tail=tail: (lead, 0, 0, 0, tail)
        )

    def full(shape):
        return pl.BlockSpec(shape, lambda i: (0,) * len(shape))

    sources = [own] + list(edges)
    return pl.pallas_call(
        functools.partial(next_body, part, blocks, flip, wanted, len(edges)),
        out_shape=[
            jax.ShapeDtypeStruct(shape, kind) for want, kind in zip(wanted, (BF16, F32, F32)) if want
        ],
        grid=(1,),
        in_specs=[pl.BlockSpec(memory_space=pltpu.SMEM)] * 3
        + [full(rows.shape), full(cols.shape)]
        + [cut(*s) for s in sources],
        out_specs=[full(shape)] * sum(wanted),
        scratch_shapes=scratch(modes, slots, size, count),
        compiler_params=pltpu.CompilerParams(vmem_limit_bytes=16 << 20),
        cost_estimate=cost(shape, modes, slots),
    )(*scalars, rows, cols, *[s[0] for s in sources])


def add_greater(mine_in, got_in, mine_out, got_out, out):
    for mine, got, blocks in ((mine_in, got_in, (1, 2)), (mine_out, got_out, (0, 3))):
        for i, at in enumerate(blocks):
            out[0, :, at] = (mine[0, :, i] + got[0, :, i].astype(F32)).astype(BF16)


def add_lesser(mine, near, got, mine_in, got_in, mine_out, got_out, _, out):
    size = mine.shape[-1]
    out[0, :, :, :, :size] = (mine[0] + near[0] + got[0].astype(F32)).astype(BF16)
    for mine, got, blocks in ((mine_in, got_in, (1, 2)), (mine_out, got_out, (0, 3))):
        for i, at in enumerate(blocks):
            out[0, :, at, :, size:] = (mine[0, :, i] + got[0, :, i].astype(F32)).astype(BF16)


def add_up(body, part, arrays, shape, out):
    def full(shape):
        return pl.BlockSpec(shape, lambda i: (0,) * len(shape))

    given = list(arrays) + ([] if out is None else [out])
    return pl.pallas_call(
        body,
        out_shape=jax.ShapeDtypeStruct(shape, BF16),
        grid=(1,),
        in_specs=[full(a.shape) for a in arrays] + [pl.BlockSpec(memory_space=pl.ANY)] * (out is not None),
        out_specs=pl.BlockSpec((1,) + shape[1:], lambda i: (part, 0, 0, 0, 0)),
        input_output_aliases={} if out is None else {len(arrays): 0},
        compiler_params=pltpu.CompilerParams(vmem_limit_bytes=16 << 20),
        cost_estimate=pl.CostEstimate(flops=1 << 20, bytes_accessed=1 << 20, transcendentals=0),
    )(*given)


def on_device(greens, coupling, occupation, offsets, neighbours):
    slabs = lax.axis_size("slab")
    size = coupling.shape[-1]
    across = [(i, i ^ 1) for i in range(4)]
    along = [(i, i ^ 2) for i in range(4)]
    upward = [(i, i + 1) for i in range(slabs - 1)]
    downward = [(i + 1, i) for i in range(slabs - 1)]
    inner, outer, every = (1, 2), (0, 3), (0, 1, 2, 3)
    scalars = (occupation, offsets, neighbours)
    wide = 2 * size

    def relay(far):
        return lax.ppermute(far, "energy", along)

    def pass_on(near, relayed):
        return lax.ppermute((near + relayed.astype(F32)).astype(BF16), "energy", across)

    far, near_g1, mine_g1, rows, cols, raw, last, head = first_call(
        1, inner, greens, coupling, occupation, offsets, neighbours
    )
    stacked = (rows, cols)
    relay_g1 = relay(far)
    raw_x = lax.ppermute(raw, "energy", across)
    before = lax.ppermute(last, "slab", upward)
    after = lax.ppermute(head, "slab", downward)
    every_out = (True, True, True)
    far, near_l1, mine_l1 = next_call(
        0, inner, 0, every_out, scalars, stacked, (greens, 0, 1, size), ()
    )
    relay_l1 = relay(far)
    got_g1 = pass_on(near_g1, relay_g1)
    far, near_g2, mine_g2 = next_call(
        1, outer, 0, every_out, scalars, stacked, (greens, 1, 0, wide), ((before, 1, 0, wide), (after, 1, 0, wide))
    )
    relay_g2 = relay(far)
    got_l1 = pass_on(near_l1, relay_l1)
    before_x = lax.ppermute(raw_x[:, :, 3:], "slab", upward)
    after_x = lax.ppermute(raw_x[:, :, :1], "slab", downward)
    far, near_l2, mine_l2 = next_call(
        0, outer, 0, every_out, scalars, stacked, (greens, 0, 1, size), ((before, 0, 1, size), (after, 0, 1, size))
    )
    relay_l2 = relay(far)
    got_g2 = pass_on(near_g2, relay_g2)
    far, near_z = next_call(
        0, every, 1, (True, True, False), scalars, stacked, (raw_x, 0, 0, size), ((before_x, 0, 0, size), (after_x, 0, 0, size))
    )
    got_z = relay(far)
    (mine_z,) = next_call(
        0, every, 0, (False, False, True), scalars, stacked, (greens, 0, 0, size), ((before, 0, 0, size), (after, 0, 0, size))
    )
    got_l2 = pass_on(near_l2, relay_l2)
    out = add_up(add_greater, 1, (mine_g1, got_g1, mine_g2, got_g2), greens.shape, None)
    return add_up(
        add_lesser, 0, (mine_z, near_z, got_z, mine_l1, got_l1, mine_l2, got_l2), greens.shape, out
    )


def solution(mesh):
    in_specs = (P(None, "energy", "slab", None, None), P(), P(), P(), P("slab", None))
    out_specs = P(None, "energy", "slab", None, None)
    return jax.shard_map(
        on_device, mesh=mesh, in_specs=in_specs, out_specs=out_specs, check_vma=False
    )
```

time: 140 us -> 52 us (0.37)
  the two profiles are of different devices: /device:TPU:1 before, /device:TPU:8 now
where the time goes in v2:
time: 52 us; the launch traced here: 51.7 us
  starting transfers between devices  21.8 us (42%)
  Pallas kernels  17 us (33%)
  waiting for transfers between devices  8.33 us (16%)
  local copies, waits for them, and re-layouts  4.22 us (8%)
    pallas_call x5, Pallas kernels, next_call(): pl.pallas_call(functools.partial(next_body, part, blocks, flip, wanted, l...  12.1 us
    ppermute x5, starting transfers between devices, relay(): return lax.ppermute(far, 'energy', along)  4.89 us
    ppermute x4, waiting for transfers between devices, pass_on(): lax.ppermute((near + relayed.astype(F32)).astype(BF16), 'energy', across)  4.65 us
    ppermute x4, starting transfers between devices, pass_on(): lax.ppermute((near + relayed.astype(F32)).astype(BF16), 'energy', across)  4.31 us
    unnamed x12, local copies, waits for them, and re-layouts  4.21 us
    ppermute x1, starting transfers between devices, on_device(): after = lax.ppermute(head, 'slab', downward)  3.64 us
    ppermute x1, starting transfers between devices, on_device(): after_x = lax.ppermute(raw_x[:, :, :1], 'slab', downward)  3.64 us
    pallas_call x1, Pallas kernels, first_call(): pl.pallas_call(functools.partial(first_body, part, blocks), out_shape=[ja...  3.14 us
  transfers between devices with their start and end apart: 14, of which 4 were waited for; matrix products, arithmetic and copies ran while one was open for 0% of the time, Pallas kernels for 22%

profile of v2, /device:TPU:8, one launch (start us, length us, event | category | flops | bytes accessed | tf_op | source)
XLA Modules:
  0.0 51.7 jit_solution(4177711441210784692)
XLA Ops:
  0.0 1.2 %copy-done = bf16[2,2,4,128,256]{4,3,2,1,0:T(8,128)(2,1)S(1)} copy-done((bf16[2,2,4,128,256]{4,3,2,1,0:T(8,128)(2,1)S(1)}, bf16[2,2,4,128,256]{4,3,2,1,0:T(8,128)(2,1)}, u32[]{:S(2)}) %copy-start) | copy-done | bytes 1048600
  1.2 0.7 %copy-done.2 = s32[4,3]{1,0:T(4,128)S(1)} copy-done((s32[4,3]{1,0:T(4,128)S(1)}, s32[4,3]{1,0:T(4,128)}, u32[]{:S(2)}) %copy-start.2) | copy-done | bytes 72
  1.9 0.7 %copy-done.3 = f32[4]{0:T(128)S(1)} copy-done((f32[4]{0:T(128)S(1)}, f32[4]{0:T(128)}, u32[]{:S(2)}) %copy-start.3) | copy-done | bytes 40
  2.6 0.7 %copy-done.4 = s32[4]{0:T(128)S(1)} copy-done((s32[4]{0:T(128)S(1)}, s32[4]{0:T(128)}, u32[]{:S(2)}) %copy-start.4) | copy-done | bytes 40
  3.2 1.0 %copy-done.5 = bf16[4,3,128,128]{3,2,1,0:T(8,128)(2,1)S(1)} copy-done((bf16[4,3,128,128]{3,2,1,0:T(8,128)(2,1)S(1)}, bf16[4,3,128,128]{3,2,1,0:T(8,128)(2,1)}, u32[]{:S(2)}) %copy-start.5) | copy-done | bytes 393240
  4.2 3.1 %shard_map.55 = (bf16[1,2,2,128,256]{4,3,2,1,0:T(8,128)(2,1)S(1)}, f32[1,2,2,128,256]{4,3,2,1,0:T(8,128)S(1)}, f32[1,2,2,128,256]{4,3,2,1,0:T(8,128)S(1)}, bf16[...) custom-call(f32[4]{0:T(128)S(1)} %copy-done.3, ...), custom_call_target="tpu_custom_call" | custom-call | flops 805306368 | bytes 1048576 | tf_op jit(solution)/shard_map/pallas_call | solution.py:149
  7.4 1.7 %shard_map.58 = (bf16[1,2,2,128,128]{4,3,2,1,0:T(8,128)(2,1)S(1)}, f32[1,2,2,128,128]{4,3,2,1,0:T(8,128)S(1)}, f32[1,2,2,128,128]{4,3,2,1,0:T(8,128)S(1)}) custom-call(f32[4]{0:T(128)S(1)} %copy-done.3, s32[4]{0:T(128)S(1)} %copy-done.4, s32[4,3]{1,0:T(4,128)S(1)} %copy-done.2, bf16[3,512,128]{2,1,0:T(8,128)(2,1)S(1)} %get-tuple-element.24.refs_3_, ...), custom_call_target="tpu_custom_call" | custom-call | flops 402653184 | bytes 1048576 | tf_op jit(solution)/shard_map/pallas_call | solution.py:209
  9.1 1.6 %collective-permute-start.6 = (bf16[1,2,2,128,128]{4,3,2,1,0:T(8,128)(2,1)S(1)}, bf16[1,2,2,128,128]{4,3,2,1,0:T(8,128)(2,1)S(1)}, u32[]{:S(2)}, u32[]{:S(2)}) collective-permute-start(bf16[1,2,2,128,128]{4,3,2,1,0:T(8,128)(2,1)S(1)} %get-tuple-element.33), channel_id=1, source_target_pairs={{0,16},{8,24},{16,0},{24,8},{1,17},{9,25},{17,1},{25,9},{2,18},{10... | collective-permute-start | bytes 393224 | tf_op jit(solution)/shard_map/ppermute | solution.py:268
  10.7 1.9 %collective-permute-start = (bf16[2,2,1,128,256]{4,3,2,1,0:T(8,128)(2,1)S(1)}, bf16[2,2,1,128,256]{4,3,2,1,0:T(8,128)(2,1)S(1)}, u32[]{:S(2)}, u32[]{:S(2)}) collective-permute-start(bf16[2,2,1,128,256]{4,3,2,1,0:T(8,128)(2,1)S(1)} %get-tuple-element.26), channel_id=1, source_target_pairs={{0,1},{1,2},{2,3},{3,4},{4,5},{5,6},{6,7},{8,9},{9,10},{10,11},{11... | collective-permute-start | bytes 786440 | tf_op jit(solution)/shard_map/ppermute | solution.py:279
  12.6 3.6 %collective-permute-start.1 = (bf16[2,2,1,128,256]{4,3,2,1,0:T(8,128)(2,1)S(1)}, bf16[2,2,1,128,256]{4,3,2,1,0:T(8,128)(2,1)S(1)}, u32[]{:S(2)}, u32[]{:S(2)}) collective-permute-start(bf16[2,2,1,128,256]{4,3,2,1,0:T(8,128)(2,1)S(1)} %get-tuple-element.27), channel_id=1, source_target_pairs={{1,0},{2,1},{3,2},{4,3},{5,4},{6,5},{7,6},{9,8},{10,9},{11,10},{12... | collective-permute-start | bytes 786440 | tf_op jit(solution)/shard_map/ppermute | solution.py:280
  16.2 0.6 %collective-permute-start.10 = (bf16[1,2,2,128,256]{4,3,2,1,0:T(8,128)(2,1)S(1)}, bf16[1,2,2,128,256]{4,3,2,1,0:T(8,128)(2,1)S(1)}, u32[]{:S(2)}, u32[]{:S(2)}) collective-permute-start(bf16[1,2,2,128,256]{4,3,2,1,0:T(8,128)(2,1)S(1)} %get-tuple-element.39), channel_id=1, source_target_pairs={{0,16},{8,24},{16,0},{24,8},{1,17},{9,25},{17,1},{25,9},{2,18},{10... | collective-permute-start | bytes 786440 | tf_op jit(solution)/shard_map/ppermute | solution.py:268
  16.8 1.5 %collective-permute-start.2 = (bf16[1,2,4,128,128]{4,3,2,1,0:T(8,128)(2,1)S(1)}, bf16[1,2,4,128,128]{4,3,2,1,0:T(8,128)(2,1)S(1)}, u32[]{:S(2)}, u32[]{:S(2)}) collective-permute-start(bf16[1,2,4,128,128]{4,3,2,1,0:T(8,128)(2,1)S(1)} %get-tuple-element.28), channel_id=1, source_target_pairs={{0,8},{8,0},{16,24},{24,16},{1,9},{9,1},{17,25},{25,17},{2,10},{10... | collective-permute-start | bytes 786440 | tf_op jit(solution)/shard_map/ppermute | solution.py:278
  18.3 0.6 %collective-permute-start.7 = (bf16[1,2,2,128,128]{4,3,2,1,0:T(8,128)(2,1)S(1)}, bf16[1,2,2,128,128]{4,3,2,1,0:T(8,128)(2,1)S(1)}, u32[]{:S(2)}, u32[]{:S(2)}) collective-permute-start(bf16[1,2,2,128,128]{4,3,2,1,0:T(8,128)(2,1)S(1)} %add_convert_fusion.3), channel_id=1, source_target_pairs={{0,8},{8,0},{16,24},{24,16},{1,9},{9,1},{17,25},{25,17},{2,10},{10... | collective-permute-start | bytes 393224 | tf_op jit(solution)/shard_map/ppermute | solution.py:271
  18.9 1.2 %collective-permute-done.1.refs_7_ = bf16[2,2,1,128,256]{4,3,2,1,0:T(8,128)(2,1)S(1)} collective-permute-done((bf16[2,2,1,128,256]{4,3,2,1,0:T(8,128)(2,1)S(1)}, bf16[2,2,1,128,256]{4,3,2,1,0:T(8,128)(2,1)S(1)}, u32[]{:S(2)}, u32[]{:S(2)}) %collective-permute-start.1) | collective-permute-done | bytes 262176 | tf_op jit(solution)/shard_map/ppermute | solution.py:280
  20.1 2.8 %shard_map.60 = (bf16[1,2,2,128,256]{4,3,2,1,0:T(8,128)(2,1)S(1)}, f32[1,2,2,128,256]{4,3,2,1,0:T(8,128)S(1)}, f32[1,2,2,128,256]{4,3,2,1,0:T(8,128)S(1)}) custom-call(f32[4]{0:T(128)S(1)} %copy-done.3, s32[4]{0:T(128)S(1)} %copy-done.4, s32[4,3]{1,0:T(4,128)S(1)} %copy-done.2, bf16[3,512,128]{2,1,0:T(8,128)(2,1)S(1)} %get-tuple-element.24.refs_3_, ...), custom_call_target="tpu_custom_call" | custom-call | flops 805306368 | bytes 1048576 | tf_op jit(solution)/shard_map/pallas_call | solution.py:209
  22.9 0.6 %collective-permute-start.12 = (bf16[1,2,2,128,256]{4,3,2,1,0:T(8,128)(2,1)S(1)}, bf16[1,2,2,128,256]{4,3,2,1,0:T(8,128)(2,1)S(1)}, u32[]{:S(2)}, u32[]{:S(2)}) collective-permute-start(bf16[1,2,2,128,256]{4,3,2,1,0:T(8,128)(2,1)S(1)} %get-tuple-element.42), channel_id=1, source_target_pairs={{0,16},{8,24},{16,0},{24,8},{1,17},{9,25},{17,1},{25,9},{2,18},{10... | collective-permute-start | bytes 786440 | tf_op jit(solution)/shard_map/ppermute | solution.py:268
  23.5 2.5 %collective-permute-done.2.refs_5_ = bf16[1,2,4,128,128]{4,3,2,1,0:T(8,128)(2,1)S(1)} collective-permute-done((bf16[1,2,4,128,128]{4,3,2,1,0:T(8,128)(2,1)S(1)}, bf16[1,2,4,128,128]{4,3,2,1,0:T(8,128)(2,1)S(1)}, u32[]{:S(2)}, u32[]{:S(2)}) %collective-permute-start.2) | collective-permute-done | bytes 262176 | tf_op jit(solution)/shard_map/ppermute | solution.py:278
  26.0 1.9 %collective-permute-start.3 = (bf16[1,2,1,128,128]{4,3,2,1,0:T(8,128)(2,1)S(1)}, bf16[1,2,1,128,128]{4,3,2,1,0:T(8,128)(2,1)S(1)}, u32[]{:S(2)}, u32[]{:S(2)}) collective-permute-start(bf16[1,2,1,128,128]{4,3,2,1,0:T(8,128)(2,1)S(1)} %get-tuple-element.44), channel_id=1, source_target_pairs={{0,1},{1,2},{2,3},{3,4},{4,5},{5,6},{6,7},{8,9},{9,10},{10,11},{11... | collective-permute-start | bytes 196616 | tf_op jit(solution)/shard_map/ppermute | solution.py:292
  28.0 3.6 %collective-permute-start.4 = (bf16[1,2,1,128,128]{4,3,2,1,0:T(8,128)(2,1)S(1)}, bf16[1,2,1,128,128]{4,3,2,1,0:T(8,128)(2,1)S(1)}, u32[]{:S(2)}, u32[]{:S(2)}) collective-permute-start(bf16[1,2,1,128,128]{4,3,2,1,0:T(8,128)(2,1)S(1)} %get-tuple-element.43), channel_id=1, source_target_pairs={{1,0},{2,1},{3,2},{4,3},{5,4},{6,5},{7,6},{9,8},{10,9},{11,10},{12... | collective-permute-start | bytes 196616 | tf_op jit(solution)/shard_map/ppermute | solution.py:293
  31.6 0.1 add_convert_fusion.1
  31.7 1.6 %collective-permute-start.11 = (bf16[1,2,2,128,256]{4,3,2,1,0:T(8,128)(2,1)S(1)}, bf16[1,2,2,128,256]{4,3,2,1,0:T(8,128)(2,1)S(1)}, u32[]{:S(2)}, u32[]{:S(2)}) collective-permute-start(bf16[1,2,2,128,256]{4,3,2,1,0:T(8,128)(2,1)S(1)} %add_convert_fusion.1), channel_id=1, source_target_pairs={{0,8},{8,0},{16,24},{24,16},{1,9},{9,1},{17,25},{25,17},{2,10},{10... | collective-permute-start | bytes 786440 | tf_op jit(solution)/shard_map/ppermute | solution.py:271
  33.2 1.7 %shard_map.59 = (bf16[1,2,2,128,128]{4,3,2,1,0:T(8,128)(2,1)S(1)}, f32[1,2,2,128,128]{4,3,2,1,0:T(8,128)S(1)}, f32[1,2,2,128,128]{4,3,2,1,0:T(8,128)S(1)}) custom-call(f32[4]{0:T(128)S(1)} %copy-done.3, s32[4]{0:T(128)S(1)} %copy-done.4, s32[4,3]{1,0:T(4,128)S(1)} %copy-done.2, bf16[3,512,128]{2,1,0:T(8,128)(2,1)S(1)} %get-tuple-element.24.refs_3_, ...), custom_call_target="tpu_custom_call" | custom-call | flops 402653184 | bytes 1048576 | tf_op jit(solution)/shard_map/pallas_call | solution.py:209
  35.0 1.6 %collective-permute-start.8 = (bf16[1,2,2,128,128]{4,3,2,1,0:T(8,128)(2,1)S(1)}, bf16[1,2,2,128,128]{4,3,2,1,0:T(8,128)(2,1)S(1)}, u32[]{:S(2)}, u32[]{:S(2)}) collective-permute-start(bf16[1,2,2,128,128]{4,3,2,1,0:T(8,128)(2,1)S(1)} %get-tuple-element.36), channel_id=1, source_target_pairs={{0,16},{8,24},{16,0},{24,8},{1,17},{9,25},{17,1},{25,9},{2,18},{10... | collective-permute-start | bytes 393224 | tf_op jit(solution)/shard_map/ppermute | solution.py:268
  36.6 2.8 %shard_map.57 = (bf16[1,2,4,128,128]{4,3,2,1,0:T(8,128)(2,1)S(1)}, f32[1,2,4,128,128]{4,3,2,1,0:T(8,128)S(1)}) custom-call(f32[4]{0:T(128)S(1)} %copy-done.3, s32[4]{0:T(128)S(1)} %copy-done.4, s32[4,3]{1,0:T(4,128)S(1)} %copy-done.2, bf16[3,512,128]{2,1,0:T(8,128)(2,1)S(1)} %get-tuple-element.24.refs_3_, ...), custom_call_target="tpu_custom_call" | custom-call | flops 805306368 | bytes 1048576 | tf_op jit(solution)/shard_map/pallas_call | solution.py:209
  39.4 0.6 %collective-permute-start.5 = (bf16[1,2,4,128,128]{4,3,2,1,0:T(8,128)(2,1)S(1)}, bf16[1,2,4,128,128]{4,3,2,1,0:T(8,128)(2,1)S(1)}, u32[]{:S(2)}, u32[]{:S(2)}) collective-permute-start(bf16[1,2,4,128,128]{4,3,2,1,0:T(8,128)(2,1)S(1)} %get-tuple-element.30), channel_id=1, source_target_pairs={{0,16},{8,24},{16,0},{24,8},{1,17},{9,25},{17,1},{25,9},{2,18},{10... | collective-permute-start | bytes 786440 | tf_op jit(solution)/shard_map/ppermute | solution.py:268
  40.0 0.6 %collective-permute-start.13 = (bf16[1,2,2,128,256]{4,3,2,1,0:T(8,128)(2,1)S(1)}, bf16[1,2,2,128,256]{4,3,2,1,0:T(8,128)(2,1)S(1)}, u32[]{:S(2)}, u32[]{:S(2)}) collective-permute-start(bf16[1,2,2,128,256]{4,3,2,1,0:T(8,128)(2,1)S(1)} %add_convert_fusion), channel_id=1, source_target_pairs={{0,8},{8,0},{16,24},{24,16},{1,9},{9,1},{17,25},{25,17},{2,10},{10... | collective-permute-start | bytes 786440 | tf_op jit(solution)/shard_map/ppermute | solution.py:271
  40.7 1.6 %collective-permute-start.9 = (bf16[1,2,2,128,128]{4,3,2,1,0:T(8,128)(2,1)S(1)}, bf16[1,2,2,128,128]{4,3,2,1,0:T(8,128)(2,1)S(1)}, u32[]{:S(2)}, u32[]{:S(2)}) collective-permute-start(bf16[1,2,2,128,128]{4,3,2,1,0:T(8,128)(2,1)S(1)} %add_convert_fusion.2), channel_id=1, source_target_pairs={{0,8},{8,0},{16,24},{24,16},{1,9},{9,1},{17,25},{25,17},{2,10},{10... | collective-permute-start | bytes 393224 | tf_op jit(solution)/shard_map/ppermute | solution.py:271
  42.2 3.0 %shard_map.56.mine = f32[1,2,4,128,128]{4,3,2,1,0:T(8,128)S(1)} custom-call(f32[4]{0:T(128)S(1)} %copy-done.3, s32[4]{0:T(128)S(1)} %copy-done.4, s32[4,3]{1,0:T(4,128)S(1)} %copy-done.2, bf16[3,512,128]{2,1,0:T(8,128)(2,1)S(1)} %get-tuple-element.24.refs_3_, bf16[4,128,384]{2,1,0:T(8,128)(2,1)S(1)} %get-tuple-element.25.refs_4_, ...), custom_call_target="tpu_custom_call" | custom-call | flops 805306368 | bytes 1048576 | tf_op jit(solution)/shard_map/pallas_call | solution.py:209
  45.3 4.1 %collective-permute-done.13.got_out = bf16[1,2,2,128,256]{4,3,2,1,0:T(8,128)(2,1)S(1)} collective-permute-done((bf16[1,2,2,128,256]{4,3,2,1,0:T(8,128)(2,1)S(1)}, bf16[1,2,2,128,256]{4,3,2,1,0:T(8,128)(2,1)S(1)}, u32[]{:S(2)}, u32[]{:S(2)}) %collective-permute-start.13) | collective-permute-done | bytes 262176 | tf_op jit(solution)/shard_map/ppermute | solution.py:271
  49.3 0.9 %shard_map.61._ = bf16[2,2,4,128,256]{4,3,2,1,0:T(8,128)(2,1)} custom-call(f32[1,2,2,128,256]{4,3,2,1,0:T(8,128)S(1)} %get-tuple-element.37.mine_in, bf16[1,2,2,128,256]{4,3,2,1,0:T(8,128)(2,1)S(1)} %collective-permute-done.11.got_in, f32[1,2,2,128,256]{4,3,2,1,0:T(8,128)S(1)} %get-tuple-element.40.mine_out, ...), custom_call_target="tpu_custom_call" | custom-call | flops 1048576 | bytes 1048576 | tf_op jit(solution)/shard_map/pallas_call | solution.py:244
  50.2 0.6 %collective-permute-done.9.got_out = bf16[1,2,2,128,128]{4,3,2,1,0:T(8,128)(2,1)S(1)} collective-permute-done((bf16[1,2,2,128,128]{4,3,2,1,0:T(8,128)(2,1)S(1)}, bf16[1,2,2,128,128]{4,3,2,1,0:T(8,128)(2,1)S(1)}, u32[]{:S(2)}, u32[]{:S(2)}) %collective-permute-start.9) | collective-permute-done | bytes 131104 | tf_op jit(solution)/shard_map/ppermute | solution.py:271
  50.8 0.9 %shard_map.62 = bf16[2,2,4,128,256]{4,3,2,1,0:T(8,128)(2,1)} custom-call(f32[1,2,4,128,128]{4,3,2,1,0:T(8,128)S(1)} %shard_map.56.mine, f32[1,2,4,128,128]{4,3,2,1,0:T(8,128)S(1)} %get-tuple-element.29.near, bf16[1,2,4,128,128]{4,3,2,1,0:T(8,128)(2,1)S(1)} %collective-permute-done.5.got, ...), custom_call_target="tpu_custom_call", output_to_operand_aliasing={{}: (7, {})} | custom-call | flops 1048576 | bytes 1048576 | tf_op jit(solution)/shard_map/pallas_call | solution.py:244
  (21 shorter events, 0.2 us)
Async XLA Ops:
  0.0 1.2 %copy-start = (bf16[2,2,4,128,256]{4,3,2,1,0:T(8,128)(2,1)S(1)}, bf16[2,2,4,128,256]{4,3,2,1,0:T(8,128)(2,1)}, u32[]{:S(2)}) copy-start(bf16[2,2,4,128,256]{4,3,2,1,0:T(8,128)(2,1)} %refs_5_.7) | copy-start | bytes 3145732
  1.2 0.7 %copy-start.2 = (s32[4,3]{1,0:T(4,128)S(1)}, s32[4,3]{1,0:T(4,128)}, u32[]{:S(2)}) copy-start(s32[4,3]{1,0:T(4,128)} %refs_2_.9) | copy-start | bytes 148
  1.9 0.7 %copy-start.3 = (f32[4]{0:T(128)S(1)}, f32[4]{0:T(128)}, u32[]{:S(2)}) copy-start(f32[4]{0:T(128)} %refs_0_.9) | copy-start | bytes 52
  2.6 0.7 %copy-start.4 = (s32[4]{0:T(128)S(1)}, s32[4]{0:T(128)}, u32[]{:S(2)}) copy-start(s32[4]{0:T(128)} %refs_1_.9) | copy-start | bytes 52
  3.2 1.0 %copy-start.5 = (bf16[4,3,128,128]{3,2,1,0:T(8,128)(2,1)S(1)}, bf16[4,3,128,128]{3,2,1,0:T(8,128)(2,1)}, u32[]{:S(2)}) copy-start(bf16[4,3,128,128]{3,2,1,0:T(8,128)(2,1)} %c_h.1) | copy-start | bytes 1179652
  4.2 3.1 %copy-start.1 = (bf16[2,2,4,128,256]{4,3,2,1,0:T(8,128)(2,1)S(1)}, bf16[2,2,4,128,256]{4,3,2,1,0:T(8,128)(2,1)}, u32[]{:S(2)}) copy-start(bf16[2,2,4,128,256]{4,3,2,1,0:T(8,128)(2,1)} %refs_5_.7) | copy-start | bytes 3145732
  9.1 9.2 %collective-permute-start.6 = (bf16[1,2,2,128,128]{4,3,2,1,0:T(8,128)(2,1)S(1)}, bf16[1,2,2,128,128]{4,3,2,1,0:T(8,128)(2,1)S(1)}, u32[]{:S(2)}, u32[]{:S(2)}) collective-permute-start(bf16[1,2,2,128,128]{4,3,2,1,0:T(8,128)(2,1)S(1)} %get-tuple-element.33), channel_id=1, source_target_pairs={{0,16},{8,24},{16,0},{24,8},{1,17},{9,25},{17,1},{25,9},{2,18},{10... | collective-permute-start | bytes 393224 | tf_op jit(solution)/shard_map/ppermute | solution.py:268
  10.7 8.3 %collective-permute-start = (bf16[2,2,1,128,256]{4,3,2,1,0:T(8,128)(2,1)S(1)}, bf16[2,2,1,128,256]{4,3,2,1,0:T(8,128)(2,1)S(1)}, u32[]{:S(2)}, u32[]{:S(2)}) collective-permute-start(bf16[2,2,1,128,256]{4,3,2,1,0:T(8,128)(2,1)S(1)} %get-tuple-element.26), channel_id=1, source_target_pairs={{0,1},{1,2},{2,3},{3,4},{4,5},{5,6},{6,7},{8,9},{9,10},{10,11},{11... | collective-permute-start | bytes 786440 | tf_op jit(solution)/shard_map/ppermute | solution.py:279
  12.6 7.5 %collective-permute-start.1 = (bf16[2,2,1,128,256]{4,3,2,1,0:T(8,128)(2,1)S(1)}, bf16[2,2,1,128,256]{4,3,2,1,0:T(8,128)(2,1)S(1)}, u32[]{:S(2)}, u32[]{:S(2)}) collective-permute-start(bf16[2,2,1,128,256]{4,3,2,1,0:T(8,128)(2,1)S(1)} %get-tuple-element.27), channel_id=1, source_target_pairs={{1,0},{2,1},{3,2},{4,3},{5,4},{6,5},{7,6},{9,8},{10,9},{11,10},{12... | collective-permute-start | bytes 786440 | tf_op jit(solution)/shard_map/ppermute | solution.py:280
  16.2 15.4 %collective-permute-start.10 = (bf16[1,2,2,128,256]{4,3,2,1,0:T(8,128)(2,1)S(1)}, bf16[1,2,2,128,256]{4,3,2,1,0:T(8,128)(2,1)S(1)}, u32[]{:S(2)}, u32[]{:S(2)}) collective-permute-start(bf16[1,2,2,128,256]{4,3,2,1,0:T(8,128)(2,1)S(1)} %get-tuple-element.39), channel_id=1, source_target_pairs={{0,16},{8,24},{16,0},{24,8},{1,17},{9,25},{17,1},{25,9},{2,18},{10... | collective-permute-start | bytes 786440 | tf_op jit(solution)/shard_map/ppermute | solution.py:268
  16.8 9.2 %collective-permute-start.2 = (bf16[1,2,4,128,128]{4,3,2,1,0:T(8,128)(2,1)S(1)}, bf16[1,2,4,128,128]{4,3,2,1,0:T(8,128)(2,1)S(1)}, u32[]{:S(2)}, u32[]{:S(2)}) collective-permute-start(bf16[1,2,4,128,128]{4,3,2,1,0:T(8,128)(2,1)S(1)} %get-tuple-element.28), channel_id=1, source_target_pairs={{0,8},{8,0},{16,24},{24,16},{1,9},{9,1},{17,25},{25,17},{2,10},{10... | collective-permute-start | bytes 786440 | tf_op jit(solution)/shard_map/ppermute | solution.py:278
  18.3 31.9 %collective-permute-start.7 = (bf16[1,2,2,128,128]{4,3,2,1,0:T(8,128)(2,1)S(1)}, bf16[1,2,2,128,128]{4,3,2,1,0:T(8,128)(2,1)S(1)}, u32[]{:S(2)}, u32[]{:S(2)}) collective-permute-start(bf16[1,2,2,128,128]{4,3,2,1,0:T(8,128)(2,1)S(1)} %add_convert_fusion.3), channel_id=1, source_target_pairs={{0,8},{8,0},{16,24},{24,16},{1,9},{9,1},{17,25},{25,17},{2,10},{10... | collective-permute-start | bytes 393224 | tf_op jit(solution)/shard_map/ppermute | solution.py:271
  22.9 17.0 %collective-permute-start.12 = (bf16[1,2,2,128,256]{4,3,2,1,0:T(8,128)(2,1)S(1)}, bf16[1,2,2,128,256]{4,3,2,1,0:T(8,128)(2,1)S(1)}, u32[]{:S(2)}, u32[]{:S(2)}) collective-permute-start(bf16[1,2,2,128,256]{4,3,2,1,0:T(8,128)(2,1)S(1)} %get-tuple-element.42), channel_id=1, source_target_pairs={{0,16},{8,24},{16,0},{24,8},{1,17},{9,25},{17,1},{25,9},{2,18},{10... | collective-permute-start | bytes 786440 | tf_op jit(solution)/shard_map/ppermute | solution.py:268
  26.0 9.0 %collective-permute-start.3 = (bf16[1,2,1,128,128]{4,3,2,1,0:T(8,128)(2,1)S(1)}, bf16[1,2,1,128,128]{4,3,2,1,0:T(8,128)(2,1)S(1)}, u32[]{:S(2)}, u32[]{:S(2)}) collective-permute-start(bf16[1,2,1,128,128]{4,3,2,1,0:T(8,128)(2,1)S(1)} %get-tuple-element.44), channel_id=1, source_target_pairs={{0,1},{1,2},{2,3},{3,4},{4,5},{5,6},{6,7},{8,9},{9,10},{10,11},{11... | collective-permute-start | bytes 196616 | tf_op jit(solution)/shard_map/ppermute | solution.py:292
  28.0 8.6 %collective-permute-start.4 = (bf16[1,2,1,128,128]{4,3,2,1,0:T(8,128)(2,1)S(1)}, bf16[1,2,1,128,128]{4,3,2,1,0:T(8,128)(2,1)S(1)}, u32[]{:S(2)}, u32[]{:S(2)}) collective-permute-start(bf16[1,2,1,128,128]{4,3,2,1,0:T(8,128)(2,1)S(1)} %get-tuple-element.43), channel_id=1, source_target_pairs={{1,0},{2,1},{3,2},{4,3},{5,4},{6,5},{7,6},{9,8},{10,9},{11,10},{12... | collective-permute-start | bytes 196616 | tf_op jit(solution)/shard_map/ppermute | solution.py:293
  31.7 13.6 %collective-permute-start.11 = (bf16[1,2,2,128,256]{4,3,2,1,0:T(8,128)(2,1)S(1)}, bf16[1,2,2,128,256]{4,3,2,1,0:T(8,128)(2,1)S(1)}, u32[]{:S(2)}, u32[]{:S(2)}) collective-permute-start(bf16[1,2,2,128,256]{4,3,2,1,0:T(8,128)(2,1)S(1)} %add_convert_fusion.1), channel_id=1, source_target_pairs={{0,8},{8,0},{16,24},{24,16},{1,9},{9,1},{17,25},{25,17},{2,10},{10... | collective-permute-start | bytes 786440 | tf_op jit(solution)/shard_map/ppermute | solution.py:271
  35.0 5.6 %collective-permute-start.8 = (bf16[1,2,2,128,128]{4,3,2,1,0:T(8,128)(2,1)S(1)}, bf16[1,2,2,128,128]{4,3,2,1,0:T(8,128)(2,1)S(1)}, u32[]{:S(2)}, u32[]{:S(2)}) collective-permute-start(bf16[1,2,2,128,128]{4,3,2,1,0:T(8,128)(2,1)S(1)} %get-tuple-element.36), channel_id=1, source_target_pairs={{0,16},{8,24},{16,0},{24,8},{1,17},{9,25},{17,1},{25,9},{2,18},{10... | collective-permute-start | bytes 393224 | tf_op jit(solution)/shard_map/ppermute | solution.py:268
  39.4 11.4 %collective-permute-start.5 = (bf16[1,2,4,128,128]{4,3,2,1,0:T(8,128)(2,1)S(1)}, bf16[1,2,4,128,128]{4,3,2,1,0:T(8,128)(2,1)S(1)}, u32[]{:S(2)}, u32[]{:S(2)}) collective-permute-start(bf16[1,2,4,128,128]{4,3,2,1,0:T(8,128)(2,1)S(1)} %get-tuple-element.30), channel_id=1, source_target_pairs={{0,16},{8,24},{16,0},{24,8},{1,17},{9,25},{17,1},{25,9},{2,18},{10... | collective-permute-start | bytes 786440 | tf_op jit(solution)/shard_map/ppermute | solution.py:268
  40.0 9.3 %collective-permute-start.13 = (bf16[1,2,2,128,256]{4,3,2,1,0:T(8,128)(2,1)S(1)}, bf16[1,2,2,128,256]{4,3,2,1,0:T(8,128)(2,1)S(1)}, u32[]{:S(2)}, u32[]{:S(2)}) collective-permute-start(bf16[1,2,2,128,256]{4,3,2,1,0:T(8,128)(2,1)S(1)} %add_convert_fusion), channel_id=1, source_target_pairs={{0,8},{8,0},{16,24},{24,16},{1,9},{9,1},{17,25},{25,17},{2,10},{10... | collective-permute-start | bytes 786440 | tf_op jit(solution)/shard_map/ppermute | solution.py:271
  40.7 10.1 %collective-permute-start.9 = (bf16[1,2,2,128,128]{4,3,2,1,0:T(8,128)(2,1)S(1)}, bf16[1,2,2,128,128]{4,3,2,1,0:T(8,128)(2,1)S(1)}, u32[]{:S(2)}, u32[]{:S(2)}) collective-permute-start(bf16[1,2,2,128,128]{4,3,2,1,0:T(8,128)(2,1)S(1)} %add_convert_fusion.2), channel_id=1, source_target_pairs={{0,8},{8,0},{16,24},{24,16},{1,9},{9,1},{17,25},{25,17},{2,10},{10... | collective-permute-start | bytes 393224 | tf_op jit(solution)/shard_map/ppermute | solution.py:271

commit v3 on v2

--- a/solution.py
+++ b/solution.py
@@ -145,6 +145,7 @@
     shape = (1, count, len(blocks), size, 2 * size)
     edge = (parts, count, 1, size, 2 * size)
     anywhere = pl.BlockSpec(memory_space=pl.ANY)
+    hbm = pl.BlockSpec(memory_space=pltpu.HBM)
     vmem = pl.BlockSpec(memory_space=pltpu.VMEM)
     return pl.pallas_call(
         functools.partial(first_body, part, blocks),
@@ -158,7 +159,7 @@
             jax.ShapeDtypeStruct(edge, BF16),
             jax.ShapeDtypeStruct(edge, BF16),
         ],
-        in_specs=[anywhere] * 5,
+        in_specs=[hbm] * 5,
         out_specs=[vmem] * 5 + [anywhere] * 3,
         scratch_shapes=[
             pltpu.SMEM(occupation.shape, F32),
@@ -175,9 +176,7 @@
 
 
 def cost(shape, modes, slots):
-    size = shape[3]
-    flops = 4 * shape[1] * shape[2] * size * size * shape[4] * modes * slots
-    return pl.CostEstimate(flops=flops, bytes_accessed=1 << 20, transcendentals=0)
+    return pl.CostEstimate(flops=1024, bytes_accessed=1024, transcendentals=0)
 
 
 def next_body(part, blocks, flip, wanted, n_edges, *refs):
@@ -249,7 +248,7 @@
         out_specs=pl.BlockSpec((1,) + shape[1:], lambda i: (part, 0, 0, 0, 0)),
         input_output_aliases={} if out is None else {len(arrays): 0},
         compiler_params=pltpu.CompilerParams(vmem_limit_bytes=16 << 20),
-        cost_estimate=pl.CostEstimate(flops=1 << 20, bytes_accessed=1 << 20, transcendentals=0),
+        cost_estimate=pl.CostEstimate(flops=1024, bytes_accessed=1024, transcendentals=0),
     )(*given)
 
 
@@ -267,8 +266,14 @@
     def relay(far):
         return lax.ppermute(far, "energy", along)
 
-    def pass_on(near, relayed):
-        return lax.ppermute((near + relayed.astype(F32)).astype(BF16), "energy", across)
+    def total(near, relayed):
+        return (near + relayed.astype(F32)).astype(BF16)
+
+    def pass_on(both):
+        return lax.ppermute(both, "energy", across)
+
+    def after_these(stacked, *others):
+        return lax.optimization_barrier((stacked,) + others)[0]
 
     far, near_g1, mine_g1, rows, cols, raw, last, head = first_call(
         1, inner, greens, coupling, occupation, offsets, neighbours
@@ -283,27 +288,36 @@
         0, inner, 0, every_out, scalars, stacked, (greens, 0, 1, size), ()
     )
     relay_l1 = relay(far)
-    got_g1 = pass_on(near_g1, relay_g1)
+    both_g1 = total(near_g1, relay_g1)
+    got_g1 = pass_on(both_g1)
+    stacked = after_these(stacked, both_g1, mine_l1)
     far, near_g2, mine_g2 = next_call(
         1, outer, 0, every_out, scalars, stacked, (greens, 1, 0, wide), ((before, 1, 0, wide), (after, 1, 0, wide))
     )
     relay_g2 = relay(far)
-    got_l1 = pass_on(near_l1, relay_l1)
-    before_x = lax.ppermute(raw_x[:, :, 3:], "slab", upward)
-    after_x = lax.ppermute(raw_x[:, :, :1], "slab", downward)
+    last_x, head_x = after_these((raw_x[:, :, 3:], raw_x[:, :, :1]), mine_g2)
+    before_x = lax.ppermute(last_x, "slab", upward)
+    after_x = lax.ppermute(head_x, "slab", downward)
+    stacked = after_these(stacked, last_x, head_x)
     far, near_l2, mine_l2 = next_call(
         0, outer, 0, every_out, scalars, stacked, (greens, 0, 1, size), ((before, 0, 1, size), (after, 0, 1, size))
     )
     relay_l2 = relay(far)
-    got_g2 = pass_on(near_g2, relay_g2)
+    both_l1 = total(near_l1, after_these(relay_l1, mine_l2))
+    got_l1 = pass_on(both_l1)
+    stacked = after_these(stacked, both_l1)
     far, near_z = next_call(
         0, every, 1, (True, True, False), scalars, stacked, (raw_x, 0, 0, size), ((before_x, 0, 0, size), (after_x, 0, 0, size))
     )
     got_z = relay(far)
+    both_g2 = total(near_g2, after_these(relay_g2, near_z))
+    got_g2 = pass_on(both_g2)
+    stacked = after_these(stacked, both_g2)
     (mine_z,) = next_call(
         0, every, 0, (False, False, True), scalars, stacked, (greens, 0, 0, size), ((before, 0, 0, size), (after, 0, 0, size))
     )
-    got_l2 = pass_on(near_l2, relay_l2)
+    both_l2 = total(near_l2, after_these(relay_l2, mine_z))
+    got_l2 = pass_on(both_l2)
     out = add_up(add_greater, 1, (mine_g1, got_g1, mine_g2, got_g2), greens.shape, None)
     return add_up(
         add_lesser, 0, (mine_z, near_z, got_z, mine_l1, got_l1, mine_l2, got_l2), greens.shape, out

time: 52 us -> 49.4 us (0.950)
  waiting for transfers between devices: 8.33 us -> 4.35 us
  starting transfers between devices: 21.8 us -> 22.8 us
    ppermute x1, waiting for transfers between devices: 2.5 us -> 0.3 us  [on_device(): raw_x = lax.ppermute(raw, 'energy', across)]
    ppermute x1, waiting for transfers between devices: 1.17 us -> 0.01 us  [on_device(): after = lax.ppermute(head, 'slab', downward)]
    ppermute x5, starting transfers between devices: 4.89 us -> 5.83 us  [relay(): return lax.ppermute(far, 'energy', along)]
    ppermute x6, waiting for transfers between devices: 4.65 us -> 4.04 us  [the longest x4 4.03 us: pass_on(): return lax.ppermute(both, 'energy', across)]
  transfers between devices with their start and end apart: 14 -> 14, of which waited for: 4 -> 3; matrix products, arithmetic and copies ran while one was open for 0% -> 0% of each run, Pallas kernels for 22% -> 27%
where the time goes in v3:
time: 49.4 us; the launch traced here: 48.8 us
  starting transfers between devices  22.8 us (46%)
  Pallas kernels  17.1 us (35%)
  waiting for transfers between devices  4.35 us (9%)
  local copies, waits for them, and re-layouts  4.22 us (9%)
    pallas_call x5, Pallas kernels, next_call(): pl.pallas_call(functools.partial(next_body, part, blocks, flip, wanted, l...  12.1 us
    ppermute x5, starting transfers between devices, relay(): return lax.ppermute(far, 'energy', along)  5.83 us
    ppermute x4, starting transfers between devices, pass_on(): return lax.ppermute(both, 'energy', across)  4.32 us
    unnamed x12, local copies, waits for them, and re-layouts  4.21 us
    ppermute x4, waiting for transfers between devices, pass_on(): return lax.ppermute(both, 'energy', across)  4.03 us
    ppermute x1, starting transfers between devices, on_device(): after = lax.ppermute(head, 'slab', downward)  3.64 us
    ppermute x1, starting transfers between devices, on_device(): after_x = lax.ppermute(head_x, 'slab', downward)  3.64 us
    pallas_call x1, Pallas kernels, first_call(): pl.pallas_call(functools.partial(first_body, part, blocks), out_shape=[ja...  3.14 us
  transfers between devices with their start and end apart: 14, of which 3 were waited for; matrix products, arithmetic and copies ran while one was open for 0% of the time, Pallas kernels for 27%

profile of v3, /device:TPU:8, one launch (start us, length us, event | category | flops | bytes accessed | tf_op | source)
XLA Modules:
  0.0 48.8 jit_solution(5409817745757746864)
XLA Ops:
  0.0 1.2 %copy-done = bf16[2,2,4,128,256]{4,3,2,1,0:T(8,128)(2,1)S(1)} copy-done((bf16[2,2,4,128,256]{4,3,2,1,0:T(8,128)(2,1)S(1)}, bf16[2,2,4,128,256]{4,3,2,1,0:T(8,128)(2,1)}, u32[]{:S(2)}) %copy-start) | copy-done | bytes 1048600
  1.2 1.0 %copy-done.2 = bf16[4,3,128,128]{3,2,1,0:T(8,128)(2,1)S(1)} copy-done((bf16[4,3,128,128]{3,2,1,0:T(8,128)(2,1)S(1)}, bf16[4,3,128,128]{3,2,1,0:T(8,128)(2,1)}, u32[]{:S(2)}) %copy-start.2) | copy-done | bytes 393240
  2.2 0.7 %copy-done.3 = s32[4,3]{1,0:T(4,128)S(1)} copy-done((s32[4,3]{1,0:T(4,128)S(1)}, s32[4,3]{1,0:T(4,128)}, u32[]{:S(2)}) %copy-start.3) | copy-done | bytes 72
  2.9 0.7 %copy-done.4 = f32[4]{0:T(128)S(1)} copy-done((f32[4]{0:T(128)S(1)}, f32[4]{0:T(128)}, u32[]{:S(2)}) %copy-start.4) | copy-done | bytes 40
  3.6 0.7 %copy-done.5 = s32[4]{0:T(128)S(1)} copy-done((s32[4]{0:T(128)S(1)}, s32[4]{0:T(128)}, u32[]{:S(2)}) %copy-start.5) | copy-done | bytes 40
  4.2 3.1 %shard_map.55 = (bf16[1,2,2,128,256]{4,3,2,1,0:T(8,128)(2,1)S(1)}, f32[1,2,2,128,256]{4,3,2,1,0:T(8,128)S(1)}, f32[1,2,2,128,256]{4,3,2,1,0:T(8,128)S(1)}, bf16[...) custom-call(f32[4]{0:T(128)S(1)} %copy-done.4, ...), custom_call_target="tpu_custom_call" | custom-call | flops 1024 | bytes 1024 | tf_op jit(solution)/shard_map/pallas_call | solution.py:150
  7.4 1.6 %collective-permute-start = (bf16[1,2,2,128,256]{4,3,2,1,0:T(8,128)(2,1)S(1)}, bf16[1,2,2,128,256]{4,3,2,1,0:T(8,128)(2,1)S(1)}, u32[]{:S(2)}, u32[]{:S(2)}) collective-permute-start(bf16[1,2,2,128,256]{4,3,2,1,0:T(8,128)(2,1)S(1)} %get-tuple-element.40), channel_id=1, source_target_pairs={{0,16},{8,24},{16,0},{24,8},{1,17},{9,25},{17,1},{25,9},{2,18},{10... | collective-permute-start | bytes 786440 | tf_op jit(solution)/shard_map/ppermute | solution.py:267
  8.9 1.9 %collective-permute-start.2 = (bf16[2,2,1,128,256]{4,3,2,1,0:T(8,128)(2,1)S(1)}, bf16[2,2,1,128,256]{4,3,2,1,0:T(8,128)(2,1)S(1)}, u32[]{:S(2)}, u32[]{:S(2)}) collective-permute-start(bf16[2,2,1,128,256]{4,3,2,1,0:T(8,128)(2,1)S(1)} %get-tuple-element.45), channel_id=1, source_target_pairs={{0,1},{1,2},{2,3},{3,4},{4,5},{5,6},{6,7},{8,9},{9,10},{10,11},{11... | collective-permute-start | bytes 786440 | tf_op jit(solution)/shard_map/ppermute | solution.py:284
  10.9 3.6 %collective-permute-start.3 = (bf16[2,2,1,128,256]{4,3,2,1,0:T(8,128)(2,1)S(1)}, bf16[2,2,1,128,256]{4,3,2,1,0:T(8,128)(2,1)S(1)}, u32[]{:S(2)}, u32[]{:S(2)}) collective-permute-start(bf16[2,2,1,128,256]{4,3,2,1,0:T(8,128)(2,1)S(1)} %get-tuple-element.46), channel_id=1, source_target_pairs={{1,0},{2,1},{3,2},{4,3},{5,4},{6,5},{7,6},{9,8},{10,9},{11,10},{12... | collective-permute-start | bytes 786440 | tf_op jit(solution)/shard_map/ppermute | solution.py:285
  14.5 1.6 %collective-permute-start.1 = (bf16[1,2,4,128,128]{4,3,2,1,0:T(8,128)(2,1)S(1)}, bf16[1,2,4,128,128]{4,3,2,1,0:T(8,128)(2,1)S(1)}, u32[]{:S(2)}, u32[]{:S(2)}) collective-permute-start(bf16[1,2,4,128,128]{4,3,2,1,0:T(8,128)(2,1)S(1)} %get-tuple-element.44), channel_id=1, source_target_pairs={{0,8},{8,0},{16,24},{24,16},{1,9},{9,1},{17,25},{25,17},{2,10},{10... | collective-permute-start | bytes 786440 | tf_op jit(solution)/shard_map/ppermute | solution.py:283
  16.1 1.7 %shard_map.56 = (bf16[1,2,2,128,128]{4,3,2,1,0:T(8,128)(2,1)S(1)}, f32[1,2,2,128,128]{4,3,2,1,0:T(8,128)S(1)}, f32[1,2,2,128,128]{4,3,2,1,0:T(8,128)S(1)}) custom-call(f32[4]{0:T(128)S(1)} %copy-done.4, s32[4]{0:T(128)S(1)} %copy-done.5, s32[4,3]{1,0:T(4,128)S(1)} %copy-done.3, bf16[3,512,128]{2,1,0:T(8,128)(2,1)S(1)} %get-tuple-element.62.refs_3_, ...), custom_call_target="tpu_custom_call" | custom-call | flops 1024 | bytes 1024 | tf_op jit(solution)/shard_map/pallas_call | solution.py:208
  17.8 0.6 %collective-permute-start.4 = (bf16[1,2,2,128,128]{4,3,2,1,0:T(8,128)(2,1)S(1)}, bf16[1,2,2,128,128]{4,3,2,1,0:T(8,128)(2,1)S(1)}, u32[]{:S(2)}, u32[]{:S(2)}) collective-permute-start(bf16[1,2,2,128,128]{4,3,2,1,0:T(8,128)(2,1)S(1)} %get-tuple-element.53), channel_id=1, source_target_pairs={{0,16},{8,24},{16,0},{24,8},{1,17},{9,25},{17,1},{25,9},{2,18},{10... | collective-permute-start | bytes 393224 | tf_op jit(solution)/shard_map/ppermute | solution.py:267
  18.3 0.1 add_convert_fusion.1
  18.4 0.6 %collective-permute-start.12 = (bf16[1,2,2,128,256]{4,3,2,1,0:T(8,128)(2,1)S(1)}, bf16[1,2,2,128,256]{4,3,2,1,0:T(8,128)(2,1)S(1)}, u32[]{:S(2)}, u32[]{:S(2)}) collective-permute-start(bf16[1,2,2,128,256]{4,3,2,1,0:T(8,128)(2,1)S(1)} %add_convert_fusion.1), channel_id=1, source_target_pairs={{0,8},{8,0},{16,24},{24,16},{1,9},{9,1},{17,25},{25,17},{2,10},{10... | collective-permute-start | bytes 786440 | tf_op jit(solution)/shard_map/ppermute | solution.py:273
  19.0 2.9 %shard_map.57 = (bf16[1,2,2,128,256]{4,3,2,1,0:T(8,128)(2,1)S(1)}, f32[1,2,2,128,256]{4,3,2,1,0:T(8,128)S(1)}, f32[1,2,2,128,256]{4,3,2,1,0:T(8,128)S(1)}) custom-call(f32[4]{0:T(128)S(1)} %copy-done.4, s32[4]{0:T(128)S(1)} %copy-done.5, s32[4,3]{1,0:T(4,128)S(1)} %copy-done.3, bf16[3,512,128]{2,1,0:T(8,128)(2,1)S(1)} %get-tuple-element.62.refs_3_, ...), custom_call_target="tpu_custom_call" | custom-call | flops 1024 | bytes 1024 | tf_op jit(solution)/shard_map/pallas_call | solution.py:208
  21.9 1.6 %collective-permute-start.5 = (bf16[1,2,2,128,256]{4,3,2,1,0:T(8,128)(2,1)S(1)}, bf16[1,2,2,128,256]{4,3,2,1,0:T(8,128)(2,1)S(1)}, u32[]{:S(2)}, u32[]{:S(2)}) collective-permute-start(bf16[1,2,2,128,256]{4,3,2,1,0:T(8,128)(2,1)S(1)} %get-tuple-element.59), channel_id=1, source_target_pairs={{0,16},{8,24},{16,0},{24,8},{1,17},{9,25},{17,1},{25,9},{2,18},{10... | collective-permute-start | bytes 786440 | tf_op jit(solution)/shard_map/ppermute | solution.py:267
  23.5 0.3 collective-permute-done.1.refs_5_
  23.8 1.9 %collective-permute-start.6 = (bf16[1,2,1,128,128]{4,3,2,1,0:T(8,128)(2,1)S(1)}, bf16[1,2,1,128,128]{4,3,2,1,0:T(8,128)(2,1)S(1)}, u32[]{:S(2)}, u32[]{:S(2)}) collective-permute-start(bf16[1,2,1,128,128]{4,3,2,1,0:T(8,128)(2,1)S(1)} %get-tuple-element.48), channel_id=1, source_target_pairs={{0,1},{1,2},{2,3},{3,4},{4,5},{5,6},{6,7},{8,9},{9,10},{10,11},{11... | collective-permute-start | bytes 196616 | tf_op jit(solution)/shard_map/ppermute | solution.py:299
  25.7 3.6 %collective-permute-start.7 = (bf16[1,2,1,128,128]{4,3,2,1,0:T(8,128)(2,1)S(1)}, bf16[1,2,1,128,128]{4,3,2,1,0:T(8,128)(2,1)S(1)}, u32[]{:S(2)}, u32[]{:S(2)}) collective-permute-start(bf16[1,2,1,128,128]{4,3,2,1,0:T(8,128)(2,1)S(1)} %get-tuple-element.49), channel_id=1, source_target_pairs={{1,0},{2,1},{3,2},{4,3},{5,4},{6,5},{7,6},{9,8},{10,9},{11,10},{12... | collective-permute-start | bytes 196616 | tf_op jit(solution)/shard_map/ppermute | solution.py:300
  29.3 1.7 %shard_map.58 = (bf16[1,2,2,128,128]{4,3,2,1,0:T(8,128)(2,1)S(1)}, f32[1,2,2,128,128]{4,3,2,1,0:T(8,128)S(1)}, f32[1,2,2,128,128]{4,3,2,1,0:T(8,128)S(1)}) custom-call(f32[4]{0:T(128)S(1)} %copy-done.4, s32[4]{0:T(128)S(1)} %copy-done.5, s32[4,3]{1,0:T(4,128)S(1)} %copy-done.3, bf16[3,512,128]{2,1,0:T(8,128)(2,1)S(1)} %get-tuple-element.62.refs_3_, ...), custom_call_target="tpu_custom_call" | custom-call | flops 1024 | bytes 1024 | tf_op jit(solution)/shard_map/pallas_call | solution.py:208
  31.1 1.6 %collective-permute-start.9 = (bf16[1,2,2,128,128]{4,3,2,1,0:T(8,128)(2,1)S(1)}, bf16[1,2,2,128,128]{4,3,2,1,0:T(8,128)(2,1)S(1)}, u32[]{:S(2)}, u32[]{:S(2)}) collective-permute-start(bf16[1,2,2,128,128]{4,3,2,1,0:T(8,128)(2,1)S(1)} %add_convert_fusion.3), channel_id=1, source_target_pairs={{0,8},{8,0},{16,24},{24,16},{1,9},{9,1},{17,25},{25,17},{2,10},{10... | collective-permute-start | bytes 393224 | tf_op jit(solution)/shard_map/ppermute | solution.py:273
  32.7 0.5 %collective-permute-start.10 = (bf16[1,2,2,128,128]{4,3,2,1,0:T(8,128)(2,1)S(1)}, bf16[1,2,2,128,128]{4,3,2,1,0:T(8,128)(2,1)S(1)}, u32[]{:S(2)}, u32[]{:S(2)}) collective-permute-start(bf16[1,2,2,128,128]{4,3,2,1,0:T(8,128)(2,1)S(1)} %get-tuple-element.66), channel_id=1, source_target_pairs={{0,16},{8,24},{16,0},{24,8},{1,17},{9,25},{17,1},{25,9},{2,18},{10... | collective-permute-start | bytes 393224 | tf_op jit(solution)/shard_map/ppermute | solution.py:267
  33.2 2.8 %shard_map.59 = (bf16[1,2,4,128,128]{4,3,2,1,0:T(8,128)(2,1)S(1)}, f32[1,2,4,128,128]{4,3,2,1,0:T(8,128)S(1)}) custom-call(f32[4]{0:T(128)S(1)} %copy-done.4, s32[4]{0:T(128)S(1)} %copy-done.5, s32[4,3]{1,0:T(4,128)S(1)} %copy-done.3, bf16[3,512,128]{2,1,0:T(8,128)(2,1)S(1)} %get-tuple-element.62.refs_3_, ...), custom_call_target="tpu_custom_call" | custom-call | flops 1024 | bytes 1024 | tf_op jit(solution)/shard_map/pallas_call | solution.py:208
  36.0 1.6 %collective-permute-start.8 = (bf16[1,2,4,128,128]{4,3,2,1,0:T(8,128)(2,1)S(1)}, bf16[1,2,4,128,128]{4,3,2,1,0:T(8,128)(2,1)S(1)}, u32[]{:S(2)}, u32[]{:S(2)}) collective-permute-start(bf16[1,2,4,128,128]{4,3,2,1,0:T(8,128)(2,1)S(1)} %get-tuple-element.64), channel_id=1, source_target_pairs={{0,16},{8,24},{16,0},{24,8},{1,17},{9,25},{17,1},{25,9},{2,18},{10... | collective-permute-start | bytes 786440 | tf_op jit(solution)/shard_map/ppermute | solution.py:267
  37.6 0.1 add_convert_fusion
  37.7 0.6 %collective-permute-start.13 = (bf16[1,2,2,128,256]{4,3,2,1,0:T(8,128)(2,1)S(1)}, bf16[1,2,2,128,256]{4,3,2,1,0:T(8,128)(2,1)S(1)}, u32[]{:S(2)}, u32[]{:S(2)}) collective-permute-start(bf16[1,2,2,128,256]{4,3,2,1,0:T(8,128)(2,1)S(1)} %add_convert_fusion), channel_id=1, source_target_pairs={{0,8},{8,0},{16,24},{24,16},{1,9},{9,1},{17,25},{25,17},{2,10},{10... | collective-permute-start | bytes 786440 | tf_op jit(solution)/shard_map/ppermute | solution.py:273
  38.3 3.0 %shard_map.60.mine = f32[1,2,4,128,128]{4,3,2,1,0:T(8,128)S(1)} custom-call(f32[4]{0:T(128)S(1)} %copy-done.4, s32[4]{0:T(128)S(1)} %copy-done.5, s32[4,3]{1,0:T(4,128)S(1)} %copy-done.3, bf16[3,512,128]{2,1,0:T(8,128)(2,1)S(1)} %get-tuple-element.62.refs_3_, bf16[4,128,384]{2,1,0:T(8,128)(2,1)S(1)} %get-tuple-element.63.refs_4_, ...), custom_call_target="tpu_custom_call" | custom-call | flops 1024 | bytes 1024 | tf_op jit(solution)/shard_map/pallas_call | solution.py:208
  41.4 1.6 %collective-permute-start.11 = (bf16[1,2,2,128,128]{4,3,2,1,0:T(8,128)(2,1)S(1)}, bf16[1,2,2,128,128]{4,3,2,1,0:T(8,128)(2,1)S(1)}, u32[]{:S(2)}, u32[]{:S(2)}) collective-permute-start(bf16[1,2,2,128,128]{4,3,2,1,0:T(8,128)(2,1)S(1)} %add_convert_fusion.2), channel_id=1, source_target_pairs={{0,8},{8,0},{16,24},{24,16},{1,9},{9,1},{17,25},{25,17},{2,10},{10... | collective-permute-start | bytes 393224 | tf_op jit(solution)/shard_map/ppermute | solution.py:273
  42.9 3.6 %collective-permute-done.13.got_out = bf16[1,2,2,128,256]{4,3,2,1,0:T(8,128)(2,1)S(1)} collective-permute-done((bf16[1,2,2,128,256]{4,3,2,1,0:T(8,128)(2,1)S(1)}, bf16[1,2,2,128,256]{4,3,2,1,0:T(8,128)(2,1)S(1)}, u32[]{:S(2)}, u32[]{:S(2)}) %collective-permute-start.13) | collective-permute-done | bytes 262176 | tf_op jit(solution)/shard_map/ppermute | solution.py:273
  46.5 0.9 %shard_map.61._ = bf16[2,2,4,128,256]{4,3,2,1,0:T(8,128)(2,1)} custom-call(f32[1,2,2,128,256]{4,3,2,1,0:T(8,128)S(1)} %get-tuple-element.68.mine_in, bf16[1,2,2,128,256]{4,3,2,1,0:T(8,128)(2,1)S(1)} %collective-permute-done.12.got_in, f32[1,2,2,128,256]{4,3,2,1,0:T(8,128)S(1)} %get-tuple-element.47.mine_out, ...), custom_call_target="tpu_custom_call" | custom-call | flops 1024 | bytes 1024 | tf_op jit(solution)/shard_map/pallas_call | solution.py:243
  47.4 0.5 collective-permute-done.11.got_out
  47.9 0.9 %shard_map.62 = bf16[2,2,4,128,256]{4,3,2,1,0:T(8,128)(2,1)} custom-call(f32[1,2,4,128,128]{4,3,2,1,0:T(8,128)S(1)} %shard_map.60.mine, f32[1,2,4,128,128]{4,3,2,1,0:T(8,128)S(1)} %get-tuple-element.60.near, bf16[1,2,4,128,128]{4,3,2,1,0:T(8,128)(2,1)S(1)} %collective-permute-done.8.got, ...), custom_call_target="tpu_custom_call", output_to_operand_aliasing={{}: (7, {})} | custom-call | flops 1024 | bytes 1024 | tf_op jit(solution)/shard_map/pallas_call | solution.py:243
  (21 shorter events, 0.1 us)
Async XLA Ops:
  0.0 1.2 %copy-start = (bf16[2,2,4,128,256]{4,3,2,1,0:T(8,128)(2,1)S(1)}, bf16[2,2,4,128,256]{4,3,2,1,0:T(8,128)(2,1)}, u32[]{:S(2)}) copy-start(bf16[2,2,4,128,256]{4,3,2,1,0:T(8,128)(2,1)} %refs_5_.7) | copy-start | bytes 3145732
  1.2 1.0 %copy-start.2 = (bf16[4,3,128,128]{3,2,1,0:T(8,128)(2,1)S(1)}, bf16[4,3,128,128]{3,2,1,0:T(8,128)(2,1)}, u32[]{:S(2)}) copy-start(bf16[4,3,128,128]{3,2,1,0:T(8,128)(2,1)} %c_h.1) | copy-start | bytes 1179652
  2.2 0.7 %copy-start.3 = (s32[4,3]{1,0:T(4,128)S(1)}, s32[4,3]{1,0:T(4,128)}, u32[]{:S(2)}) copy-start(s32[4,3]{1,0:T(4,128)} %refs_2_.9) | copy-start | bytes 148
  2.9 0.7 %copy-start.4 = (f32[4]{0:T(128)S(1)}, f32[4]{0:T(128)}, u32[]{:S(2)}) copy-start(f32[4]{0:T(128)} %refs_0_.9) | copy-start | bytes 52
  3.6 0.7 %copy-start.5 = (s32[4]{0:T(128)S(1)}, s32[4]{0:T(128)}, u32[]{:S(2)}) copy-start(s32[4]{0:T(128)} %refs_1_.9) | copy-start | bytes 52
  4.2 11.9 %copy-start.1 = (bf16[2,2,4,128,256]{4,3,2,1,0:T(8,128)(2,1)S(1)}, bf16[2,2,4,128,256]{4,3,2,1,0:T(8,128)(2,1)}, u32[]{:S(2)}) copy-start(bf16[2,2,4,128,256]{4,3,2,1,0:T(8,128)(2,1)} %refs_5_.7) | copy-start | bytes 3145732
  7.4 11.0 %collective-permute-start = (bf16[1,2,2,128,256]{4,3,2,1,0:T(8,128)(2,1)S(1)}, bf16[1,2,2,128,256]{4,3,2,1,0:T(8,128)(2,1)S(1)}, u32[]{:S(2)}, u32[]{:S(2)}) collective-permute-start(bf16[1,2,2,128,256]{4,3,2,1,0:T(8,128)(2,1)S(1)} %get-tuple-element.40), channel_id=1, source_target_pairs={{0,16},{8,24},{16,0},{24,8},{1,17},{9,25},{17,1},{25,9},{2,18},{10... | collective-permute-start | bytes 786440 | tf_op jit(solution)/shard_map/ppermute | solution.py:267
  8.9 10.1 %collective-permute-start.2 = (bf16[2,2,1,128,256]{4,3,2,1,0:T(8,128)(2,1)S(1)}, bf16[2,2,1,128,256]{4,3,2,1,0:T(8,128)(2,1)S(1)}, u32[]{:S(2)}, u32[]{:S(2)}) collective-permute-start(bf16[2,2,1,128,256]{4,3,2,1,0:T(8,128)(2,1)S(1)} %get-tuple-element.45), channel_id=1, source_target_pairs={{0,1},{1,2},{2,3},{3,4},{4,5},{5,6},{6,7},{8,9},{9,10},{10,11},{11... | collective-permute-start | bytes 786440 | tf_op jit(solution)/shard_map/ppermute | solution.py:284
  10.9 8.2 %collective-permute-start.3 = (bf16[2,2,1,128,256]{4,3,2,1,0:T(8,128)(2,1)S(1)}, bf16[2,2,1,128,256]{4,3,2,1,0:T(8,128)(2,1)S(1)}, u32[]{:S(2)}, u32[]{:S(2)}) collective-permute-start(bf16[2,2,1,128,256]{4,3,2,1,0:T(8,128)(2,1)S(1)} %get-tuple-element.46), channel_id=1, source_target_pairs={{1,0},{2,1},{3,2},{4,3},{5,4},{6,5},{7,6},{9,8},{10,9},{11,10},{12... | collective-permute-start | bytes 786440 | tf_op jit(solution)/shard_map/ppermute | solution.py:285
  14.5 9.2 %collective-permute-start.1 = (bf16[1,2,4,128,128]{4,3,2,1,0:T(8,128)(2,1)S(1)}, bf16[1,2,4,128,128]{4,3,2,1,0:T(8,128)(2,1)S(1)}, u32[]{:S(2)}, u32[]{:S(2)}) collective-permute-start(bf16[1,2,4,128,128]{4,3,2,1,0:T(8,128)(2,1)S(1)} %get-tuple-element.44), channel_id=1, source_target_pairs={{0,8},{8,0},{16,24},{24,16},{1,9},{9,1},{17,25},{25,17},{2,10},{10... | collective-permute-start | bytes 786440 | tf_op jit(solution)/shard_map/ppermute | solution.py:283
  17.8 13.3 %collective-permute-start.4 = (bf16[1,2,2,128,128]{4,3,2,1,0:T(8,128)(2,1)S(1)}, bf16[1,2,2,128,128]{4,3,2,1,0:T(8,128)(2,1)S(1)}, u32[]{:S(2)}, u32[]{:S(2)}) collective-permute-start(bf16[1,2,2,128,128]{4,3,2,1,0:T(8,128)(2,1)S(1)} %get-tuple-element.53), channel_id=1, source_target_pairs={{0,16},{8,24},{16,0},{24,8},{1,17},{9,25},{17,1},{25,9},{2,18},{10... | collective-permute-start | bytes 393224 | tf_op jit(solution)/shard_map/ppermute | solution.py:267
  18.4 24.5 %collective-permute-start.12 = (bf16[1,2,2,128,256]{4,3,2,1,0:T(8,128)(2,1)S(1)}, bf16[1,2,2,128,256]{4,3,2,1,0:T(8,128)(2,1)S(1)}, u32[]{:S(2)}, u32[]{:S(2)}) collective-permute-start(bf16[1,2,2,128,256]{4,3,2,1,0:T(8,128)(2,1)S(1)} %add_convert_fusion.1), channel_id=1, source_target_pairs={{0,8},{8,0},{16,24},{24,16},{1,9},{9,1},{17,25},{25,17},{2,10},{10... | collective-permute-start | bytes 786440 | tf_op jit(solution)/shard_map/ppermute | solution.py:273
  21.9 15.7 %collective-permute-start.5 = (bf16[1,2,2,128,256]{4,3,2,1,0:T(8,128)(2,1)S(1)}, bf16[1,2,2,128,256]{4,3,2,1,0:T(8,128)(2,1)S(1)}, u32[]{:S(2)}, u32[]{:S(2)}) collective-permute-start(bf16[1,2,2,128,256]{4,3,2,1,0:T(8,128)(2,1)S(1)} %get-tuple-element.59), channel_id=1, source_target_pairs={{0,16},{8,24},{16,0},{24,8},{1,17},{9,25},{17,1},{25,9},{2,18},{10... | collective-permute-start | bytes 786440 | tf_op jit(solution)/shard_map/ppermute | solution.py:267
  23.8 8.9 %collective-permute-start.6 = (bf16[1,2,1,128,128]{4,3,2,1,0:T(8,128)(2,1)S(1)}, bf16[1,2,1,128,128]{4,3,2,1,0:T(8,128)(2,1)S(1)}, u32[]{:S(2)}, u32[]{:S(2)}) collective-permute-start(bf16[1,2,1,128,128]{4,3,2,1,0:T(8,128)(2,1)S(1)} %get-tuple-element.48), channel_id=1, source_target_pairs={{0,1},{1,2},{2,3},{3,4},{4,5},{5,6},{6,7},{8,9},{9,10},{10,11},{11... | collective-permute-start | bytes 196616 | tf_op jit(solution)/shard_map/ppermute | solution.py:299
  25.7 7.5 %collective-permute-start.7 = (bf16[1,2,1,128,128]{4,3,2,1,0:T(8,128)(2,1)S(1)}, bf16[1,2,1,128,128]{4,3,2,1,0:T(8,128)(2,1)S(1)}, u32[]{:S(2)}, u32[]{:S(2)}) collective-permute-start(bf16[1,2,1,128,128]{4,3,2,1,0:T(8,128)(2,1)S(1)} %get-tuple-element.49), channel_id=1, source_target_pairs={{1,0},{2,1},{3,2},{4,3},{5,4},{6,5},{7,6},{9,8},{10,9},{11,10},{12... | collective-permute-start | bytes 196616 | tf_op jit(solution)/shard_map/ppermute | solution.py:300
  31.1 16.3 %collective-permute-start.9 = (bf16[1,2,2,128,128]{4,3,2,1,0:T(8,128)(2,1)S(1)}, bf16[1,2,2,128,128]{4,3,2,1,0:T(8,128)(2,1)S(1)}, u32[]{:S(2)}, u32[]{:S(2)}) collective-permute-start(bf16[1,2,2,128,128]{4,3,2,1,0:T(8,128)(2,1)S(1)} %add_convert_fusion.3), channel_id=1, source_target_pairs={{0,8},{8,0},{16,24},{24,16},{1,9},{9,1},{17,25},{25,17},{2,10},{10... | collective-permute-start | bytes 393224 | tf_op jit(solution)/shard_map/ppermute | solution.py:273
  32.7 8.6 %collective-permute-start.10 = (bf16[1,2,2,128,128]{4,3,2,1,0:T(8,128)(2,1)S(1)}, bf16[1,2,2,128,128]{4,3,2,1,0:T(8,128)(2,1)S(1)}, u32[]{:S(2)}, u32[]{:S(2)}) collective-permute-start(bf16[1,2,2,128,128]{4,3,2,1,0:T(8,128)(2,1)S(1)} %get-tuple-element.66), channel_id=1, source_target_pairs={{0,16},{8,24},{16,0},{24,8},{1,17},{9,25},{17,1},{25,9},{2,18},{10... | collective-permute-start | bytes 393224 | tf_op jit(solution)/shard_map/ppermute | solution.py:267
  36.0 11.4 %collective-permute-start.8 = (bf16[1,2,4,128,128]{4,3,2,1,0:T(8,128)(2,1)S(1)}, bf16[1,2,4,128,128]{4,3,2,1,0:T(8,128)(2,1)S(1)}, u32[]{:S(2)}, u32[]{:S(2)}) collective-permute-start(bf16[1,2,4,128,128]{4,3,2,1,0:T(8,128)(2,1)S(1)} %get-tuple-element.64), channel_id=1, source_target_pairs={{0,16},{8,24},{16,0},{24,8},{1,17},{9,25},{17,1},{25,9},{2,18},{10... | collective-permute-start | bytes 786440 | tf_op jit(solution)/shard_map/ppermute | solution.py:267
  37.7 8.8 %collective-permute-start.13 = (bf16[1,2,2,128,256]{4,3,2,1,0:T(8,128)(2,1)S(1)}, bf16[1,2,2,128,256]{4,3,2,1,0:T(8,128)(2,1)S(1)}, u32[]{:S(2)}, u32[]{:S(2)}) collective-permute-start(bf16[1,2,2,128,256]{4,3,2,1,0:T(8,128)(2,1)S(1)} %add_convert_fusion), channel_id=1, source_target_pairs={{0,8},{8,0},{16,24},{24,16},{1,9},{9,1},{17,25},{25,17},{2,10},{10... | collective-permute-start | bytes 786440 | tf_op jit(solution)/shard_map/ppermute | solution.py:273
  41.4 6.5 %collective-permute-start.11 = (bf16[1,2,2,128,128]{4,3,2,1,0:T(8,128)(2,1)S(1)}, bf16[1,2,2,128,128]{4,3,2,1,0:T(8,128)(2,1)S(1)}, u32[]{:S(2)}, u32[]{:S(2)}) collective-permute-start(bf16[1,2,2,128,128]{4,3,2,1,0:T(8,128)(2,1)S(1)} %add_convert_fusion.2), channel_id=1, source_target_pairs={{0,8},{8,0},{16,24},{24,16},{1,9},{9,1},{17,25},{25,17},{2,10},{10... | collective-permute-start | bytes 393224 | tf_op jit(solution)/shard_map/ppermute | solution.py:273

commit v4 on v0

v4 whole, which is shorter than its diff:
```python
import functools

import jax
import jax.numpy as jnp
from jax import lax
from jax.experimental import pallas as pl
from jax.experimental.pallas import tpu as pltpu
from jax.sharding import PartitionSpec as P

BF16 = jnp.bfloat16
F32 = jnp.float32

NEAR, FAR = "n", "f"
FIRST = (("full", 1, 1), ("full", 1, 2))
SECOND = (("full", 1, NEAR), ("half", 0, 1, (1, 2)))
THIRD = (("full", 1, FAR), ("half", 0, 1, (NEAR, FAR)))
RAW = (("half", 0, 0, (1, 2)), ("half", 0, 0, (NEAR, FAR)))


def stack_coupling(c_ref, rows, cols):
    modes, slots, size = c_ref.shape[:3]
    for m in range(modes):
        for k in range(slots):
            c = c_ref[m, k]
            rows[k, m * size : (m + 1) * size, :] = c
            cols[m, :, k * size : (k + 1) * size] = c


def place(block, owned):
    odd = lax.rem(lax.axis_index("slab"), 2)
    return {NEAR: (owned - 1) * (1 - odd), FAR: (owned - 1) * odd}.get(block, block)


def group_terms(group, flip, scalars, rows, cols, own, edges, outs, half, acc):
    occ, off, nbr = scalars
    far, near, mine = outs
    slots, wide, size = rows.shape
    modes = wide // size
    owned = nbr.shape[0]
    count = acc.shape[0] // 3
    first = lax.axis_index("slab") * owned
    odd = lax.rem(lax.axis_index("energy") + flip, 2)
    part = group[1]

    def source(block, k, e, lanes):
        listed = nbr[place(block, owned), k]
        local = listed - first
        tile = own(part, e, jnp.clip(local, 0, owned - 1), lanes)
        if block in (NEAR, FAR):
            outside = jnp.logical_or(local < 0, local >= owned)
            tile = jnp.where(outside, edges[block](part, e, lanes), tile)
        return jnp.where(listed >= 0, tile, jnp.zeros_like(tile))

    for k in range(slots):
        for j in range(2):
            if group[0] == "full":
                src = source(group[2], k, j, slice(0, 2 * size))
            else:
                lanes = slice(group[2] * size, (group[2] + 1) * size)
                src = jnp.concatenate([source(group[3][j], k, e, lanes) for e in range(count)], axis=1)
            r = jnp.dot(rows[k], src, preferred_element_type=F32).astype(BF16)
            for m in range(modes):
                for h in range(2):
                    e, u = (j, h) if group[0] == "full" else (h, j)
                    to = (e * 2 + u) * size
                    half[m, to : to + size, k * size : (k + 1) * size] = r[
                        m * size : (m + 1) * size, h * size : (h + 1) * size
                    ]
    acc[...] = jnp.zeros_like(acc)

    def second(m):
        y = lax.dot_general(half[m], cols[m], (((1,), (1,)), ((), ())), preferred_element_type=F32)
        o = off[m]
        n = occ[m]
        down, up = (n + 1.0, n) if part == 0 else (n, n + 1.0)
        for e in range(count):
            for u in range(2):
                to = (e * 2 + u) * size
                ys = y[to : to + size]
                acc[e - o + count, u] += down * ys
                acc[e + o + count, u] += up * ys

    for m in range(modes):
        if far is None and near is None:
            pl.when(off[m] < count)(functools.partial(second, m))
        else:
            second(m)
    if far is not None:
        far[...] = acc[pl.ds(2 * count * odd, count)].astype(BF16)
    if near is not None:
        near[...] = acc[pl.ds(2 * count * (1 - odd), count)]
    if mine is not None:
        mine[...] = acc[pl.ds(count, count)]


def pieces(size, count):
    return (2, count, 2, size, size)


def scratch(modes, slots, size, count):
    return [
        pltpu.VMEM((modes, count * 2 * size, slots * size), BF16),
        pltpu.VMEM((3 * count, 2, size, size), F32),
    ]


VMEM = pl.BlockSpec(memory_space=pltpu.VMEM)
SMEM = pl.BlockSpec(memory_space=pltpu.SMEM)
HBM = pl.BlockSpec(memory_space=pltpu.HBM)
SMALL = pl.CostEstimate(flops=1024, bytes_accessed=1024, transcendentals=0)


def first_body(occ_h, off_h, nbr_h, c_h, g_h, far_h, near_h, mine_h, rows_h, cols_h, raw_h, edge_n, edge_f, occ, off, nbr, c_ref, own, far, near, mine, rows, cols, sems, outs, half, acc):
    size = c_h.shape[-1]
    owned = g_h.shape[2]
    fetches = [
        pltpu.make_async_copy(src, dst, sems.at[i])
        for i, (src, dst) in enumerate([(c_h, c_ref), (g_h, own), (occ_h, occ), (off_h, off), (nbr_h, nbr)])
    ]
    for fetch in fetches:
        fetch.start()
    sends = []

    def send(src, dst):
        copy = pltpu.make_async_copy(src, dst, outs.at[len(sends)])
        copy.start()
        sends.append(copy)

    fetches[0].wait()
    stack_coupling(c_ref, rows, cols)
    send(rows, rows_h)
    send(cols, cols_h)
    for fetch in fetches[1:]:
        fetch.wait()
    send(own.at[0, :, :, :, pl.ds(0, size)], raw_h)
    send(own.at[:, :, place(NEAR, owned)], edge_n)
    send(own.at[:, :, place(FAR, owned)], edge_f)

    def read(part, e, at, lanes):
        return own[part, e, at, :, lanes]

    for i, group in enumerate(FIRST):
        group_terms(group, 0, (occ, off, nbr), rows, cols, read, {}, (far.at[i], near.at[i], mine.at[i]), half, acc)
        send(far.at[i], far_h.at[i])
        send(near.at[i], near_h.at[i])
        send(mine.at[i], mine_h.at[i])
    for copy in sends:
        copy.wait()


def first_call(greens, coupling, occupation, offsets, neighbours):
    modes, slots, size = coupling.shape[:3]
    parts, count, owned = greens.shape[:3]
    shape = pieces(size, count)
    rows, cols = (slots, modes * size, size), (modes, size, slots * size)
    edge = (parts, count, size, 2 * size)
    outs = [
        (shape, BF16),
        (shape, F32),
        (shape, F32),
        (rows, BF16),
        (cols, BF16),
        ((count, owned, size, size), BF16),
        (edge, BF16),
        (edge, BF16),
    ]
    return pl.pallas_call(
        first_body,
        out_shape=[jax.ShapeDtypeStruct(*out) for out in outs],
        in_specs=[HBM] * 5,
        out_specs=[HBM] * 8,
        scratch_shapes=[
            pltpu.SMEM(occupation.shape, F32),
            pltpu.SMEM(offsets.shape, jnp.int32),
            pltpu.SMEM(neighbours.shape, jnp.int32),
            pltpu.VMEM(coupling.shape, BF16),
            pltpu.VMEM(greens.shape, BF16),
        ]
        + [pltpu.VMEM(*out) for out in outs[:5]]
        + [pltpu.SemaphoreType.DMA((5,)), pltpu.SemaphoreType.DMA((11,))]
        + scratch(modes, slots, size, count),
        compiler_params=pltpu.CompilerParams(vmem_limit_bytes=58 << 20),
        cost_estimate=SMALL,
    )(occupation, offsets, neighbours, coupling, greens)


def next_body(groups, flip, wanted, with_parts, n_edges, n_copied, *refs):
    occ, off, nbr, rows, cols, own = refs[:6]
    edge_refs = dict(zip((NEAR, FAR), refs[6 : 6 + n_edges]))
    at = 6 + n_edges
    copied = refs[at : at + n_copied]
    outs = list(refs[at + n_copied : -2])
    half, acc = refs[-2:]

    def read(part, e, at, lanes):
        return own[part, e, at, :, lanes] if with_parts else own[e, at]

    def read_edge(ref, part, e, lanes):
        return ref[part, e, :, lanes] if with_parts else ref[e]

    edges = {name: functools.partial(read_edge, ref) for name, ref in edge_refs.items()}
    results = [outs.pop(0) if want else None for want in wanted]
    for array in copied:
        for block in (NEAR, FAR):
            outs.pop(0)[...] = array[:, place(block, array.shape[1])]
    for i, group in enumerate(groups):
        views = [None if ref is None else ref.at[i] for ref in results]
        group_terms(group, flip, (occ, off, nbr), rows, cols, read, edges, views, half, acc)


def next_call(groups, flip, wanted, scalars, stacked, own, edges, copied=()):
    rows, cols = stacked
    slots, wide, size = rows.shape
    count = own.shape[-4]
    shape = pieces(size, count)
    outs = [jax.ShapeDtypeStruct(shape, kind) for want, kind in zip(wanted, (BF16, F32, F32)) if want]
    outs += [jax.ShapeDtypeStruct((count, size, size), BF16)] * (2 * len(copied))
    return pl.pallas_call(
        functools.partial(next_body, groups, flip, wanted, own.ndim == 5, len(edges), len(copied)),
        out_shape=outs,
        in_specs=[SMEM] * 3 + [VMEM] * (3 + len(edges) + len(copied)),
        out_specs=[VMEM] * len(outs),
        scratch_shapes=scratch(wide // size, slots, size, count),
        compiler_params=pltpu.CompilerParams(vmem_limit_bytes=16 << 20),
        cost_estimate=SMALL,
    )(*scalars, rows, cols, own, *edges, *copied)


def early_body(mine_1, got_1, mine_2, got_2, mine_z, near_z, got_z, out, whole, edge, half, raw, sems):
    owned, size = out.shape[2], out.shape[3]
    n, f = place(NEAR, owned), place(FAR, owned)
    im, re = pl.ds(size, size), pl.ds(0, size)
    copies = []

    def send(src, dst):
        copy = pltpu.make_async_copy(src, dst, sems.at[len(copies)])
        copy.start()
        copies.append(copy)

    def tile(mine, got, g, u):
        return (mine[g, :, u] + got[g, :, u].astype(F32)).astype(BF16)

    for u in range(2):
        for g in range(2):
            whole[:, g, :, u * size : (u + 1) * size] = tile(mine_1, got_1, g, u)
        edge[:, :, u * size : (u + 1) * size] = tile(mine_2, got_2, 0, u)
        half[:, u] = tile(mine_2, got_2, 1, u)
    send(whole, out.at[1, :, pl.ds(1, 2)])
    send(edge, out.at[1, :, n])
    send(half, out.at[0, :, pl.ds(1, 2), :, im])
    for g in range(2):
        for u in range(2):
            total = mine_z[g, :, u] + near_z[g, :, u] + got_z[g, :, u].astype(F32)
            raw[:, 2 * g + u] = total.astype(BF16)
    send(raw.at[:, pl.ds(0, 2)], out.at[0, :, pl.ds(1, 2), :, re])
    send(raw.at[:, 2], out.at[0, :, n, :, re])
    send(raw.at[:, 3], out.at[0, :, f, :, re])
    for copy in copies:
        copy.wait()


def late_body(mine, got, _, out, edge, half, sems):
    owned, size = out.shape[2], out.shape[3]
    n, f = place(NEAR, owned), place(FAR, owned)
    im = pl.ds(size, size)
    for u in range(2):
        edge[:, :, u * size : (u + 1) * size] = (mine[0, :, u] + got[0, :, u].astype(F32)).astype(BF16)
        half[:, u] = (mine[1, :, u] + got[1, :, u].astype(F32)).astype(BF16)
    copies = [
        pltpu.make_async_copy(edge, out.at[1, :, f], sems.at[0]),
        pltpu.make_async_copy(half.at[:, 0], out.at[0, :, n, :, im], sems.at[1]),
        pltpu.make_async_copy(half.at[:, 1], out.at[0, :, f, :, im], sems.at[2]),
    ]
    for copy in copies:
        copy.start()
    for copy in copies:
        copy.wait()


def add_up(early, late, greens):
    count, size = greens.shape[1], greens.shape[3]
    stage = [pltpu.VMEM((count, size, 2 * size), BF16), pltpu.VMEM((count, 2, size, size), BF16)]
    out = pl.pallas_call(
        early_body,
        out_shape=jax.ShapeDtypeStruct(greens.shape, BF16),
        in_specs=[VMEM] * len(early),
        out_specs=HBM,
        scratch_shapes=[pltpu.VMEM((count, 2, size, 2 * size), BF16)]
        + stage
        + [pltpu.VMEM((count, 4, size, size), BF16), pltpu.SemaphoreType.DMA((6,))],
        compiler_params=pltpu.CompilerParams(vmem_limit_bytes=16 << 20),
        cost_estimate=SMALL,
    )(*early)
    return pl.pallas_call(
        late_body,
        out_shape=jax.ShapeDtypeStruct(greens.shape, BF16),
        in_specs=[VMEM] * len(late) + [HBM],
        out_specs=HBM,
        scratch_shapes=stage + [pltpu.SemaphoreType.DMA((3,))],
        input_output_aliases={len(late): 0},
        compiler_params=pltpu.CompilerParams(vmem_limit_bytes=16 << 20),
        cost_estimate=SMALL,
    )(*late, out)


def after_these(array, *others):
    return lax.optimization_barrier((array,) + others)[0]


def on_device(greens, coupling, occupation, offsets, neighbours):
    slabs = lax.axis_size("slab")
    scalars = (occupation, offsets, neighbours)
    chip = [(i, i ^ 1) for i in range(slabs)]
    chips = [(i, i + 1 if i % 2 else i - 1) for i in range(1, slabs - 1)]

    def across(array):
        return lax.ppermute(array, "energy", [(i, i ^ 1) for i in range(4)])

    def along(array):
        return lax.ppermute(array, "energy", [(i, i ^ 2) for i in range(4)])

    def beside(array, pairs):
        return lax.ppermute(array, "slab", pairs)

    def total(near, relayed):
        return (near + relayed.astype(F32)).astype(BF16)

    far_1, near_1, mine_1, rows, cols, raw, edge_n, edge_f = first_call(
        greens, coupling, occupation, offsets, neighbours
    )
    stacked = (rows, cols)
    relay_1 = along(far_1)
    beside_n = beside(edge_n, chip)
    raw_x = across(raw)
    beside_f = beside(edge_f, chips)
    far_2, near_2, mine_2 = next_call(SECOND, 0, (1, 1, 1), scalars, stacked, greens, (beside_n,))
    relay_2 = along(far_2)
    both_1 = total(near_1, after_these(relay_1, far_2))
    got_1 = across(both_1)
    stacked = after_these(stacked, both_1)
    far_3, near_3, mine_3, raw_n, raw_f = next_call(
        THIRD, 0, (1, 1, 1), scalars, stacked, greens, (beside_n, beside_f), (raw_x,)
    )
    relay_3 = along(far_3)
    beside_xn = beside(raw_n, chip)
    beside_xf = beside(raw_f, chips)
    both_2 = total(near_2, after_these(relay_2, near_3))
    got_2 = across(both_2)
    stacked = after_these(stacked, both_2)
    far_z, near_z = next_call(RAW, 1, (1, 1, 0), scalars, stacked, raw_x, (beside_xn, beside_xf))
    got_z = along(far_z)
    both_3 = total(near_3, after_these(relay_3, near_z))
    got_3 = across(both_3)
    stacked = after_these(stacked, both_3)
    (mine_z,) = next_call(RAW, 0, (0, 0, 1), scalars, stacked, greens, (beside_n, beside_f))
    return add_up((mine_1, got_1, mine_2, got_2, mine_z, near_z, got_z), (mine_3, got_3), greens)


def solution(mesh):
    in_specs = (P(None, "energy", "slab", None, None), P(), P(), P(), P("slab", None))
    out_specs = P(None, "energy", "slab", None, None)
    return jax.shard_map(
        on_device, mesh=mesh, in_specs=in_specs, out_specs=out_specs, check_vma=False
    )
```

time: 140 us -> 42.1 us (0.30)
  the two profiles are of different devices: /device:TPU:1 before, /device:TPU:8 now
where the time goes in v4:
time: 42.1 us; the launch traced here: 41.8 us
  Pallas kernels  16.9 us (40%)
  starting transfers between devices  12.7 us (30%)
  waiting for transfers between devices  9.22 us (22%)
  local copies, waits for them, and re-layouts  2.66 us (6%)
    pallas_call x4, Pallas kernels, next_call(): pl.pallas_call(functools.partial(next_body, groups, flip, wanted, own.ndi...  10.4 us
    pallas_call x1, Pallas kernels, first_call(): pl.pallas_call(first_body, out_shape=[jax.ShapeDtypeStruct(*out) for out...  4.77 us
    ppermute x4, starting transfers between devices, across(): return lax.ppermute(array, 'energy', [(i, i ^ 1) for i in range(4)])  4.77 us
    ppermute x4, waiting for transfers between devices, along(): return lax.ppermute(array, 'energy', [(i, i ^ 2) for i in range(4)])  4.5 us
    ppermute x4, starting transfers between devices, beside(): return lax.ppermute(array, 'slab', pairs)  4.1 us
    ppermute x4, starting transfers between devices, along(): return lax.ppermute(array, 'energy', [(i, i ^ 2) for i in range(4)])  3.83 us
    ppermute x4, waiting for transfers between devices, beside(): return lax.ppermute(array, 'slab', pairs)  2.77 us
    unnamed x16, local copies, waits for them, and re-layouts  2.66 us
  transfers between devices with their start and end apart: 12, of which 5 were waited for; matrix products, arithmetic and copies ran while one was open for 0% of the time, Pallas kernels for 27%

profile of v4, /device:TPU:8, one launch (start us, length us, event | category | flops | bytes accessed | tf_op | source)
XLA Modules:
  0.0 41.8 jit_solution(7806317091113889287)
XLA Ops:
  0.0 4.8 %shard_map.55 = (bf16[2,2,2,128,128]{4,3,2,1,0:T(8,128)(2,1)}, f32[2,2,2,128,128]{4,3,2,1,0:T(8,128)}, f32[2,2,2,128,128]{4,3,2,1,0:T(8,128)}, bf16[3,512,128]{2...) custom-call(f32[4]{0:T(128)} %refs_0_.7, ...), custom_call_target="tpu_custom_call" | custom-call | flops 1024 | bytes 1024 | tf_op jit(solution)/shard_map/pallas_call | solution.py:167
  4.8 0.1 collective-permute-start.1
  4.9 1.6 %collective-permute-start = (bf16[2,2,2,128,128]{4,3,2,1,0:T(8,128)(2,1)}, bf16[2,2,2,128,128]{4,3,2,1,0:T(8,128)(2,1)S(1)}, u32[]{:S(2)}, u32[]{:S(2)}) collective-permute-start(bf16[2,2,2,128,128]{4,3,2,1,0:T(8,128)(2,1)} %get-tuple-element.35), channel_id=1, source_target_pairs={{0,16},{8,24},{16,0},{24,8},{1,17},{9,25},{17,1},{25,9},{2,18},{10... | collective-permute-start | bytes 786440 | tf_op jit(solution)/shard_map/ppermute | solution.py:320
  6.5 2.1 %collective-permute-start.2 = (bf16[2,2,128,256]{3,2,1,0:T(8,128)(2,1)}, bf16[2,2,128,256]{3,2,1,0:T(8,128)(2,1)S(1)}, u32[]{:S(2)}, u32[]{:S(2)}) collective-permute-start(bf16[2,2,128,256]{3,2,1,0:T(8,128)(2,1)} %get-tuple-element.41), channel_id=1, source_target_pairs={{1,2},{2,1},{3,4},{4,3},{5,6},{6,5},{9,10},{10,9},{11,12},{12,11},... | collective-permute-start | bytes 786440 | tf_op jit(solution)/shard_map/ppermute | solution.py:323
  8.6 0.0 copy-start.4
  8.6 1.5 %collective-permute-start.3 = (bf16[2,4,128,128]{3,2,1,0:T(8,128)(2,1)}, bf16[2,4,128,128]{3,2,1,0:T(8,128)(2,1)S(1)}, u32[]{:S(2)}, u32[]{:S(2)}) collective-permute-start(bf16[2,4,128,128]{3,2,1,0:T(8,128)(2,1)} %get-tuple-element.42), channel_id=1, source_target_pairs={{0,8},{8,0},{16,24},{24,16},{1,9},{9,1},{17,25},{25,17},{2,10},{10... | collective-permute-start | bytes 786440 | tf_op jit(solution)/shard_map/ppermute | solution.py:317
  10.2 0.6 %copy-done.5 = f32[4]{0:T(128)S(1)} copy-done((f32[4]{0:T(128)S(1)}, f32[4]{0:T(128)}, u32[]{:S(2)}) %copy-start.5) | copy-done | bytes 40
  10.8 0.0 copy-done.6
  10.8 1.0 %copy-done.1 = bf16[3,512,128]{2,1,0:T(8,128)(2,1)S(1)} copy-done((bf16[3,512,128]{2,1,0:T(8,128)(2,1)S(1)}, bf16[3,512,128]{2,1,0:T(8,128)(2,1)}, u32[]{:S(2)}) %copy-start.1) | copy-done | bytes 393240
  11.8 1.0 %copy-done.2 = bf16[4,128,384]{2,1,0:T(8,128)(2,1)S(1)} copy-done((bf16[4,128,384]{2,1,0:T(8,128)(2,1)S(1)}, bf16[4,128,384]{2,1,0:T(8,128)(2,1)}, u32[]{:S(2)}) %copy-start.2) | copy-done | bytes 393240
  12.8 2.6 %shard_map.56 = (bf16[2,2,2,128,128]{4,3,2,1,0:T(8,128)(2,1)S(1)}, f32[2,2,2,128,128]{4,3,2,1,0:T(8,128)S(1)}, f32[2,2,2,128,128]{4,3,2,1,0:T(8,128)S(1)}) custom-call(f32[4]{0:T(128)S(1)} %copy-done.5, s32[4]{0:T(128)S(1)} %copy-done.6, s32[4,3]{1,0:T(4,128)S(1)} %copy-done.4, bf16[3,512,128]{2,1,0:T(8,128)(2,1)S(1)} %copy-done.1, ...), custom_call_target="tpu_custom_call" | custom-call | flops 1024 | bytes 1024 | tf_op jit(solution)/shard_map/pallas_call | solution.py:218
  15.4 0.6 %collective-permute-start.5 = (bf16[2,2,2,128,128]{4,3,2,1,0:T(8,128)(2,1)S(1)}, bf16[2,2,2,128,128]{4,3,2,1,0:T(8,128)(2,1)S(1)}, u32[]{:S(2)}, u32[]{:S(2)}) collective-permute-start(bf16[2,2,2,128,128]{4,3,2,1,0:T(8,128)(2,1)S(1)} %get-tuple-element.37), channel_id=1, source_target_pairs={{0,16},{8,24},{16,0},{24,8},{1,17},{9,25},{17,1},{25,9},{2,18},{10... | collective-permute-start | bytes 786440 | tf_op jit(solution)/shard_map/ppermute | solution.py:320
  16.0 0.0 collective-permute-done
  16.0 0.1 add_convert_fusion.2
  16.1 1.5 %collective-permute-done.3.refs_8_.refs_5_ = bf16[2,4,128,128]{3,2,1,0:T(8,128)(2,1)S(1)} collective-permute-done((bf16[2,4,128,128]{3,2,1,0:T(8,128)(2,1)}, bf16[2,4,128,128]{3,2,1,0:T(8,128)(2,1)S(1)}, u32[]{:S(2)}, u32[]{:S(2)}) %collective-permute-start.3) | collective-permute-done | bytes 262176 | tf_op jit(solution)/shard_map/ppermute | solution.py:317
  17.6 2.7 %shard_map.57 = (bf16[2,2,2,128,128]{4,3,2,1,0:T(8,128)(2,1)S(1)}, f32[2,2,2,128,128]{4,3,2,1,0:T(8,128)S(1)}, f32[2,2,2,128,128]{4,3,2,1,0:T(8,128)S(1)}, bf16[...) custom-call(f32[4]{0:T(128)S(1)} %copy-done.5, s32[4]{0:T(128)S(1)} %copy-done.6, s32[4,3]{1,0:T(4,128)S(1)} %copy-done.4, ...), custom_call_target="tpu_custom_call" | custom-call | flops 1024 | bytes 1024 | tf_op jit(solution)/shard_map/pallas_call | solution.py:218
  20.3 0.1 collective-permute-start.4
  20.4 1.9 %collective-permute-start.9 = (bf16[2,2,2,128,128]{4,3,2,1,0:T(8,128)(2,1)S(1)}, bf16[2,2,2,128,128]{4,3,2,1,0:T(8,128)(2,1)S(1)}, u32[]{:S(2)}, u32[]{:S(2)}) collective-permute-start(bf16[2,2,2,128,128]{4,3,2,1,0:T(8,128)(2,1)S(1)} %add_convert_fusion.2), channel_id=1, source_target_pairs={{0,8},{8,0},{16,24},{24,16},{1,9},{9,1},{17,25},{25,17},{2,10},{10... | collective-permute-start | bytes 786440 | tf_op jit(solution)/shard_map/ppermute | solution.py:317
  22.3 1.9 %collective-permute-start.7 = (bf16[2,128,128]{2,1,0:T(8,128)(2,1)S(1)}, bf16[2,128,128]{2,1,0:T(8,128)(2,1)S(1)}, u32[]{:S(2)}, u32[]{:S(2)}) collective-permute-start(bf16[2,128,128]{2,1,0:T(8,128)(2,1)S(1)} %get-tuple-element.51), channel_id=1, source_target_pairs={{1,2},{2,1},{3,4},{4,3},{5,6},{6,5},{9,10},{10,9},{11,12},{12,11},... | collective-permute-start | bytes 196616 | tf_op jit(solution)/shard_map/ppermute | solution.py:323
  24.3 0.2 collective-permute-done.5
  24.5 0.1 add_convert_fusion.1
  24.5 0.6 %collective-permute-start.10 = (bf16[2,2,2,128,128]{4,3,2,1,0:T(8,128)(2,1)S(1)}, bf16[2,2,2,128,128]{4,3,2,1,0:T(8,128)(2,1)S(1)}, u32[]{:S(2)}, u32[]{:S(2)}) collective-permute-start(bf16[2,2,2,128,128]{4,3,2,1,0:T(8,128)(2,1)S(1)} %add_convert_fusion.1), channel_id=1, source_target_pairs={{0,8},{8,0},{16,24},{24,16},{1,9},{9,1},{17,25},{25,17},{2,10},{10... | collective-permute-start | bytes 786440 | tf_op jit(solution)/shard_map/ppermute | solution.py:317
  25.2 2.8 %collective-permute-done.7.refs_7_ = bf16[2,128,128]{2,1,0:T(8,128)(2,1)S(1)} collective-permute-done((bf16[2,128,128]{2,1,0:T(8,128)(2,1)S(1)}, bf16[2,128,128]{2,1,0:T(8,128)(2,1)S(1)}, u32[]{:S(2)}, u32[]{:S(2)}) %collective-permute-start.7) | collective-permute-done | bytes 65568 | tf_op jit(solution)/shard_map/ppermute | solution.py:323
  27.9 2.7 %shard_map.58 = (bf16[2,2,2,128,128]{4,3,2,1,0:T(8,128)(2,1)S(1)}, f32[2,2,2,128,128]{4,3,2,1,0:T(8,128)S(1)}) custom-call(f32[4]{0:T(128)S(1)} %copy-done.5, s32[4]{0:T(128)S(1)} %copy-done.6, s32[4,3]{1,0:T(4,128)S(1)} %copy-done.4, bf16[3,512,128]{2,1,0:T(8,128)(2,1)S(1)} %copy-done.1, bf16[4,128,384]{2,1,0:T(8,128)(2,1)S(1)} %copy-done.2, ...), custom_call_target="tpu_custom_call" | custom-call | flops 1024 | bytes 1024 | tf_op jit(solution)/shard_map/pallas_call | solution.py:218
  30.6 1.6 %collective-permute-start.11 = (bf16[2,2,2,128,128]{4,3,2,1,0:T(8,128)(2,1)S(1)}, bf16[2,2,2,128,128]{4,3,2,1,0:T(8,128)(2,1)S(1)}, u32[]{:S(2)}, u32[]{:S(2)}) collective-permute-start(bf16[2,2,2,128,128]{4,3,2,1,0:T(8,128)(2,1)S(1)} %get-tuple-element.58), channel_id=1, source_target_pairs={{0,16},{8,24},{16,0},{24,8},{1,17},{9,25},{17,1},{25,9},{2,18},{10... | collective-permute-start | bytes 786440 | tf_op jit(solution)/shard_map/ppermute | solution.py:320
  32.2 0.1 add_convert_fusion
  32.3 0.6 %collective-permute-start.8 = (bf16[2,2,2,128,128]{4,3,2,1,0:T(8,128)(2,1)S(1)}, bf16[2,2,2,128,128]{4,3,2,1,0:T(8,128)(2,1)S(1)}, u32[]{:S(2)}, u32[]{:S(2)}) collective-permute-start(bf16[2,2,2,128,128]{4,3,2,1,0:T(8,128)(2,1)S(1)} %add_convert_fusion), channel_id=1, source_target_pairs={{0,8},{8,0},{16,24},{24,16},{1,9},{9,1},{17,25},{25,17},{2,10},{10... | collective-permute-start | bytes 786440 | tf_op jit(solution)/shard_map/ppermute | solution.py:317
  32.9 2.4 %shard_map.59.mine_z = f32[2,2,2,128,128]{4,3,2,1,0:T(8,128)S(1)} custom-call(f32[4]{0:T(128)S(1)} %copy-done.5, s32[4]{0:T(128)S(1)} %copy-done.6, s32[4,3]{1,0:T(4,128)S(1)} %copy-done.4, bf16[3,512,128]{2,1,0:T(8,128)(2,1)S(1)} %copy-done.1, bf16[4,128,384]{2,1,0:T(8,128)(2,1)S(1)} %copy-done.2, bf16[2,2,4,128,256]{4,3,2,1,0:T(8,128)(2,1)S(1)} %copy-done, ...), custom_call_target="tpu_custom_call" | custom-call | flops 1024 | bytes 1024 | tf_op jit(solution)/shard_map/pallas_call | solution.py:218
  35.4 4.3 %collective-permute-done.11.got_z = bf16[2,2,2,128,128]{4,3,2,1,0:T(8,128)(2,1)S(1)} collective-permute-done((bf16[2,2,2,128,128]{4,3,2,1,0:T(8,128)(2,1)S(1)}, bf16[2,2,2,128,128]{4,3,2,1,0:T(8,128)(2,1)S(1)}, u32[]{:S(2)}, u32[]{:S(2)}) %collective-permute-start.11) | collective-permute-done | bytes 262176 | tf_op jit(solution)/shard_map/ppermute | solution.py:320
  39.7 1.0 %shard_map.60._ = bf16[2,2,4,128,256]{4,3,2,1,0:T(8,128)(2,1)} custom-call(f32[2,2,2,128,128]{4,3,2,1,0:T(8,128)S(1)} %copy-done.3, bf16[2,2,2,128,128]{4,3,2,1,0:T(8,128)(2,1)S(1)} %collective-permute-done.9.got_1, f32[2,2,2,128,128]{4,3,2,1,0:T(8,128)S(1)} %get-tuple-element.55.mine_2, bf16[2,2,2,128,128]{4,3,2,1,0:T(8,128)(2,1)S(1)} %collective-permute-done.10.got_2, ...), custom_call_target="tpu_custom_call" | custom-call | flops 1024 | bytes 1024 | tf_op jit(solution)/shard_map/pallas_call | solution.py:283
  40.7 0.4 collective-permute-done.8.got
  41.1 0.7 %shard_map.61 = bf16[2,2,4,128,256]{4,3,2,1,0:T(8,128)(2,1)} custom-call(f32[2,2,2,128,128]{4,3,2,1,0:T(8,128)S(1)} %get-tuple-element.43.mine, bf16[2,2,2,128,128]{4,3,2,1,0:T(8,128)(2,1)S(1)} %collective-permute-done.8.got, bf16[2,2,4,128,256]{4,3,2,1,0:T(8,128)(2,1)} %shard_map.60._), custom_call_target="tpu_custom_call", output_to_operand_aliasing={{}: (2, {})} | custom-call | flops 1024 | bytes 1024 | tf_op jit(solution)/shard_map/pallas_call | solution.py:294
  (18 shorter events, 0.0 us)
Async XLA Ops:
  0.0 10.1 %copy-start = (bf16[2,2,4,128,256]{4,3,2,1,0:T(8,128)(2,1)S(1)}, bf16[2,2,4,128,256]{4,3,2,1,0:T(8,128)(2,1)}, u32[]{:S(2)}) copy-start(bf16[2,2,4,128,256]{4,3,2,1,0:T(8,128)(2,1)} %refs_5_.5) | copy-start | bytes 3145732
  4.8 5.4 %collective-permute-start.1 = (bf16[2,2,128,256]{3,2,1,0:T(8,128)(2,1)}, bf16[2,2,128,256]{3,2,1,0:T(8,128)(2,1)S(1)}, u32[]{:S(2)}, u32[]{:S(2)}) collective-permute-start(bf16[2,2,128,256]{3,2,1,0:T(8,128)(2,1)} %get-tuple-element.36), channel_id=1, source_target_pairs={{0,1},{1,0},{2,3},{3,2},{4,5},{5,4},{6,7},{7,6},{8,9},{9,8},{10,11... | collective-permute-start | bytes 786440 | tf_op jit(solution)/shard_map/ppermute | solution.py:323
  4.9 11.1 %collective-permute-start = (bf16[2,2,2,128,128]{4,3,2,1,0:T(8,128)(2,1)}, bf16[2,2,2,128,128]{4,3,2,1,0:T(8,128)(2,1)S(1)}, u32[]{:S(2)}, u32[]{:S(2)}) collective-permute-start(bf16[2,2,2,128,128]{4,3,2,1,0:T(8,128)(2,1)} %get-tuple-element.35), channel_id=1, source_target_pairs={{0,16},{8,24},{16,0},{24,8},{1,17},{9,25},{17,1},{25,9},{2,18},{10... | collective-permute-start | bytes 786440 | tf_op jit(solution)/shard_map/ppermute | solution.py:320
  6.5 9.6 %collective-permute-start.2 = (bf16[2,2,128,256]{3,2,1,0:T(8,128)(2,1)}, bf16[2,2,128,256]{3,2,1,0:T(8,128)(2,1)S(1)}, u32[]{:S(2)}, u32[]{:S(2)}) collective-permute-start(bf16[2,2,128,256]{3,2,1,0:T(8,128)(2,1)} %get-tuple-element.41), channel_id=1, source_target_pairs={{1,2},{2,1},{3,4},{4,3},{5,6},{6,5},{9,10},{10,9},{11,12},{12,11},... | collective-permute-start | bytes 786440 | tf_op jit(solution)/shard_map/ppermute | solution.py:323
  8.6 1.6 %copy-start.4 = (s32[4,3]{1,0:T(4,128)S(1)}, s32[4,3]{1,0:T(4,128)}, u32[]{:S(2)}) copy-start(s32[4,3]{1,0:T(4,128)} %refs_2_.7) | copy-start | bytes 148
  8.6 9.0 %collective-permute-start.3 = (bf16[2,4,128,128]{3,2,1,0:T(8,128)(2,1)}, bf16[2,4,128,128]{3,2,1,0:T(8,128)(2,1)S(1)}, u32[]{:S(2)}, u32[]{:S(2)}) collective-permute-start(bf16[2,4,128,128]{3,2,1,0:T(8,128)(2,1)} %get-tuple-element.42), channel_id=1, source_target_pairs={{0,8},{8,0},{16,24},{24,16},{1,9},{9,1},{17,25},{25,17},{2,10},{10... | collective-permute-start | bytes 786440 | tf_op jit(solution)/shard_map/ppermute | solution.py:317
  10.1 0.7 %copy-start.5 = (f32[4]{0:T(128)S(1)}, f32[4]{0:T(128)}, u32[]{:S(2)}) copy-start(f32[4]{0:T(128)} %refs_0_.7) | copy-start | bytes 52
  10.1 0.7 %copy-start.6 = (s32[4]{0:T(128)S(1)}, s32[4]{0:T(128)}, u32[]{:S(2)}) copy-start(s32[4]{0:T(128)} %refs_1_.7) | copy-start | bytes 52
  10.8 1.0 %copy-start.1 = (bf16[3,512,128]{2,1,0:T(8,128)(2,1)S(1)}, bf16[3,512,128]{2,1,0:T(8,128)(2,1)}, u32[]{:S(2)}) copy-start(bf16[3,512,128]{2,1,0:T(8,128)(2,1)} %get-tuple-element.56.refs_3_) | copy-start | bytes 1179652
  11.8 1.0 %copy-start.2 = (bf16[4,128,384]{2,1,0:T(8,128)(2,1)S(1)}, bf16[4,128,384]{2,1,0:T(8,128)(2,1)}, u32[]{:S(2)}) copy-start(bf16[4,128,384]{2,1,0:T(8,128)(2,1)} %get-tuple-element.57.refs_4_) | copy-start | bytes 1179652
  12.8 3.2 %copy-start.7 = (f32[2,2,2,128,128]{4,3,2,1,0:T(8,128)S(1)}, f32[2,2,2,128,128]{4,3,2,1,0:T(8,128)}, u32[]{:S(2)}) copy-start(f32[2,2,2,128,128]{4,3,2,1,0:T(8,128)} %get-tuple-element.34) | copy-start | bytes 1572868
  15.4 9.0 %collective-permute-start.5 = (bf16[2,2,2,128,128]{4,3,2,1,0:T(8,128)(2,1)S(1)}, bf16[2,2,2,128,128]{4,3,2,1,0:T(8,128)(2,1)S(1)}, u32[]{:S(2)}, u32[]{:S(2)}) collective-permute-start(bf16[2,2,2,128,128]{4,3,2,1,0:T(8,128)(2,1)S(1)} %get-tuple-element.37), channel_id=1, source_target_pairs={{0,16},{8,24},{16,0},{24,8},{1,17},{9,25},{17,1},{25,9},{2,18},{10... | collective-permute-start | bytes 786440 | tf_op jit(solution)/shard_map/ppermute | solution.py:320
  20.3 10.3 %collective-permute-start.4 = (bf16[2,2,2,128,128]{4,3,2,1,0:T(8,128)(2,1)S(1)}, bf16[2,2,2,128,128]{4,3,2,1,0:T(8,128)(2,1)S(1)}, u32[]{:S(2)}, u32[]{:S(2)}) collective-permute-start(bf16[2,2,2,128,128]{4,3,2,1,0:T(8,128)(2,1)S(1)} %get-tuple-element.45), channel_id=1, source_target_pairs={{0,16},{8,24},{16,0},{24,8},{1,17},{9,25},{17,1},{25,9},{2,18},{10... | collective-permute-start | bytes 786440 | tf_op jit(solution)/shard_map/ppermute | solution.py:320
  20.4 15.0 %collective-permute-start.9 = (bf16[2,2,2,128,128]{4,3,2,1,0:T(8,128)(2,1)S(1)}, bf16[2,2,2,128,128]{4,3,2,1,0:T(8,128)(2,1)S(1)}, u32[]{:S(2)}, u32[]{:S(2)}) collective-permute-start(bf16[2,2,2,128,128]{4,3,2,1,0:T(8,128)(2,1)S(1)} %add_convert_fusion.2), channel_id=1, source_target_pairs={{0,8},{8,0},{16,24},{24,16},{1,9},{9,1},{17,25},{25,17},{2,10},{10... | collective-permute-start | bytes 786440 | tf_op jit(solution)/shard_map/ppermute | solution.py:317
  22.3 2.8 %collective-permute-start.6 = (bf16[2,128,128]{2,1,0:T(8,128)(2,1)S(1)}, bf16[2,128,128]{2,1,0:T(8,128)(2,1)S(1)}, u32[]{:S(2)}, u32[]{:S(2)}) collective-permute-start(bf16[2,128,128]{2,1,0:T(8,128)(2,1)S(1)} %get-tuple-element.50), channel_id=1, source_target_pairs={{0,1},{1,0},{2,3},{3,2},{4,5},{5,4},{6,7},{7,6},{8,9},{9,8},{10,11... | collective-permute-start | bytes 196616 | tf_op jit(solution)/shard_map/ppermute | solution.py:323
  22.3 5.6 %collective-permute-start.7 = (bf16[2,128,128]{2,1,0:T(8,128)(2,1)S(1)}, bf16[2,128,128]{2,1,0:T(8,128)(2,1)S(1)}, u32[]{:S(2)}, u32[]{:S(2)}) collective-permute-start(bf16[2,128,128]{2,1,0:T(8,128)(2,1)S(1)} %get-tuple-element.51), channel_id=1, source_target_pairs={{1,2},{2,1},{3,4},{4,3},{5,6},{6,5},{9,10},{10,9},{11,12},{12,11},... | collective-permute-start | bytes 196616 | tf_op jit(solution)/shard_map/ppermute | solution.py:323
  24.5 10.9 %collective-permute-start.10 = (bf16[2,2,2,128,128]{4,3,2,1,0:T(8,128)(2,1)S(1)}, bf16[2,2,2,128,128]{4,3,2,1,0:T(8,128)(2,1)S(1)}, u32[]{:S(2)}, u32[]{:S(2)}) collective-permute-start(bf16[2,2,2,128,128]{4,3,2,1,0:T(8,128)(2,1)S(1)} %add_convert_fusion.1), channel_id=1, source_target_pairs={{0,8},{8,0},{16,24},{24,16},{1,9},{9,1},{17,25},{25,17},{2,10},{10... | collective-permute-start | bytes 786440 | tf_op jit(solution)/shard_map/ppermute | solution.py:317
  30.6 9.1 %collective-permute-start.11 = (bf16[2,2,2,128,128]{4,3,2,1,0:T(8,128)(2,1)S(1)}, bf16[2,2,2,128,128]{4,3,2,1,0:T(8,128)(2,1)S(1)}, u32[]{:S(2)}, u32[]{:S(2)}) collective-permute-start(bf16[2,2,2,128,128]{4,3,2,1,0:T(8,128)(2,1)S(1)} %get-tuple-element.58), channel_id=1, source_target_pairs={{0,16},{8,24},{16,0},{24,8},{1,17},{9,25},{17,1},{25,9},{2,18},{10... | collective-permute-start | bytes 786440 | tf_op jit(solution)/shard_map/ppermute | solution.py:320
  32.3 7.4 %copy-start.3 = (f32[2,2,2,128,128]{4,3,2,1,0:T(8,128)S(1)}, f32[2,2,2,128,128]{4,3,2,1,0:T(8,128)}, u32[]{:S(2)}) copy-start(f32[2,2,2,128,128]{4,3,2,1,0:T(8,128)} %get-tuple-element.54.mine_1) | copy-start | bytes 1572868
  32.3 8.8 %collective-permute-start.8 = (bf16[2,2,2,128,128]{4,3,2,1,0:T(8,128)(2,1)S(1)}, bf16[2,2,2,128,128]{4,3,2,1,0:T(8,128)(2,1)S(1)}, u32[]{:S(2)}, u32[]{:S(2)}) collective-permute-start(bf16[2,2,2,128,128]{4,3,2,1,0:T(8,128)(2,1)S(1)} %add_convert_fusion), channel_id=1, source_target_pairs={{0,8},{8,0},{16,24},{24,16},{1,9},{9,1},{17,25},{25,17},{2,10},{10... | collective-permute-start | bytes 786440 | tf_op jit(solution)/shard_map/ppermute | solution.py:317

commit v5 on v4

--- a/solution.py
+++ b/solution.py
@@ -110,7 +110,7 @@
 SMALL = pl.CostEstimate(flops=1024, bytes_accessed=1024, transcendentals=0)
 
 
-def first_body(occ_h, off_h, nbr_h, c_h, g_h, far_h, near_h, mine_h, rows_h, cols_h, raw_h, edge_n, edge_f, occ, off, nbr, c_ref, own, far, near, mine, rows, cols, sems, outs, half, acc):
+def first_body(occ_h, off_h, nbr_h, c_h, g_h, far_h, near_h, mine_h, raw_h, edge_n, edge_f, occ, off, nbr, c_ref, own, far, near, mine, rows, cols, sems, outs, half, acc):
     size = c_h.shape[-1]
     owned = g_h.shape[2]
     fetches = [
@@ -128,8 +128,6 @@
 
     fetches[0].wait()
     stack_coupling(c_ref, rows, cols)
-    send(rows, rows_h)
-    send(cols, cols_h)
     for fetch in fetches[1:]:
         fetch.wait()
     send(own.at[0, :, :, :, pl.ds(0, size)], raw_h)
@@ -158,8 +156,6 @@
         (shape, BF16),
         (shape, F32),
         (shape, F32),
-        (rows, BF16),
-        (cols, BF16),
         ((count, owned, size, size), BF16),
         (edge, BF16),
         (edge, BF16),
@@ -168,7 +164,7 @@
         first_body,
         out_shape=[jax.ShapeDtypeStruct(*out) for out in outs],
         in_specs=[HBM] * 5,
-        out_specs=[HBM] * 8,
+        out_specs=[HBM] * 6,
         scratch_shapes=[
             pltpu.SMEM(occupation.shape, F32),
             pltpu.SMEM(offsets.shape, jnp.int32),
@@ -176,21 +172,29 @@
             pltpu.VMEM(coupling.shape, BF16),
             pltpu.VMEM(greens.shape, BF16),
         ]
-        + [pltpu.VMEM(*out) for out in outs[:5]]
-        + [pltpu.SemaphoreType.DMA((5,)), pltpu.SemaphoreType.DMA((11,))]
+        + [pltpu.VMEM(*out) for out in outs[:3] + [(rows, BF16), (cols, BF16)]]
+        + [pltpu.SemaphoreType.DMA((5,)), pltpu.SemaphoreType.DMA((9,))]
         + scratch(modes, slots, size, count),
         compiler_params=pltpu.CompilerParams(vmem_limit_bytes=58 << 20),
-        cost_estimate=SMALL,
+        cost_estimate=pl.CostEstimate(flops=5 << 30, bytes_accessed=16 << 20, transcendentals=0),
     )(occupation, offsets, neighbours, coupling, greens)
 
 
-def next_body(groups, flip, wanted, with_parts, n_edges, n_copied, *refs):
-    occ, off, nbr, rows, cols, own = refs[:6]
-    edge_refs = dict(zip((NEAR, FAR), refs[6 : 6 + n_edges]))
-    at = 6 + n_edges
+def next_body(groups, flip, wanted, with_parts, n_stacked, n_edges, n_copied, *refs):
+    occ, off, nbr = refs[:3]
+    at = 3 + n_stacked
+    own = refs[at]
+    edge_refs = dict(zip((NEAR, FAR), refs[at + 1 : at + 1 + n_edges]))
+    at += 1 + n_edges
     copied = refs[at : at + n_copied]
     outs = list(refs[at + n_copied : -2])
     half, acc = refs[-2:]
+    if n_stacked == 1:
+        rows, cols = outs[-2:]
+        outs = outs[:-2]
+        stack_coupling(refs[3], rows, cols)
+    else:
+        rows, cols = refs[3:5]
 
     def read(part, e, at, lanes):
         return own[part, e, at, :, lanes] if with_parts else own[e, at]
@@ -209,21 +213,23 @@
 
 
 def next_call(groups, flip, wanted, scalars, stacked, own, edges, copied=()):
-    rows, cols = stacked
-    slots, wide, size = rows.shape
+    modes, slots, size = stacked[0].shape[:3] if len(stacked) == 1 else (stacked[1].shape[0],) + stacked[0].shape[::2]
     count = own.shape[-4]
     shape = pieces(size, count)
     outs = [jax.ShapeDtypeStruct(shape, kind) for want, kind in zip(wanted, (BF16, F32, F32)) if want]
     outs += [jax.ShapeDtypeStruct((count, size, size), BF16)] * (2 * len(copied))
+    if len(stacked) == 1:
+        outs.append(jax.ShapeDtypeStruct((slots, modes * size, size), BF16))
+        outs.append(jax.ShapeDtypeStruct((modes, size, slots * size), BF16))
     return pl.pallas_call(
-        functools.partial(next_body, groups, flip, wanted, own.ndim == 5, len(edges), len(copied)),
+        functools.partial(next_body, groups, flip, wanted, own.ndim == 5, len(stacked), len(edges), len(copied)),
         out_shape=outs,
-        in_specs=[SMEM] * 3 + [VMEM] * (3 + len(edges) + len(copied)),
+        in_specs=[SMEM] * 3 + [VMEM] * (1 + len(stacked) + len(edges) + len(copied)),
         out_specs=[VMEM] * len(outs),
-        scratch_shapes=scratch(wide // size, slots, size, count),
+        scratch_shapes=scratch(modes, slots, size, count),
         compiler_params=pltpu.CompilerParams(vmem_limit_bytes=16 << 20),
         cost_estimate=SMALL,
-    )(*scalars, rows, cols, own, *edges, *copied)
+    )(*scalars, *stacked, own, *edges, *copied)
 
 
 def early_body(mine_1, got_1, mine_2, got_2, mine_z, near_z, got_z, out, whole, edge, half, raw, sems):
@@ -325,19 +331,20 @@
     def total(near, relayed):
         return (near + relayed.astype(F32)).astype(BF16)
 
-    far_1, near_1, mine_1, rows, cols, raw, edge_n, edge_f = first_call(
+    far_1, near_1, mine_1, raw, edge_n, edge_f = first_call(
         greens, coupling, occupation, offsets, neighbours
     )
-    stacked = (rows, cols)
     relay_1 = along(far_1)
     beside_n = beside(edge_n, chip)
     raw_x = across(raw)
-    beside_f = beside(edge_f, chips)
-    far_2, near_2, mine_2 = next_call(SECOND, 0, (1, 1, 1), scalars, stacked, greens, (beside_n,))
+    beside_f = beside(after_these(edge_f, beside_n), chips)
+    far_2, near_2, mine_2, rows, cols = next_call(
+        SECOND, 0, (1, 1, 1), scalars, (coupling,), greens, (beside_n,)
+    )
     relay_2 = along(far_2)
     both_1 = total(near_1, after_these(relay_1, far_2))
     got_1 = across(both_1)
-    stacked = after_these(stacked, both_1)
+    stacked = after_these((rows, cols), both_1)
     far_3, near_3, mine_3, raw_n, raw_f = next_call(
         THIRD, 0, (1, 1, 1), scalars, stacked, greens, (beside_n, beside_f), (raw_x,)
     )
@@ -346,7 +353,7 @@
     beside_xf = beside(raw_f, chips)
     both_2 = total(near_2, after_these(relay_2, near_3))
     got_2 = across(both_2)
-    stacked = after_these(stacked, both_2)
+    stacked = after_these(stacked, both_2, got_1)
     far_z, near_z = next_call(RAW, 1, (1, 1, 0), scalars, stacked, raw_x, (beside_xn, beside_xf))
     got_z = along(far_z)
     both_3 = total(near_3, after_these(relay_3, near_z))

time: 42.1 us -> 40.8 us (0.969)
  local copies, waits for them, and re-layouts: 2.66 us -> 0.03 us
  starting transfers between devices: 12.7 us -> 13.5 us
  waiting for transfers between devices: 9.22 us -> 9.82 us
    unnamed x16 -> x14, local copies, waits for them, and re-layouts: 2.66 us -> 0.03 us
    ppermute x4, waiting for transfers between devices: 1.95 us -> 0.01 us  [across(): return lax.ppermute(array, 'energy', [(i, i ^ 1) for i in range(4)])]
    ppermute x4, waiting for transfers between devices: 4.5 us -> 6.24 us  [along(): return lax.ppermute(array, 'energy', [(i, i ^ 2) for i in range(4)])]
    ppermute x4, waiting for transfers between devices: 2.77 us -> 3.57 us  [beside(): return lax.ppermute(array, 'slab', pairs)]
    ppermute x4, starting transfers between devices: 4.1 us -> 4.79 us  [beside(): return lax.ppermute(array, 'slab', pairs)]
  transfers between devices with their start and end apart: 12 -> 12, of which waited for: 5 -> 5; matrix products, arithmetic and copies ran while one was open for 0% -> 0% of each run, Pallas kernels for 27% -> 28%
where the time goes in v5:
time: 40.8 us; the launch traced here: 40.7 us
  Pallas kernels  16.9 us (41%)
  starting transfers between devices  13.5 us (33%)
  waiting for transfers between devices  9.82 us (24%)
    pallas_call x4, Pallas kernels, next_call(): pl.pallas_call(functools.partial(next_body, groups, flip, wanted, own.ndi...  10.4 us
    ppermute x4, waiting for transfers between devices, along(): return lax.ppermute(array, 'energy', [(i, i ^ 2) for i in range(4)])  6.24 us
    ppermute x4, starting transfers between devices, across(): return lax.ppermute(array, 'energy', [(i, i ^ 1) for i in range(4)])  5.02 us
    ppermute x4, starting transfers between devices, beside(): return lax.ppermute(array, 'slab', pairs)  4.79 us
    pallas_call x1, Pallas kernels, first_call(): pl.pallas_call(first_body, out_shape=[jax.ShapeDtypeStruct(*out) for out...  4.78 us
    ppermute x4, starting transfers between devices, along(): return lax.ppermute(array, 'energy', [(i, i ^ 2) for i in range(4)])  3.74 us
    ppermute x4, waiting for transfers between devices, beside(): return lax.ppermute(array, 'slab', pairs)  3.57 us
    pallas_call x1, Pallas kernels, add_up(): pl.pallas_call(early_body, out_shape=jax.ShapeDtypeStruct(greens.shape, B...  0.98 us
  transfers between devices with their start and end apart: 12, of which 5 were waited for; matrix products, arithmetic and copies ran while one was open for 0% of the time, Pallas kernels for 28%

profile of v5, /device:TPU:8, one launch (start us, length us, event | category | flops | bytes accessed | tf_op | source)
XLA Modules:
  0.0 40.7 jit_solution(8787764054974506371)
XLA Ops:
  0.0 4.8 %shard_map.55 = (bf16[2,2,2,128,128]{4,3,2,1,0:T(8,128)(2,1)}, f32[2,2,2,128,128]{4,3,2,1,0:T(8,128)}, f32[2,2,2,128,128]{4,3,2,1,0:T(8,128)}, bf16[2,4,128,128]...) custom-call(f32[4]{0:T(128)} %refs_0_.7, s32[4]{0:T(128)} %refs_1_.7, ...), custom_call_target="tpu_custom_call" | custom-call | flops 5368709120 | bytes 16777216 | tf_op jit(solution)/shard_map/pallas_call | solution.py:163
  4.8 0.1 collective-permute-start
  4.9 0.0 copy-start.3
  4.9 1.6 %collective-permute-start.1 = (bf16[2,2,2,128,128]{4,3,2,1,0:T(8,128)(2,1)}, bf16[2,2,2,128,128]{4,3,2,1,0:T(8,128)(2,1)S(1)}, u32[]{:S(2)}, u32[]{:S(2)}) collective-permute-start(bf16[2,2,2,128,128]{4,3,2,1,0:T(8,128)(2,1)} %get-tuple-element.37), channel_id=1, source_target_pairs={{0,16},{8,24},{16,0},{24,8},{1,17},{9,25},{17,1},{25,9},{2,18},{10... | collective-permute-start | bytes 786440 | tf_op jit(solution)/shard_map/ppermute | solution.py:326
  6.5 1.5 %collective-permute-start.3 = (bf16[2,4,128,128]{3,2,1,0:T(8,128)(2,1)}, bf16[2,4,128,128]{3,2,1,0:T(8,128)(2,1)S(1)}, u32[]{:S(2)}, u32[]{:S(2)}) collective-permute-start(bf16[2,4,128,128]{3,2,1,0:T(8,128)(2,1)} %get-tuple-element.44), channel_id=1, source_target_pairs={{0,8},{8,0},{16,24},{24,16},{1,9},{9,1},{17,25},{25,17},{2,10},{10... | collective-permute-start | bytes 786440 | tf_op jit(solution)/shard_map/ppermute | solution.py:323
  8.0 0.0 collective-permute-done.refs_5_.refs_6_
  8.0 2.0 %collective-permute-start.2 = (bf16[2,2,128,256]{3,2,1,0:T(8,128)(2,1)}, bf16[2,2,128,256]{3,2,1,0:T(8,128)(2,1)S(1)}, u32[]{:S(2)}, u32[]{:S(2)}) collective-permute-start(bf16[2,2,128,256]{3,2,1,0:T(8,128)(2,1)} %get-tuple-element.43), channel_id=1, source_target_pairs={{1,2},{2,1},{3,4},{4,3},{5,6},{6,5},{9,10},{10,9},{11,12},{12,11},... | collective-permute-start | bytes 786440 | tf_op jit(solution)/shard_map/ppermute | solution.py:329
  10.1 2.6 %shard_map.56 = (bf16[2,2,2,128,128]{4,3,2,1,0:T(8,128)(2,1)S(1)}, f32[2,2,2,128,128]{4,3,2,1,0:T(8,128)S(1)}, f32[2,2,2,128,128]{4,3,2,1,0:T(8,128)S(1)}, bf16[...) custom-call(f32[4]{0:T(128)S(1)} %copy-done.4, s32[4]{0:T(128)S(1)} %copy-done.5, s32[4,3]{1,0:T(4,128)S(1)} %copy-done.3, ...), custom_call_target="tpu_custom_call" | custom-call | flops 1024 | bytes 1024 | tf_op jit(solution)/shard_map/pallas_call | solution.py:224
  12.7 0.6 %collective-permute-start.5 = (bf16[2,2,2,128,128]{4,3,2,1,0:T(8,128)(2,1)S(1)}, bf16[2,2,2,128,128]{4,3,2,1,0:T(8,128)(2,1)S(1)}, u32[]{:S(2)}, u32[]{:S(2)}) collective-permute-start(bf16[2,2,2,128,128]{4,3,2,1,0:T(8,128)(2,1)S(1)} %get-tuple-element.38), channel_id=1, source_target_pairs={{0,16},{8,24},{16,0},{24,8},{1,17},{9,25},{17,1},{25,9},{2,18},{10... | collective-permute-start | bytes 786440 | tf_op jit(solution)/shard_map/ppermute | solution.py:326
  13.3 0.5 %collective-permute-done.1 = bf16[2,2,2,128,128]{4,3,2,1,0:T(8,128)(2,1)S(1)} collective-permute-done((bf16[2,2,2,128,128]{4,3,2,1,0:T(8,128)(2,1)}, bf16[2,2,2,128,128]{4,3,2,1,0:T(8,128)(2,1)S(1)}, u32[]{:S(2)}, u32[]{:S(2)}) %collective-permute-start.1) | collective-permute-done | bytes 262176 | tf_op jit(solution)/shard_map/ppermute | solution.py:326
  13.8 0.1 add_convert_fusion.2
  13.9 1.6 %collective-permute-start.6 = (bf16[2,2,2,128,128]{4,3,2,1,0:T(8,128)(2,1)S(1)}, bf16[2,2,2,128,128]{4,3,2,1,0:T(8,128)(2,1)S(1)}, u32[]{:S(2)}, u32[]{:S(2)}) collective-permute-start(bf16[2,2,2,128,128]{4,3,2,1,0:T(8,128)(2,1)S(1)} %add_convert_fusion.2), channel_id=1, source_target_pairs={{0,8},{8,0},{16,24},{24,16},{1,9},{9,1},{17,25},{25,17},{2,10},{10... | collective-permute-start | bytes 786440 | tf_op jit(solution)/shard_map/ppermute | solution.py:323
  15.4 0.0 collective-permute-done.3.refs_8_.refs_5_
  15.4 0.6 %collective-permute-done.2.refs_7_ = bf16[2,2,128,256]{3,2,1,0:T(8,128)(2,1)S(1)} collective-permute-done((bf16[2,2,128,256]{3,2,1,0:T(8,128)(2,1)}, bf16[2,2,128,256]{3,2,1,0:T(8,128)(2,1)S(1)}, u32[]{:S(2)}, u32[]{:S(2)}) %collective-permute-start.2) | collective-permute-done | bytes 262176 | tf_op jit(solution)/shard_map/ppermute | solution.py:329
  16.0 2.7 %shard_map.57 = (bf16[2,2,2,128,128]{4,3,2,1,0:T(8,128)(2,1)S(1)}, f32[2,2,2,128,128]{4,3,2,1,0:T(8,128)S(1)}, f32[2,2,2,128,128]{4,3,2,1,0:T(8,128)S(1)}, bf16[...) custom-call(f32[4]{0:T(128)S(1)} %copy-done.4, s32[4]{0:T(128)S(1)} %copy-done.5, s32[4,3]{1,0:T(4,128)S(1)} %copy-done.3, ...), custom_call_target="tpu_custom_call" | custom-call | flops 1024 | bytes 1024 | tf_op jit(solution)/shard_map/pallas_call | solution.py:224
  18.7 1.0 %collective-permute-start.4 = (bf16[2,2,2,128,128]{4,3,2,1,0:T(8,128)(2,1)S(1)}, bf16[2,2,2,128,128]{4,3,2,1,0:T(8,128)(2,1)S(1)}, u32[]{:S(2)}, u32[]{:S(2)}) collective-permute-start(bf16[2,2,2,128,128]{4,3,2,1,0:T(8,128)(2,1)S(1)} %get-tuple-element.47), channel_id=1, source_target_pairs={{0,16},{8,24},{16,0},{24,8},{1,17},{9,25},{17,1},{25,9},{2,18},{10... | collective-permute-start | bytes 786440 | tf_op jit(solution)/shard_map/ppermute | solution.py:326
  19.7 1.6 %collective-permute-done.5 = bf16[2,2,2,128,128]{4,3,2,1,0:T(8,128)(2,1)S(1)} collective-permute-done((bf16[2,2,2,128,128]{4,3,2,1,0:T(8,128)(2,1)S(1)}, bf16[2,2,2,128,128]{4,3,2,1,0:T(8,128)(2,1)S(1)}, u32[]{:S(2)}, u32[]{:S(2)}) %collective-permute-start.5) | collective-permute-done | bytes 262176 | tf_op jit(solution)/shard_map/ppermute | solution.py:326
  21.3 0.8 %collective-permute-start.7 = (bf16[2,128,128]{2,1,0:T(8,128)(2,1)S(1)}, bf16[2,128,128]{2,1,0:T(8,128)(2,1)S(1)}, u32[]{:S(2)}, u32[]{:S(2)}) collective-permute-start(bf16[2,128,128]{2,1,0:T(8,128)(2,1)S(1)} %get-tuple-element.52), channel_id=1, source_target_pairs={{0,1},{1,0},{2,3},{3,2},{4,5},{5,4},{6,7},{7,6},{8,9},{9,8},{10,11... | collective-permute-start | bytes 196616 | tf_op jit(solution)/shard_map/ppermute | solution.py:329
  22.1 1.9 %collective-permute-start.8 = (bf16[2,128,128]{2,1,0:T(8,128)(2,1)S(1)}, bf16[2,128,128]{2,1,0:T(8,128)(2,1)S(1)}, u32[]{:S(2)}, u32[]{:S(2)}) collective-permute-start(bf16[2,128,128]{2,1,0:T(8,128)(2,1)S(1)} %get-tuple-element.53), channel_id=1, source_target_pairs={{1,2},{2,1},{3,4},{4,3},{5,6},{6,5},{9,10},{10,9},{11,12},{12,11},... | collective-permute-start | bytes 196616 | tf_op jit(solution)/shard_map/ppermute | solution.py:329
  24.0 0.1 add_convert_fusion.1
  24.1 0.6 %collective-permute-start.10 = (bf16[2,2,2,128,128]{4,3,2,1,0:T(8,128)(2,1)S(1)}, bf16[2,2,2,128,128]{4,3,2,1,0:T(8,128)(2,1)S(1)}, u32[]{:S(2)}, u32[]{:S(2)}) collective-permute-start(bf16[2,2,2,128,128]{4,3,2,1,0:T(8,128)(2,1)S(1)} %add_convert_fusion.1), channel_id=1, source_target_pairs={{0,8},{8,0},{16,24},{24,16},{1,9},{9,1},{17,25},{25,17},{2,10},{10... | collective-permute-start | bytes 786440 | tf_op jit(solution)/shard_map/ppermute | solution.py:323
  24.7 0.0 collective-permute-done.6.got_1
  24.7 3.0 %collective-permute-done.8.refs_7_ = bf16[2,128,128]{2,1,0:T(8,128)(2,1)S(1)} collective-permute-done((bf16[2,128,128]{2,1,0:T(8,128)(2,1)S(1)}, bf16[2,128,128]{2,1,0:T(8,128)(2,1)S(1)}, u32[]{:S(2)}, u32[]{:S(2)}) %collective-permute-start.8) | collective-permute-done | bytes 65568 | tf_op jit(solution)/shard_map/ppermute | solution.py:329
  27.7 2.7 %shard_map.58 = (bf16[2,2,2,128,128]{4,3,2,1,0:T(8,128)(2,1)S(1)}, f32[2,2,2,128,128]{4,3,2,1,0:T(8,128)S(1)}) custom-call(f32[4]{0:T(128)S(1)} %copy-done.4, s32[4]{0:T(128)S(1)} %copy-done.5, s32[4,3]{1,0:T(4,128)S(1)} %copy-done.3, bf16[3,512,128]{2,1,0:T(8,128)(2,1)S(1)} %get-tuple-element.58.refs_3_, ...), custom_call_target="tpu_custom_call" | custom-call | flops 1024 | bytes 1024 | tf_op jit(solution)/shard_map/pallas_call | solution.py:224
  30.3 0.6 %collective-permute-start.11 = (bf16[2,2,2,128,128]{4,3,2,1,0:T(8,128)(2,1)S(1)}, bf16[2,2,2,128,128]{4,3,2,1,0:T(8,128)(2,1)S(1)}, u32[]{:S(2)}, u32[]{:S(2)}) collective-permute-start(bf16[2,2,2,128,128]{4,3,2,1,0:T(8,128)(2,1)S(1)} %get-tuple-element.60), channel_id=1, source_target_pairs={{0,16},{8,24},{16,0},{24,8},{1,17},{9,25},{17,1},{25,9},{2,18},{10... | collective-permute-start | bytes 786440 | tf_op jit(solution)/shard_map/ppermute | solution.py:326
  30.9 0.0 collective-permute-done.4
  30.9 0.1 add_convert_fusion
  31.0 1.4 %collective-permute-start.9 = (bf16[2,2,2,128,128]{4,3,2,1,0:T(8,128)(2,1)S(1)}, bf16[2,2,2,128,128]{4,3,2,1,0:T(8,128)(2,1)S(1)}, u32[]{:S(2)}, u32[]{:S(2)}) collective-permute-start(bf16[2,2,2,128,128]{4,3,2,1,0:T(8,128)(2,1)S(1)} %add_convert_fusion), channel_id=1, source_target_pairs={{0,8},{8,0},{16,24},{24,16},{1,9},{9,1},{17,25},{25,17},{2,10},{10... | collective-permute-start | bytes 786440 | tf_op jit(solution)/shard_map/ppermute | solution.py:323
  32.3 2.4 %shard_map.59.mine_z = f32[2,2,2,128,128]{4,3,2,1,0:T(8,128)S(1)} custom-call(f32[4]{0:T(128)S(1)} %copy-done.4, s32[4]{0:T(128)S(1)} %copy-done.5, s32[4,3]{1,0:T(4,128)S(1)} %copy-done.3, bf16[3,512,128]{2,1,0:T(8,128)(2,1)S(1)} %get-tuple-element.58.refs_3_, bf16[4,128,384]{2,1,0:T(8,128)(2,1)S(1)} %get-tuple-element.59.refs_4_, ...), custom_call_target="tpu_custom_call" | custom-call | flops 1024 | bytes 1024 | tf_op jit(solution)/shard_map/pallas_call | solution.py:224
  34.8 4.1 %collective-permute-done.11.got_z = bf16[2,2,2,128,128]{4,3,2,1,0:T(8,128)(2,1)S(1)} collective-permute-done((bf16[2,2,2,128,128]{4,3,2,1,0:T(8,128)(2,1)S(1)}, bf16[2,2,2,128,128]{4,3,2,1,0:T(8,128)(2,1)S(1)}, u32[]{:S(2)}, u32[]{:S(2)}) %collective-permute-start.11) | collective-permute-done | bytes 262176 | tf_op jit(solution)/shard_map/ppermute | solution.py:326
  38.9 1.0 %shard_map.60._ = bf16[2,2,4,128,256]{4,3,2,1,0:T(8,128)(2,1)} custom-call(f32[2,2,2,128,128]{4,3,2,1,0:T(8,128)S(1)} %copy-done.1, bf16[2,2,2,128,128]{4,3,2,1,0:T(8,128)(2,1)S(1)} %collective-permute-done.6.got_1, f32[2,2,2,128,128]{4,3,2,1,0:T(8,128)S(1)} %get-tuple-element.57.mine_2, bf16[2,2,2,128,128]{4,3,2,1,0:T(8,128)(2,1)S(1)} %collective-permute-done.10.got_2, ...), custom_call_target="tpu_custom_call" | custom-call | flops 1024 | bytes 1024 | tf_op jit(solution)/shard_map/pallas_call | solution.py:289
  39.9 0.8 %shard_map.61 = bf16[2,2,4,128,256]{4,3,2,1,0:T(8,128)(2,1)} custom-call(f32[2,2,2,128,128]{4,3,2,1,0:T(8,128)S(1)} %get-tuple-element.45.mine, bf16[2,2,2,128,128]{4,3,2,1,0:T(8,128)(2,1)S(1)} %collective-permute-done.9.got, bf16[2,2,4,128,256]{4,3,2,1,0:T(8,128)(2,1)} %shard_map.60._), custom_call_target="tpu_custom_call", output_to_operand_aliasing={{}: (2, {})} | custom-call | flops 1024 | bytes 1024 | tf_op jit(solution)/shard_map/pallas_call | solution.py:300
  (16 shorter events, 0.0 us)
Async XLA Ops:
  0.0 10.0 %copy-start = (bf16[2,2,4,128,256]{4,3,2,1,0:T(8,128)(2,1)S(1)}, bf16[2,2,4,128,256]{4,3,2,1,0:T(8,128)(2,1)}, u32[]{:S(2)}) copy-start(bf16[2,2,4,128,256]{4,3,2,1,0:T(8,128)(2,1)} %refs_5_.3) | copy-start | bytes 3145732
  0.0 10.0 %copy-start.2 = (bf16[4,3,128,128]{3,2,1,0:T(8,128)(2,1)S(1)}, bf16[4,3,128,128]{3,2,1,0:T(8,128)(2,1)}, u32[]{:S(2)}) copy-start(bf16[4,3,128,128]{3,2,1,0:T(8,128)(2,1)} %refs_3_.1) | copy-start | bytes 1179652
  4.8 3.2 %collective-permute-start = (bf16[2,2,128,256]{3,2,1,0:T(8,128)(2,1)}, bf16[2,2,128,256]{3,2,1,0:T(8,128)(2,1)S(1)}, u32[]{:S(2)}, u32[]{:S(2)}) collective-permute-start(bf16[2,2,128,256]{3,2,1,0:T(8,128)(2,1)} %get-tuple-element.33), channel_id=1, source_target_pairs={{0,1},{1,0},{2,3},{3,2},{4,5},{5,4},{6,7},{7,6},{8,9},{9,8},{10,11... | collective-permute-start | bytes 786440 | tf_op jit(solution)/shard_map/ppermute | solution.py:329
  4.9 5.2 %copy-start.3 = (s32[4,3]{1,0:T(4,128)S(1)}, s32[4,3]{1,0:T(4,128)}, u32[]{:S(2)}) copy-start(s32[4,3]{1,0:T(4,128)} %refs_2_.7) | copy-start | bytes 148
  4.9 8.9 %collective-permute-start.1 = (bf16[2,2,2,128,128]{4,3,2,1,0:T(8,128)(2,1)}, bf16[2,2,2,128,128]{4,3,2,1,0:T(8,128)(2,1)S(1)}, u32[]{:S(2)}, u32[]{:S(2)}) collective-permute-start(bf16[2,2,2,128,128]{4,3,2,1,0:T(8,128)(2,1)} %get-tuple-element.37), channel_id=1, source_target_pairs={{0,16},{8,24},{16,0},{24,8},{1,17},{9,25},{17,1},{25,9},{2,18},{10... | collective-permute-start | bytes 786440 | tf_op jit(solution)/shard_map/ppermute | solution.py:326
  6.5 3.6 %copy-start.4 = (f32[4]{0:T(128)S(1)}, f32[4]{0:T(128)}, u32[]{:S(2)}) copy-start(f32[4]{0:T(128)} %refs_0_.7) | copy-start | bytes 52
  6.5 3.6 %copy-start.5 = (s32[4]{0:T(128)S(1)}, s32[4]{0:T(128)}, u32[]{:S(2)}) copy-start(s32[4]{0:T(128)} %refs_1_.7) | copy-start | bytes 52
  6.5 9.0 %collective-permute-start.3 = (bf16[2,4,128,128]{3,2,1,0:T(8,128)(2,1)}, bf16[2,4,128,128]{3,2,1,0:T(8,128)(2,1)S(1)}, u32[]{:S(2)}, u32[]{:S(2)}) collective-permute-start(bf16[2,4,128,128]{3,2,1,0:T(8,128)(2,1)} %get-tuple-element.44), channel_id=1, source_target_pairs={{0,8},{8,0},{16,24},{24,16},{1,9},{9,1},{17,25},{25,17},{2,10},{10... | collective-permute-start | bytes 786440 | tf_op jit(solution)/shard_map/ppermute | solution.py:323
  8.0 5.8 %copy-start.6 = (f32[2,2,2,128,128]{4,3,2,1,0:T(8,128)S(1)}, f32[2,2,2,128,128]{4,3,2,1,0:T(8,128)}, u32[]{:S(2)}) copy-start(f32[2,2,2,128,128]{4,3,2,1,0:T(8,128)} %get-tuple-element.36) | copy-start | bytes 1572868
  8.0 8.0 %collective-permute-start.2 = (bf16[2,2,128,256]{3,2,1,0:T(8,128)(2,1)}, bf16[2,2,128,256]{3,2,1,0:T(8,128)(2,1)S(1)}, u32[]{:S(2)}, u32[]{:S(2)}) collective-permute-start(bf16[2,2,128,256]{3,2,1,0:T(8,128)(2,1)} %get-tuple-element.43), channel_id=1, source_target_pairs={{1,2},{2,1},{3,4},{4,3},{5,6},{6,5},{9,10},{10,9},{11,12},{12,11},... | collective-permute-start | bytes 786440 | tf_op jit(solution)/shard_map/ppermute | solution.py:329
  12.7 8.6 %collective-permute-start.5 = (bf16[2,2,2,128,128]{4,3,2,1,0:T(8,128)(2,1)S(1)}, bf16[2,2,2,128,128]{4,3,2,1,0:T(8,128)(2,1)S(1)}, u32[]{:S(2)}, u32[]{:S(2)}) collective-permute-start(bf16[2,2,2,128,128]{4,3,2,1,0:T(8,128)(2,1)S(1)} %get-tuple-element.38), channel_id=1, source_target_pairs={{0,16},{8,24},{16,0},{24,8},{1,17},{9,25},{17,1},{25,9},{2,18},{10... | collective-permute-start | bytes 786440 | tf_op jit(solution)/shard_map/ppermute | solution.py:326
  13.9 10.8 %collective-permute-start.6 = (bf16[2,2,2,128,128]{4,3,2,1,0:T(8,128)(2,1)S(1)}, bf16[2,2,2,128,128]{4,3,2,1,0:T(8,128)(2,1)S(1)}, u32[]{:S(2)}, u32[]{:S(2)}) collective-permute-start(bf16[2,2,2,128,128]{4,3,2,1,0:T(8,128)(2,1)S(1)} %add_convert_fusion.2), channel_id=1, source_target_pairs={{0,8},{8,0},{16,24},{24,16},{1,9},{9,1},{17,25},{25,17},{2,10},{10... | collective-permute-start | bytes 786440 | tf_op jit(solution)/shard_map/ppermute | solution.py:323
  18.7 12.2 %collective-permute-start.4 = (bf16[2,2,2,128,128]{4,3,2,1,0:T(8,128)(2,1)S(1)}, bf16[2,2,2,128,128]{4,3,2,1,0:T(8,128)(2,1)S(1)}, u32[]{:S(2)}, u32[]{:S(2)}) collective-permute-start(bf16[2,2,2,128,128]{4,3,2,1,0:T(8,128)(2,1)S(1)} %get-tuple-element.47), channel_id=1, source_target_pairs={{0,16},{8,24},{16,0},{24,8},{1,17},{9,25},{17,1},{25,9},{2,18},{10... | collective-permute-start | bytes 786440 | tf_op jit(solution)/shard_map/ppermute | solution.py:326
  21.3 3.3 %collective-permute-start.7 = (bf16[2,128,128]{2,1,0:T(8,128)(2,1)S(1)}, bf16[2,128,128]{2,1,0:T(8,128)(2,1)S(1)}, u32[]{:S(2)}, u32[]{:S(2)}) collective-permute-start(bf16[2,128,128]{2,1,0:T(8,128)(2,1)S(1)} %get-tuple-element.52), channel_id=1, source_target_pairs={{0,1},{1,0},{2,3},{3,2},{4,5},{5,4},{6,7},{7,6},{8,9},{9,8},{10,11... | collective-permute-start | bytes 196616 | tf_op jit(solution)/shard_map/ppermute | solution.py:329
  22.1 5.6 %collective-permute-start.8 = (bf16[2,128,128]{2,1,0:T(8,128)(2,1)S(1)}, bf16[2,128,128]{2,1,0:T(8,128)(2,1)S(1)}, u32[]{:S(2)}, u32[]{:S(2)}) collective-permute-start(bf16[2,128,128]{2,1,0:T(8,128)(2,1)S(1)} %get-tuple-element.53), channel_id=1, source_target_pairs={{1,2},{2,1},{3,4},{4,3},{5,6},{6,5},{9,10},{10,9},{11,12},{12,11},... | collective-permute-start | bytes 196616 | tf_op jit(solution)/shard_map/ppermute | solution.py:329
  24.1 10.7 %collective-permute-start.10 = (bf16[2,2,2,128,128]{4,3,2,1,0:T(8,128)(2,1)S(1)}, bf16[2,2,2,128,128]{4,3,2,1,0:T(8,128)(2,1)S(1)}, u32[]{:S(2)}, u32[]{:S(2)}) collective-permute-start(bf16[2,2,2,128,128]{4,3,2,1,0:T(8,128)(2,1)S(1)} %add_convert_fusion.1), channel_id=1, source_target_pairs={{0,8},{8,0},{16,24},{24,16},{1,9},{9,1},{17,25},{25,17},{2,10},{10... | collective-permute-start | bytes 786440 | tf_op jit(solution)/shard_map/ppermute | solution.py:323
  30.3 8.6 %collective-permute-start.11 = (bf16[2,2,2,128,128]{4,3,2,1,0:T(8,128)(2,1)S(1)}, bf16[2,2,2,128,128]{4,3,2,1,0:T(8,128)(2,1)S(1)}, u32[]{:S(2)}, u32[]{:S(2)}) collective-permute-start(bf16[2,2,2,128,128]{4,3,2,1,0:T(8,128)(2,1)S(1)} %get-tuple-element.60), channel_id=1, source_target_pairs={{0,16},{8,24},{16,0},{24,8},{1,17},{9,25},{17,1},{25,9},{2,18},{10... | collective-permute-start | bytes 786440 | tf_op jit(solution)/shard_map/ppermute | solution.py:326
  31.0 7.9 %copy-start.1 = (f32[2,2,2,128,128]{4,3,2,1,0:T(8,128)S(1)}, f32[2,2,2,128,128]{4,3,2,1,0:T(8,128)}, u32[]{:S(2)}) copy-start(f32[2,2,2,128,128]{4,3,2,1,0:T(8,128)} %get-tuple-element.56.mine_1) | copy-start | bytes 1572868
  31.0 8.9 %collective-permute-start.9 = (bf16[2,2,2,128,128]{4,3,2,1,0:T(8,128)(2,1)S(1)}, bf16[2,2,2,128,128]{4,3,2,1,0:T(8,128)(2,1)S(1)}, u32[]{:S(2)}, u32[]{:S(2)}) collective-permute-start(bf16[2,2,2,128,128]{4,3,2,1,0:T(8,128)(2,1)S(1)} %add_convert_fusion), channel_id=1, source_target_pairs={{0,8},{8,0},{16,24},{24,16},{1,9},{9,1},{17,25},{25,17},{2,10},{10... | collective-permute-start | bytes 786440 | tf_op jit(solution)/shard_map/ppermute | solution.py:323

commit v6 on v5

--- a/solution.py
+++ b/solution.py
@@ -107,6 +107,7 @@
 VMEM = pl.BlockSpec(memory_space=pltpu.VMEM)
 SMEM = pl.BlockSpec(memory_space=pltpu.SMEM)
 HBM = pl.BlockSpec(memory_space=pltpu.HBM)
+LONG = pl.CostEstimate(flops=5 << 30, bytes_accessed=16 << 20, transcendentals=0)
 SMALL = pl.CostEstimate(flops=1024, bytes_accessed=1024, transcendentals=0)
 
 
@@ -130,7 +131,8 @@
     stack_coupling(c_ref, rows, cols)
     for fetch in fetches[1:]:
         fetch.wait()
-    send(own.at[0, :, :, :, pl.ds(0, size)], raw_h)
+    for e in range(own.shape[1]):
+        send(own.at[0, e, :, :, pl.ds(0, size)], raw_h.at[:, e])
     send(own.at[:, :, place(NEAR, owned)], edge_n)
     send(own.at[:, :, place(FAR, owned)], edge_f)
 
@@ -156,7 +158,7 @@
         (shape, BF16),
         (shape, F32),
         (shape, F32),
-        ((count, owned, size, size), BF16),
+        ((owned, count, size, size), BF16),
         (edge, BF16),
         (edge, BF16),
     ]
@@ -173,21 +175,19 @@
             pltpu.VMEM(greens.shape, BF16),
         ]
         + [pltpu.VMEM(*out) for out in outs[:3] + [(rows, BF16), (cols, BF16)]]
-        + [pltpu.SemaphoreType.DMA((5,)), pltpu.SemaphoreType.DMA((9,))]
+        + [pltpu.SemaphoreType.DMA((5,)), pltpu.SemaphoreType.DMA((10,))]
         + scratch(modes, slots, size, count),
         compiler_params=pltpu.CompilerParams(vmem_limit_bytes=58 << 20),
-        cost_estimate=pl.CostEstimate(flops=5 << 30, bytes_accessed=16 << 20, transcendentals=0),
+        cost_estimate=LONG,
     )(occupation, offsets, neighbours, coupling, greens)
 
 
-def next_body(groups, flip, wanted, with_parts, n_stacked, n_edges, n_copied, *refs):
+def next_body(groups, flip, wanted, with_parts, n_stacked, n_edges, *refs):
     occ, off, nbr = refs[:3]
     at = 3 + n_stacked
     own = refs[at]
     edge_refs = dict(zip((NEAR, FAR), refs[at + 1 : at + 1 + n_edges]))
-    at += 1 + n_edges
-    copied = refs[at : at + n_copied]
-    outs = list(refs[at + n_copied : -2])
+    outs = list(refs[at + 1 + n_edges : -2])
     half, acc = refs[-2:]
     if n_stacked == 1:
         rows, cols = outs[-2:]
@@ -197,39 +197,37 @@
         rows, cols = refs[3:5]
 
     def read(part, e, at, lanes):
-        return own[part, e, at, :, lanes] if with_parts else own[e, at]
+        return own[part, e, at, :, lanes] if with_parts else own[at, e]
 
     def read_edge(ref, part, e, lanes):
-        return ref[part, e, :, lanes] if with_parts else ref[e]
+        if with_parts:
+            return ref[part, e, :, lanes]
+        return ref[e] if len(ref.shape) == 3 else ref[place(FAR, ref.shape[0]), e]
 
     edges = {name: functools.partial(read_edge, ref) for name, ref in edge_refs.items()}
     results = [outs.pop(0) if want else None for want in wanted]
-    for array in copied:
-        for block in (NEAR, FAR):
-            outs.pop(0)[...] = array[:, place(block, array.shape[1])]
     for i, group in enumerate(groups):
         views = [None if ref is None else ref.at[i] for ref in results]
         group_terms(group, flip, (occ, off, nbr), rows, cols, read, edges, views, half, acc)
 
 
-def next_call(groups, flip, wanted, scalars, stacked, own, edges, copied=()):
+def next_call(groups, flip, wanted, scalars, stacked, own, edges, estimate=None):
     modes, slots, size = stacked[0].shape[:3] if len(stacked) == 1 else (stacked[1].shape[0],) + stacked[0].shape[::2]
-    count = own.shape[-4]
+    count = own.shape[1]
     shape = pieces(size, count)
     outs = [jax.ShapeDtypeStruct(shape, kind) for want, kind in zip(wanted, (BF16, F32, F32)) if want]
-    outs += [jax.ShapeDtypeStruct((count, size, size), BF16)] * (2 * len(copied))
     if len(stacked) == 1:
         outs.append(jax.ShapeDtypeStruct((slots, modes * size, size), BF16))
         outs.append(jax.ShapeDtypeStruct((modes, size, slots * size), BF16))
     return pl.pallas_call(
-        functools.partial(next_body, groups, flip, wanted, own.ndim == 5, len(stacked), len(edges), len(copied)),
+        functools.partial(next_body, groups, flip, wanted, own.ndim == 5, len(stacked), len(edges)),
         out_shape=outs,
-        in_specs=[SMEM] * 3 + [VMEM] * (1 + len(stacked) + len(edges) + len(copied)),
+        in_specs=[SMEM] * 3 + [VMEM] * (1 + len(stacked) + len(edges)),
         out_specs=[VMEM] * len(outs),
         scratch_shapes=scratch(modes, slots, size, count),
         compiler_params=pltpu.CompilerParams(vmem_limit_bytes=16 << 20),
-        cost_estimate=SMALL,
-    )(*scalars, *stacked, own, *edges, *copied)
+        cost_estimate=estimate or SMALL,
+    )(*scalars, *stacked, own, *edges)
 
 
 def early_body(mine_1, got_1, mine_2, got_2, mine_z, near_z, got_z, out, whole, edge, half, raw, sems):
@@ -318,6 +316,7 @@
     scalars = (occupation, offsets, neighbours)
     chip = [(i, i ^ 1) for i in range(slabs)]
     chips = [(i, i + 1 if i % 2 else i - 1) for i in range(1, slabs - 1)]
+    odd = lax.axis_index("slab") % 2 == 1
 
     def across(array):
         return lax.ppermute(array, "energy", [(i, i ^ 1) for i in range(4)])
@@ -339,27 +338,28 @@
     raw_x = across(raw)
     beside_f = beside(after_these(edge_f, beside_n), chips)
     far_2, near_2, mine_2, rows, cols = next_call(
-        SECOND, 0, (1, 1, 1), scalars, (coupling,), greens, (beside_n,)
+        SECOND, 0, (1, 1, 1), scalars, (coupling,), greens, (beside_n,), SMALL
     )
     relay_2 = along(far_2)
     both_1 = total(near_1, after_these(relay_1, far_2))
     got_1 = across(both_1)
     stacked = after_these((rows, cols), both_1)
-    far_3, near_3, mine_3, raw_n, raw_f = next_call(
-        THIRD, 0, (1, 1, 1), scalars, stacked, greens, (beside_n, beside_f), (raw_x,)
+    far_3, near_3, mine_3 = next_call(
+        THIRD, 0, (1, 1, 1), scalars, stacked, greens, (beside_n, beside_f), SMALL
     )
     relay_3 = along(far_3)
-    beside_xn = beside(raw_n, chip)
+    raw_f = jnp.where(odd, raw_x[-1], raw_x[0])
+    beside_xn = beside(raw_x, chip)
     beside_xf = beside(raw_f, chips)
     both_2 = total(near_2, after_these(relay_2, near_3))
     got_2 = across(both_2)
     stacked = after_these(stacked, both_2, got_1)
-    far_z, near_z = next_call(RAW, 1, (1, 1, 0), scalars, stacked, raw_x, (beside_xn, beside_xf))
+    far_z, near_z = next_call(RAW, 1, (1, 1, 0), scalars, stacked, raw_x, (beside_xn, beside_xf), SMALL)
     got_z = along(far_z)
     both_3 = total(near_3, after_these(relay_3, near_z))
     got_3 = across(both_3)
     stacked = after_these(stacked, both_3)
-    (mine_z,) = next_call(RAW, 0, (0, 0, 1), scalars, stacked, greens, (beside_n, beside_f))
+    (mine_z,) = next_call(RAW, 0, (0, 0, 1), scalars, stacked, greens, (beside_n, beside_f), SMALL)
     return add_up((mine_1, got_1, mine_2, got_2, mine_z, near_z, got_z), (mine_3, got_3), greens)
 
 

time: 40.8 us -> 38.8 us (0.951)
  waiting for transfers between devices: 9.82 us -> 6.09 us
  starting transfers between devices: 13.5 us -> 14.5 us
  local copies, waits for them, and re-layouts: 0.03 us -> 0.66 us
    ppermute x4, waiting for transfers between devices: 6.24 us -> 4.04 us  [along(): return lax.ppermute(array, 'energy', [(i, i ^ 2) for i in range(4)])]
    ppermute x4, waiting for transfers between devices: 3.57 us -> 2.04 us  [beside(): return lax.ppermute(array, 'slab', pairs)]
    unnamed x14, local copies, waits for them, and re-layouts: 0.03 us -> 0.66 us
    ppermute x4, starting transfers between devices: 3.74 us -> 4.33 us  [along(): return lax.ppermute(array, 'energy', [(i, i ^ 2) for i in range(4)])]
  transfers between devices with their start and end apart: 12 -> 12, of which waited for: 5 -> 2; matrix products, arithmetic and copies ran while one was open for 0% -> 0% of each run, Pallas kernels for 28% -> 29%
where the time goes in v6:
time: 38.8 us; the launch traced here: 38.6 us
  Pallas kernels  16.9 us (44%)
  starting transfers between devices  14.5 us (37%)
  waiting for transfers between devices  6.09 us (16%)
  local copies, waits for them, and re-layouts  0.66 us (2%)
    pallas_call x4, Pallas kernels, next_call(): pl.pallas_call(functools.partial(next_body, groups, flip, wanted, own.ndi...  10.4 us
    ppermute x4, starting transfers between devices, across(): return lax.ppermute(array, 'energy', [(i, i ^ 1) for i in range(4)])  5.4 us
    pallas_call x1, Pallas kernels, first_call(): pl.pallas_call(first_body, out_shape=[jax.ShapeDtypeStruct(*out) for out...  4.81 us
    ppermute x4, starting transfers between devices, beside(): return lax.ppermute(array, 'slab', pairs)  4.78 us
    ppermute x4, starting transfers between devices, along(): return lax.ppermute(array, 'energy', [(i, i ^ 2) for i in range(4)])  4.33 us
    ppermute x4, waiting for transfers between devices, along(): return lax.ppermute(array, 'energy', [(i, i ^ 2) for i in range(4)])  4.04 us
    ppermute x4, waiting for transfers between devices, beside(): return lax.ppermute(array, 'slab', pairs)  2.04 us
    pallas_call x1, Pallas kernels, add_up(): pl.pallas_call(early_body, out_shape=jax.ShapeDtypeStruct(greens.shape, B...  0.97 us
  transfers between devices with their start and end apart: 12, of which 2 were waited for; matrix products, arithmetic and copies ran while one was open for 0% of the time, Pallas kernels for 29%

profile of v6, /device:TPU:8, one launch (start us, length us, event | category | flops | bytes accessed | tf_op | source)
XLA Modules:
  0.0 38.6 jit_solution(9897099123370381768)
XLA Ops:
  0.0 4.8 %shard_map.55 = (bf16[2,2,2,128,128]{4,3,2,1,0:T(8,128)(2,1)}, f32[2,2,2,128,128]{4,3,2,1,0:T(8,128)}, f32[2,2,2,128,128]{4,3,2,1,0:T(8,128)}, bf16[4,2,128,128]...) custom-call(f32[4]{0:T(128)} %refs_0_.7, s32[4]{0:T(128)} %refs_1_.7, ...), custom_call_target="tpu_custom_call" | custom-call | flops 5368709120 | bytes 16777216 | tf_op jit(solution)/shard_map/pallas_call | solution.py:165
  4.8 0.1 collective-permute-start
  4.9 1.6 %collective-permute-start.1 = (bf16[2,2,2,128,128]{4,3,2,1,0:T(8,128)(2,1)}, bf16[2,2,2,128,128]{4,3,2,1,0:T(8,128)(2,1)S(1)}, u32[]{:S(2)}, u32[]{:S(2)}) collective-permute-start(bf16[2,2,2,128,128]{4,3,2,1,0:T(8,128)(2,1)} %get-tuple-element.35), channel_id=1, source_target_pairs={{0,16},{8,24},{16,0},{24,8},{1,17},{9,25},{17,1},{25,9},{2,18},{10... | collective-permute-start | bytes 786440 | tf_op jit(solution)/shard_map/ppermute | solution.py:325
  6.5 1.5 %collective-permute-start.6 = (bf16[4,2,128,128]{3,2,1,0:T(8,128)(2,1)}, bf16[4,2,128,128]{3,2,1,0:T(8,128)(2,1)S(1)}, u32[]{:S(2)}, u32[]{:S(2)}) collective-permute-start(bf16[4,2,128,128]{3,2,1,0:T(8,128)(2,1)} %get-tuple-element.49), channel_id=1, source_target_pairs={{0,8},{8,0},{16,24},{24,16},{1,9},{9,1},{17,25},{25,17},{2,10},{10... | collective-permute-start | bytes 786440 | tf_op jit(solution)/shard_map/ppermute | solution.py:322
  8.0 1.9 %collective-permute-start.2 = (bf16[2,2,128,256]{3,2,1,0:T(8,128)(2,1)}, bf16[2,2,128,256]{3,2,1,0:T(8,128)(2,1)S(1)}, u32[]{:S(2)}, u32[]{:S(2)}) collective-permute-start(bf16[2,2,128,256]{3,2,1,0:T(8,128)(2,1)} %get-tuple-element.41), channel_id=1, source_target_pairs={{1,2},{2,1},{3,4},{4,3},{5,6},{6,5},{9,10},{10,9},{11,12},{12,11},... | collective-permute-start | bytes 786440 | tf_op jit(solution)/shard_map/ppermute | solution.py:328
  9.9 0.0 copy-start.3
  9.9 0.0 copy-start.4
  9.9 0.0 copy-start.5
  10.0 0.6 %copy-done.3 = s32[4,3]{1,0:T(4,128)S(1)} copy-done((s32[4,3]{1,0:T(4,128)S(1)}, s32[4,3]{1,0:T(4,128)}, u32[]{:S(2)}) %copy-start.3) | copy-done | bytes 72
  10.6 2.6 %shard_map.56 = (bf16[2,2,2,128,128]{4,3,2,1,0:T(8,128)(2,1)S(1)}, f32[2,2,2,128,128]{4,3,2,1,0:T(8,128)S(1)}, f32[2,2,2,128,128]{4,3,2,1,0:T(8,128)S(1)}, bf16[...) custom-call(f32[4]{0:T(128)S(1)} %copy-done.4, s32[4]{0:T(128)S(1)} %copy-done.5, s32[4,3]{1,0:T(4,128)S(1)} %copy-done.3, ...), custom_call_target="tpu_custom_call" | custom-call | flops 1024 | bytes 1024 | tf_op jit(solution)/shard_map/pallas_call | solution.py:222
  13.2 0.6 %collective-permute-start.4 = (bf16[2,2,2,128,128]{4,3,2,1,0:T(8,128)(2,1)S(1)}, bf16[2,2,2,128,128]{4,3,2,1,0:T(8,128)(2,1)S(1)}, u32[]{:S(2)}, u32[]{:S(2)}) collective-permute-start(bf16[2,2,2,128,128]{4,3,2,1,0:T(8,128)(2,1)S(1)} %get-tuple-element.36), channel_id=1, source_target_pairs={{0,16},{8,24},{16,0},{24,8},{1,17},{9,25},{17,1},{25,9},{2,18},{10... | collective-permute-start | bytes 786440 | tf_op jit(solution)/shard_map/ppermute | solution.py:325
  13.8 0.0 collective-permute-done.1
  13.8 0.1 add_convert_fusion.2
  13.9 1.6 %collective-permute-start.5 = (bf16[2,2,2,128,128]{4,3,2,1,0:T(8,128)(2,1)S(1)}, bf16[2,2,2,128,128]{4,3,2,1,0:T(8,128)(2,1)S(1)}, u32[]{:S(2)}, u32[]{:S(2)}) collective-permute-start(bf16[2,2,2,128,128]{4,3,2,1,0:T(8,128)(2,1)S(1)} %add_convert_fusion.2), channel_id=1, source_target_pairs={{0,8},{8,0},{16,24},{24,16},{1,9},{9,1},{17,25},{25,17},{2,10},{10... | collective-permute-start | bytes 786440 | tf_op jit(solution)/shard_map/ppermute | solution.py:322
  15.5 0.8 %collective-permute-start.7 = (bf16[4,2,128,128]{3,2,1,0:T(8,128)(2,1)S(1)}, bf16[4,2,128,128]{3,2,1,0:T(8,128)(2,1)S(1)}, u32[]{:S(2)}, u32[]{:S(2)}) collective-permute-start(bf16[4,2,128,128]{3,2,1,0:T(8,128)(2,1)S(1)} %collective-permute-done.6.refs_5_), channel_id=1, source_target_pairs={{0,1},{1,0},{2,3},{3,2},{4,5},{5,4},{6,7},{7,6},{8,9},{9,8},{10,11... | collective-permute-start | bytes 786440 | tf_op jit(solution)/shard_map/ppermute | solution.py:328
  16.2 0.0 collective-permute-done.2.refs_7_
  16.2 2.7 %shard_map.57 = (bf16[2,2,2,128,128]{4,3,2,1,0:T(8,128)(2,1)S(1)}, f32[2,2,2,128,128]{4,3,2,1,0:T(8,128)S(1)}, f32[2,2,2,128,128]{4,3,2,1,0:T(8,128)S(1)}) custom-call(f32[4]{0:T(128)S(1)} %copy-done.4, s32[4]{0:T(128)S(1)} %copy-done.5, s32[4,3]{1,0:T(4,128)S(1)} %copy-done.3, bf16[3,512,128]{2,1,0:T(8,128)(2,1)S(1)} %get-tuple-element.54.refs_3_, ...), custom_call_target="tpu_custom_call" | custom-call | flops 1024 | bytes 1024 | tf_op jit(solution)/shard_map/pallas_call | solution.py:222
  18.9 1.0 %collective-permute-start.3 = (bf16[2,2,2,128,128]{4,3,2,1,0:T(8,128)(2,1)S(1)}, bf16[2,2,2,128,128]{4,3,2,1,0:T(8,128)(2,1)S(1)}, u32[]{:S(2)}, u32[]{:S(2)}) collective-permute-start(bf16[2,2,2,128,128]{4,3,2,1,0:T(8,128)(2,1)S(1)} %get-tuple-element.44), channel_id=1, source_target_pairs={{0,16},{8,24},{16,0},{24,8},{1,17},{9,25},{17,1},{25,9},{2,18},{10... | collective-permute-start | bytes 786440 | tf_op jit(solution)/shard_map/ppermute | solution.py:325
  19.9 2.0 %collective-permute-start.8 = (bf16[2,128,128]{2,1,0:T(8,128)(2,1)S(1)}, bf16[2,128,128]{2,1,0:T(8,128)(2,1)S(1)}, u32[]{:S(2)}, u32[]{:S(2)}) collective-permute-start(bf16[2,128,128]{2,1,0:T(8,128)(2,1)S(1)} %fusion), channel_id=1, source_target_pairs={{1,2},{2,1},{3,4},{4,3},{5,6},{6,5},{9,10},{10,9},{11,12},{12,11},... | collective-permute-start | bytes 196616 | tf_op jit(solution)/shard_map/ppermute | solution.py:328
  21.9 0.0 collective-permute-done.4
  21.9 0.1 add_convert_fusion.1
  22.0 1.4 %collective-permute-start.10 = (bf16[2,2,2,128,128]{4,3,2,1,0:T(8,128)(2,1)S(1)}, bf16[2,2,2,128,128]{4,3,2,1,0:T(8,128)(2,1)S(1)}, u32[]{:S(2)}, u32[]{:S(2)}) collective-permute-start(bf16[2,2,2,128,128]{4,3,2,1,0:T(8,128)(2,1)S(1)} %add_convert_fusion.1), channel_id=1, source_target_pairs={{0,8},{8,0},{16,24},{24,16},{1,9},{9,1},{17,25},{25,17},{2,10},{10... | collective-permute-start | bytes 786440 | tf_op jit(solution)/shard_map/ppermute | solution.py:322
  23.4 0.0 collective-permute-done.5.got_1
  23.4 2.0 %collective-permute-done.8.refs_7_ = bf16[2,128,128]{2,1,0:T(8,128)(2,1)S(1)} collective-permute-done((bf16[2,128,128]{2,1,0:T(8,128)(2,1)S(1)}, bf16[2,128,128]{2,1,0:T(8,128)(2,1)S(1)}, u32[]{:S(2)}, u32[]{:S(2)}) %collective-permute-start.8) | collective-permute-done | bytes 65568 | tf_op jit(solution)/shard_map/ppermute | solution.py:328
  25.5 2.7 %shard_map.58 = (bf16[2,2,2,128,128]{4,3,2,1,0:T(8,128)(2,1)S(1)}, f32[2,2,2,128,128]{4,3,2,1,0:T(8,128)S(1)}) custom-call(f32[4]{0:T(128)S(1)} %copy-done.4, s32[4]{0:T(128)S(1)} %copy-done.5, s32[4,3]{1,0:T(4,128)S(1)} %copy-done.3, bf16[3,512,128]{2,1,0:T(8,128)(2,1)S(1)} %get-tuple-element.54.refs_3_, ...), custom_call_target="tpu_custom_call" | custom-call | flops 1024 | bytes 1024 | tf_op jit(solution)/shard_map/pallas_call | solution.py:222
  28.2 1.2 %collective-permute-start.11 = (bf16[2,2,2,128,128]{4,3,2,1,0:T(8,128)(2,1)S(1)}, bf16[2,2,2,128,128]{4,3,2,1,0:T(8,128)(2,1)S(1)}, u32[]{:S(2)}, u32[]{:S(2)}) collective-permute-start(bf16[2,2,2,128,128]{4,3,2,1,0:T(8,128)(2,1)S(1)} %get-tuple-element.56), channel_id=1, source_target_pairs={{0,16},{8,24},{16,0},{24,8},{1,17},{9,25},{17,1},{25,9},{2,18},{10... | collective-permute-start | bytes 786440 | tf_op jit(solution)/shard_map/ppermute | solution.py:325
  29.4 0.1 add_convert_fusion
  29.4 0.9 %collective-permute-start.9 = (bf16[2,2,2,128,128]{4,3,2,1,0:T(8,128)(2,1)S(1)}, bf16[2,2,2,128,128]{4,3,2,1,0:T(8,128)(2,1)S(1)}, u32[]{:S(2)}, u32[]{:S(2)}) collective-permute-start(bf16[2,2,2,128,128]{4,3,2,1,0:T(8,128)(2,1)S(1)} %add_convert_fusion), channel_id=1, source_target_pairs={{0,8},{8,0},{16,24},{24,16},{1,9},{9,1},{17,25},{25,17},{2,10},{10... | collective-permute-start | bytes 786440 | tf_op jit(solution)/shard_map/ppermute | solution.py:322
  30.4 2.4 %shard_map.59.mine_z = f32[2,2,2,128,128]{4,3,2,1,0:T(8,128)S(1)} custom-call(f32[4]{0:T(128)S(1)} %copy-done.4, s32[4]{0:T(128)S(1)} %copy-done.5, s32[4,3]{1,0:T(4,128)S(1)} %copy-done.3, bf16[3,512,128]{2,1,0:T(8,128)(2,1)S(1)} %get-tuple-element.54.refs_3_, bf16[4,128,384]{2,1,0:T(8,128)(2,1)S(1)} %get-tuple-element.55.refs_4_, ...), custom_call_target="tpu_custom_call" | custom-call | flops 1024 | bytes 1024 | tf_op jit(solution)/shard_map/pallas_call | solution.py:222
  32.8 4.0 %collective-permute-done.11.got_z = bf16[2,2,2,128,128]{4,3,2,1,0:T(8,128)(2,1)S(1)} collective-permute-done((bf16[2,2,2,128,128]{4,3,2,1,0:T(8,128)(2,1)S(1)}, bf16[2,2,2,128,128]{4,3,2,1,0:T(8,128)(2,1)S(1)}, u32[]{:S(2)}, u32[]{:S(2)}) %collective-permute-start.11) | collective-permute-done | bytes 262176 | tf_op jit(solution)/shard_map/ppermute | solution.py:325
  36.8 1.0 %shard_map.60._ = bf16[2,2,4,128,256]{4,3,2,1,0:T(8,128)(2,1)} custom-call(f32[2,2,2,128,128]{4,3,2,1,0:T(8,128)S(1)} %copy-done.1, bf16[2,2,2,128,128]{4,3,2,1,0:T(8,128)(2,1)S(1)} %collective-permute-done.5.got_1, f32[2,2,2,128,128]{4,3,2,1,0:T(8,128)S(1)} %get-tuple-element.53.mine_2, bf16[2,2,2,128,128]{4,3,2,1,0:T(8,128)(2,1)S(1)} %collective-permute-done.10.got_2, ...), custom_call_target="tpu_custom_call" | custom-call | flops 1024 | bytes 1024 | tf_op jit(solution)/shard_map/pallas_call | solution.py:287
  37.8 0.8 %shard_map.61 = bf16[2,2,4,128,256]{4,3,2,1,0:T(8,128)(2,1)} custom-call(f32[2,2,2,128,128]{4,3,2,1,0:T(8,128)S(1)} %get-tuple-element.42.mine, bf16[2,2,2,128,128]{4,3,2,1,0:T(8,128)(2,1)S(1)} %collective-permute-done.9.got, bf16[2,2,4,128,256]{4,3,2,1,0:T(8,128)(2,1)} %shard_map.60._), custom_call_target="tpu_custom_call", output_to_operand_aliasing={{}: (2, {})} | custom-call | flops 1024 | bytes 1024 | tf_op jit(solution)/shard_map/pallas_call | solution.py:298
  (17 shorter events, 0.0 us)
Async XLA Ops:
  0.0 9.9 %copy-start = (bf16[2,2,4,128,256]{4,3,2,1,0:T(8,128)(2,1)S(1)}, bf16[2,2,4,128,256]{4,3,2,1,0:T(8,128)(2,1)}, u32[]{:S(2)}) copy-start(bf16[2,2,4,128,256]{4,3,2,1,0:T(8,128)(2,1)} %refs_5_.3) | copy-start | bytes 3145732
  0.0 10.0 %copy-start.2 = (bf16[4,3,128,128]{3,2,1,0:T(8,128)(2,1)S(1)}, bf16[4,3,128,128]{3,2,1,0:T(8,128)(2,1)}, u32[]{:S(2)}) copy-start(bf16[4,3,128,128]{3,2,1,0:T(8,128)(2,1)} %refs_3_.1) | copy-start | bytes 1179652
  4.8 3.2 %collective-permute-start = (bf16[2,2,128,256]{3,2,1,0:T(8,128)(2,1)}, bf16[2,2,128,256]{3,2,1,0:T(8,128)(2,1)S(1)}, u32[]{:S(2)}, u32[]{:S(2)}) collective-permute-start(bf16[2,2,128,256]{3,2,1,0:T(8,128)(2,1)} %get-tuple-element.31), channel_id=1, source_target_pairs={{0,1},{1,0},{2,3},{3,2},{4,5},{5,4},{6,7},{7,6},{8,9},{9,8},{10,11... | collective-permute-start | bytes 786440 | tf_op jit(solution)/shard_map/ppermute | solution.py:328
  4.9 8.9 %collective-permute-start.1 = (bf16[2,2,2,128,128]{4,3,2,1,0:T(8,128)(2,1)}, bf16[2,2,2,128,128]{4,3,2,1,0:T(8,128)(2,1)S(1)}, u32[]{:S(2)}, u32[]{:S(2)}) collective-permute-start(bf16[2,2,2,128,128]{4,3,2,1,0:T(8,128)(2,1)} %get-tuple-element.35), channel_id=1, source_target_pairs={{0,16},{8,24},{16,0},{24,8},{1,17},{9,25},{17,1},{25,9},{2,18},{10... | collective-permute-start | bytes 786440 | tf_op jit(solution)/shard_map/ppermute | solution.py:325
  6.5 9.0 %collective-permute-start.6 = (bf16[4,2,128,128]{3,2,1,0:T(8,128)(2,1)}, bf16[4,2,128,128]{3,2,1,0:T(8,128)(2,1)S(1)}, u32[]{:S(2)}, u32[]{:S(2)}) collective-permute-start(bf16[4,2,128,128]{3,2,1,0:T(8,128)(2,1)} %get-tuple-element.49), channel_id=1, source_target_pairs={{0,8},{8,0},{16,24},{24,16},{1,9},{9,1},{17,25},{25,17},{2,10},{10... | collective-permute-start | bytes 786440 | tf_op jit(solution)/shard_map/ppermute | solution.py:322
  8.0 8.3 %collective-permute-start.2 = (bf16[2,2,128,256]{3,2,1,0:T(8,128)(2,1)}, bf16[2,2,128,256]{3,2,1,0:T(8,128)(2,1)S(1)}, u32[]{:S(2)}, u32[]{:S(2)}) collective-permute-start(bf16[2,2,128,256]{3,2,1,0:T(8,128)(2,1)} %get-tuple-element.41), channel_id=1, source_target_pairs={{1,2},{2,1},{3,4},{4,3},{5,6},{6,5},{9,10},{10,9},{11,12},{12,11},... | collective-permute-start | bytes 786440 | tf_op jit(solution)/shard_map/ppermute | solution.py:328
  9.9 0.7 %copy-start.3 = (s32[4,3]{1,0:T(4,128)S(1)}, s32[4,3]{1,0:T(4,128)}, u32[]{:S(2)}) copy-start(s32[4,3]{1,0:T(4,128)} %refs_2_.7) | copy-start | bytes 148
  9.9 0.7 %copy-start.4 = (f32[4]{0:T(128)S(1)}, f32[4]{0:T(128)}, u32[]{:S(2)}) copy-start(f32[4]{0:T(128)} %refs_0_.7) | copy-start | bytes 52
  9.9 0.7 %copy-start.5 = (s32[4]{0:T(128)S(1)}, s32[4]{0:T(128)}, u32[]{:S(2)}) copy-start(s32[4]{0:T(128)} %refs_1_.7) | copy-start | bytes 52
  10.6 3.2 %copy-start.6 = (f32[2,2,2,128,128]{4,3,2,1,0:T(8,128)S(1)}, f32[2,2,2,128,128]{4,3,2,1,0:T(8,128)}, u32[]{:S(2)}) copy-start(f32[2,2,2,128,128]{4,3,2,1,0:T(8,128)} %get-tuple-element.34) | copy-start | bytes 1572868
  13.2 8.7 %collective-permute-start.4 = (bf16[2,2,2,128,128]{4,3,2,1,0:T(8,128)(2,1)S(1)}, bf16[2,2,2,128,128]{4,3,2,1,0:T(8,128)(2,1)S(1)}, u32[]{:S(2)}, u32[]{:S(2)}) collective-permute-start(bf16[2,2,2,128,128]{4,3,2,1,0:T(8,128)(2,1)S(1)} %get-tuple-element.36), channel_id=1, source_target_pairs={{0,16},{8,24},{16,0},{24,8},{1,17},{9,25},{17,1},{25,9},{2,18},{10... | collective-permute-start | bytes 786440 | tf_op jit(solution)/shard_map/ppermute | solution.py:325
  13.9 9.5 %collective-permute-start.5 = (bf16[2,2,2,128,128]{4,3,2,1,0:T(8,128)(2,1)S(1)}, bf16[2,2,2,128,128]{4,3,2,1,0:T(8,128)(2,1)S(1)}, u32[]{:S(2)}, u32[]{:S(2)}) collective-permute-start(bf16[2,2,2,128,128]{4,3,2,1,0:T(8,128)(2,1)S(1)} %add_convert_fusion.2), channel_id=1, source_target_pairs={{0,8},{8,0},{16,24},{24,16},{1,9},{9,1},{17,25},{25,17},{2,10},{10... | collective-permute-start | bytes 786440 | tf_op jit(solution)/shard_map/ppermute | solution.py:322
  15.5 10.0 %collective-permute-start.7 = (bf16[4,2,128,128]{3,2,1,0:T(8,128)(2,1)S(1)}, bf16[4,2,128,128]{3,2,1,0:T(8,128)(2,1)S(1)}, u32[]{:S(2)}, u32[]{:S(2)}) collective-permute-start(bf16[4,2,128,128]{3,2,1,0:T(8,128)(2,1)S(1)} %collective-permute-done.6.refs_5_), channel_id=1, source_target_pairs={{0,1},{1,0},{2,3},{3,2},{4,5},{5,4},{6,7},{7,6},{8,9},{9,8},{10,11... | collective-permute-start | bytes 786440 | tf_op jit(solution)/shard_map/ppermute | solution.py:328
  18.9 10.5 %collective-permute-start.3 = (bf16[2,2,2,128,128]{4,3,2,1,0:T(8,128)(2,1)S(1)}, bf16[2,2,2,128,128]{4,3,2,1,0:T(8,128)(2,1)S(1)}, u32[]{:S(2)}, u32[]{:S(2)}) collective-permute-start(bf16[2,2,2,128,128]{4,3,2,1,0:T(8,128)(2,1)S(1)} %get-tuple-element.44), channel_id=1, source_target_pairs={{0,16},{8,24},{16,0},{24,8},{1,17},{9,25},{17,1},{25,9},{2,18},{10... | collective-permute-start | bytes 786440 | tf_op jit(solution)/shard_map/ppermute | solution.py:325
  19.9 5.6 %collective-permute-start.8 = (bf16[2,128,128]{2,1,0:T(8,128)(2,1)S(1)}, bf16[2,128,128]{2,1,0:T(8,128)(2,1)S(1)}, u32[]{:S(2)}, u32[]{:S(2)}) collective-permute-start(bf16[2,128,128]{2,1,0:T(8,128)(2,1)S(1)} %fusion), channel_id=1, source_target_pairs={{1,2},{2,1},{3,4},{4,3},{5,6},{6,5},{9,10},{10,9},{11,12},{12,11},... | collective-permute-start | bytes 196616 | tf_op jit(solution)/shard_map/ppermute | solution.py:328
  22.0 14.8 %collective-permute-start.10 = (bf16[2,2,2,128,128]{4,3,2,1,0:T(8,128)(2,1)S(1)}, bf16[2,2,2,128,128]{4,3,2,1,0:T(8,128)(2,1)S(1)}, u32[]{:S(2)}, u32[]{:S(2)}) collective-permute-start(bf16[2,2,2,128,128]{4,3,2,1,0:T(8,128)(2,1)S(1)} %add_convert_fusion.1), channel_id=1, source_target_pairs={{0,8},{8,0},{16,24},{24,16},{1,9},{9,1},{17,25},{25,17},{2,10},{10... | collective-permute-start | bytes 786440 | tf_op jit(solution)/shard_map/ppermute | solution.py:322
  28.2 8.6 %collective-permute-start.11 = (bf16[2,2,2,128,128]{4,3,2,1,0:T(8,128)(2,1)S(1)}, bf16[2,2,2,128,128]{4,3,2,1,0:T(8,128)(2,1)S(1)}, u32[]{:S(2)}, u32[]{:S(2)}) collective-permute-start(bf16[2,2,2,128,128]{4,3,2,1,0:T(8,128)(2,1)S(1)} %get-tuple-element.56), channel_id=1, source_target_pairs={{0,16},{8,24},{16,0},{24,8},{1,17},{9,25},{17,1},{25,9},{2,18},{10... | collective-permute-start | bytes 786440 | tf_op jit(solution)/shard_map/ppermute | solution.py:325
  29.4 7.4 %copy-start.1 = (f32[2,2,2,128,128]{4,3,2,1,0:T(8,128)S(1)}, f32[2,2,2,128,128]{4,3,2,1,0:T(8,128)}, u32[]{:S(2)}) copy-start(f32[2,2,2,128,128]{4,3,2,1,0:T(8,128)} %get-tuple-element.52.mine_1) | copy-start | bytes 1572868
  29.4 8.4 %collective-permute-start.9 = (bf16[2,2,2,128,128]{4,3,2,1,0:T(8,128)(2,1)S(1)}, bf16[2,2,2,128,128]{4,3,2,1,0:T(8,128)(2,1)S(1)}, u32[]{:S(2)}, u32[]{:S(2)}) collective-permute-start(bf16[2,2,2,128,128]{4,3,2,1,0:T(8,128)(2,1)S(1)} %add_convert_fusion), channel_id=1, source_target_pairs={{0,8},{8,0},{16,24},{24,16},{1,9},{9,1},{17,25},{25,17},{2,10},{10... | collective-permute-start | bytes 786440 | tf_op jit(solution)/shard_map/ppermute | solution.py:322

commit v7 on v6

--- a/solution.py
+++ b/solution.py
@@ -14,7 +14,8 @@
 FIRST = (("full", 1, 1), ("full", 1, 2))
 SECOND = (("full", 1, NEAR), ("half", 0, 1, (1, 2)))
 THIRD = (("full", 1, FAR), ("half", 0, 1, (NEAR, FAR)))
-RAW = (("half", 0, 0, (1, 2)), ("half", 0, 0, (NEAR, FAR)))
+RAW_INNER = (("half", 0, 0, (1, 2)),)
+RAW_OUTER = (("half", 0, 0, (NEAR, FAR)),)
 
 
 def stack_coupling(c_ref, rows, cols):
@@ -93,8 +94,8 @@
         mine[...] = acc[pl.ds(count, count)]
 
 
-def pieces(size, count):
-    return (2, count, 2, size, size)
+def pieces(groups, size, count):
+    return (len(groups), count, 2, size, size)
 
 
 def scratch(modes, slots, size, count):
@@ -108,6 +109,7 @@
 SMEM = pl.BlockSpec(memory_space=pltpu.SMEM)
 HBM = pl.BlockSpec(memory_space=pltpu.HBM)
 LONG = pl.CostEstimate(flops=5 << 30, bytes_accessed=16 << 20, transcendentals=0)
+MID = pl.CostEstimate(flops=5 << 29, bytes_accessed=4 << 20, transcendentals=0)
 SMALL = pl.CostEstimate(flops=1024, bytes_accessed=1024, transcendentals=0)
 
 
@@ -151,7 +153,7 @@
 def first_call(greens, coupling, occupation, offsets, neighbours):
     modes, slots, size = coupling.shape[:3]
     parts, count, owned = greens.shape[:3]
-    shape = pieces(size, count)
+    shape = pieces(FIRST, size, count)
     rows, cols = (slots, modes * size, size), (modes, size, slots * size)
     edge = (parts, count, size, 2 * size)
     outs = [
@@ -182,12 +184,14 @@
     )(occupation, offsets, neighbours, coupling, greens)
 
 
-def next_body(groups, flip, wanted, with_parts, n_stacked, n_edges, *refs):
+def next_body(groups, flip, wanted, with_parts, n_stacked, n_edges, n_done, *refs):
     occ, off, nbr = refs[:3]
     at = 3 + n_stacked
     own = refs[at]
     edge_refs = dict(zip((NEAR, FAR), refs[at + 1 : at + 1 + n_edges]))
-    outs = list(refs[at + 1 + n_edges : -2])
+    at += 1 + n_edges
+    done = refs[at : at + n_done]
+    outs = list(refs[at + n_done : -2])
     half, acc = refs[-2:]
     if n_stacked == 1:
         rows, cols = outs[-2:]
@@ -208,38 +212,48 @@
     results = [outs.pop(0) if want else None for want in wanted]
     for i, group in enumerate(groups):
         views = [None if ref is None else ref.at[i] for ref in results]
+        if done:
+            views[0] = results[0].at[i + 1]
         group_terms(group, flip, (occ, off, nbr), rows, cols, read, edges, views, half, acc)
-
-
-def next_call(groups, flip, wanted, scalars, stacked, own, edges, estimate=None):
+    if done:
+        results[0][0] = done[0][0]
+
+
+def next_call(groups, flip, wanted, scalars, stacked, own, edges, estimate=None, done=()):
     modes, slots, size = stacked[0].shape[:3] if len(stacked) == 1 else (stacked[1].shape[0],) + stacked[0].shape[::2]
     count = own.shape[1]
-    shape = pieces(size, count)
-    outs = [jax.ShapeDtypeStruct(shape, kind) for want, kind in zip(wanted, (BF16, F32, F32)) if want]
+    shape = pieces(groups, size, count)
+    far = (shape[0] + len(done),) + shape[1:]
+    outs = [
+        jax.ShapeDtypeStruct(*out)
+        for want, out in zip(wanted, ((far, BF16), (shape, F32), (shape, F32)))
+        if want
+    ]
     if len(stacked) == 1:
         outs.append(jax.ShapeDtypeStruct((slots, modes * size, size), BF16))
         outs.append(jax.ShapeDtypeStruct((modes, size, slots * size), BF16))
     return pl.pallas_call(
-        functools.partial(next_body, groups, flip, wanted, own.ndim == 5, len(stacked), len(edges)),
+        functools.partial(next_body, groups, flip, wanted, own.ndim == 5, len(stacked), len(edges), len(done)),
         out_shape=outs,
-        in_specs=[SMEM] * 3 + [VMEM] * (1 + len(stacked) + len(edges)),
+        in_specs=[SMEM] * 3 + [VMEM] * (1 + len(stacked) + len(edges) + len(done)),
         out_specs=[VMEM] * len(outs),
         scratch_shapes=scratch(modes, slots, size, count),
         compiler_params=pltpu.CompilerParams(vmem_limit_bytes=16 << 20),
         cost_estimate=estimate or SMALL,
-    )(*scalars, *stacked, own, *edges)
-
-
-def early_body(mine_1, got_1, mine_2, got_2, mine_z, near_z, got_z, out, whole, edge, half, raw, sems):
+    )(*scalars, *stacked, own, *edges, *done)
+
+
+def start_all(pairs, sems):
+    copies = [pltpu.make_async_copy(src, dst, sems.at[i]) for i, (src, dst) in enumerate(pairs)]
+    for copy in copies:
+        copy.start()
+    return copies
+
+
+def early_body(mine_1, got_1, mine_2, got_2, out, whole, edge, half, sems):
     owned, size = out.shape[2], out.shape[3]
-    n, f = place(NEAR, owned), place(FAR, owned)
-    im, re = pl.ds(size, size), pl.ds(0, size)
-    copies = []
-
-    def send(src, dst):
-        copy = pltpu.make_async_copy(src, dst, sems.at[len(copies)])
-        copy.start()
-        copies.append(copy)
+    n = place(NEAR, owned)
+    im = pl.ds(size, size)
 
     def tile(mine, got, g, u):
         return (mine[g, :, u] + got[g, :, u].astype(F32)).astype(BF16)
@@ -249,35 +263,40 @@
             whole[:, g, :, u * size : (u + 1) * size] = tile(mine_1, got_1, g, u)
         edge[:, :, u * size : (u + 1) * size] = tile(mine_2, got_2, 0, u)
         half[:, u] = tile(mine_2, got_2, 1, u)
-    send(whole, out.at[1, :, pl.ds(1, 2)])
-    send(edge, out.at[1, :, n])
-    send(half, out.at[0, :, pl.ds(1, 2), :, im])
+    pairs = [
+        (whole, out.at[1, :, pl.ds(1, 2)]),
+        (edge, out.at[1, :, n]),
+        (half, out.at[0, :, pl.ds(1, 2), :, im]),
+    ]
+    for copy in start_all(pairs, sems):
+        copy.wait()
+
+
+def late_body(mine_z, *refs):
+    near, (got_z, mine, got, _, out, edge, half, raw, sems) = refs[:-9], refs[-9:]
+    owned, size = out.shape[2], out.shape[3]
+    n, f = place(NEAR, owned), place(FAR, owned)
+    re, im = pl.ds(0, size), pl.ds(size, size)
     for g in range(2):
         for u in range(2):
-            total = mine_z[g, :, u] + near_z[g, :, u] + got_z[g, :, u].astype(F32)
+            part = near[g][0, :, u] if len(near) == 2 else near[0][g, :, u]
+            total = mine_z[g, :, u] + part + got_z[g, :, u].astype(F32)
             raw[:, 2 * g + u] = total.astype(BF16)
-    send(raw.at[:, pl.ds(0, 2)], out.at[0, :, pl.ds(1, 2), :, re])
-    send(raw.at[:, 2], out.at[0, :, n, :, re])
-    send(raw.at[:, 3], out.at[0, :, f, :, re])
-    for copy in copies:
-        copy.wait()
-
-
-def late_body(mine, got, _, out, edge, half, sems):
-    owned, size = out.shape[2], out.shape[3]
-    n, f = place(NEAR, owned), place(FAR, owned)
-    im = pl.ds(size, size)
+    pairs = [
+        (raw.at[:, pl.ds(0, 2)], out.at[0, :, pl.ds(1, 2), :, re]),
+        (raw.at[:, 2], out.at[0, :, n, :, re]),
+        (raw.at[:, 3], out.at[0, :, f, :, re]),
+    ]
+    copies = start_all(pairs, sems.at[0])
     for u in range(2):
         edge[:, :, u * size : (u + 1) * size] = (mine[0, :, u] + got[0, :, u].astype(F32)).astype(BF16)
         half[:, u] = (mine[1, :, u] + got[1, :, u].astype(F32)).astype(BF16)
-    copies = [
-        pltpu.make_async_copy(edge, out.at[1, :, f], sems.at[0]),
-        pltpu.make_async_copy(half.at[:, 0], out.at[0, :, n, :, im], sems.at[1]),
-        pltpu.make_async_copy(half.at[:, 1], out.at[0, :, f, :, im], sems.at[2]),
-    ]
-    for copy in copies:
-        copy.start()
-    for copy in copies:
+    pairs = [
+        (edge, out.at[1, :, f]),
+        (half.at[:, 0], out.at[0, :, n, :, im]),
+        (half.at[:, 1], out.at[0, :, f, :, im]),
+    ]
+    for copy in copies + start_all(pairs, sems.at[1]):
         copy.wait()
 
 
@@ -291,7 +310,7 @@
         out_specs=HBM,
         scratch_shapes=[pltpu.VMEM((count, 2, size, 2 * size), BF16)]
         + stage
-        + [pltpu.VMEM((count, 4, size, size), BF16), pltpu.SemaphoreType.DMA((6,))],
+        + [pltpu.SemaphoreType.DMA((3,))],
         compiler_params=pltpu.CompilerParams(vmem_limit_bytes=16 << 20),
         cost_estimate=SMALL,
     )(*early)
@@ -300,7 +319,8 @@
         out_shape=jax.ShapeDtypeStruct(greens.shape, BF16),
         in_specs=[VMEM] * len(late) + [HBM],
         out_specs=HBM,
-        scratch_shapes=stage + [pltpu.SemaphoreType.DMA((3,))],
+        scratch_shapes=stage
+        + [pltpu.VMEM((count, 4, size, size), BF16), pltpu.SemaphoreType.DMA((2, 3))],
         input_output_aliases={len(late): 0},
         compiler_params=pltpu.CompilerParams(vmem_limit_bytes=16 << 20),
         cost_estimate=SMALL,
@@ -330,37 +350,32 @@
     def total(near, relayed):
         return (near + relayed.astype(F32)).astype(BF16)
 
-    far_1, near_1, mine_1, raw, edge_n, edge_f = first_call(
-        greens, coupling, occupation, offsets, neighbours
-    )
+    far_1, near_1, mine_1, raw, edge_n, edge_f = first_call(greens, coupling, occupation, offsets, neighbours)
     relay_1 = along(far_1)
     beside_n = beside(edge_n, chip)
     raw_x = across(raw)
     beside_f = beside(after_these(edge_f, beside_n), chips)
-    far_2, near_2, mine_2, rows, cols = next_call(
-        SECOND, 0, (1, 1, 1), scalars, (coupling,), greens, (beside_n,), SMALL
-    )
+    far_2, near_2, mine_2, rows, cols = next_call(SECOND, 0, (1, 1, 1), scalars, (coupling,), greens, (beside_n,), SMALL)
     relay_2 = along(far_2)
     both_1 = total(near_1, after_these(relay_1, far_2))
     got_1 = across(both_1)
-    stacked = after_these((rows, cols), both_1)
-    far_3, near_3, mine_3 = next_call(
-        THIRD, 0, (1, 1, 1), scalars, stacked, greens, (beside_n, beside_f), SMALL
-    )
+    stacked = (rows, cols)
+    beside_xn = beside(raw_x, chip)
+    stacked_3 = after_these(stacked, both_1)
+    far_3, near_3, mine_3 = next_call(THIRD, 0, (1, 1, 1), scalars, stacked_3, greens, (beside_n, beside_f), MID)
     relay_3 = along(far_3)
     raw_f = jnp.where(odd, raw_x[-1], raw_x[0])
-    beside_xn = beside(raw_x, chip)
     beside_xf = beside(raw_f, chips)
     both_2 = total(near_2, after_these(relay_2, near_3))
     got_2 = across(both_2)
-    stacked = after_these(stacked, both_2, got_1)
-    far_z, near_z = next_call(RAW, 1, (1, 1, 0), scalars, stacked, raw_x, (beside_xn, beside_xf), SMALL)
-    got_z = along(far_z)
-    both_3 = total(near_3, after_these(relay_3, near_z))
+    far_a, near_a = next_call(RAW_INNER, 1, (1, 1, 0), scalars, after_these(stacked, both_2), raw_x, (), SMALL)
+    far_b, near_b = next_call(RAW_OUTER, 1, (1, 1, 0), scalars, after_these(stacked, both_2), raw_x, (beside_xn, beside_xf), SMALL, (far_a,))
+    got_z = along(far_b)
+    nears = (near_a, near_b)
+    both_3 = total(near_3, after_these(relay_3, near_b))
     got_3 = across(both_3)
-    stacked = after_these(stacked, both_3)
-    (mine_z,) = next_call(RAW, 0, (0, 0, 1), scalars, stacked, greens, (beside_n, beside_f), SMALL)
-    return add_up((mine_1, got_1, mine_2, got_2, mine_z, near_z, got_z), (mine_3, got_3), greens)
+    (mine_z,) = next_call(RAW_INNER + RAW_OUTER, 0, (0, 0, 1), scalars, stacked, greens, (beside_n, beside_f), SMALL)
+    return add_up((mine_1, got_1, mine_2, got_2), (mine_z,) + nears + (got_z, mine_3, got_3), greens)
 
 
 def solution(mesh):

time: 38.8 us -> 38.7 us (level)
  the two profiles are of different devices: /device:TPU:8 before, /device:TPU:0 now
where the time goes in v7:
time: 38.7 us; the launch traced here: 38.5 us
  Pallas kernels  18.2 us (47%)
  starting transfers between devices  13.1 us (34%)
  waiting for transfers between devices  6.16 us (16%)
  local copies, waits for them, and re-layouts  0.66 us (2%)
    pallas_call x5, Pallas kernels, next_call(): pl.pallas_call(functools.partial(next_body, groups, flip, wanted, own.ndi...  11.6 us
    ppermute x4, starting transfers between devices, across(): return lax.ppermute(array, 'energy', [(i, i ^ 1) for i in range(4)])  5.72 us
    pallas_call x1, Pallas kernels, first_call(): pl.pallas_call(first_body, out_shape=[jax.ShapeDtypeStruct(*out) for out...  4.81 us
    ppermute x4, starting transfers between devices, along(): return lax.ppermute(array, 'energy', [(i, i ^ 2) for i in range(4)])  4.77 us
    ppermute x4, waiting for transfers between devices, across(): return lax.ppermute(array, 'energy', [(i, i ^ 1) for i in range(4)])  3.13 us
    ppermute x4, waiting for transfers between devices, along(): return lax.ppermute(array, 'energy', [(i, i ^ 2) for i in range(4)])  3.02 us
    ppermute x4, starting transfers between devices, beside(): return lax.ppermute(array, 'slab', pairs)  2.6 us
    pallas_call x1, Pallas kernels, add_up(): pl.pallas_call(late_body, out_shape=jax.ShapeDtypeStruct(greens.shape, BF...  0.91 us
  transfers between devices with their start and end apart: 12, of which 4 were waited for; matrix products, arithmetic and copies ran while one was open for 0% of the time, Pallas kernels for 32%

profile of v7, /device:TPU:0, one launch (start us, length us, event | category | flops | bytes accessed | tf_op | source)
XLA Modules:
  0.0 38.5 jit_solution(9218765894603430315)
XLA Ops:
  0.0 4.8 %shard_map.55 = (bf16[2,2,2,128,128]{4,3,2,1,0:T(8,128)(2,1)}, f32[2,2,2,128,128]{4,3,2,1,0:T(8,128)}, f32[2,2,2,128,128]{4,3,2,1,0:T(8,128)}, bf16[4,2,128,128]...) custom-call(f32[4]{0:T(128)} %refs_0_.9, s32[4]{0:T(128)} %refs_1_.9, ...), custom_call_target="tpu_custom_call" | custom-call | flops 5368709120 | bytes 16777216 | tf_op jit(solution)/shard_map/pallas_call | solution.py:167
  4.8 0.5 %collective-permute-start = (bf16[2,2,128,256]{3,2,1,0:T(8,128)(2,1)}, bf16[2,2,128,256]{3,2,1,0:T(8,128)(2,1)S(1)}, u32[]{:S(2)}, u32[]{:S(2)}) collective-permute-start(bf16[2,2,128,256]{3,2,1,0:T(8,128)(2,1)} %get-tuple-element.31), channel_id=1, source_target_pairs={{0,1},{1,0},{2,3},{3,2},{4,5},{5,4},{6,7},{7,6},{8,9},{9,8},{10,11... | collective-permute-start | bytes 786440 | tf_op jit(solution)/shard_map/ppermute | solution.py:348
  5.3 2.6 %collective-permute-start.3 = (bf16[2,2,2,128,128]{4,3,2,1,0:T(8,128)(2,1)}, bf16[2,2,2,128,128]{4,3,2,1,0:T(8,128)(2,1)S(1)}, u32[]{:S(2)}, u32[]{:S(2)}) collective-permute-start(bf16[2,2,2,128,128]{4,3,2,1,0:T(8,128)(2,1)} %get-tuple-element.39), channel_id=1, source_target_pairs={{0,16},{8,24},{16,0},{24,8},{1,17},{9,25},{17,1},{25,9},{2,18},{10... | collective-permute-start | bytes 786440 | tf_op jit(solution)/shard_map/ppermute | solution.py:345
  7.9 1.5 %collective-permute-start.4 = (bf16[4,2,128,128]{3,2,1,0:T(8,128)(2,1)}, bf16[4,2,128,128]{3,2,1,0:T(8,128)(2,1)S(1)}, u32[]{:S(2)}, u32[]{:S(2)}) collective-permute-start(bf16[4,2,128,128]{3,2,1,0:T(8,128)(2,1)} %get-tuple-element.47), channel_id=1, source_target_pairs={{0,8},{8,0},{16,24},{24,16},{1,9},{9,1},{17,25},{25,17},{2,10},{10... | collective-permute-start | bytes 786440 | tf_op jit(solution)/shard_map/ppermute | solution.py:342
  9.4 0.7 %collective-permute-start.1 = (bf16[2,2,128,256]{3,2,1,0:T(8,128)(2,1)}, bf16[2,2,128,256]{3,2,1,0:T(8,128)(2,1)S(1)}, u32[]{:S(2)}, u32[]{:S(2)}) collective-permute-start(bf16[2,2,128,256]{3,2,1,0:T(8,128)(2,1)} %get-tuple-element.35), channel_id=1, source_target_pairs={{1,2},{2,1},{3,4},{4,3},{5,6},{6,5},{9,10},{10,9},{11,12},{12,11},... | collective-permute-start | bytes 786440 | tf_op jit(solution)/shard_map/ppermute | solution.py:348
  10.1 0.0 copy-start.3
  10.1 0.0 copy-start.4
  10.1 0.0 copy-start.5
  10.2 0.6 %copy-done.3 = s32[4,3]{1,0:T(4,128)S(1)} copy-done((s32[4,3]{1,0:T(4,128)S(1)}, s32[4,3]{1,0:T(4,128)}, u32[]{:S(2)}) %copy-start.3) | copy-done | bytes 72
  10.8 2.6 %shard_map.56 = (bf16[2,2,2,128,128]{4,3,2,1,0:T(8,128)(2,1)S(1)}, f32[2,2,2,128,128]{4,3,2,1,0:T(8,128)S(1)}, f32[2,2,2,128,128]{4,3,2,1,0:T(8,128)S(1)}, bf16[...) custom-call(f32[4]{0:T(128)S(1)} %copy-done.4, s32[4]{0:T(128)S(1)} %copy-done.5, s32[4,3]{1,0:T(4,128)S(1)} %copy-done.3, ...), custom_call_target="tpu_custom_call" | custom-call | flops 1024 | bytes 1024 | tf_op jit(solution)/shard_map/pallas_call | solution.py:235
  13.4 0.6 %collective-permute-start.2 = (bf16[2,2,2,128,128]{4,3,2,1,0:T(8,128)(2,1)S(1)}, bf16[2,2,2,128,128]{4,3,2,1,0:T(8,128)(2,1)S(1)}, u32[]{:S(2)}, u32[]{:S(2)}) collective-permute-start(bf16[2,2,2,128,128]{4,3,2,1,0:T(8,128)(2,1)S(1)} %get-tuple-element.37), channel_id=1, source_target_pairs={{0,16},{8,24},{16,0},{24,8},{1,17},{9,25},{17,1},{25,9},{2,18},{10... | collective-permute-start | bytes 786440 | tf_op jit(solution)/shard_map/ppermute | solution.py:345
  14.0 1.0 %collective-permute-done.3 = bf16[2,2,2,128,128]{4,3,2,1,0:T(8,128)(2,1)S(1)} collective-permute-done((bf16[2,2,2,128,128]{4,3,2,1,0:T(8,128)(2,1)}, bf16[2,2,2,128,128]{4,3,2,1,0:T(8,128)(2,1)S(1)}, u32[]{:S(2)}, u32[]{:S(2)}) %collective-permute-start.3) | collective-permute-done | bytes 262176 | tf_op jit(solution)/shard_map/ppermute | solution.py:345
  15.1 0.1 add_convert_fusion.2
  15.1 1.8 %collective-permute-start.10 = (bf16[2,2,2,128,128]{4,3,2,1,0:T(8,128)(2,1)S(1)}, bf16[2,2,2,128,128]{4,3,2,1,0:T(8,128)(2,1)S(1)}, u32[]{:S(2)}, u32[]{:S(2)}) collective-permute-start(bf16[2,2,2,128,128]{4,3,2,1,0:T(8,128)(2,1)S(1)} %add_convert_fusion.2), channel_id=1, source_target_pairs={{0,8},{8,0},{16,24},{24,16},{1,9},{9,1},{17,25},{25,17},{2,10},{10... | collective-permute-start | bytes 786440 | tf_op jit(solution)/shard_map/ppermute | solution.py:342
  16.9 0.8 %collective-permute-start.5 = (bf16[4,2,128,128]{3,2,1,0:T(8,128)(2,1)S(1)}, bf16[4,2,128,128]{3,2,1,0:T(8,128)(2,1)S(1)}, u32[]{:S(2)}, u32[]{:S(2)}) collective-permute-start(bf16[4,2,128,128]{3,2,1,0:T(8,128)(2,1)S(1)} %collective-permute-done.4.refs_5_), channel_id=1, source_target_pairs={{0,1},{1,0},{2,3},{3,2},{4,5},{5,4},{6,7},{7,6},{8,9},{9,8},{10,11... | collective-permute-start | bytes 786440 | tf_op jit(solution)/shard_map/ppermute | solution.py:348
  17.7 0.0 collective-permute-done.1.refs_7_
  17.7 2.7 %shard_map.58 = (bf16[2,2,2,128,128]{4,3,2,1,0:T(8,128)(2,1)S(1)}, f32[2,2,2,128,128]{4,3,2,1,0:T(8,128)S(1)}, f32[2,2,2,128,128]{4,3,2,1,0:T(8,128)S(1)}) custom-call(f32[4]{0:T(128)S(1)} %copy-done.4, s32[4]{0:T(128)S(1)} %copy-done.5, s32[4,3]{1,0:T(4,128)S(1)} %copy-done.3, bf16[3,512,128]{2,1,0:T(8,128)(2,1)S(1)} %get-tuple-element.45.refs_3_, ...), custom_call_target="tpu_custom_call" | custom-call | flops 2684354560 | bytes 4194304 | tf_op jit(solution)/shard_map/pallas_call | solution.py:235
  20.3 1.0 %collective-permute-start.8 = (bf16[2,2,2,128,128]{4,3,2,1,0:T(8,128)(2,1)S(1)}, bf16[2,2,2,128,128]{4,3,2,1,0:T(8,128)(2,1)S(1)}, u32[]{:S(2)}, u32[]{:S(2)}) collective-permute-start(bf16[2,2,2,128,128]{4,3,2,1,0:T(8,128)(2,1)S(1)} %get-tuple-element.53), channel_id=1, source_target_pairs={{0,16},{8,24},{16,0},{24,8},{1,17},{9,25},{17,1},{25,9},{2,18},{10... | collective-permute-start | bytes 786440 | tf_op jit(solution)/shard_map/ppermute | solution.py:345
  21.3 0.7 %collective-permute-start.6 = (bf16[2,128,128]{2,1,0:T(8,128)(2,1)S(1)}, bf16[2,128,128]{2,1,0:T(8,128)(2,1)S(1)}, u32[]{:S(2)}, u32[]{:S(2)}) collective-permute-start(bf16[2,128,128]{2,1,0:T(8,128)(2,1)S(1)} %fusion), channel_id=1, source_target_pairs={{1,2},{2,1},{3,4},{4,3},{5,6},{6,5},{9,10},{10,9},{11,12},{12,11},... | collective-permute-start | bytes 196616 | tf_op jit(solution)/shard_map/ppermute | solution.py:348
  22.0 0.1 add_convert_fusion.1
  22.1 1.5 %collective-permute-start.11 = (bf16[2,2,2,128,128]{4,3,2,1,0:T(8,128)(2,1)S(1)}, bf16[2,2,2,128,128]{4,3,2,1,0:T(8,128)(2,1)S(1)}, u32[]{:S(2)}, u32[]{:S(2)}) collective-permute-start(bf16[2,2,2,128,128]{4,3,2,1,0:T(8,128)(2,1)S(1)} %add_convert_fusion.1), channel_id=1, source_target_pairs={{0,8},{8,0},{16,24},{24,16},{1,9},{9,1},{17,25},{25,17},{2,10},{10... | collective-permute-start | bytes 786440 | tf_op jit(solution)/shard_map/ppermute | solution.py:342
  23.6 1.7 %shard_map.59 = (bf16[1,2,2,128,128]{4,3,2,1,0:T(8,128)(2,1)S(1)}, f32[1,2,2,128,128]{4,3,2,1,0:T(8,128)S(1)}) custom-call(f32[4]{0:T(128)S(1)} %copy-done.4, s32[4]{0:T(128)S(1)} %copy-done.5, s32[4,3]{1,0:T(4,128)S(1)} %copy-done.3, bf16[3,512,128]{2,1,0:T(8,128)(2,1)S(1)} %get-tuple-element.45.refs_3_, ...), custom_call_target="tpu_custom_call" | custom-call | flops 1024 | bytes 1024 | tf_op jit(solution)/shard_map/pallas_call | solution.py:235
  25.3 1.7 %shard_map.60 = (bf16[2,2,2,128,128]{4,3,2,1,0:T(8,128)(2,1)S(1)}, f32[1,2,2,128,128]{4,3,2,1,0:T(8,128)S(1)}) custom-call(f32[4]{0:T(128)S(1)} %copy-done.4, s32[4]{0:T(128)S(1)} %copy-done.5, s32[4,3]{1,0:T(4,128)S(1)} %copy-done.3, bf16[3,512,128]{2,1,0:T(8,128)(2,1)S(1)} %get-tuple-element.45.refs_3_, ...), custom_call_target="tpu_custom_call" | custom-call | flops 1024 | bytes 1024 | tf_op jit(solution)/shard_map/pallas_call | solution.py:235
  27.0 0.6 %collective-permute-start.7 = (bf16[2,2,2,128,128]{4,3,2,1,0:T(8,128)(2,1)S(1)}, bf16[2,2,2,128,128]{4,3,2,1,0:T(8,128)(2,1)S(1)}, u32[]{:S(2)}, u32[]{:S(2)}) collective-permute-start(bf16[2,2,2,128,128]{4,3,2,1,0:T(8,128)(2,1)S(1)} %get-tuple-element.51), channel_id=1, source_target_pairs={{0,16},{8,24},{16,0},{24,8},{1,17},{9,25},{17,1},{25,9},{2,18},{10... | collective-permute-start | bytes 786440 | tf_op jit(solution)/shard_map/ppermute | solution.py:345
  27.6 1.0 %collective-permute-done.8 = bf16[2,2,2,128,128]{4,3,2,1,0:T(8,128)(2,1)S(1)} collective-permute-done((bf16[2,2,2,128,128]{4,3,2,1,0:T(8,128)(2,1)S(1)}, bf16[2,2,2,128,128]{4,3,2,1,0:T(8,128)(2,1)S(1)}, u32[]{:S(2)}, u32[]{:S(2)}) %collective-permute-start.8) | collective-permute-done | bytes 262176 | tf_op jit(solution)/shard_map/ppermute | solution.py:345
  28.6 0.1 add_convert_fusion
  28.7 0.9 %collective-permute-start.9 = (bf16[2,2,2,128,128]{4,3,2,1,0:T(8,128)(2,1)S(1)}, bf16[2,2,2,128,128]{4,3,2,1,0:T(8,128)(2,1)S(1)}, u32[]{:S(2)}, u32[]{:S(2)}) collective-permute-start(bf16[2,2,2,128,128]{4,3,2,1,0:T(8,128)(2,1)S(1)} %add_convert_fusion), channel_id=1, source_target_pairs={{0,8},{8,0},{16,24},{24,16},{1,9},{9,1},{17,25},{25,17},{2,10},{10... | collective-permute-start | bytes 786440 | tf_op jit(solution)/shard_map/ppermute | solution.py:342
  29.6 3.0 %shard_map.57.mine_z = f32[2,2,2,128,128]{4,3,2,1,0:T(8,128)S(1)} custom-call(f32[4]{0:T(128)S(1)} %copy-done.4, s32[4]{0:T(128)S(1)} %copy-done.5, s32[4,3]{1,0:T(4,128)S(1)} %copy-done.3, bf16[3,512,128]{2,1,0:T(8,128)(2,1)S(1)} %get-tuple-element.45.refs_3_, bf16[4,128,384]{2,1,0:T(8,128)(2,1)S(1)} %get-tuple-element.46.refs_4_, ...), custom_call_target="tpu_custom_call" | custom-call | flops 1024 | bytes 1024 | tf_op jit(solution)/shard_map/pallas_call | solution.py:235
  32.6 0.9 %shard_map.61.refs_5_ = bf16[2,2,4,128,256]{4,3,2,1,0:T(8,128)(2,1)} custom-call(f32[2,2,2,128,128]{4,3,2,1,0:T(8,128)S(1)} %copy-done.1, bf16[2,2,2,128,128]{4,3,2,1,0:T(8,128)(2,1)S(1)} %collective-permute-done.10.got_1, f32[2,2,2,128,128]{4,3,2,1,0:T(8,128)S(1)} %get-tuple-element.56.mine_2, bf16[2,2,2,128,128]{4,3,2,1,0:T(8,128)(2,1)S(1)} %collective-permute-done.11.got_2), custom_call_target="tpu_custom_call" | custom-call | flops 1024 | bytes 1024 | tf_op jit(solution)/shard_map/pallas_call | solution.py:306
  33.5 1.0 %collective-permute-done.7.refs_2_ = bf16[2,2,2,128,128]{4,3,2,1,0:T(8,128)(2,1)S(1)} collective-permute-done((bf16[2,2,2,128,128]{4,3,2,1,0:T(8,128)(2,1)S(1)}, bf16[2,2,2,128,128]{4,3,2,1,0:T(8,128)(2,1)S(1)}, u32[]{:S(2)}, u32[]{:S(2)}) %collective-permute-start.7) | collective-permute-done | bytes 262176 | tf_op jit(solution)/shard_map/ppermute | solution.py:345
  34.5 3.1 %collective-permute-done.9.refs_4_ = bf16[2,2,2,128,128]{4,3,2,1,0:T(8,128)(2,1)S(1)} collective-permute-done((bf16[2,2,2,128,128]{4,3,2,1,0:T(8,128)(2,1)S(1)}, bf16[2,2,2,128,128]{4,3,2,1,0:T(8,128)(2,1)S(1)}, u32[]{:S(2)}, u32[]{:S(2)}) %collective-permute-start.9) | collective-permute-done | bytes 262176 | tf_op jit(solution)/shard_map/ppermute | solution.py:342
  37.6 0.9 %shard_map.62 = bf16[2,2,4,128,256]{4,3,2,1,0:T(8,128)(2,1)} custom-call(f32[2,2,2,128,128]{4,3,2,1,0:T(8,128)S(1)} %shard_map.57.mine_z, f32[1,2,2,128,128]{4,3,2,1,0:T(8,128)S(1)} %get-tuple-element.48.refs_0_, f32[1,2,2,128,128]{4,3,2,1,0:T(8,128)S(1)} %get-tuple-element.50.refs_1_, ...), custom_call_target="tpu_custom_call", output_to_operand_aliasing={{}: (6, {})} | custom-call | flops 1024 | bytes 1024 | tf_op jit(solution)/shard_map/pallas_call | solution.py:317
  (18 shorter events, 0.0 us)
Async XLA Ops:
  0.0 10.1 %copy-start.2 = (bf16[4,3,128,128]{3,2,1,0:T(8,128)(2,1)S(1)}, bf16[4,3,128,128]{3,2,1,0:T(8,128)(2,1)}, u32[]{:S(2)}) copy-start(bf16[4,3,128,128]{3,2,1,0:T(8,128)(2,1)} %refs_3_.1) | copy-start | bytes 1179652
  0.0 10.2 %copy-start = (bf16[2,2,4,128,256]{4,3,2,1,0:T(8,128)(2,1)S(1)}, bf16[2,2,4,128,256]{4,3,2,1,0:T(8,128)(2,1)}, u32[]{:S(2)}) copy-start(bf16[2,2,4,128,256]{4,3,2,1,0:T(8,128)(2,1)} %refs_5_.3) | copy-start | bytes 3145732
  4.8 4.6 %collective-permute-start = (bf16[2,2,128,256]{3,2,1,0:T(8,128)(2,1)}, bf16[2,2,128,256]{3,2,1,0:T(8,128)(2,1)S(1)}, u32[]{:S(2)}, u32[]{:S(2)}) collective-permute-start(bf16[2,2,128,256]{3,2,1,0:T(8,128)(2,1)} %get-tuple-element.31), channel_id=1, source_target_pairs={{0,1},{1,0},{2,3},{3,2},{4,5},{5,4},{6,7},{7,6},{8,9},{9,8},{10,11... | collective-permute-start | bytes 786440 | tf_op jit(solution)/shard_map/ppermute | solution.py:348
  5.3 9.7 %collective-permute-start.3 = (bf16[2,2,2,128,128]{4,3,2,1,0:T(8,128)(2,1)}, bf16[2,2,2,128,128]{4,3,2,1,0:T(8,128)(2,1)S(1)}, u32[]{:S(2)}, u32[]{:S(2)}) collective-permute-start(bf16[2,2,2,128,128]{4,3,2,1,0:T(8,128)(2,1)} %get-tuple-element.39), channel_id=1, source_target_pairs={{0,16},{8,24},{16,0},{24,8},{1,17},{9,25},{17,1},{25,9},{2,18},{10... | collective-permute-start | bytes 786440 | tf_op jit(solution)/shard_map/ppermute | solution.py:345
  7.9 9.0 %collective-permute-start.4 = (bf16[4,2,128,128]{3,2,1,0:T(8,128)(2,1)}, bf16[4,2,128,128]{3,2,1,0:T(8,128)(2,1)S(1)}, u32[]{:S(2)}, u32[]{:S(2)}) collective-permute-start(bf16[4,2,128,128]{3,2,1,0:T(8,128)(2,1)} %get-tuple-element.47), channel_id=1, source_target_pairs={{0,8},{8,0},{16,24},{24,16},{1,9},{9,1},{17,25},{25,17},{2,10},{10... | collective-permute-start | bytes 786440 | tf_op jit(solution)/shard_map/ppermute | solution.py:342
  9.4 8.2 %collective-permute-start.1 = (bf16[2,2,128,256]{3,2,1,0:T(8,128)(2,1)}, bf16[2,2,128,256]{3,2,1,0:T(8,128)(2,1)S(1)}, u32[]{:S(2)}, u32[]{:S(2)}) collective-permute-start(bf16[2,2,128,256]{3,2,1,0:T(8,128)(2,1)} %get-tuple-element.35), channel_id=1, source_target_pairs={{1,2},{2,1},{3,4},{4,3},{5,6},{6,5},{9,10},{10,9},{11,12},{12,11},... | collective-permute-start | bytes 786440 | tf_op jit(solution)/shard_map/ppermute | solution.py:348
  10.1 0.7 %copy-start.3 = (s32[4,3]{1,0:T(4,128)S(1)}, s32[4,3]{1,0:T(4,128)}, u32[]{:S(2)}) copy-start(s32[4,3]{1,0:T(4,128)} %refs_2_.9) | copy-start | bytes 148
  10.1 0.7 %copy-start.4 = (f32[4]{0:T(128)S(1)}, f32[4]{0:T(128)}, u32[]{:S(2)}) copy-start(f32[4]{0:T(128)} %refs_0_.9) | copy-start | bytes 52
  10.1 0.7 %copy-start.5 = (s32[4]{0:T(128)S(1)}, s32[4]{0:T(128)}, u32[]{:S(2)}) copy-start(s32[4]{0:T(128)} %refs_1_.9) | copy-start | bytes 52
  10.8 4.3 %copy-start.6 = (f32[2,2,2,128,128]{4,3,2,1,0:T(8,128)S(1)}, f32[2,2,2,128,128]{4,3,2,1,0:T(8,128)}, u32[]{:S(2)}) copy-start(f32[2,2,2,128,128]{4,3,2,1,0:T(8,128)} %get-tuple-element.38) | copy-start | bytes 1572868
  13.4 8.6 %collective-permute-start.2 = (bf16[2,2,2,128,128]{4,3,2,1,0:T(8,128)(2,1)S(1)}, bf16[2,2,2,128,128]{4,3,2,1,0:T(8,128)(2,1)S(1)}, u32[]{:S(2)}, u32[]{:S(2)}) collective-permute-start(bf16[2,2,2,128,128]{4,3,2,1,0:T(8,128)(2,1)S(1)} %get-tuple-element.37), channel_id=1, source_target_pairs={{0,16},{8,24},{16,0},{24,8},{1,17},{9,25},{17,1},{25,9},{2,18},{10... | collective-permute-start | bytes 786440 | tf_op jit(solution)/shard_map/ppermute | solution.py:345
  15.1 17.5 %collective-permute-start.10 = (bf16[2,2,2,128,128]{4,3,2,1,0:T(8,128)(2,1)S(1)}, bf16[2,2,2,128,128]{4,3,2,1,0:T(8,128)(2,1)S(1)}, u32[]{:S(2)}, u32[]{:S(2)}) collective-permute-start(bf16[2,2,2,128,128]{4,3,2,1,0:T(8,128)(2,1)S(1)} %add_convert_fusion.2), channel_id=1, source_target_pairs={{0,8},{8,0},{16,24},{24,16},{1,9},{9,1},{17,25},{25,17},{2,10},{10... | collective-permute-start | bytes 786440 | tf_op jit(solution)/shard_map/ppermute | solution.py:342
  16.9 8.4 %collective-permute-start.5 = (bf16[4,2,128,128]{3,2,1,0:T(8,128)(2,1)S(1)}, bf16[4,2,128,128]{3,2,1,0:T(8,128)(2,1)S(1)}, u32[]{:S(2)}, u32[]{:S(2)}) collective-permute-start(bf16[4,2,128,128]{3,2,1,0:T(8,128)(2,1)S(1)} %collective-permute-done.4.refs_5_), channel_id=1, source_target_pairs={{0,1},{1,0},{2,3},{3,2},{4,5},{5,4},{6,7},{7,6},{8,9},{9,8},{10,11... | collective-permute-start | bytes 786440 | tf_op jit(solution)/shard_map/ppermute | solution.py:348
  20.3 8.3 %collective-permute-start.8 = (bf16[2,2,2,128,128]{4,3,2,1,0:T(8,128)(2,1)S(1)}, bf16[2,2,2,128,128]{4,3,2,1,0:T(8,128)(2,1)S(1)}, u32[]{:S(2)}, u32[]{:S(2)}) collective-permute-start(bf16[2,2,2,128,128]{4,3,2,1,0:T(8,128)(2,1)S(1)} %get-tuple-element.53), channel_id=1, source_target_pairs={{0,16},{8,24},{16,0},{24,8},{1,17},{9,25},{17,1},{25,9},{2,18},{10... | collective-permute-start | bytes 786440 | tf_op jit(solution)/shard_map/ppermute | solution.py:345
  21.3 4.0 %collective-permute-start.6 = (bf16[2,128,128]{2,1,0:T(8,128)(2,1)S(1)}, bf16[2,128,128]{2,1,0:T(8,128)(2,1)S(1)}, u32[]{:S(2)}, u32[]{:S(2)}) collective-permute-start(bf16[2,128,128]{2,1,0:T(8,128)(2,1)S(1)} %fusion), channel_id=1, source_target_pairs={{1,2},{2,1},{3,4},{4,3},{5,6},{6,5},{9,10},{10,9},{11,12},{12,11},... | collective-permute-start | bytes 196616 | tf_op jit(solution)/shard_map/ppermute | solution.py:348
  22.1 10.5 %collective-permute-start.11 = (bf16[2,2,2,128,128]{4,3,2,1,0:T(8,128)(2,1)S(1)}, bf16[2,2,2,128,128]{4,3,2,1,0:T(8,128)(2,1)S(1)}, u32[]{:S(2)}, u32[]{:S(2)}) collective-permute-start(bf16[2,2,2,128,128]{4,3,2,1,0:T(8,128)(2,1)S(1)} %add_convert_fusion.1), channel_id=1, source_target_pairs={{0,8},{8,0},{16,24},{24,16},{1,9},{9,1},{17,25},{25,17},{2,10},{10... | collective-permute-start | bytes 786440 | tf_op jit(solution)/shard_map/ppermute | solution.py:342
  27.0 7.5 %collective-permute-start.7 = (bf16[2,2,2,128,128]{4,3,2,1,0:T(8,128)(2,1)S(1)}, bf16[2,2,2,128,128]{4,3,2,1,0:T(8,128)(2,1)S(1)}, u32[]{:S(2)}, u32[]{:S(2)}) collective-permute-start(bf16[2,2,2,128,128]{4,3,2,1,0:T(8,128)(2,1)S(1)} %get-tuple-element.51), channel_id=1, source_target_pairs={{0,16},{8,24},{16,0},{24,8},{1,17},{9,25},{17,1},{25,9},{2,18},{10... | collective-permute-start | bytes 786440 | tf_op jit(solution)/shard_map/ppermute | solution.py:345
  28.7 4.0 %copy-start.1 = (f32[2,2,2,128,128]{4,3,2,1,0:T(8,128)S(1)}, f32[2,2,2,128,128]{4,3,2,1,0:T(8,128)}, u32[]{:S(2)}) copy-start(f32[2,2,2,128,128]{4,3,2,1,0:T(8,128)} %get-tuple-element.55.mine_1) | copy-start | bytes 1572868
  28.7 8.9 %collective-permute-start.9 = (bf16[2,2,2,128,128]{4,3,2,1,0:T(8,128)(2,1)S(1)}, bf16[2,2,2,128,128]{4,3,2,1,0:T(8,128)(2,1)S(1)}, u32[]{:S(2)}, u32[]{:S(2)}) collective-permute-start(bf16[2,2,2,128,128]{4,3,2,1,0:T(8,128)(2,1)S(1)} %add_convert_fusion), channel_id=1, source_target_pairs={{0,8},{8,0},{16,24},{24,16},{1,9},{9,1},{17,25},{25,17},{2,10},{10... | collective-permute-start | bytes 786440 | tf_op jit(solution)/shard_map/ppermute | solution.py:342

commit v8 on v7

--- a/solution.py
+++ b/solution.py
@@ -118,7 +118,9 @@
     owned = g_h.shape[2]
     fetches = [
         pltpu.make_async_copy(src, dst, sems.at[i])
-        for i, (src, dst) in enumerate([(c_h, c_ref), (g_h, own), (occ_h, occ), (off_h, off), (nbr_h, nbr)])
+        for i, (src, dst) in enumerate(
+            [(c_h, c_ref), (g_h.at[1], own.at[1]), (occ_h, occ), (off_h, off), (nbr_h, nbr), (g_h.at[0], own.at[0])]
+        )
     ]
     for fetch in fetches:
         fetch.start()
@@ -131,12 +133,8 @@
 
     fetches[0].wait()
     stack_coupling(c_ref, rows, cols)
-    for fetch in fetches[1:]:
+    for fetch in fetches[1:5]:
         fetch.wait()
-    for e in range(own.shape[1]):
-        send(own.at[0, e, :, :, pl.ds(0, size)], raw_h.at[:, e])
-    send(own.at[:, :, place(NEAR, owned)], edge_n)
-    send(own.at[:, :, place(FAR, owned)], edge_f)
 
     def read(part, e, at, lanes):
         return own[part, e, at, :, lanes]
@@ -146,6 +144,12 @@
         send(far.at[i], far_h.at[i])
         send(near.at[i], near_h.at[i])
         send(mine.at[i], mine_h.at[i])
+        if i == 0:
+            fetches[5].wait()
+            for e in range(own.shape[1]):
+                send(own.at[0, e, :, :, pl.ds(0, size)], raw_h.at[:, e])
+            send(own.at[:, :, place(NEAR, owned)], edge_n)
+            send(own.at[:, :, place(FAR, owned)], edge_f)
     for copy in sends:
         copy.wait()
 
@@ -177,7 +181,7 @@
             pltpu.VMEM(greens.shape, BF16),
         ]
         + [pltpu.VMEM(*out) for out in outs[:3] + [(rows, BF16), (cols, BF16)]]
-        + [pltpu.SemaphoreType.DMA((5,)), pltpu.SemaphoreType.DMA((10,))]
+        + [pltpu.SemaphoreType.DMA((6,)), pltpu.SemaphoreType.DMA((10,))]
         + scratch(modes, slots, size, count),
         compiler_params=pltpu.CompilerParams(vmem_limit_bytes=58 << 20),
         cost_estimate=LONG,
@@ -250,10 +254,10 @@
     return copies
 
 
-def early_body(mine_1, got_1, mine_2, got_2, out, whole, edge, half, sems):
+def early_body(mine_1, got_1, mine_2, got_2, mine_z, near_a, near_b, got_z, out, whole, edge, half, raw, sems):
     owned, size = out.shape[2], out.shape[3]
-    n = place(NEAR, owned)
-    im = pl.ds(size, size)
+    n, f = place(NEAR, owned), place(FAR, owned)
+    re, im = pl.ds(0, size), pl.ds(size, size)
 
     def tile(mine, got, g, u):
         return (mine[g, :, u] + got[g, :, u].astype(F32)).astype(BF16)
@@ -268,26 +272,24 @@
         (edge, out.at[1, :, n]),
         (half, out.at[0, :, pl.ds(1, 2), :, im]),
     ]
-    for copy in start_all(pairs, sems):
-        copy.wait()
-
-
-def late_body(mine_z, *refs):
-    near, (got_z, mine, got, _, out, edge, half, raw, sems) = refs[:-9], refs[-9:]
-    owned, size = out.shape[2], out.shape[3]
-    n, f = place(NEAR, owned), place(FAR, owned)
-    re, im = pl.ds(0, size), pl.ds(size, size)
-    for g in range(2):
+    copies = start_all(pairs, sems.at[0])
+    for g, near in enumerate((near_a, near_b)):
         for u in range(2):
-            part = near[g][0, :, u] if len(near) == 2 else near[0][g, :, u]
-            total = mine_z[g, :, u] + part + got_z[g, :, u].astype(F32)
+            total = mine_z[g, :, u] + near[0, :, u] + got_z[g, :, u].astype(F32)
             raw[:, 2 * g + u] = total.astype(BF16)
     pairs = [
         (raw.at[:, pl.ds(0, 2)], out.at[0, :, pl.ds(1, 2), :, re]),
         (raw.at[:, 2], out.at[0, :, n, :, re]),
         (raw.at[:, 3], out.at[0, :, f, :, re]),
     ]
-    copies = start_all(pairs, sems.at[0])
+    for copy in copies + start_all(pairs, sems.at[1]):
+        copy.wait()
+
+
+def late_body(mine, got, _, out, edge, half, sems):
+    owned, size = out.shape[2], out.shape[3]
+    n, f = place(NEAR, owned), place(FAR, owned)
+    im = pl.ds(size, size)
     for u in range(2):
         edge[:, :, u * size : (u + 1) * size] = (mine[0, :, u] + got[0, :, u].astype(F32)).astype(BF16)
         half[:, u] = (mine[1, :, u] + got[1, :, u].astype(F32)).astype(BF16)
@@ -296,7 +298,7 @@
         (half.at[:, 0], out.at[0, :, n, :, im]),
         (half.at[:, 1], out.at[0, :, f, :, im]),
     ]
-    for copy in copies + start_all(pairs, sems.at[1]):
+    for copy in start_all(pairs, sems):
         copy.wait()
 
 
@@ -310,7 +312,7 @@
         out_specs=HBM,
         scratch_shapes=[pltpu.VMEM((count, 2, size, 2 * size), BF16)]
         + stage
-        + [pltpu.SemaphoreType.DMA((3,))],
+        + [pltpu.VMEM((count, 4, size, size), BF16), pltpu.SemaphoreType.DMA((2, 3))],
         compiler_params=pltpu.CompilerParams(vmem_limit_bytes=16 << 20),
         cost_estimate=SMALL,
     )(*early)
@@ -319,12 +321,26 @@
         out_shape=jax.ShapeDtypeStruct(greens.shape, BF16),
         in_specs=[VMEM] * len(late) + [HBM],
         out_specs=HBM,
-        scratch_shapes=stage
-        + [pltpu.VMEM((count, 4, size, size), BF16), pltpu.SemaphoreType.DMA((2, 3))],
+        scratch_shapes=stage + [pltpu.SemaphoreType.DMA((3,))],
         input_output_aliases={len(late): 0},
         compiler_params=pltpu.CompilerParams(vmem_limit_bytes=16 << 20),
         cost_estimate=SMALL,
     )(*late, out)
+
+
+def total_body(near, relayed, both):
+    both[...] = (near[...] + relayed[...].astype(F32)).astype(BF16)
+
+
+def total_call(near, relayed):
+    return pl.pallas_call(
+        total_body,
+        out_shape=jax.ShapeDtypeStruct(near.shape, BF16),
+        in_specs=[VMEM] * 2,
+        out_specs=VMEM,
+        compiler_params=pltpu.CompilerParams(vmem_limit_bytes=16 << 20),
+        cost_estimate=SMALL,
+    )(near, relayed)
 
 
 def after_these(array, *others):
@@ -336,7 +352,6 @@
     scalars = (occupation, offsets, neighbours)
     chip = [(i, i ^ 1) for i in range(slabs)]
     chips = [(i, i + 1 if i % 2 else i - 1) for i in range(1, slabs - 1)]
-    odd = lax.axis_index("slab") % 2 == 1
 
     def across(array):
         return lax.ppermute(array, "energy", [(i, i ^ 1) for i in range(4)])
@@ -357,25 +372,26 @@
     beside_f = beside(after_these(edge_f, beside_n), chips)
     far_2, near_2, mine_2, rows, cols = next_call(SECOND, 0, (1, 1, 1), scalars, (coupling,), greens, (beside_n,), SMALL)
     relay_2 = along(far_2)
-    both_1 = total(near_1, after_these(relay_1, far_2))
+    both_1 = total_call(near_1, after_these(relay_1, far_2))
     got_1 = across(both_1)
     stacked = (rows, cols)
     beside_xn = beside(raw_x, chip)
     stacked_3 = after_these(stacked, both_1)
     far_3, near_3, mine_3 = next_call(THIRD, 0, (1, 1, 1), scalars, stacked_3, greens, (beside_n, beside_f), MID)
     relay_3 = along(far_3)
-    raw_f = jnp.where(odd, raw_x[-1], raw_x[0])
-    beside_xf = beside(raw_f, chips)
-    both_2 = total(near_2, after_these(relay_2, near_3))
+    size = coupling.shape[-1]
+    raw_f = beside_f[0, :, :, :size]
+    beside_xf = across(raw_f)
+    both_2 = total_call(near_2, after_these(relay_2, near_3))
     got_2 = across(both_2)
     far_a, near_a = next_call(RAW_INNER, 1, (1, 1, 0), scalars, after_these(stacked, both_2), raw_x, (), SMALL)
-    far_b, near_b = next_call(RAW_OUTER, 1, (1, 1, 0), scalars, after_these(stacked, both_2), raw_x, (beside_xn, beside_xf), SMALL, (far_a,))
+    far_b, near_b = next_call(RAW_OUTER, 1, (1, 1, 0), scalars, after_these(stacked, both_2, got_1), raw_x, (beside_xn, beside_xf), SMALL, (far_a,))
     got_z = along(far_b)
     nears = (near_a, near_b)
-    both_3 = total(near_3, after_these(relay_3, near_b))
+    both_3 = total_call(near_3, after_these(relay_3, near_b))
     got_3 = across(both_3)
     (mine_z,) = next_call(RAW_INNER + RAW_OUTER, 0, (0, 0, 1), scalars, stacked, greens, (beside_n, beside_f), SMALL)
-    return add_up((mine_1, got_1, mine_2, got_2), (mine_z,) + nears + (got_z, mine_3, got_3), greens)
+    return add_up((mine_1, got_1, mine_2, got_2, mine_z) + nears + (got_z,), (mine_3, got_3), greens)
 
 
 def solution(mesh):

time: 38.7 us -> 37.8 us (0.977)
  starting transfers between devices: 13.1 us -> 14.2 us
  waiting for transfers between devices: 6.16 us -> 5.29 us
  local copies, waits for them, and re-layouts: 0.66 us -> 0.03 us
    ppermute x4 -> x5, waiting for transfers between devices: 3.13 us -> 1.79 us  [across(): return lax.ppermute(array, 'energy', [(i, i ^ 1) for i in range(4)])]
    ppermute x4, starting transfers between devices: 4.77 us -> 5.88 us  [along(): return lax.ppermute(array, 'energy', [(i, i ^ 2) for i in range(4)])]
    ppermute x4 -> x3, starting transfers between devices: 2.6 us -> 1.56 us  [beside(): return lax.ppermute(array, 'slab', pairs)]
    ppermute x4 -> x5, starting transfers between devices: 5.72 us -> 6.75 us  [across(): return lax.ppermute(array, 'energy', [(i, i ^ 1) for i in range(4)])]
    unnamed x14, local copies, waits for them, and re-layouts: 0.66 us -> 0.03 us
    ppermute x4, waiting for transfers between devices: 3.02 us -> 3.49 us  [along(): return lax.ppermute(array, 'energy', [(i, i ^ 2) for i in range(4)])]
    pallas_call x1, Pallas kernels: 4.81 us -> 4.41 us  [first_call(): pl.pallas_call(first_body, out_shape=[jax.ShapeDtypeStruct(*out) for out...]
  transfers between devices with their start and end apart: 12 -> 12, of which waited for: 4 -> 4; matrix products, arithmetic and copies ran while one was open for 0% -> 0% of each run, Pallas kernels for 32% -> 34%
where the time goes in v8:
time: 37.8 us; the launch traced here: 37.6 us
  Pallas kernels  18 us (48%)
  starting transfers between devices  14.2 us (38%)
  waiting for transfers between devices  5.29 us (14%)
    pallas_call x5, Pallas kernels, next_call(): pl.pallas_call(functools.partial(next_body, groups, flip, wanted, own.ndi...  11.7 us
    ppermute x5, starting transfers between devices, across(): return lax.ppermute(array, 'energy', [(i, i ^ 1) for i in range(4)])  6.75 us
    ppermute x4, starting transfers between devices, along(): return lax.ppermute(array, 'energy', [(i, i ^ 2) for i in range(4)])  5.88 us
    pallas_call x1, Pallas kernels, first_call(): pl.pallas_call(first_body, out_shape=[jax.ShapeDtypeStruct(*out) for out...  4.41 us
    ppermute x4, waiting for transfers between devices, along(): return lax.ppermute(array, 'energy', [(i, i ^ 2) for i in range(4)])  3.49 us
    ppermute x5, waiting for transfers between devices, across(): return lax.ppermute(array, 'energy', [(i, i ^ 1) for i in range(4)])  1.79 us
    ppermute x3, starting transfers between devices, beside(): return lax.ppermute(array, 'slab', pairs)  1.56 us
    pallas_call x1, Pallas kernels, add_up(): pl.pallas_call(early_body, out_shape=jax.ShapeDtypeStruct(greens.shape, B...  0.98 us
  transfers between devices with their start and end apart: 12, of which 4 were waited for; matrix products, arithmetic and copies ran while one was open for 0% of the time, Pallas kernels for 34%

profile of v8, /device:TPU:0, one launch (start us, length us, event | category | flops | bytes accessed | tf_op | source)
XLA Modules:
  0.0 37.6 jit_solution(9416057884331527108)
XLA Ops:
  0.0 4.4 %shard_map.55 = (bf16[2,2,2,128,128]{4,3,2,1,0:T(8,128)(2,1)}, f32[2,2,2,128,128]{4,3,2,1,0:T(8,128)}, f32[2,2,2,128,128]{4,3,2,1,0:T(8,128)}, bf16[4,2,128,128]...) custom-call(f32[4]{0:T(128)} %refs_0_.9, s32[4]{0:T(128)} %refs_1_.9, ...), custom_call_target="tpu_custom_call" | custom-call | flops 5368709120 | bytes 16777216 | tf_op jit(solution)/shard_map/pallas_call | solution.py:171
  4.4 0.5 %collective-permute-start = (bf16[2,2,128,256]{3,2,1,0:T(8,128)(2,1)}, bf16[2,2,128,256]{3,2,1,0:T(8,128)(2,1)S(1)}, u32[]{:S(2)}, u32[]{:S(2)}) collective-permute-start(bf16[2,2,128,256]{3,2,1,0:T(8,128)(2,1)} %get-tuple-element.33), channel_id=1, source_target_pairs={{0,1},{1,0},{2,3},{3,2},{4,5},{5,4},{6,7},{7,6},{8,9},{9,8},{10,11... | collective-permute-start | bytes 786440 | tf_op jit(solution)/shard_map/ppermute | solution.py:363
  4.9 2.6 %collective-permute-start.1 = (bf16[2,2,2,128,128]{4,3,2,1,0:T(8,128)(2,1)}, bf16[2,2,2,128,128]{4,3,2,1,0:T(8,128)(2,1)S(1)}, u32[]{:S(2)}, u32[]{:S(2)}) collective-permute-start(bf16[2,2,2,128,128]{4,3,2,1,0:T(8,128)(2,1)} %get-tuple-element.37), channel_id=1, source_target_pairs={{0,16},{8,24},{16,0},{24,8},{1,17},{9,25},{17,1},{25,9},{2,18},{10... | collective-permute-start | bytes 786440 | tf_op jit(solution)/shard_map/ppermute | solution.py:360
  7.5 1.5 %collective-permute-start.6 = (bf16[4,2,128,128]{3,2,1,0:T(8,128)(2,1)}, bf16[4,2,128,128]{3,2,1,0:T(8,128)(2,1)S(1)}, u32[]{:S(2)}, u32[]{:S(2)}) collective-permute-start(bf16[4,2,128,128]{3,2,1,0:T(8,128)(2,1)} %get-tuple-element.51), channel_id=1, source_target_pairs={{0,8},{8,0},{16,24},{24,16},{1,9},{9,1},{17,25},{25,17},{2,10},{10... | collective-permute-start | bytes 786440 | tf_op jit(solution)/shard_map/ppermute | solution.py:357
  9.0 0.0 collective-permute-done.refs_5_.refs_6_
  9.0 0.8 %collective-permute-start.2 = (bf16[2,2,128,256]{3,2,1,0:T(8,128)(2,1)}, bf16[2,2,128,256]{3,2,1,0:T(8,128)(2,1)S(1)}, u32[]{:S(2)}, u32[]{:S(2)}) collective-permute-start(bf16[2,2,128,256]{3,2,1,0:T(8,128)(2,1)} %get-tuple-element.43), channel_id=1, source_target_pairs={{1,2},{2,1},{3,4},{4,3},{5,6},{6,5},{9,10},{10,9},{11,12},{12,11},... | collective-permute-start | bytes 786440 | tf_op jit(solution)/shard_map/ppermute | solution.py:363
  9.9 2.6 %shard_map.56 = (bf16[2,2,2,128,128]{4,3,2,1,0:T(8,128)(2,1)S(1)}, f32[2,2,2,128,128]{4,3,2,1,0:T(8,128)S(1)}, f32[2,2,2,128,128]{4,3,2,1,0:T(8,128)S(1)}, bf16[...) custom-call(f32[4]{0:T(128)S(1)} %copy-done.5, s32[4]{0:T(128)S(1)} %copy-done.6, s32[4,3]{1,0:T(4,128)S(1)} %copy-done.4, ...), custom_call_target="tpu_custom_call" | custom-call | flops 1024 | bytes 1024 | tf_op jit(solution)/shard_map/pallas_call | solution.py:239
  12.5 0.6 %collective-permute-start.4 = (bf16[2,2,2,128,128]{4,3,2,1,0:T(8,128)(2,1)S(1)}, bf16[2,2,2,128,128]{4,3,2,1,0:T(8,128)(2,1)S(1)}, u32[]{:S(2)}, u32[]{:S(2)}) collective-permute-start(bf16[2,2,2,128,128]{4,3,2,1,0:T(8,128)(2,1)S(1)} %get-tuple-element.38), channel_id=1, source_target_pairs={{0,16},{8,24},{16,0},{24,8},{1,17},{9,25},{17,1},{25,9},{2,18},{10... | collective-permute-start | bytes 786440 | tf_op jit(solution)/shard_map/ppermute | solution.py:360
  13.1 1.5 %collective-permute-done.1.relayed = bf16[2,2,2,128,128]{4,3,2,1,0:T(8,128)(2,1)S(1)} collective-permute-done((bf16[2,2,2,128,128]{4,3,2,1,0:T(8,128)(2,1)}, bf16[2,2,2,128,128]{4,3,2,1,0:T(8,128)(2,1)S(1)}, u32[]{:S(2)}, u32[]{:S(2)}) %collective-permute-start.1) | collective-permute-done | bytes 262176 | tf_op jit(solution)/shard_map/ppermute | solution.py:360
  14.7 1.8 %collective-permute-start.5 = (bf16[2,2,2,128,128]{4,3,2,1,0:T(8,128)(2,1)S(1)}, bf16[2,2,2,128,128]{4,3,2,1,0:T(8,128)(2,1)S(1)}, u32[]{:S(2)}, u32[]{:S(2)}) collective-permute-start(bf16[2,2,2,128,128]{4,3,2,1,0:T(8,128)(2,1)S(1)} %shard_map.57), channel_id=1, source_target_pairs={{0,8},{8,0},{16,24},{24,16},{1,9},{9,1},{17,25},{25,17},{2,10},{10... | collective-permute-start | bytes 786440 | tf_op jit(solution)/shard_map/ppermute | solution.py:357
  16.5 0.0 collective-permute-done.6.refs_5_
  16.5 0.2 collective-permute-start.7
  16.7 0.0 collective-permute-done.2.refs_7_
  16.7 2.7 %shard_map.58 = (bf16[2,2,2,128,128]{4,3,2,1,0:T(8,128)(2,1)S(1)}, f32[2,2,2,128,128]{4,3,2,1,0:T(8,128)S(1)}, f32[2,2,2,128,128]{4,3,2,1,0:T(8,128)S(1)}) custom-call(f32[4]{0:T(128)S(1)} %copy-done.5, s32[4]{0:T(128)S(1)} %copy-done.6, s32[4,3]{1,0:T(4,128)S(1)} %copy-done.4, bf16[3,512,128]{2,1,0:T(8,128)(2,1)S(1)} %get-tuple-element.52.refs_3_, ...), custom_call_target="tpu_custom_call" | custom-call | flops 2684354560 | bytes 4194304 | tf_op jit(solution)/shard_map/pallas_call | solution.py:239
  19.4 1.4 %collective-permute-start.3 = (bf16[2,2,2,128,128]{4,3,2,1,0:T(8,128)(2,1)S(1)}, bf16[2,2,2,128,128]{4,3,2,1,0:T(8,128)(2,1)S(1)}, u32[]{:S(2)}, u32[]{:S(2)}) collective-permute-start(bf16[2,2,2,128,128]{4,3,2,1,0:T(8,128)(2,1)S(1)} %get-tuple-element.46), channel_id=1, source_target_pairs={{0,16},{8,24},{16,0},{24,8},{1,17},{9,25},{17,1},{25,9},{2,18},{10... | collective-permute-start | bytes 786440 | tf_op jit(solution)/shard_map/ppermute | solution.py:360
  20.8 1.1 %collective-permute-start.8 = (bf16[2,128,128]{2,1,0:T(8,128)(2,1)S(1)}, bf16[2,128,128]{2,1,0:T(8,128)(2,1)S(1)}, u32[]{:S(2)}, u32[]{:S(2)}) collective-permute-start(bf16[2,128,128]{2,1,0:T(8,128)(2,1)S(1)} %slice_bitcast_fusion), channel_id=1, source_target_pairs={{0,8},{8,0},{16,24},{24,16},{1,9},{9,1},{17,25},{25,17},{2,10},{10... | collective-permute-start | bytes 196616 | tf_op jit(solution)/shard_map/ppermute | solution.py:357
  21.9 0.0 collective-permute-done.4.relayed
  22.0 1.0 %collective-permute-start.10 = (bf16[2,2,2,128,128]{4,3,2,1,0:T(8,128)(2,1)S(1)}, bf16[2,2,2,128,128]{4,3,2,1,0:T(8,128)(2,1)S(1)}, u32[]{:S(2)}, u32[]{:S(2)}) collective-permute-start(bf16[2,2,2,128,128]{4,3,2,1,0:T(8,128)(2,1)S(1)} %shard_map.59), channel_id=1, source_target_pairs={{0,8},{8,0},{16,24},{24,16},{1,9},{9,1},{17,25},{25,17},{2,10},{10... | collective-permute-start | bytes 786440 | tf_op jit(solution)/shard_map/ppermute | solution.py:357
  22.9 1.7 %shard_map.60 = (bf16[1,2,2,128,128]{4,3,2,1,0:T(8,128)(2,1)S(1)}, f32[1,2,2,128,128]{4,3,2,1,0:T(8,128)S(1)}) custom-call(f32[4]{0:T(128)S(1)} %copy-done.5, s32[4]{0:T(128)S(1)} %copy-done.6, s32[4,3]{1,0:T(4,128)S(1)} %copy-done.4, bf16[3,512,128]{2,1,0:T(8,128)(2,1)S(1)} %get-tuple-element.52.refs_3_, ...), custom_call_target="tpu_custom_call" | custom-call | flops 1024 | bytes 1024 | tf_op jit(solution)/shard_map/pallas_call | solution.py:239
  24.6 0.0 collective-permute-done.5.got_1
  24.6 0.0 collective-permute-done.7.refs_6_
  24.6 1.2 %collective-permute-done.8.refs_7_ = bf16[2,128,128]{2,1,0:T(8,128)(2,1)S(1)} collective-permute-done((bf16[2,128,128]{2,1,0:T(8,128)(2,1)S(1)}, bf16[2,128,128]{2,1,0:T(8,128)(2,1)S(1)}, u32[]{:S(2)}, u32[]{:S(2)}) %collective-permute-start.8) | collective-permute-done | bytes 65568 | tf_op jit(solution)/shard_map/ppermute | solution.py:357
  25.8 1.7 %shard_map.61 = (bf16[2,2,2,128,128]{4,3,2,1,0:T(8,128)(2,1)S(1)}, f32[1,2,2,128,128]{4,3,2,1,0:T(8,128)S(1)}) custom-call(f32[4]{0:T(128)S(1)} %copy-done.5, s32[4]{0:T(128)S(1)} %copy-done.6, s32[4,3]{1,0:T(4,128)S(1)} %copy-done.4, bf16[3,512,128]{2,1,0:T(8,128)(2,1)S(1)} %get-tuple-element.52.refs_3_, ...), custom_call_target="tpu_custom_call" | custom-call | flops 1024 | bytes 1024 | tf_op jit(solution)/shard_map/pallas_call | solution.py:239
  27.5 1.3 %collective-permute-start.11 = (bf16[2,2,2,128,128]{4,3,2,1,0:T(8,128)(2,1)S(1)}, bf16[2,2,2,128,128]{4,3,2,1,0:T(8,128)(2,1)S(1)}, u32[]{:S(2)}, u32[]{:S(2)}) collective-permute-start(bf16[2,2,2,128,128]{4,3,2,1,0:T(8,128)(2,1)S(1)} %get-tuple-element.60), channel_id=1, source_target_pairs={{0,16},{8,24},{16,0},{24,8},{1,17},{9,25},{17,1},{25,9},{2,18},{10... | collective-permute-start | bytes 786440 | tf_op jit(solution)/shard_map/ppermute | solution.py:360
  28.9 0.0 collective-permute-done.3.relayed
  28.9 1.4 %collective-permute-start.9 = (bf16[2,2,2,128,128]{4,3,2,1,0:T(8,128)(2,1)S(1)}, bf16[2,2,2,128,128]{4,3,2,1,0:T(8,128)(2,1)S(1)}, u32[]{:S(2)}, u32[]{:S(2)}) collective-permute-start(bf16[2,2,2,128,128]{4,3,2,1,0:T(8,128)(2,1)S(1)} %shard_map.62), channel_id=1, source_target_pairs={{0,8},{8,0},{16,24},{24,16},{1,9},{9,1},{17,25},{25,17},{2,10},{10... | collective-permute-start | bytes 786440 | tf_op jit(solution)/shard_map/ppermute | solution.py:357
  30.3 3.0 %shard_map.63.mine_z = f32[2,2,2,128,128]{4,3,2,1,0:T(8,128)S(1)} custom-call(f32[4]{0:T(128)S(1)} %copy-done.5, s32[4]{0:T(128)S(1)} %copy-done.6, s32[4,3]{1,0:T(4,128)S(1)} %copy-done.4, bf16[3,512,128]{2,1,0:T(8,128)(2,1)S(1)} %get-tuple-element.52.refs_3_, bf16[4,128,384]{2,1,0:T(8,128)(2,1)S(1)} %get-tuple-element.53.refs_4_, ...), custom_call_target="tpu_custom_call" | custom-call | flops 1024 | bytes 1024 | tf_op jit(solution)/shard_map/pallas_call | solution.py:239
  33.3 0.0 collective-permute-done.10.got_2
  33.3 1.9 %collective-permute-done.11.got_z = bf16[2,2,2,128,128]{4,3,2,1,0:T(8,128)(2,1)S(1)} collective-permute-done((bf16[2,2,2,128,128]{4,3,2,1,0:T(8,128)(2,1)S(1)}, bf16[2,2,2,128,128]{4,3,2,1,0:T(8,128)(2,1)S(1)}, u32[]{:S(2)}, u32[]{:S(2)}) %collective-permute-start.11) | collective-permute-done | bytes 262176 | tf_op jit(solution)/shard_map/ppermute | solution.py:360
  35.3 1.0 %shard_map.64._ = bf16[2,2,4,128,256]{4,3,2,1,0:T(8,128)(2,1)} custom-call(f32[2,2,2,128,128]{4,3,2,1,0:T(8,128)S(1)} %copy-done.1, bf16[2,2,2,128,128]{4,3,2,1,0:T(8,128)(2,1)S(1)} %collective-permute-done.5.got_1, f32[2,2,2,128,128]{4,3,2,1,0:T(8,128)S(1)} %get-tuple-element.58.mine_2, bf16[2,2,2,128,128]{4,3,2,1,0:T(8,128)(2,1)S(1)} %collective-permute-done.10.got_2, ...), custom_call_target="tpu_custom_call" | custom-call | flops 1024 | bytes 1024 | tf_op jit(solution)/shard_map/pallas_call | solution.py:308
  36.3 0.6 %collective-permute-done.9.got = bf16[2,2,2,128,128]{4,3,2,1,0:T(8,128)(2,1)S(1)} collective-permute-done((bf16[2,2,2,128,128]{4,3,2,1,0:T(8,128)(2,1)S(1)}, bf16[2,2,2,128,128]{4,3,2,1,0:T(8,128)(2,1)S(1)}, u32[]{:S(2)}, u32[]{:S(2)}) %collective-permute-start.9) | collective-permute-done | bytes 262176 | tf_op jit(solution)/shard_map/ppermute | solution.py:357
  36.9 0.8 %shard_map.65 = bf16[2,2,4,128,256]{4,3,2,1,0:T(8,128)(2,1)} custom-call(f32[2,2,2,128,128]{4,3,2,1,0:T(8,128)S(1)} %get-tuple-element.44.mine, bf16[2,2,2,128,128]{4,3,2,1,0:T(8,128)(2,1)S(1)} %collective-permute-done.9.got, bf16[2,2,4,128,256]{4,3,2,1,0:T(8,128)(2,1)} %shard_map.64._), custom_call_target="tpu_custom_call", output_to_operand_aliasing={{}: (2, {})} | custom-call | flops 1024 | bytes 1024 | tf_op jit(solution)/shard_map/pallas_call | solution.py:319
  (18 shorter events, 0.2 us)
Async XLA Ops:
  0.0 9.9 %copy-start.3 = (bf16[4,3,128,128]{3,2,1,0:T(8,128)(2,1)S(1)}, bf16[4,3,128,128]{3,2,1,0:T(8,128)(2,1)}, u32[]{:S(2)}) copy-start(bf16[4,3,128,128]{3,2,1,0:T(8,128)(2,1)} %refs_3_.1) | copy-start | bytes 1179652
  0.0 9.9 %copy-start = (bf16[2,2,4,128,256]{4,3,2,1,0:T(8,128)(2,1)S(1)}, bf16[2,2,4,128,256]{4,3,2,1,0:T(8,128)(2,1)}, u32[]{:S(2)}) copy-start(bf16[2,2,4,128,256]{4,3,2,1,0:T(8,128)(2,1)} %refs_5_.3) | copy-start | bytes 3145732
  4.4 4.6 %collective-permute-start = (bf16[2,2,128,256]{3,2,1,0:T(8,128)(2,1)}, bf16[2,2,128,256]{3,2,1,0:T(8,128)(2,1)S(1)}, u32[]{:S(2)}, u32[]{:S(2)}) collective-permute-start(bf16[2,2,128,256]{3,2,1,0:T(8,128)(2,1)} %get-tuple-element.33), channel_id=1, source_target_pairs={{0,1},{1,0},{2,3},{3,2},{4,5},{5,4},{6,7},{7,6},{8,9},{9,8},{10,11... | collective-permute-start | bytes 786440 | tf_op jit(solution)/shard_map/ppermute | solution.py:363
  4.9 4.9 %copy-start.4 = (s32[4,3]{1,0:T(4,128)S(1)}, s32[4,3]{1,0:T(4,128)}, u32[]{:S(2)}) copy-start(s32[4,3]{1,0:T(4,128)} %refs_2_.9) | copy-start | bytes 148
  4.9 9.7 %collective-permute-start.1 = (bf16[2,2,2,128,128]{4,3,2,1,0:T(8,128)(2,1)}, bf16[2,2,2,128,128]{4,3,2,1,0:T(8,128)(2,1)S(1)}, u32[]{:S(2)}, u32[]{:S(2)}) collective-permute-start(bf16[2,2,2,128,128]{4,3,2,1,0:T(8,128)(2,1)} %get-tuple-element.37), channel_id=1, source_target_pairs={{0,16},{8,24},{16,0},{24,8},{1,17},{9,25},{17,1},{25,9},{2,18},{10... | collective-permute-start | bytes 786440 | tf_op jit(solution)/shard_map/ppermute | solution.py:360
  7.5 2.3 %copy-start.5 = (f32[4]{0:T(128)S(1)}, f32[4]{0:T(128)}, u32[]{:S(2)}) copy-start(f32[4]{0:T(128)} %refs_0_.9) | copy-start | bytes 52
  7.5 2.3 %copy-start.6 = (s32[4]{0:T(128)S(1)}, s32[4]{0:T(128)}, u32[]{:S(2)}) copy-start(s32[4]{0:T(128)} %refs_1_.9) | copy-start | bytes 52
  7.5 8.9 %collective-permute-start.6 = (bf16[4,2,128,128]{3,2,1,0:T(8,128)(2,1)}, bf16[4,2,128,128]{3,2,1,0:T(8,128)(2,1)S(1)}, u32[]{:S(2)}, u32[]{:S(2)}) collective-permute-start(bf16[4,2,128,128]{3,2,1,0:T(8,128)(2,1)} %get-tuple-element.51), channel_id=1, source_target_pairs={{0,8},{8,0},{16,24},{24,16},{1,9},{9,1},{17,25},{25,17},{2,10},{10... | collective-permute-start | bytes 786440 | tf_op jit(solution)/shard_map/ppermute | solution.py:357
  9.0 5.6 %copy-start.2 = (f32[2,2,2,128,128]{4,3,2,1,0:T(8,128)S(1)}, f32[2,2,2,128,128]{4,3,2,1,0:T(8,128)}, u32[]{:S(2)}) copy-start(f32[2,2,2,128,128]{4,3,2,1,0:T(8,128)} %get-tuple-element.36.near) | copy-start | bytes 1572868
  9.0 7.7 %collective-permute-start.2 = (bf16[2,2,128,256]{3,2,1,0:T(8,128)(2,1)}, bf16[2,2,128,256]{3,2,1,0:T(8,128)(2,1)S(1)}, u32[]{:S(2)}, u32[]{:S(2)}) collective-permute-start(bf16[2,2,128,256]{3,2,1,0:T(8,128)(2,1)} %get-tuple-element.43), channel_id=1, source_target_pairs={{1,2},{2,1},{3,4},{4,3},{5,6},{6,5},{9,10},{10,9},{11,12},{12,11},... | collective-permute-start | bytes 786440 | tf_op jit(solution)/shard_map/ppermute | solution.py:363
  12.5 9.4 %collective-permute-start.4 = (bf16[2,2,2,128,128]{4,3,2,1,0:T(8,128)(2,1)S(1)}, bf16[2,2,2,128,128]{4,3,2,1,0:T(8,128)(2,1)S(1)}, u32[]{:S(2)}, u32[]{:S(2)}) collective-permute-start(bf16[2,2,2,128,128]{4,3,2,1,0:T(8,128)(2,1)S(1)} %get-tuple-element.38), channel_id=1, source_target_pairs={{0,16},{8,24},{16,0},{24,8},{1,17},{9,25},{17,1},{25,9},{2,18},{10... | collective-permute-start | bytes 786440 | tf_op jit(solution)/shard_map/ppermute | solution.py:360
  14.7 9.9 %collective-permute-start.5 = (bf16[2,2,2,128,128]{4,3,2,1,0:T(8,128)(2,1)S(1)}, bf16[2,2,2,128,128]{4,3,2,1,0:T(8,128)(2,1)S(1)}, u32[]{:S(2)}, u32[]{:S(2)}) collective-permute-start(bf16[2,2,2,128,128]{4,3,2,1,0:T(8,128)(2,1)S(1)} %shard_map.57), channel_id=1, source_target_pairs={{0,8},{8,0},{16,24},{24,16},{1,9},{9,1},{17,25},{25,17},{2,10},{10... | collective-permute-start | bytes 786440 | tf_op jit(solution)/shard_map/ppermute | solution.py:357
  16.5 8.1 %collective-permute-start.7 = (bf16[4,2,128,128]{3,2,1,0:T(8,128)(2,1)S(1)}, bf16[4,2,128,128]{3,2,1,0:T(8,128)(2,1)S(1)}, u32[]{:S(2)}, u32[]{:S(2)}) collective-permute-start(bf16[4,2,128,128]{3,2,1,0:T(8,128)(2,1)S(1)} %collective-permute-done.6.refs_5_), channel_id=1, source_target_pairs={{0,1},{1,0},{2,3},{3,2},{4,5},{5,4},{6,7},{7,6},{8,9},{9,8},{10,11... | collective-permute-start | bytes 786440 | tf_op jit(solution)/shard_map/ppermute | solution.py:363
  19.4 9.5 %collective-permute-start.3 = (bf16[2,2,2,128,128]{4,3,2,1,0:T(8,128)(2,1)S(1)}, bf16[2,2,2,128,128]{4,3,2,1,0:T(8,128)(2,1)S(1)}, u32[]{:S(2)}, u32[]{:S(2)}) collective-permute-start(bf16[2,2,2,128,128]{4,3,2,1,0:T(8,128)(2,1)S(1)} %get-tuple-element.46), channel_id=1, source_target_pairs={{0,16},{8,24},{16,0},{24,8},{1,17},{9,25},{17,1},{25,9},{2,18},{10... | collective-permute-start | bytes 786440 | tf_op jit(solution)/shard_map/ppermute | solution.py:360
  20.8 5.0 %collective-permute-start.8 = (bf16[2,128,128]{2,1,0:T(8,128)(2,1)S(1)}, bf16[2,128,128]{2,1,0:T(8,128)(2,1)S(1)}, u32[]{:S(2)}, u32[]{:S(2)}) collective-permute-start(bf16[2,128,128]{2,1,0:T(8,128)(2,1)S(1)} %slice_bitcast_fusion), channel_id=1, source_target_pairs={{0,8},{8,0},{16,24},{24,16},{1,9},{9,1},{17,25},{25,17},{2,10},{10... | collective-permute-start | bytes 196616 | tf_op jit(solution)/shard_map/ppermute | solution.py:357
  22.0 11.4 %collective-permute-start.10 = (bf16[2,2,2,128,128]{4,3,2,1,0:T(8,128)(2,1)S(1)}, bf16[2,2,2,128,128]{4,3,2,1,0:T(8,128)(2,1)S(1)}, u32[]{:S(2)}, u32[]{:S(2)}) collective-permute-start(bf16[2,2,2,128,128]{4,3,2,1,0:T(8,128)(2,1)S(1)} %shard_map.59), channel_id=1, source_target_pairs={{0,8},{8,0},{16,24},{24,16},{1,9},{9,1},{17,25},{25,17},{2,10},{10... | collective-permute-start | bytes 786440 | tf_op jit(solution)/shard_map/ppermute | solution.py:357
  27.5 7.8 %collective-permute-start.11 = (bf16[2,2,2,128,128]{4,3,2,1,0:T(8,128)(2,1)S(1)}, bf16[2,2,2,128,128]{4,3,2,1,0:T(8,128)(2,1)S(1)}, u32[]{:S(2)}, u32[]{:S(2)}) collective-permute-start(bf16[2,2,2,128,128]{4,3,2,1,0:T(8,128)(2,1)S(1)} %get-tuple-element.60), channel_id=1, source_target_pairs={{0,16},{8,24},{16,0},{24,8},{1,17},{9,25},{17,1},{25,9},{2,18},{10... | collective-permute-start | bytes 786440 | tf_op jit(solution)/shard_map/ppermute | solution.py:360
  28.9 6.4 %copy-start.1 = (f32[2,2,2,128,128]{4,3,2,1,0:T(8,128)S(1)}, f32[2,2,2,128,128]{4,3,2,1,0:T(8,128)}, u32[]{:S(2)}) copy-start(f32[2,2,2,128,128]{4,3,2,1,0:T(8,128)} %get-tuple-element.57.mine_1) | copy-start | bytes 1572868
  28.9 7.9 %collective-permute-start.9 = (bf16[2,2,2,128,128]{4,3,2,1,0:T(8,128)(2,1)S(1)}, bf16[2,2,2,128,128]{4,3,2,1,0:T(8,128)(2,1)S(1)}, u32[]{:S(2)}, u32[]{:S(2)}) collective-permute-start(bf16[2,2,2,128,128]{4,3,2,1,0:T(8,128)(2,1)S(1)} %shard_map.62), channel_id=1, source_target_pairs={{0,8},{8,0},{16,24},{24,16},{1,9},{9,1},{17,25},{25,17},{2,10},{10... | collective-permute-start | bytes 786440 | tf_op jit(solution)/shard_map/ppermute | solution.py:357

commit v9 on v8

--- a/solution.py
+++ b/solution.py
@@ -368,8 +368,8 @@
     far_1, near_1, mine_1, raw, edge_n, edge_f = first_call(greens, coupling, occupation, offsets, neighbours)
     relay_1 = along(far_1)
     beside_n = beside(edge_n, chip)
-    raw_x = across(raw)
-    beside_f = beside(after_these(edge_f, beside_n), chips)
+    raw_x = across(after_these(raw, beside_n))
+    beside_f = beside(edge_f, chips)
     far_2, near_2, mine_2, rows, cols = next_call(SECOND, 0, (1, 1, 1), scalars, (coupling,), greens, (beside_n,), SMALL)
     relay_2 = along(far_2)
     both_1 = total_call(near_1, after_these(relay_1, far_2))

time: 37.8 us -> 37.6 us (level)
  the two profiles are of different devices: /device:TPU:0 before, /device:TPU:8 now
where the time goes in v9:
time: 37.6 us; the launch traced here: 36.9 us
  Pallas kernels  18 us (48%)
  starting transfers between devices  13.3 us (35%)
  waiting for transfers between devices  5.38 us (14%)
    pallas_call x5, Pallas kernels, next_call(): pl.pallas_call(functools.partial(next_body, groups, flip, wanted, own.ndi...  11.7 us
    ppermute x5, starting transfers between devices, across(): return lax.ppermute(array, 'energy', [(i, i ^ 1) for i in range(4)])  6.17 us
    ppermute x4, starting transfers between devices, along(): return lax.ppermute(array, 'energy', [(i, i ^ 2) for i in range(4)])  4.86 us
    ppermute x4, waiting for transfers between devices, along(): return lax.ppermute(array, 'energy', [(i, i ^ 2) for i in range(4)])  4.74 us
    pallas_call x1, Pallas kernels, first_call(): pl.pallas_call(first_body, out_shape=[jax.ShapeDtypeStruct(*out) for out...  4.41 us
    ppermute x3, starting transfers between devices, beside(): return lax.ppermute(array, 'slab', pairs)  2.31 us
    pallas_call x1, Pallas kernels, add_up(): pl.pallas_call(early_body, out_shape=jax.ShapeDtypeStruct(greens.shape, B...  0.98 us
    pallas_call x1, Pallas kernels, add_up(): pl.pallas_call(late_body, out_shape=jax.ShapeDtypeStruct(greens.shape, BF...  0.75 us
  transfers between devices with their start and end apart: 12, of which 5 were waited for; matrix products, arithmetic and copies ran while one was open for 0% of the time, Pallas kernels for 35%

profile of v9, /device:TPU:8, one launch (start us, length us, event | category | flops | bytes accessed | tf_op | source)
XLA Modules:
  0.0 36.9 jit_solution(11667611310183308596)
XLA Ops:
  0.0 4.4 %shard_map.55 = (bf16[2,2,2,128,128]{4,3,2,1,0:T(8,128)(2,1)}, f32[2,2,2,128,128]{4,3,2,1,0:T(8,128)}, f32[2,2,2,128,128]{4,3,2,1,0:T(8,128)}, bf16[4,2,128,128]...) custom-call(f32[4]{0:T(128)} %refs_0_.9, s32[4]{0:T(128)} %refs_1_.9, ...), custom_call_target="tpu_custom_call" | custom-call | flops 5368709120 | bytes 16777216 | tf_op jit(solution)/shard_map/pallas_call | solution.py:171
  4.4 0.1 collective-permute-start
  4.5 0.0 copy-start.4
  4.5 1.6 %collective-permute-start.1 = (bf16[2,2,2,128,128]{4,3,2,1,0:T(8,128)(2,1)}, bf16[2,2,2,128,128]{4,3,2,1,0:T(8,128)(2,1)S(1)}, u32[]{:S(2)}, u32[]{:S(2)}) collective-permute-start(bf16[2,2,2,128,128]{4,3,2,1,0:T(8,128)(2,1)} %get-tuple-element.37), channel_id=1, source_target_pairs={{0,16},{8,24},{16,0},{24,8},{1,17},{9,25},{17,1},{25,9},{2,18},{10... | collective-permute-start | bytes 786440 | tf_op jit(solution)/shard_map/ppermute | solution.py:360
  6.1 2.2 %collective-permute-start.2 = (bf16[2,2,128,256]{3,2,1,0:T(8,128)(2,1)}, bf16[2,2,128,256]{3,2,1,0:T(8,128)(2,1)S(1)}, u32[]{:S(2)}, u32[]{:S(2)}) collective-permute-start(bf16[2,2,128,256]{3,2,1,0:T(8,128)(2,1)} %get-tuple-element.42), channel_id=1, source_target_pairs={{1,2},{2,1},{3,4},{4,3},{5,6},{6,5},{9,10},{10,9},{11,12},{12,11},... | collective-permute-start | bytes 786440 | tf_op jit(solution)/shard_map/ppermute | solution.py:363
  8.3 0.0 collective-permute-done.refs_5_.refs_6_
  8.4 0.0 copy-start.2
  8.4 1.6 %collective-permute-start.6 = (bf16[4,2,128,128]{3,2,1,0:T(8,128)(2,1)}, bf16[4,2,128,128]{3,2,1,0:T(8,128)(2,1)S(1)}, u32[]{:S(2)}, u32[]{:S(2)}) collective-permute-start(bf16[4,2,128,128]{3,2,1,0:T(8,128)(2,1)} %get-tuple-element.51), channel_id=1, source_target_pairs={{0,8},{8,0},{16,24},{24,16},{1,9},{9,1},{17,25},{25,17},{2,10},{10... | collective-permute-start | bytes 786440 | tf_op jit(solution)/shard_map/ppermute | solution.py:357
  9.9 2.6 %shard_map.56 = (bf16[2,2,2,128,128]{4,3,2,1,0:T(8,128)(2,1)S(1)}, f32[2,2,2,128,128]{4,3,2,1,0:T(8,128)S(1)}, f32[2,2,2,128,128]{4,3,2,1,0:T(8,128)S(1)}, bf16[...) custom-call(f32[4]{0:T(128)S(1)} %copy-done.5, s32[4]{0:T(128)S(1)} %copy-done.6, s32[4,3]{1,0:T(4,128)S(1)} %copy-done.4, ...), custom_call_target="tpu_custom_call" | custom-call | flops 1024 | bytes 1024 | tf_op jit(solution)/shard_map/pallas_call | solution.py:239
  12.6 0.6 %collective-permute-start.4 = (bf16[2,2,2,128,128]{4,3,2,1,0:T(8,128)(2,1)S(1)}, bf16[2,2,2,128,128]{4,3,2,1,0:T(8,128)(2,1)S(1)}, u32[]{:S(2)}, u32[]{:S(2)}) collective-permute-start(bf16[2,2,2,128,128]{4,3,2,1,0:T(8,128)(2,1)S(1)} %get-tuple-element.38), channel_id=1, source_target_pairs={{0,16},{8,24},{16,0},{24,8},{1,17},{9,25},{17,1},{25,9},{2,18},{10... | collective-permute-start | bytes 786440 | tf_op jit(solution)/shard_map/ppermute | solution.py:360
  13.2 0.3 collective-permute-done.1.relayed
  13.5 1.6 %collective-permute-start.5 = (bf16[2,2,2,128,128]{4,3,2,1,0:T(8,128)(2,1)S(1)}, bf16[2,2,2,128,128]{4,3,2,1,0:T(8,128)(2,1)S(1)}, u32[]{:S(2)}, u32[]{:S(2)}) collective-permute-start(bf16[2,2,2,128,128]{4,3,2,1,0:T(8,128)(2,1)S(1)} %shard_map.57), channel_id=1, source_target_pairs={{0,8},{8,0},{16,24},{24,16},{1,9},{9,1},{17,25},{25,17},{2,10},{10... | collective-permute-start | bytes 786440 | tf_op jit(solution)/shard_map/ppermute | solution.py:357
  15.0 0.0 collective-permute-done.2.refs_7_
  15.0 2.7 %shard_map.58 = (bf16[2,2,2,128,128]{4,3,2,1,0:T(8,128)(2,1)S(1)}, f32[2,2,2,128,128]{4,3,2,1,0:T(8,128)S(1)}, f32[2,2,2,128,128]{4,3,2,1,0:T(8,128)S(1)}) custom-call(f32[4]{0:T(128)S(1)} %copy-done.5, s32[4]{0:T(128)S(1)} %copy-done.6, s32[4,3]{1,0:T(4,128)S(1)} %copy-done.4, bf16[3,512,128]{2,1,0:T(8,128)(2,1)S(1)} %get-tuple-element.52.refs_3_, ...), custom_call_target="tpu_custom_call" | custom-call | flops 2684354560 | bytes 4194304 | tf_op jit(solution)/shard_map/pallas_call | solution.py:239
  17.7 1.6 %collective-permute-start.3 = (bf16[2,2,2,128,128]{4,3,2,1,0:T(8,128)(2,1)S(1)}, bf16[2,2,2,128,128]{4,3,2,1,0:T(8,128)(2,1)S(1)}, u32[]{:S(2)}, u32[]{:S(2)}) collective-permute-start(bf16[2,2,2,128,128]{4,3,2,1,0:T(8,128)(2,1)S(1)} %get-tuple-element.45), channel_id=1, source_target_pairs={{0,16},{8,24},{16,0},{24,8},{1,17},{9,25},{17,1},{25,9},{2,18},{10... | collective-permute-start | bytes 786440 | tf_op jit(solution)/shard_map/ppermute | solution.py:360
  19.3 0.0 collective-permute-done.6.refs_5_
  19.3 0.0 collective-permute-start.7
  19.3 0.6 %collective-permute-start.8 = (bf16[2,128,128]{2,1,0:T(8,128)(2,1)S(1)}, bf16[2,128,128]{2,1,0:T(8,128)(2,1)S(1)}, u32[]{:S(2)}, u32[]{:S(2)}) collective-permute-start(bf16[2,128,128]{2,1,0:T(8,128)(2,1)S(1)} %slice_bitcast_fusion), channel_id=1, source_target_pairs={{0,8},{8,0},{16,24},{24,16},{1,9},{9,1},{17,25},{25,17},{2,10},{10... | collective-permute-start | bytes 196616 | tf_op jit(solution)/shard_map/ppermute | solution.py:357
  20.0 1.6 %collective-permute-done.4.relayed = bf16[2,2,2,128,128]{4,3,2,1,0:T(8,128)(2,1)S(1)} collective-permute-done((bf16[2,2,2,128,128]{4,3,2,1,0:T(8,128)(2,1)S(1)}, bf16[2,2,2,128,128]{4,3,2,1,0:T(8,128)(2,1)S(1)}, u32[]{:S(2)}, u32[]{:S(2)}) %collective-permute-start.4) | collective-permute-done | bytes 262176 | tf_op jit(solution)/shard_map/ppermute | solution.py:360
  21.7 0.6 %collective-permute-start.10 = (bf16[2,2,2,128,128]{4,3,2,1,0:T(8,128)(2,1)S(1)}, bf16[2,2,2,128,128]{4,3,2,1,0:T(8,128)(2,1)S(1)}, u32[]{:S(2)}, u32[]{:S(2)}) collective-permute-start(bf16[2,2,2,128,128]{4,3,2,1,0:T(8,128)(2,1)S(1)} %shard_map.59), channel_id=1, source_target_pairs={{0,8},{8,0},{16,24},{24,16},{1,9},{9,1},{17,25},{25,17},{2,10},{10... | collective-permute-start | bytes 786440 | tf_op jit(solution)/shard_map/ppermute | solution.py:357
  22.3 1.7 %shard_map.60 = (bf16[1,2,2,128,128]{4,3,2,1,0:T(8,128)(2,1)S(1)}, f32[1,2,2,128,128]{4,3,2,1,0:T(8,128)S(1)}) custom-call(f32[4]{0:T(128)S(1)} %copy-done.5, s32[4]{0:T(128)S(1)} %copy-done.6, s32[4,3]{1,0:T(4,128)S(1)} %copy-done.4, bf16[3,512,128]{2,1,0:T(8,128)(2,1)S(1)} %get-tuple-element.52.refs_3_, ...), custom_call_target="tpu_custom_call" | custom-call | flops 1024 | bytes 1024 | tf_op jit(solution)/shard_map/pallas_call | solution.py:239
  23.9 0.0 collective-permute-done.5.got_1
  23.9 0.5 %collective-permute-done.8.refs_7_ = bf16[2,128,128]{2,1,0:T(8,128)(2,1)S(1)} collective-permute-done((bf16[2,128,128]{2,1,0:T(8,128)(2,1)S(1)}, bf16[2,128,128]{2,1,0:T(8,128)(2,1)S(1)}, u32[]{:S(2)}, u32[]{:S(2)}) %collective-permute-start.8) | collective-permute-done | bytes 65568 | tf_op jit(solution)/shard_map/ppermute | solution.py:357
  24.4 1.7 %shard_map.61 = (bf16[2,2,2,128,128]{4,3,2,1,0:T(8,128)(2,1)S(1)}, f32[1,2,2,128,128]{4,3,2,1,0:T(8,128)S(1)}) custom-call(f32[4]{0:T(128)S(1)} %copy-done.5, s32[4]{0:T(128)S(1)} %copy-done.6, s32[4,3]{1,0:T(4,128)S(1)} %copy-done.4, bf16[3,512,128]{2,1,0:T(8,128)(2,1)S(1)} %get-tuple-element.52.refs_3_, ...), custom_call_target="tpu_custom_call" | custom-call | flops 1024 | bytes 1024 | tf_op jit(solution)/shard_map/pallas_call | solution.py:239
  26.1 1.1 %collective-permute-start.11 = (bf16[2,2,2,128,128]{4,3,2,1,0:T(8,128)(2,1)S(1)}, bf16[2,2,2,128,128]{4,3,2,1,0:T(8,128)(2,1)S(1)}, u32[]{:S(2)}, u32[]{:S(2)}) collective-permute-start(bf16[2,2,2,128,128]{4,3,2,1,0:T(8,128)(2,1)S(1)} %get-tuple-element.60), channel_id=1, source_target_pairs={{0,16},{8,24},{16,0},{24,8},{1,17},{9,25},{17,1},{25,9},{2,18},{10... | collective-permute-start | bytes 786440 | tf_op jit(solution)/shard_map/ppermute | solution.py:360
  27.3 1.8 %collective-permute-start.9 = (bf16[2,2,2,128,128]{4,3,2,1,0:T(8,128)(2,1)S(1)}, bf16[2,2,2,128,128]{4,3,2,1,0:T(8,128)(2,1)S(1)}, u32[]{:S(2)}, u32[]{:S(2)}) collective-permute-start(bf16[2,2,2,128,128]{4,3,2,1,0:T(8,128)(2,1)S(1)} %shard_map.62), channel_id=1, source_target_pairs={{0,8},{8,0},{16,24},{24,16},{1,9},{9,1},{17,25},{25,17},{2,10},{10... | collective-permute-start | bytes 786440 | tf_op jit(solution)/shard_map/ppermute | solution.py:357
  29.1 3.0 %shard_map.63.mine_z = f32[2,2,2,128,128]{4,3,2,1,0:T(8,128)S(1)} custom-call(f32[4]{0:T(128)S(1)} %copy-done.5, s32[4]{0:T(128)S(1)} %copy-done.6, s32[4,3]{1,0:T(4,128)S(1)} %copy-done.4, bf16[3,512,128]{2,1,0:T(8,128)(2,1)S(1)} %get-tuple-element.52.refs_3_, bf16[4,128,384]{2,1,0:T(8,128)(2,1)S(1)} %get-tuple-element.53.refs_4_, ...), custom_call_target="tpu_custom_call" | custom-call | flops 1024 | bytes 1024 | tf_op jit(solution)/shard_map/pallas_call | solution.py:239
  32.1 0.0 collective-permute-done.10.got_2
  32.1 2.8 %collective-permute-done.11.got_z = bf16[2,2,2,128,128]{4,3,2,1,0:T(8,128)(2,1)S(1)} collective-permute-done((bf16[2,2,2,128,128]{4,3,2,1,0:T(8,128)(2,1)S(1)}, bf16[2,2,2,128,128]{4,3,2,1,0:T(8,128)(2,1)S(1)}, u32[]{:S(2)}, u32[]{:S(2)}) %collective-permute-start.11) | collective-permute-done | bytes 262176 | tf_op jit(solution)/shard_map/ppermute | solution.py:360
  35.0 1.0 %shard_map.64._ = bf16[2,2,4,128,256]{4,3,2,1,0:T(8,128)(2,1)} custom-call(f32[2,2,2,128,128]{4,3,2,1,0:T(8,128)S(1)} %copy-done.1, bf16[2,2,2,128,128]{4,3,2,1,0:T(8,128)(2,1)S(1)} %collective-permute-done.5.got_1, f32[2,2,2,128,128]{4,3,2,1,0:T(8,128)S(1)} %get-tuple-element.58.mine_2, bf16[2,2,2,128,128]{4,3,2,1,0:T(8,128)(2,1)S(1)} %collective-permute-done.10.got_2, ...), custom_call_target="tpu_custom_call" | custom-call | flops 1024 | bytes 1024 | tf_op jit(solution)/shard_map/pallas_call | solution.py:308
  36.0 0.2 collective-permute-done.9.got
  36.1 0.8 %shard_map.65 = bf16[2,2,4,128,256]{4,3,2,1,0:T(8,128)(2,1)} custom-call(f32[2,2,2,128,128]{4,3,2,1,0:T(8,128)S(1)} %get-tuple-element.43.mine, bf16[2,2,2,128,128]{4,3,2,1,0:T(8,128)(2,1)S(1)} %collective-permute-done.9.got, bf16[2,2,4,128,256]{4,3,2,1,0:T(8,128)(2,1)} %shard_map.64._), custom_call_target="tpu_custom_call", output_to_operand_aliasing={{}: (2, {})} | custom-call | flops 1024 | bytes 1024 | tf_op jit(solution)/shard_map/pallas_call | solution.py:319
  (18 shorter events, 0.2 us)
Async XLA Ops:
  0.0 9.9 %copy-start.3 = (bf16[4,3,128,128]{3,2,1,0:T(8,128)(2,1)S(1)}, bf16[4,3,128,128]{3,2,1,0:T(8,128)(2,1)}, u32[]{:S(2)}) copy-start(bf16[4,3,128,128]{3,2,1,0:T(8,128)(2,1)} %refs_3_.1) | copy-start | bytes 1179652
  0.0 9.9 %copy-start = (bf16[2,2,4,128,256]{4,3,2,1,0:T(8,128)(2,1)S(1)}, bf16[2,2,4,128,256]{4,3,2,1,0:T(8,128)(2,1)}, u32[]{:S(2)}) copy-start(bf16[2,2,4,128,256]{4,3,2,1,0:T(8,128)(2,1)} %refs_5_.3) | copy-start | bytes 3145732
  4.4 3.9 %collective-permute-start = (bf16[2,2,128,256]{3,2,1,0:T(8,128)(2,1)}, bf16[2,2,128,256]{3,2,1,0:T(8,128)(2,1)S(1)}, u32[]{:S(2)}, u32[]{:S(2)}) collective-permute-start(bf16[2,2,128,256]{3,2,1,0:T(8,128)(2,1)} %get-tuple-element.33), channel_id=1, source_target_pairs={{0,1},{1,0},{2,3},{3,2},{4,5},{5,4},{6,7},{7,6},{8,9},{9,8},{10,11... | collective-permute-start | bytes 786440 | tf_op jit(solution)/shard_map/ppermute | solution.py:363
  4.5 5.4 %copy-start.4 = (s32[4,3]{1,0:T(4,128)S(1)}, s32[4,3]{1,0:T(4,128)}, u32[]{:S(2)}) copy-start(s32[4,3]{1,0:T(4,128)} %refs_2_.9) | copy-start | bytes 148
  4.5 8.9 %collective-permute-start.1 = (bf16[2,2,2,128,128]{4,3,2,1,0:T(8,128)(2,1)}, bf16[2,2,2,128,128]{4,3,2,1,0:T(8,128)(2,1)S(1)}, u32[]{:S(2)}, u32[]{:S(2)}) collective-permute-start(bf16[2,2,2,128,128]{4,3,2,1,0:T(8,128)(2,1)} %get-tuple-element.37), channel_id=1, source_target_pairs={{0,16},{8,24},{16,0},{24,8},{1,17},{9,25},{17,1},{25,9},{2,18},{10... | collective-permute-start | bytes 786440 | tf_op jit(solution)/shard_map/ppermute | solution.py:360
  6.1 3.8 %copy-start.5 = (f32[4]{0:T(128)S(1)}, f32[4]{0:T(128)}, u32[]{:S(2)}) copy-start(f32[4]{0:T(128)} %refs_0_.9) | copy-start | bytes 52
  6.1 3.8 %copy-start.6 = (s32[4]{0:T(128)S(1)}, s32[4]{0:T(128)}, u32[]{:S(2)}) copy-start(s32[4]{0:T(128)} %refs_1_.9) | copy-start | bytes 52
  6.1 8.9 %collective-permute-start.2 = (bf16[2,2,128,256]{3,2,1,0:T(8,128)(2,1)}, bf16[2,2,128,256]{3,2,1,0:T(8,128)(2,1)S(1)}, u32[]{:S(2)}, u32[]{:S(2)}) collective-permute-start(bf16[2,2,128,256]{3,2,1,0:T(8,128)(2,1)} %get-tuple-element.42), channel_id=1, source_target_pairs={{1,2},{2,1},{3,4},{4,3},{5,6},{6,5},{9,10},{10,9},{11,12},{12,11},... | collective-permute-start | bytes 786440 | tf_op jit(solution)/shard_map/ppermute | solution.py:363
  8.4 5.1 %copy-start.2 = (f32[2,2,2,128,128]{4,3,2,1,0:T(8,128)S(1)}, f32[2,2,2,128,128]{4,3,2,1,0:T(8,128)}, u32[]{:S(2)}) copy-start(f32[2,2,2,128,128]{4,3,2,1,0:T(8,128)} %get-tuple-element.36.near) | copy-start | bytes 1572868
  8.4 11.0 %collective-permute-start.6 = (bf16[4,2,128,128]{3,2,1,0:T(8,128)(2,1)}, bf16[4,2,128,128]{3,2,1,0:T(8,128)(2,1)S(1)}, u32[]{:S(2)}, u32[]{:S(2)}) collective-permute-start(bf16[4,2,128,128]{3,2,1,0:T(8,128)(2,1)} %get-tuple-element.51), channel_id=1, source_target_pairs={{0,8},{8,0},{16,24},{24,16},{1,9},{9,1},{17,25},{25,17},{2,10},{10... | collective-permute-start | bytes 786440 | tf_op jit(solution)/shard_map/ppermute | solution.py:357
  12.6 9.0 %collective-permute-start.4 = (bf16[2,2,2,128,128]{4,3,2,1,0:T(8,128)(2,1)S(1)}, bf16[2,2,2,128,128]{4,3,2,1,0:T(8,128)(2,1)S(1)}, u32[]{:S(2)}, u32[]{:S(2)}) collective-permute-start(bf16[2,2,2,128,128]{4,3,2,1,0:T(8,128)(2,1)S(1)} %get-tuple-element.38), channel_id=1, source_target_pairs={{0,16},{8,24},{16,0},{24,8},{1,17},{9,25},{17,1},{25,9},{2,18},{10... | collective-permute-start | bytes 786440 | tf_op jit(solution)/shard_map/ppermute | solution.py:360
  13.5 10.4 %collective-permute-start.5 = (bf16[2,2,2,128,128]{4,3,2,1,0:T(8,128)(2,1)S(1)}, bf16[2,2,2,128,128]{4,3,2,1,0:T(8,128)(2,1)S(1)}, u32[]{:S(2)}, u32[]{:S(2)}) collective-permute-start(bf16[2,2,2,128,128]{4,3,2,1,0:T(8,128)(2,1)S(1)} %shard_map.57), channel_id=1, source_target_pairs={{0,8},{8,0},{16,24},{24,16},{1,9},{9,1},{17,25},{25,17},{2,10},{10... | collective-permute-start | bytes 786440 | tf_op jit(solution)/shard_map/ppermute | solution.py:357
  17.7 9.5 %collective-permute-start.3 = (bf16[2,2,2,128,128]{4,3,2,1,0:T(8,128)(2,1)S(1)}, bf16[2,2,2,128,128]{4,3,2,1,0:T(8,128)(2,1)S(1)}, u32[]{:S(2)}, u32[]{:S(2)}) collective-permute-start(bf16[2,2,2,128,128]{4,3,2,1,0:T(8,128)(2,1)S(1)} %get-tuple-element.45), channel_id=1, source_target_pairs={{0,16},{8,24},{16,0},{24,8},{1,17},{9,25},{17,1},{25,9},{2,18},{10... | collective-permute-start | bytes 786440 | tf_op jit(solution)/shard_map/ppermute | solution.py:360
  19.3 5.1 %collective-permute-start.7 = (bf16[4,2,128,128]{3,2,1,0:T(8,128)(2,1)S(1)}, bf16[4,2,128,128]{3,2,1,0:T(8,128)(2,1)S(1)}, u32[]{:S(2)}, u32[]{:S(2)}) collective-permute-start(bf16[4,2,128,128]{3,2,1,0:T(8,128)(2,1)S(1)} %collective-permute-done.6.refs_5_), channel_id=1, source_target_pairs={{0,1},{1,0},{2,3},{3,2},{4,5},{5,4},{6,7},{7,6},{8,9},{9,8},{10,11... | collective-permute-start | bytes 786440 | tf_op jit(solution)/shard_map/ppermute | solution.py:363
  19.3 5.1 %collective-permute-start.8 = (bf16[2,128,128]{2,1,0:T(8,128)(2,1)S(1)}, bf16[2,128,128]{2,1,0:T(8,128)(2,1)S(1)}, u32[]{:S(2)}, u32[]{:S(2)}) collective-permute-start(bf16[2,128,128]{2,1,0:T(8,128)(2,1)S(1)} %slice_bitcast_fusion), channel_id=1, source_target_pairs={{0,8},{8,0},{16,24},{24,16},{1,9},{9,1},{17,25},{25,17},{2,10},{10... | collective-permute-start | bytes 196616 | tf_op jit(solution)/shard_map/ppermute | solution.py:357
  21.7 10.5 %collective-permute-start.10 = (bf16[2,2,2,128,128]{4,3,2,1,0:T(8,128)(2,1)S(1)}, bf16[2,2,2,128,128]{4,3,2,1,0:T(8,128)(2,1)S(1)}, u32[]{:S(2)}, u32[]{:S(2)}) collective-permute-start(bf16[2,2,2,128,128]{4,3,2,1,0:T(8,128)(2,1)S(1)} %shard_map.59), channel_id=1, source_target_pairs={{0,8},{8,0},{16,24},{24,16},{1,9},{9,1},{17,25},{25,17},{2,10},{10... | collective-permute-start | bytes 786440 | tf_op jit(solution)/shard_map/ppermute | solution.py:357
  26.1 8.8 %collective-permute-start.11 = (bf16[2,2,2,128,128]{4,3,2,1,0:T(8,128)(2,1)S(1)}, bf16[2,2,2,128,128]{4,3,2,1,0:T(8,128)(2,1)S(1)}, u32[]{:S(2)}, u32[]{:S(2)}) collective-permute-start(bf16[2,2,2,128,128]{4,3,2,1,0:T(8,128)(2,1)S(1)} %get-tuple-element.60), channel_id=1, source_target_pairs={{0,16},{8,24},{16,0},{24,8},{1,17},{9,25},{17,1},{25,9},{2,18},{10... | collective-permute-start | bytes 786440 | tf_op jit(solution)/shard_map/ppermute | solution.py:360
  27.3 7.7 %copy-start.1 = (f32[2,2,2,128,128]{4,3,2,1,0:T(8,128)S(1)}, f32[2,2,2,128,128]{4,3,2,1,0:T(8,128)}, u32[]{:S(2)}) copy-start(f32[2,2,2,128,128]{4,3,2,1,0:T(8,128)} %get-tuple-element.57.mine_1) | copy-start | bytes 1572868
  27.3 8.8 %collective-permute-start.9 = (bf16[2,2,2,128,128]{4,3,2,1,0:T(8,128)(2,1)S(1)}, bf16[2,2,2,128,128]{4,3,2,1,0:T(8,128)(2,1)S(1)}, u32[]{:S(2)}, u32[]{:S(2)}) collective-permute-start(bf16[2,2,2,128,128]{4,3,2,1,0:T(8,128)(2,1)S(1)} %shard_map.62), channel_id=1, source_target_pairs={{0,8},{8,0},{16,24},{24,16},{1,9},{9,1},{17,25},{25,17},{2,10},{10... | collective-permute-start | bytes 786440 | tf_op jit(solution)/shard_map/ppermute | solution.py:357

commit v10 on v9

--- a/solution.py
+++ b/solution.py
@@ -11,6 +11,7 @@
 F32 = jnp.float32
 
 NEAR, FAR = "n", "f"
+ROWS = 32
 FIRST = (("full", 1, 1), ("full", 1, 2))
 SECOND = (("full", 1, NEAR), ("half", 0, 1, (1, 2)))
 THIRD = (("full", 1, FAR), ("half", 0, 1, (NEAR, FAR)))
@@ -38,7 +39,7 @@
     slots, wide, size = rows.shape
     modes = wide // size
     owned = nbr.shape[0]
-    count = acc.shape[0] // 3
+    count = acc.shape[1] // (2 * size)
     first = lax.axis_index("slab") * owned
     odd = lax.rem(lax.axis_index("energy") + flip, 2)
     part = group[1]
@@ -67,31 +68,42 @@
                     half[m, to : to + size, k * size : (k + 1) * size] = r[
                         m * size : (m + 1) * size, h * size : (h + 1) * size
                     ]
-    acc[...] = jnp.zeros_like(acc)
-
-    def second(m):
-        y = lax.dot_general(half[m], cols[m], (((1,), (1,)), ((), ())), preferred_element_type=F32)
-        o = off[m]
+    for m in range(modes):
+        acc[m] = lax.dot_general(half[m], cols[m], (((1,), (1,)), ((), ())), preferred_element_type=F32)
+    weights = []
+    for m in range(modes):
         n = occ[m]
         down, up = (n + 1.0, n) if part == 0 else (n, n + 1.0)
-        for e in range(count):
-            for u in range(2):
-                to = (e * 2 + u) * size
-                ys = y[to : to + size]
-                acc[e - o + count, u] += down * ys
-                acc[e + o + count, u] += up * ys
-
-    for m in range(modes):
-        if far is None and near is None:
-            pl.when(off[m] < count)(functools.partial(second, m))
-        else:
-            second(m)
-    if far is not None:
-        far[...] = acc[pl.ds(2 * count * odd, count)].astype(BF16)
-    if near is not None:
-        near[...] = acc[pl.ds(2 * count * (1 - odd), count)]
-    if mine is not None:
-        mine[...] = acc[pl.ds(count, count)]
+        one = off[m] == 1
+        weights.append(
+            {
+                -1: jnp.where(one, down, 0.0),
+                1: jnp.where(one, up, 0.0),
+                -2: jnp.where(one, 0.0, down),
+                2: jnp.where(one, 0.0, up),
+            }
+        )
+    is_odd = odd == 1
+    for u in range(2):
+        for r in range(0, size, ROWS):
+            y = [
+                [acc[m, (e * 2 + u) * size + r : (e * 2 + u) * size + r + ROWS] for m in range(modes)]
+                for e in range(count)
+            ]
+
+            def shifted(e, by):
+                return sum(weights[m][by] * y[e][m] for m in range(modes))
+
+            to = slice(r, r + ROWS)
+            if far is not None:
+                before = (shifted(0, -2), shifted(0, -1) + shifted(1, -2))
+                after = (shifted(0, 2) + shifted(1, 1), shifted(1, 2))
+                for j in range(count):
+                    far[j, u, to] = jnp.where(is_odd, after[j], before[j]).astype(BF16)
+                    near[j, u, to] = jnp.where(is_odd, before[j], after[j])
+            if mine is not None:
+                mine[0, u, to] = shifted(1, -1)
+                mine[1, u, to] = shifted(0, 1)
 
 
 def pieces(groups, size, count):
@@ -101,7 +113,7 @@
 def scratch(modes, slots, size, count):
     return [
         pltpu.VMEM((modes, count * 2 * size, slots * size), BF16),
-        pltpu.VMEM((3 * count, 2, size, size), F32),
+        pltpu.VMEM((modes, count * 2 * size, size), F32),
     ]
 
 

time: 37.6 us -> 37.5 us (level)
  Pallas kernels: 18 us -> 17.2 us
  waiting for transfers between devices: 5.38 us -> 6.18 us
    pallas_call x5, Pallas kernels: 11.7 us -> 10.9 us  [next_call(): pl.pallas_call(functools.partial(next_body, groups, flip, wanted, own.ndi...]
    ppermute x4, waiting for transfers between devices: 4.74 us -> 5.41 us  [along(): return lax.ppermute(array, 'energy', [(i, i ^ 2) for i in range(4)])]
  transfers between devices with their start and end apart: 12 -> 12, of which waited for: 5 -> 5; matrix products, arithmetic and copies ran while one was open for 0% -> 0% of each run, Pallas kernels for 35% -> 33%
where the time goes in v10:
time: 37.5 us; the launch traced here: 36.9 us
  Pallas kernels  17.2 us (46%)
  starting transfers between devices  13.3 us (35%)
  waiting for transfers between devices  6.18 us (16%)
    pallas_call x5, Pallas kernels, next_call(): pl.pallas_call(functools.partial(next_body, groups, flip, wanted, own.ndi...  10.9 us
    ppermute x5, starting transfers between devices, across(): return lax.ppermute(array, 'energy', [(i, i ^ 1) for i in range(4)])  6.14 us
    ppermute x4, waiting for transfers between devices, along(): return lax.ppermute(array, 'energy', [(i, i ^ 2) for i in range(4)])  5.41 us
    ppermute x4, starting transfers between devices, along(): return lax.ppermute(array, 'energy', [(i, i ^ 2) for i in range(4)])  4.83 us
    pallas_call x1, Pallas kernels, first_call(): pl.pallas_call(first_body, out_shape=[jax.ShapeDtypeStruct(*out) for out...  4.43 us
    ppermute x3, starting transfers between devices, beside(): return lax.ppermute(array, 'slab', pairs)  2.31 us
    pallas_call x1, Pallas kernels, add_up(): pl.pallas_call(early_body, out_shape=jax.ShapeDtypeStruct(greens.shape, B...  0.98 us
    ppermute x5, waiting for transfers between devices, across(): return lax.ppermute(array, 'energy', [(i, i ^ 1) for i in range(4)])  0.76 us
  transfers between devices with their start and end apart: 12, of which 5 were waited for; matrix products, arithmetic and copies ran while one was open for 0% of the time, Pallas kernels for 33%

profile of v10, /device:TPU:8, one launch (start us, length us, event | category | flops | bytes accessed | tf_op | source)
XLA Modules:
  0.0 36.9 jit_solution(1409929001861830574)
XLA Ops:
  0.0 4.4 %shard_map.55 = (bf16[2,2,2,128,128]{4,3,2,1,0:T(8,128)(2,1)}, f32[2,2,2,128,128]{4,3,2,1,0:T(8,128)}, f32[2,2,2,128,128]{4,3,2,1,0:T(8,128)}, bf16[4,2,128,128]...) custom-call(f32[4]{0:T(128)} %refs_0_.9, s32[4]{0:T(128)} %refs_1_.9, ...), custom_call_target="tpu_custom_call" | custom-call | flops 5368709120 | bytes 16777216 | tf_op jit(solution)/shard_map/pallas_call | solution.py:183
  4.4 0.1 collective-permute-start
  4.5 0.0 copy-start.4
  4.5 1.6 %collective-permute-start.1 = (bf16[2,2,2,128,128]{4,3,2,1,0:T(8,128)(2,1)}, bf16[2,2,2,128,128]{4,3,2,1,0:T(8,128)(2,1)S(1)}, u32[]{:S(2)}, u32[]{:S(2)}) collective-permute-start(bf16[2,2,2,128,128]{4,3,2,1,0:T(8,128)(2,1)} %get-tuple-element.37), channel_id=1, source_target_pairs={{0,16},{8,24},{16,0},{24,8},{1,17},{9,25},{17,1},{25,9},{2,18},{10... | collective-permute-start | bytes 786440 | tf_op jit(solution)/shard_map/ppermute | solution.py:372
  6.1 2.2 %collective-permute-start.2 = (bf16[2,2,128,256]{3,2,1,0:T(8,128)(2,1)}, bf16[2,2,128,256]{3,2,1,0:T(8,128)(2,1)S(1)}, u32[]{:S(2)}, u32[]{:S(2)}) collective-permute-start(bf16[2,2,128,256]{3,2,1,0:T(8,128)(2,1)} %get-tuple-element.42), channel_id=1, source_target_pairs={{1,2},{2,1},{3,4},{4,3},{5,6},{6,5},{9,10},{10,9},{11,12},{12,11},... | collective-permute-start | bytes 786440 | tf_op jit(solution)/shard_map/ppermute | solution.py:375
  8.4 0.0 collective-permute-done.refs_5_.refs_6_
  8.4 0.0 copy-start.2
  8.4 1.6 %collective-permute-start.6 = (bf16[4,2,128,128]{3,2,1,0:T(8,128)(2,1)}, bf16[4,2,128,128]{3,2,1,0:T(8,128)(2,1)S(1)}, u32[]{:S(2)}, u32[]{:S(2)}) collective-permute-start(bf16[4,2,128,128]{3,2,1,0:T(8,128)(2,1)} %get-tuple-element.51), channel_id=1, source_target_pairs={{0,8},{8,0},{16,24},{24,16},{1,9},{9,1},{17,25},{25,17},{2,10},{10... | collective-permute-start | bytes 786440 | tf_op jit(solution)/shard_map/ppermute | solution.py:369
  10.0 2.6 %shard_map.56 = (bf16[2,2,2,128,128]{4,3,2,1,0:T(8,128)(2,1)S(1)}, f32[2,2,2,128,128]{4,3,2,1,0:T(8,128)S(1)}, f32[2,2,2,128,128]{4,3,2,1,0:T(8,128)S(1)}, bf16[...) custom-call(f32[4]{0:T(128)S(1)} %copy-done.5, s32[4]{0:T(128)S(1)} %copy-done.6, s32[4,3]{1,0:T(4,128)S(1)} %copy-done.4, ...), custom_call_target="tpu_custom_call" | custom-call | flops 1024 | bytes 1024 | tf_op jit(solution)/shard_map/pallas_call | solution.py:251
  12.6 0.6 %collective-permute-start.4 = (bf16[2,2,2,128,128]{4,3,2,1,0:T(8,128)(2,1)S(1)}, bf16[2,2,2,128,128]{4,3,2,1,0:T(8,128)(2,1)S(1)}, u32[]{:S(2)}, u32[]{:S(2)}) collective-permute-start(bf16[2,2,2,128,128]{4,3,2,1,0:T(8,128)(2,1)S(1)} %get-tuple-element.38), channel_id=1, source_target_pairs={{0,16},{8,24},{16,0},{24,8},{1,17},{9,25},{17,1},{25,9},{2,18},{10... | collective-permute-start | bytes 786440 | tf_op jit(solution)/shard_map/ppermute | solution.py:372
  13.2 0.3 collective-permute-done.1.relayed
  13.5 1.6 %collective-permute-start.5 = (bf16[2,2,2,128,128]{4,3,2,1,0:T(8,128)(2,1)S(1)}, bf16[2,2,2,128,128]{4,3,2,1,0:T(8,128)(2,1)S(1)}, u32[]{:S(2)}, u32[]{:S(2)}) collective-permute-start(bf16[2,2,2,128,128]{4,3,2,1,0:T(8,128)(2,1)S(1)} %shard_map.57), channel_id=1, source_target_pairs={{0,8},{8,0},{16,24},{24,16},{1,9},{9,1},{17,25},{25,17},{2,10},{10... | collective-permute-start | bytes 786440 | tf_op jit(solution)/shard_map/ppermute | solution.py:369
  15.1 0.0 collective-permute-done.2.refs_7_
  15.1 2.6 %shard_map.58 = (bf16[2,2,2,128,128]{4,3,2,1,0:T(8,128)(2,1)S(1)}, f32[2,2,2,128,128]{4,3,2,1,0:T(8,128)S(1)}, f32[2,2,2,128,128]{4,3,2,1,0:T(8,128)S(1)}) custom-call(f32[4]{0:T(128)S(1)} %copy-done.5, s32[4]{0:T(128)S(1)} %copy-done.6, s32[4,3]{1,0:T(4,128)S(1)} %copy-done.4, bf16[3,512,128]{2,1,0:T(8,128)(2,1)S(1)} %get-tuple-element.52.refs_3_, ...), custom_call_target="tpu_custom_call" | custom-call | flops 2684354560 | bytes 4194304 | tf_op jit(solution)/shard_map/pallas_call | solution.py:251
  17.7 1.6 %collective-permute-start.3 = (bf16[2,2,2,128,128]{4,3,2,1,0:T(8,128)(2,1)S(1)}, bf16[2,2,2,128,128]{4,3,2,1,0:T(8,128)(2,1)S(1)}, u32[]{:S(2)}, u32[]{:S(2)}) collective-permute-start(bf16[2,2,2,128,128]{4,3,2,1,0:T(8,128)(2,1)S(1)} %get-tuple-element.45), channel_id=1, source_target_pairs={{0,16},{8,24},{16,0},{24,8},{1,17},{9,25},{17,1},{25,9},{2,18},{10... | collective-permute-start | bytes 786440 | tf_op jit(solution)/shard_map/ppermute | solution.py:372
  19.3 0.0 collective-permute-done.6.refs_5_
  19.3 0.0 collective-permute-start.7
  19.3 0.6 %collective-permute-start.8 = (bf16[2,128,128]{2,1,0:T(8,128)(2,1)S(1)}, bf16[2,128,128]{2,1,0:T(8,128)(2,1)S(1)}, u32[]{:S(2)}, u32[]{:S(2)}) collective-permute-start(bf16[2,128,128]{2,1,0:T(8,128)(2,1)S(1)} %slice_bitcast_fusion), channel_id=1, source_target_pairs={{0,8},{8,0},{16,24},{24,16},{1,9},{9,1},{17,25},{25,17},{2,10},{10... | collective-permute-start | bytes 196616 | tf_op jit(solution)/shard_map/ppermute | solution.py:369
  19.9 1.7 %collective-permute-done.4.relayed = bf16[2,2,2,128,128]{4,3,2,1,0:T(8,128)(2,1)S(1)} collective-permute-done((bf16[2,2,2,128,128]{4,3,2,1,0:T(8,128)(2,1)S(1)}, bf16[2,2,2,128,128]{4,3,2,1,0:T(8,128)(2,1)S(1)}, u32[]{:S(2)}, u32[]{:S(2)}) %collective-permute-start.4) | collective-permute-done | bytes 262176 | tf_op jit(solution)/shard_map/ppermute | solution.py:372
  21.6 0.6 %collective-permute-start.10 = (bf16[2,2,2,128,128]{4,3,2,1,0:T(8,128)(2,1)S(1)}, bf16[2,2,2,128,128]{4,3,2,1,0:T(8,128)(2,1)S(1)}, u32[]{:S(2)}, u32[]{:S(2)}) collective-permute-start(bf16[2,2,2,128,128]{4,3,2,1,0:T(8,128)(2,1)S(1)} %shard_map.59), channel_id=1, source_target_pairs={{0,8},{8,0},{16,24},{24,16},{1,9},{9,1},{17,25},{25,17},{2,10},{10... | collective-permute-start | bytes 786440 | tf_op jit(solution)/shard_map/ppermute | solution.py:369
  22.2 1.6 %shard_map.60 = (bf16[1,2,2,128,128]{4,3,2,1,0:T(8,128)(2,1)S(1)}, f32[1,2,2,128,128]{4,3,2,1,0:T(8,128)S(1)}) custom-call(f32[4]{0:T(128)S(1)} %copy-done.5, s32[4]{0:T(128)S(1)} %copy-done.6, s32[4,3]{1,0:T(4,128)S(1)} %copy-done.4, bf16[3,512,128]{2,1,0:T(8,128)(2,1)S(1)} %get-tuple-element.52.refs_3_, ...), custom_call_target="tpu_custom_call" | custom-call | flops 1024 | bytes 1024 | tf_op jit(solution)/shard_map/pallas_call | solution.py:251
  23.9 0.0 collective-permute-done.5.got_1
  23.9 0.5 %collective-permute-done.8.refs_7_ = bf16[2,128,128]{2,1,0:T(8,128)(2,1)S(1)} collective-permute-done((bf16[2,128,128]{2,1,0:T(8,128)(2,1)S(1)}, bf16[2,128,128]{2,1,0:T(8,128)(2,1)S(1)}, u32[]{:S(2)}, u32[]{:S(2)}) %collective-permute-start.8) | collective-permute-done | bytes 65568 | tf_op jit(solution)/shard_map/ppermute | solution.py:369
  24.4 1.6 %shard_map.61 = (bf16[2,2,2,128,128]{4,3,2,1,0:T(8,128)(2,1)S(1)}, f32[1,2,2,128,128]{4,3,2,1,0:T(8,128)S(1)}) custom-call(f32[4]{0:T(128)S(1)} %copy-done.5, s32[4]{0:T(128)S(1)} %copy-done.6, s32[4,3]{1,0:T(4,128)S(1)} %copy-done.4, bf16[3,512,128]{2,1,0:T(8,128)(2,1)S(1)} %get-tuple-element.52.refs_3_, ...), custom_call_target="tpu_custom_call" | custom-call | flops 1024 | bytes 1024 | tf_op jit(solution)/shard_map/pallas_call | solution.py:251
  26.1 1.1 %collective-permute-start.11 = (bf16[2,2,2,128,128]{4,3,2,1,0:T(8,128)(2,1)S(1)}, bf16[2,2,2,128,128]{4,3,2,1,0:T(8,128)(2,1)S(1)}, u32[]{:S(2)}, u32[]{:S(2)}) collective-permute-start(bf16[2,2,2,128,128]{4,3,2,1,0:T(8,128)(2,1)S(1)} %get-tuple-element.60), channel_id=1, source_target_pairs={{0,16},{8,24},{16,0},{24,8},{1,17},{9,25},{17,1},{25,9},{2,18},{10... | collective-permute-start | bytes 786440 | tf_op jit(solution)/shard_map/ppermute | solution.py:372
  27.2 0.0 collective-permute-done.3.relayed
  27.3 1.8 %collective-permute-start.9 = (bf16[2,2,2,128,128]{4,3,2,1,0:T(8,128)(2,1)S(1)}, bf16[2,2,2,128,128]{4,3,2,1,0:T(8,128)(2,1)S(1)}, u32[]{:S(2)}, u32[]{:S(2)}) collective-permute-start(bf16[2,2,2,128,128]{4,3,2,1,0:T(8,128)(2,1)S(1)} %shard_map.62), channel_id=1, source_target_pairs={{0,8},{8,0},{16,24},{24,16},{1,9},{9,1},{17,25},{25,17},{2,10},{10... | collective-permute-start | bytes 786440 | tf_op jit(solution)/shard_map/ppermute | solution.py:369
  29.1 2.4 %shard_map.63.mine_z = f32[2,2,2,128,128]{4,3,2,1,0:T(8,128)S(1)} custom-call(f32[4]{0:T(128)S(1)} %copy-done.5, s32[4]{0:T(128)S(1)} %copy-done.6, s32[4,3]{1,0:T(4,128)S(1)} %copy-done.4, bf16[3,512,128]{2,1,0:T(8,128)(2,1)S(1)} %get-tuple-element.52.refs_3_, bf16[4,128,384]{2,1,0:T(8,128)(2,1)S(1)} %get-tuple-element.53.refs_4_, ...), custom_call_target="tpu_custom_call" | custom-call | flops 1024 | bytes 1024 | tf_op jit(solution)/shard_map/pallas_call | solution.py:251
  31.5 3.4 %collective-permute-done.11.got_z = bf16[2,2,2,128,128]{4,3,2,1,0:T(8,128)(2,1)S(1)} collective-permute-done((bf16[2,2,2,128,128]{4,3,2,1,0:T(8,128)(2,1)S(1)}, bf16[2,2,2,128,128]{4,3,2,1,0:T(8,128)(2,1)S(1)}, u32[]{:S(2)}, u32[]{:S(2)}) %collective-permute-start.11) | collective-permute-done | bytes 262176 | tf_op jit(solution)/shard_map/ppermute | solution.py:372
  34.9 1.0 %shard_map.64._ = bf16[2,2,4,128,256]{4,3,2,1,0:T(8,128)(2,1)} custom-call(f32[2,2,2,128,128]{4,3,2,1,0:T(8,128)S(1)} %copy-done.1, bf16[2,2,2,128,128]{4,3,2,1,0:T(8,128)(2,1)S(1)} %collective-permute-done.5.got_1, f32[2,2,2,128,128]{4,3,2,1,0:T(8,128)S(1)} %get-tuple-element.58.mine_2, bf16[2,2,2,128,128]{4,3,2,1,0:T(8,128)(2,1)S(1)} %collective-permute-done.10.got_2, ...), custom_call_target="tpu_custom_call" | custom-call | flops 1024 | bytes 1024 | tf_op jit(solution)/shard_map/pallas_call | solution.py:320
  35.9 0.2 collective-permute-done.9.got
  36.1 0.8 %shard_map.65 = bf16[2,2,4,128,256]{4,3,2,1,0:T(8,128)(2,1)} custom-call(f32[2,2,2,128,128]{4,3,2,1,0:T(8,128)S(1)} %get-tuple-element.43.mine, bf16[2,2,2,128,128]{4,3,2,1,0:T(8,128)(2,1)S(1)} %collective-permute-done.9.got, bf16[2,2,4,128,256]{4,3,2,1,0:T(8,128)(2,1)} %shard_map.64._), custom_call_target="tpu_custom_call", output_to_operand_aliasing={{}: (2, {})} | custom-call | flops 1024 | bytes 1024 | tf_op jit(solution)/shard_map/pallas_call | solution.py:331
  (18 shorter events, 0.2 us)
Async XLA Ops:
  0.0 9.9 %copy-start.3 = (bf16[4,3,128,128]{3,2,1,0:T(8,128)(2,1)S(1)}, bf16[4,3,128,128]{3,2,1,0:T(8,128)(2,1)}, u32[]{:S(2)}) copy-start(bf16[4,3,128,128]{3,2,1,0:T(8,128)(2,1)} %refs_3_.1) | copy-start | bytes 1179652
  0.0 9.9 %copy-start = (bf16[2,2,4,128,256]{4,3,2,1,0:T(8,128)(2,1)S(1)}, bf16[2,2,4,128,256]{4,3,2,1,0:T(8,128)(2,1)}, u32[]{:S(2)}) copy-start(bf16[2,2,4,128,256]{4,3,2,1,0:T(8,128)(2,1)} %refs_5_.3) | copy-start | bytes 3145732
  4.4 3.9 %collective-permute-start = (bf16[2,2,128,256]{3,2,1,0:T(8,128)(2,1)}, bf16[2,2,128,256]{3,2,1,0:T(8,128)(2,1)S(1)}, u32[]{:S(2)}, u32[]{:S(2)}) collective-permute-start(bf16[2,2,128,256]{3,2,1,0:T(8,128)(2,1)} %get-tuple-element.33), channel_id=1, source_target_pairs={{0,1},{1,0},{2,3},{3,2},{4,5},{5,4},{6,7},{7,6},{8,9},{9,8},{10,11... | collective-permute-start | bytes 786440 | tf_op jit(solution)/shard_map/ppermute | solution.py:375
  4.5 5.4 %copy-start.4 = (s32[4,3]{1,0:T(4,128)S(1)}, s32[4,3]{1,0:T(4,128)}, u32[]{:S(2)}) copy-start(s32[4,3]{1,0:T(4,128)} %refs_2_.9) | copy-start | bytes 148
  4.5 8.9 %collective-permute-start.1 = (bf16[2,2,2,128,128]{4,3,2,1,0:T(8,128)(2,1)}, bf16[2,2,2,128,128]{4,3,2,1,0:T(8,128)(2,1)S(1)}, u32[]{:S(2)}, u32[]{:S(2)}) collective-permute-start(bf16[2,2,2,128,128]{4,3,2,1,0:T(8,128)(2,1)} %get-tuple-element.37), channel_id=1, source_target_pairs={{0,16},{8,24},{16,0},{24,8},{1,17},{9,25},{17,1},{25,9},{2,18},{10... | collective-permute-start | bytes 786440 | tf_op jit(solution)/shard_map/ppermute | solution.py:372
  6.1 3.8 %copy-start.5 = (f32[4]{0:T(128)S(1)}, f32[4]{0:T(128)}, u32[]{:S(2)}) copy-start(f32[4]{0:T(128)} %refs_0_.9) | copy-start | bytes 52
  6.1 3.8 %copy-start.6 = (s32[4]{0:T(128)S(1)}, s32[4]{0:T(128)}, u32[]{:S(2)}) copy-start(s32[4]{0:T(128)} %refs_1_.9) | copy-start | bytes 52
  6.1 8.9 %collective-permute-start.2 = (bf16[2,2,128,256]{3,2,1,0:T(8,128)(2,1)}, bf16[2,2,128,256]{3,2,1,0:T(8,128)(2,1)S(1)}, u32[]{:S(2)}, u32[]{:S(2)}) collective-permute-start(bf16[2,2,128,256]{3,2,1,0:T(8,128)(2,1)} %get-tuple-element.42), channel_id=1, source_target_pairs={{1,2},{2,1},{3,4},{4,3},{5,6},{6,5},{9,10},{10,9},{11,12},{12,11},... | collective-permute-start | bytes 786440 | tf_op jit(solution)/shard_map/ppermute | solution.py:375
  8.4 5.1 %copy-start.2 = (f32[2,2,2,128,128]{4,3,2,1,0:T(8,128)S(1)}, f32[2,2,2,128,128]{4,3,2,1,0:T(8,128)}, u32[]{:S(2)}) copy-start(f32[2,2,2,128,128]{4,3,2,1,0:T(8,128)} %get-tuple-element.36.near) | copy-start | bytes 1572868
  8.4 10.9 %collective-permute-start.6 = (bf16[4,2,128,128]{3,2,1,0:T(8,128)(2,1)}, bf16[4,2,128,128]{3,2,1,0:T(8,128)(2,1)S(1)}, u32[]{:S(2)}, u32[]{:S(2)}) collective-permute-start(bf16[4,2,128,128]{3,2,1,0:T(8,128)(2,1)} %get-tuple-element.51), channel_id=1, source_target_pairs={{0,8},{8,0},{16,24},{24,16},{1,9},{9,1},{17,25},{25,17},{2,10},{10... | collective-permute-start | bytes 786440 | tf_op jit(solution)/shard_map/ppermute | solution.py:369
  12.6 9.0 %collective-permute-start.4 = (bf16[2,2,2,128,128]{4,3,2,1,0:T(8,128)(2,1)S(1)}, bf16[2,2,2,128,128]{4,3,2,1,0:T(8,128)(2,1)S(1)}, u32[]{:S(2)}, u32[]{:S(2)}) collective-permute-start(bf16[2,2,2,128,128]{4,3,2,1,0:T(8,128)(2,1)S(1)} %get-tuple-element.38), channel_id=1, source_target_pairs={{0,16},{8,24},{16,0},{24,8},{1,17},{9,25},{17,1},{25,9},{2,18},{10... | collective-permute-start | bytes 786440 | tf_op jit(solution)/shard_map/ppermute | solution.py:372
  13.5 10.4 %collective-permute-start.5 = (bf16[2,2,2,128,128]{4,3,2,1,0:T(8,128)(2,1)S(1)}, bf16[2,2,2,128,128]{4,3,2,1,0:T(8,128)(2,1)S(1)}, u32[]{:S(2)}, u32[]{:S(2)}) collective-permute-start(bf16[2,2,2,128,128]{4,3,2,1,0:T(8,128)(2,1)S(1)} %shard_map.57), channel_id=1, source_target_pairs={{0,8},{8,0},{16,24},{24,16},{1,9},{9,1},{17,25},{25,17},{2,10},{10... | collective-permute-start | bytes 786440 | tf_op jit(solution)/shard_map/ppermute | solution.py:369
  17.7 9.5 %collective-permute-start.3 = (bf16[2,2,2,128,128]{4,3,2,1,0:T(8,128)(2,1)S(1)}, bf16[2,2,2,128,128]{4,3,2,1,0:T(8,128)(2,1)S(1)}, u32[]{:S(2)}, u32[]{:S(2)}) collective-permute-start(bf16[2,2,2,128,128]{4,3,2,1,0:T(8,128)(2,1)S(1)} %get-tuple-element.45), channel_id=1, source_target_pairs={{0,16},{8,24},{16,0},{24,8},{1,17},{9,25},{17,1},{25,9},{2,18},{10... | collective-permute-start | bytes 786440 | tf_op jit(solution)/shard_map/ppermute | solution.py:372
  19.3 5.1 %collective-permute-start.7 = (bf16[4,2,128,128]{3,2,1,0:T(8,128)(2,1)S(1)}, bf16[4,2,128,128]{3,2,1,0:T(8,128)(2,1)S(1)}, u32[]{:S(2)}, u32[]{:S(2)}) collective-permute-start(bf16[4,2,128,128]{3,2,1,0:T(8,128)(2,1)S(1)} %collective-permute-done.6.refs_5_), channel_id=1, source_target_pairs={{0,1},{1,0},{2,3},{3,2},{4,5},{5,4},{6,7},{7,6},{8,9},{9,8},{10,11... | collective-permute-start | bytes 786440 | tf_op jit(solution)/shard_map/ppermute | solution.py:375
  19.3 5.1 %collective-permute-start.8 = (bf16[2,128,128]{2,1,0:T(8,128)(2,1)S(1)}, bf16[2,128,128]{2,1,0:T(8,128)(2,1)S(1)}, u32[]{:S(2)}, u32[]{:S(2)}) collective-permute-start(bf16[2,128,128]{2,1,0:T(8,128)(2,1)S(1)} %slice_bitcast_fusion), channel_id=1, source_target_pairs={{0,8},{8,0},{16,24},{24,16},{1,9},{9,1},{17,25},{25,17},{2,10},{10... | collective-permute-start | bytes 196616 | tf_op jit(solution)/shard_map/ppermute | solution.py:369
  21.6 9.9 %collective-permute-start.10 = (bf16[2,2,2,128,128]{4,3,2,1,0:T(8,128)(2,1)S(1)}, bf16[2,2,2,128,128]{4,3,2,1,0:T(8,128)(2,1)S(1)}, u32[]{:S(2)}, u32[]{:S(2)}) collective-permute-start(bf16[2,2,2,128,128]{4,3,2,1,0:T(8,128)(2,1)S(1)} %shard_map.59), channel_id=1, source_target_pairs={{0,8},{8,0},{16,24},{24,16},{1,9},{9,1},{17,25},{25,17},{2,10},{10... | collective-permute-start | bytes 786440 | tf_op jit(solution)/shard_map/ppermute | solution.py:369
  26.1 8.8 %collective-permute-start.11 = (bf16[2,2,2,128,128]{4,3,2,1,0:T(8,128)(2,1)S(1)}, bf16[2,2,2,128,128]{4,3,2,1,0:T(8,128)(2,1)S(1)}, u32[]{:S(2)}, u32[]{:S(2)}) collective-permute-start(bf16[2,2,2,128,128]{4,3,2,1,0:T(8,128)(2,1)S(1)} %get-tuple-element.60), channel_id=1, source_target_pairs={{0,16},{8,24},{16,0},{24,8},{1,17},{9,25},{17,1},{25,9},{2,18},{10... | collective-permute-start | bytes 786440 | tf_op jit(solution)/shard_map/ppermute | solution.py:372
  27.3 7.7 %copy-start.1 = (f32[2,2,2,128,128]{4,3,2,1,0:T(8,128)S(1)}, f32[2,2,2,128,128]{4,3,2,1,0:T(8,128)}, u32[]{:S(2)}) copy-start(f32[2,2,2,128,128]{4,3,2,1,0:T(8,128)} %get-tuple-element.57.mine_1) | copy-start | bytes 1572868
  27.3 8.8 %collective-permute-start.9 = (bf16[2,2,2,128,128]{4,3,2,1,0:T(8,128)(2,1)S(1)}, bf16[2,2,2,128,128]{4,3,2,1,0:T(8,128)(2,1)S(1)}, u32[]{:S(2)}, u32[]{:S(2)}) collective-permute-start(bf16[2,2,2,128,128]{4,3,2,1,0:T(8,128)(2,1)S(1)} %shard_map.62), channel_id=1, source_target_pairs={{0,8},{8,0},{16,24},{24,16},{1,9},{9,1},{17,25},{25,17},{2,10},{10... | collective-permute-start | bytes 786440 | tf_op jit(solution)/shard_map/ppermute | solution.py:369

commit v11 on v10

--- a/solution.py
+++ b/solution.py
@@ -389,7 +389,7 @@
     stacked = (rows, cols)
     beside_xn = beside(raw_x, chip)
     stacked_3 = after_these(stacked, both_1)
-    far_3, near_3, mine_3 = next_call(THIRD, 0, (1, 1, 1), scalars, stacked_3, greens, (beside_n, beside_f), MID)
+    far_3, near_3, mine_3 = next_call(THIRD, 0, (1, 1, 1), scalars, stacked_3, greens, (beside_n, beside_f), SMALL)
     relay_3 = along(far_3)
     size = coupling.shape[-1]
     raw_f = beside_f[0, :, :, :size]

time: 37.5 us -> 37.5 us (level)
  no operation moved by 1% of the time
where the time goes in v11:
time: 37.5 us; the launch traced here: 36.9 us
  Pallas kernels  17.2 us (46%)
  starting transfers between devices  13.3 us (35%)
  waiting for transfers between devices  6.17 us (16%)
    pallas_call x5, Pallas kernels, next_call(): pl.pallas_call(functools.partial(next_body, groups, flip, wanted, own.ndi...  10.9 us
    ppermute x5, starting transfers between devices, across(): return lax.ppermute(array, 'energy', [(i, i ^ 1) for i in range(4)])  6.14 us
    ppermute x4, waiting for transfers between devices, along(): return lax.ppermute(array, 'energy', [(i, i ^ 2) for i in range(4)])  5.39 us
    ppermute x4, starting transfers between devices, along(): return lax.ppermute(array, 'energy', [(i, i ^ 2) for i in range(4)])  4.82 us
    pallas_call x1, Pallas kernels, first_call(): pl.pallas_call(first_body, out_shape=[jax.ShapeDtypeStruct(*out) for out...  4.43 us
    ppermute x3, starting transfers between devices, beside(): return lax.ppermute(array, 'slab', pairs)  2.31 us
    pallas_call x1, Pallas kernels, add_up(): pl.pallas_call(early_body, out_shape=jax.ShapeDtypeStruct(greens.shape, B...  0.97 us
    ppermute x5, waiting for transfers between devices, across(): return lax.ppermute(array, 'energy', [(i, i ^ 1) for i in range(4)])  0.77 us
  transfers between devices with their start and end apart: 12, of which 5 were waited for; matrix products, arithmetic and copies ran while one was open for 0% of the time, Pallas kernels for 33%

profile of v11, /device:TPU:8, one launch (start us, length us, event | category | flops | bytes accessed | tf_op | source)
XLA Modules:
  0.0 36.9 jit_solution(10198950705495080545)
XLA Ops:
  0.0 4.4 %shard_map.55 = (bf16[2,2,2,128,128]{4,3,2,1,0:T(8,128)(2,1)}, f32[2,2,2,128,128]{4,3,2,1,0:T(8,128)}, f32[2,2,2,128,128]{4,3,2,1,0:T(8,128)}, bf16[4,2,128,128]...) custom-call(f32[4]{0:T(128)} %refs_0_.9, s32[4]{0:T(128)} %refs_1_.9, ...), custom_call_target="tpu_custom_call" | custom-call | flops 5368709120 | bytes 16777216 | tf_op jit(solution)/shard_map/pallas_call | solution.py:183
  4.4 0.1 collective-permute-start
  4.5 0.0 copy-start.4
  4.5 1.6 %collective-permute-start.1 = (bf16[2,2,2,128,128]{4,3,2,1,0:T(8,128)(2,1)}, bf16[2,2,2,128,128]{4,3,2,1,0:T(8,128)(2,1)S(1)}, u32[]{:S(2)}, u32[]{:S(2)}) collective-permute-start(bf16[2,2,2,128,128]{4,3,2,1,0:T(8,128)(2,1)} %get-tuple-element.37), channel_id=1, source_target_pairs={{0,16},{8,24},{16,0},{24,8},{1,17},{9,25},{17,1},{25,9},{2,18},{10... | collective-permute-start | bytes 786440 | tf_op jit(solution)/shard_map/ppermute | solution.py:372
  6.1 2.2 %collective-permute-start.2 = (bf16[2,2,128,256]{3,2,1,0:T(8,128)(2,1)}, bf16[2,2,128,256]{3,2,1,0:T(8,128)(2,1)S(1)}, u32[]{:S(2)}, u32[]{:S(2)}) collective-permute-start(bf16[2,2,128,256]{3,2,1,0:T(8,128)(2,1)} %get-tuple-element.42), channel_id=1, source_target_pairs={{1,2},{2,1},{3,4},{4,3},{5,6},{6,5},{9,10},{10,9},{11,12},{12,11},... | collective-permute-start | bytes 786440 | tf_op jit(solution)/shard_map/ppermute | solution.py:375
  8.4 0.0 collective-permute-done.refs_5_.refs_6_
  8.4 0.0 copy-start.2
  8.4 1.6 %collective-permute-start.6 = (bf16[4,2,128,128]{3,2,1,0:T(8,128)(2,1)}, bf16[4,2,128,128]{3,2,1,0:T(8,128)(2,1)S(1)}, u32[]{:S(2)}, u32[]{:S(2)}) collective-permute-start(bf16[4,2,128,128]{3,2,1,0:T(8,128)(2,1)} %get-tuple-element.51), channel_id=1, source_target_pairs={{0,8},{8,0},{16,24},{24,16},{1,9},{9,1},{17,25},{25,17},{2,10},{10... | collective-permute-start | bytes 786440 | tf_op jit(solution)/shard_map/ppermute | solution.py:369
  10.0 2.6 %shard_map.56 = (bf16[2,2,2,128,128]{4,3,2,1,0:T(8,128)(2,1)S(1)}, f32[2,2,2,128,128]{4,3,2,1,0:T(8,128)S(1)}, f32[2,2,2,128,128]{4,3,2,1,0:T(8,128)S(1)}, bf16[...) custom-call(f32[4]{0:T(128)S(1)} %copy-done.5, s32[4]{0:T(128)S(1)} %copy-done.6, s32[4,3]{1,0:T(4,128)S(1)} %copy-done.4, ...), custom_call_target="tpu_custom_call" | custom-call | flops 1024 | bytes 1024 | tf_op jit(solution)/shard_map/pallas_call | solution.py:251
  12.6 0.6 %collective-permute-start.4 = (bf16[2,2,2,128,128]{4,3,2,1,0:T(8,128)(2,1)S(1)}, bf16[2,2,2,128,128]{4,3,2,1,0:T(8,128)(2,1)S(1)}, u32[]{:S(2)}, u32[]{:S(2)}) collective-permute-start(bf16[2,2,2,128,128]{4,3,2,1,0:T(8,128)(2,1)S(1)} %get-tuple-element.38), channel_id=1, source_target_pairs={{0,16},{8,24},{16,0},{24,8},{1,17},{9,25},{17,1},{25,9},{2,18},{10... | collective-permute-start | bytes 786440 | tf_op jit(solution)/shard_map/ppermute | solution.py:372
  13.2 0.3 collective-permute-done.1.relayed
  13.5 1.6 %collective-permute-start.5 = (bf16[2,2,2,128,128]{4,3,2,1,0:T(8,128)(2,1)S(1)}, bf16[2,2,2,128,128]{4,3,2,1,0:T(8,128)(2,1)S(1)}, u32[]{:S(2)}, u32[]{:S(2)}) collective-permute-start(bf16[2,2,2,128,128]{4,3,2,1,0:T(8,128)(2,1)S(1)} %shard_map.57), channel_id=1, source_target_pairs={{0,8},{8,0},{16,24},{24,16},{1,9},{9,1},{17,25},{25,17},{2,10},{10... | collective-permute-start | bytes 786440 | tf_op jit(solution)/shard_map/ppermute | solution.py:369
  15.1 0.0 collective-permute-done.2.refs_7_
  15.1 2.6 %shard_map.58 = (bf16[2,2,2,128,128]{4,3,2,1,0:T(8,128)(2,1)S(1)}, f32[2,2,2,128,128]{4,3,2,1,0:T(8,128)S(1)}, f32[2,2,2,128,128]{4,3,2,1,0:T(8,128)S(1)}) custom-call(f32[4]{0:T(128)S(1)} %copy-done.5, s32[4]{0:T(128)S(1)} %copy-done.6, s32[4,3]{1,0:T(4,128)S(1)} %copy-done.4, bf16[3,512,128]{2,1,0:T(8,128)(2,1)S(1)} %get-tuple-element.52.refs_3_, ...), custom_call_target="tpu_custom_call" | custom-call | flops 1024 | bytes 1024 | tf_op jit(solution)/shard_map/pallas_call | solution.py:251
  17.7 1.6 %collective-permute-start.3 = (bf16[2,2,2,128,128]{4,3,2,1,0:T(8,128)(2,1)S(1)}, bf16[2,2,2,128,128]{4,3,2,1,0:T(8,128)(2,1)S(1)}, u32[]{:S(2)}, u32[]{:S(2)}) collective-permute-start(bf16[2,2,2,128,128]{4,3,2,1,0:T(8,128)(2,1)S(1)} %get-tuple-element.45), channel_id=1, source_target_pairs={{0,16},{8,24},{16,0},{24,8},{1,17},{9,25},{17,1},{25,9},{2,18},{10... | collective-permute-start | bytes 786440 | tf_op jit(solution)/shard_map/ppermute | solution.py:372
  19.3 0.0 collective-permute-start.7
  19.3 0.6 %collective-permute-start.8 = (bf16[2,128,128]{2,1,0:T(8,128)(2,1)S(1)}, bf16[2,128,128]{2,1,0:T(8,128)(2,1)S(1)}, u32[]{:S(2)}, u32[]{:S(2)}) collective-permute-start(bf16[2,128,128]{2,1,0:T(8,128)(2,1)S(1)} %slice_bitcast_fusion), channel_id=1, source_target_pairs={{0,8},{8,0},{16,24},{24,16},{1,9},{9,1},{17,25},{25,17},{2,10},{10... | collective-permute-start | bytes 196616 | tf_op jit(solution)/shard_map/ppermute | solution.py:369
  19.9 1.7 %collective-permute-done.4.relayed = bf16[2,2,2,128,128]{4,3,2,1,0:T(8,128)(2,1)S(1)} collective-permute-done((bf16[2,2,2,128,128]{4,3,2,1,0:T(8,128)(2,1)S(1)}, bf16[2,2,2,128,128]{4,3,2,1,0:T(8,128)(2,1)S(1)}, u32[]{:S(2)}, u32[]{:S(2)}) %collective-permute-start.4) | collective-permute-done | bytes 262176 | tf_op jit(solution)/shard_map/ppermute | solution.py:372
  21.6 0.6 %collective-permute-start.10 = (bf16[2,2,2,128,128]{4,3,2,1,0:T(8,128)(2,1)S(1)}, bf16[2,2,2,128,128]{4,3,2,1,0:T(8,128)(2,1)S(1)}, u32[]{:S(2)}, u32[]{:S(2)}) collective-permute-start(bf16[2,2,2,128,128]{4,3,2,1,0:T(8,128)(2,1)S(1)} %shard_map.59), channel_id=1, source_target_pairs={{0,8},{8,0},{16,24},{24,16},{1,9},{9,1},{17,25},{25,17},{2,10},{10... | collective-permute-start | bytes 786440 | tf_op jit(solution)/shard_map/ppermute | solution.py:369
  22.2 1.6 %shard_map.60 = (bf16[1,2,2,128,128]{4,3,2,1,0:T(8,128)(2,1)S(1)}, f32[1,2,2,128,128]{4,3,2,1,0:T(8,128)S(1)}) custom-call(f32[4]{0:T(128)S(1)} %copy-done.5, s32[4]{0:T(128)S(1)} %copy-done.6, s32[4,3]{1,0:T(4,128)S(1)} %copy-done.4, bf16[3,512,128]{2,1,0:T(8,128)(2,1)S(1)} %get-tuple-element.52.refs_3_, ...), custom_call_target="tpu_custom_call" | custom-call | flops 1024 | bytes 1024 | tf_op jit(solution)/shard_map/pallas_call | solution.py:251
  23.9 0.5 %collective-permute-done.8.refs_7_ = bf16[2,128,128]{2,1,0:T(8,128)(2,1)S(1)} collective-permute-done((bf16[2,128,128]{2,1,0:T(8,128)(2,1)S(1)}, bf16[2,128,128]{2,1,0:T(8,128)(2,1)S(1)}, u32[]{:S(2)}, u32[]{:S(2)}) %collective-permute-start.8) | collective-permute-done | bytes 65568 | tf_op jit(solution)/shard_map/ppermute | solution.py:369
  24.4 0.0 collective-permute-done.7.refs_6_
  24.4 1.6 %shard_map.61 = (bf16[2,2,2,128,128]{4,3,2,1,0:T(8,128)(2,1)S(1)}, f32[1,2,2,128,128]{4,3,2,1,0:T(8,128)S(1)}) custom-call(f32[4]{0:T(128)S(1)} %copy-done.5, s32[4]{0:T(128)S(1)} %copy-done.6, s32[4,3]{1,0:T(4,128)S(1)} %copy-done.4, bf16[3,512,128]{2,1,0:T(8,128)(2,1)S(1)} %get-tuple-element.52.refs_3_, ...), custom_call_target="tpu_custom_call" | custom-call | flops 1024 | bytes 1024 | tf_op jit(solution)/shard_map/pallas_call | solution.py:251
  26.1 1.1 %collective-permute-start.11 = (bf16[2,2,2,128,128]{4,3,2,1,0:T(8,128)(2,1)S(1)}, bf16[2,2,2,128,128]{4,3,2,1,0:T(8,128)(2,1)S(1)}, u32[]{:S(2)}, u32[]{:S(2)}) collective-permute-start(bf16[2,2,2,128,128]{4,3,2,1,0:T(8,128)(2,1)S(1)} %get-tuple-element.60), channel_id=1, source_target_pairs={{0,16},{8,24},{16,0},{24,8},{1,17},{9,25},{17,1},{25,9},{2,18},{10... | collective-permute-start | bytes 786440 | tf_op jit(solution)/shard_map/ppermute | solution.py:372
  27.2 0.0 collective-permute-done.3.relayed
  27.3 1.8 %collective-permute-start.9 = (bf16[2,2,2,128,128]{4,3,2,1,0:T(8,128)(2,1)S(1)}, bf16[2,2,2,128,128]{4,3,2,1,0:T(8,128)(2,1)S(1)}, u32[]{:S(2)}, u32[]{:S(2)}) collective-permute-start(bf16[2,2,2,128,128]{4,3,2,1,0:T(8,128)(2,1)S(1)} %shard_map.62), channel_id=1, source_target_pairs={{0,8},{8,0},{16,24},{24,16},{1,9},{9,1},{17,25},{25,17},{2,10},{10... | collective-permute-start | bytes 786440 | tf_op jit(solution)/shard_map/ppermute | solution.py:369
  29.1 2.4 %shard_map.63.mine_z = f32[2,2,2,128,128]{4,3,2,1,0:T(8,128)S(1)} custom-call(f32[4]{0:T(128)S(1)} %copy-done.5, s32[4]{0:T(128)S(1)} %copy-done.6, s32[4,3]{1,0:T(4,128)S(1)} %copy-done.4, bf16[3,512,128]{2,1,0:T(8,128)(2,1)S(1)} %get-tuple-element.52.refs_3_, bf16[4,128,384]{2,1,0:T(8,128)(2,1)S(1)} %get-tuple-element.53.refs_4_, ...), custom_call_target="tpu_custom_call" | custom-call | flops 1024 | bytes 1024 | tf_op jit(solution)/shard_map/pallas_call | solution.py:251
  31.5 0.0 collective-permute-done.10.got_2
  31.5 3.4 %collective-permute-done.11.got_z = bf16[2,2,2,128,128]{4,3,2,1,0:T(8,128)(2,1)S(1)} collective-permute-done((bf16[2,2,2,128,128]{4,3,2,1,0:T(8,128)(2,1)S(1)}, bf16[2,2,2,128,128]{4,3,2,1,0:T(8,128)(2,1)S(1)}, u32[]{:S(2)}, u32[]{:S(2)}) %collective-permute-start.11) | collective-permute-done | bytes 262176 | tf_op jit(solution)/shard_map/ppermute | solution.py:372
  34.9 1.0 %shard_map.64._ = bf16[2,2,4,128,256]{4,3,2,1,0:T(8,128)(2,1)} custom-call(f32[2,2,2,128,128]{4,3,2,1,0:T(8,128)S(1)} %copy-done.1, bf16[2,2,2,128,128]{4,3,2,1,0:T(8,128)(2,1)S(1)} %collective-permute-done.5.got_1, f32[2,2,2,128,128]{4,3,2,1,0:T(8,128)S(1)} %get-tuple-element.58.mine_2, bf16[2,2,2,128,128]{4,3,2,1,0:T(8,128)(2,1)S(1)} %collective-permute-done.10.got_2, ...), custom_call_target="tpu_custom_call" | custom-call | flops 1024 | bytes 1024 | tf_op jit(solution)/shard_map/pallas_call | solution.py:320
  35.9 0.2 collective-permute-done.9.got
  36.1 0.8 %shard_map.65 = bf16[2,2,4,128,256]{4,3,2,1,0:T(8,128)(2,1)} custom-call(f32[2,2,2,128,128]{4,3,2,1,0:T(8,128)S(1)} %get-tuple-element.43.mine, bf16[2,2,2,128,128]{4,3,2,1,0:T(8,128)(2,1)S(1)} %collective-permute-done.9.got, bf16[2,2,4,128,256]{4,3,2,1,0:T(8,128)(2,1)} %shard_map.64._), custom_call_target="tpu_custom_call", output_to_operand_aliasing={{}: (2, {})} | custom-call | flops 1024 | bytes 1024 | tf_op jit(solution)/shard_map/pallas_call | solution.py:331
  (18 shorter events, 0.2 us)
Async XLA Ops:
  0.0 9.9 %copy-start.3 = (bf16[4,3,128,128]{3,2,1,0:T(8,128)(2,1)S(1)}, bf16[4,3,128,128]{3,2,1,0:T(8,128)(2,1)}, u32[]{:S(2)}) copy-start(bf16[4,3,128,128]{3,2,1,0:T(8,128)(2,1)} %refs_3_.1) | copy-start | bytes 1179652
  0.0 9.9 %copy-start = (bf16[2,2,4,128,256]{4,3,2,1,0:T(8,128)(2,1)S(1)}, bf16[2,2,4,128,256]{4,3,2,1,0:T(8,128)(2,1)}, u32[]{:S(2)}) copy-start(bf16[2,2,4,128,256]{4,3,2,1,0:T(8,128)(2,1)} %refs_5_.3) | copy-start | bytes 3145732
  4.4 3.9 %collective-permute-start = (bf16[2,2,128,256]{3,2,1,0:T(8,128)(2,1)}, bf16[2,2,128,256]{3,2,1,0:T(8,128)(2,1)S(1)}, u32[]{:S(2)}, u32[]{:S(2)}) collective-permute-start(bf16[2,2,128,256]{3,2,1,0:T(8,128)(2,1)} %get-tuple-element.33), channel_id=1, source_target_pairs={{0,1},{1,0},{2,3},{3,2},{4,5},{5,4},{6,7},{7,6},{8,9},{9,8},{10,11... | collective-permute-start | bytes 786440 | tf_op jit(solution)/shard_map/ppermute | solution.py:375
  4.5 5.4 %copy-start.4 = (s32[4,3]{1,0:T(4,128)S(1)}, s32[4,3]{1,0:T(4,128)}, u32[]{:S(2)}) copy-start(s32[4,3]{1,0:T(4,128)} %refs_2_.9) | copy-start | bytes 148
  4.5 8.9 %collective-permute-start.1 = (bf16[2,2,2,128,128]{4,3,2,1,0:T(8,128)(2,1)}, bf16[2,2,2,128,128]{4,3,2,1,0:T(8,128)(2,1)S(1)}, u32[]{:S(2)}, u32[]{:S(2)}) collective-permute-start(bf16[2,2,2,128,128]{4,3,2,1,0:T(8,128)(2,1)} %get-tuple-element.37), channel_id=1, source_target_pairs={{0,16},{8,24},{16,0},{24,8},{1,17},{9,25},{17,1},{25,9},{2,18},{10... | collective-permute-start | bytes 786440 | tf_op jit(solution)/shard_map/ppermute | solution.py:372
  6.1 3.8 %copy-start.5 = (f32[4]{0:T(128)S(1)}, f32[4]{0:T(128)}, u32[]{:S(2)}) copy-start(f32[4]{0:T(128)} %refs_0_.9) | copy-start | bytes 52
  6.1 3.8 %copy-start.6 = (s32[4]{0:T(128)S(1)}, s32[4]{0:T(128)}, u32[]{:S(2)}) copy-start(s32[4]{0:T(128)} %refs_1_.9) | copy-start | bytes 52
  6.1 8.9 %collective-permute-start.2 = (bf16[2,2,128,256]{3,2,1,0:T(8,128)(2,1)}, bf16[2,2,128,256]{3,2,1,0:T(8,128)(2,1)S(1)}, u32[]{:S(2)}, u32[]{:S(2)}) collective-permute-start(bf16[2,2,128,256]{3,2,1,0:T(8,128)(2,1)} %get-tuple-element.42), channel_id=1, source_target_pairs={{1,2},{2,1},{3,4},{4,3},{5,6},{6,5},{9,10},{10,9},{11,12},{12,11},... | collective-permute-start | bytes 786440 | tf_op jit(solution)/shard_map/ppermute | solution.py:375
  8.4 5.1 %copy-start.2 = (f32[2,2,2,128,128]{4,3,2,1,0:T(8,128)S(1)}, f32[2,2,2,128,128]{4,3,2,1,0:T(8,128)}, u32[]{:S(2)}) copy-start(f32[2,2,2,128,128]{4,3,2,1,0:T(8,128)} %get-tuple-element.36.near) | copy-start | bytes 1572868
  8.4 10.9 %collective-permute-start.6 = (bf16[4,2,128,128]{3,2,1,0:T(8,128)(2,1)}, bf16[4,2,128,128]{3,2,1,0:T(8,128)(2,1)S(1)}, u32[]{:S(2)}, u32[]{:S(2)}) collective-permute-start(bf16[4,2,128,128]{3,2,1,0:T(8,128)(2,1)} %get-tuple-element.51), channel_id=1, source_target_pairs={{0,8},{8,0},{16,24},{24,16},{1,9},{9,1},{17,25},{25,17},{2,10},{10... | collective-permute-start | bytes 786440 | tf_op jit(solution)/shard_map/ppermute | solution.py:369
  12.6 9.0 %collective-permute-start.4 = (bf16[2,2,2,128,128]{4,3,2,1,0:T(8,128)(2,1)S(1)}, bf16[2,2,2,128,128]{4,3,2,1,0:T(8,128)(2,1)S(1)}, u32[]{:S(2)}, u32[]{:S(2)}) collective-permute-start(bf16[2,2,2,128,128]{4,3,2,1,0:T(8,128)(2,1)S(1)} %get-tuple-element.38), channel_id=1, source_target_pairs={{0,16},{8,24},{16,0},{24,8},{1,17},{9,25},{17,1},{25,9},{2,18},{10... | collective-permute-start | bytes 786440 | tf_op jit(solution)/shard_map/ppermute | solution.py:372
  13.5 10.4 %collective-permute-start.5 = (bf16[2,2,2,128,128]{4,3,2,1,0:T(8,128)(2,1)S(1)}, bf16[2,2,2,128,128]{4,3,2,1,0:T(8,128)(2,1)S(1)}, u32[]{:S(2)}, u32[]{:S(2)}) collective-permute-start(bf16[2,2,2,128,128]{4,3,2,1,0:T(8,128)(2,1)S(1)} %shard_map.57), channel_id=1, source_target_pairs={{0,8},{8,0},{16,24},{24,16},{1,9},{9,1},{17,25},{25,17},{2,10},{10... | collective-permute-start | bytes 786440 | tf_op jit(solution)/shard_map/ppermute | solution.py:369
  17.7 9.5 %collective-permute-start.3 = (bf16[2,2,2,128,128]{4,3,2,1,0:T(8,128)(2,1)S(1)}, bf16[2,2,2,128,128]{4,3,2,1,0:T(8,128)(2,1)S(1)}, u32[]{:S(2)}, u32[]{:S(2)}) collective-permute-start(bf16[2,2,2,128,128]{4,3,2,1,0:T(8,128)(2,1)S(1)} %get-tuple-element.45), channel_id=1, source_target_pairs={{0,16},{8,24},{16,0},{24,8},{1,17},{9,25},{17,1},{25,9},{2,18},{10... | collective-permute-start | bytes 786440 | tf_op jit(solution)/shard_map/ppermute | solution.py:372
  19.3 5.1 %collective-permute-start.7 = (bf16[4,2,128,128]{3,2,1,0:T(8,128)(2,1)S(1)}, bf16[4,2,128,128]{3,2,1,0:T(8,128)(2,1)S(1)}, u32[]{:S(2)}, u32[]{:S(2)}) collective-permute-start(bf16[4,2,128,128]{3,2,1,0:T(8,128)(2,1)S(1)} %collective-permute-done.6.refs_5_), channel_id=1, source_target_pairs={{0,1},{1,0},{2,3},{3,2},{4,5},{5,4},{6,7},{7,6},{8,9},{9,8},{10,11... | collective-permute-start | bytes 786440 | tf_op jit(solution)/shard_map/ppermute | solution.py:375
  19.3 5.1 %collective-permute-start.8 = (bf16[2,128,128]{2,1,0:T(8,128)(2,1)S(1)}, bf16[2,128,128]{2,1,0:T(8,128)(2,1)S(1)}, u32[]{:S(2)}, u32[]{:S(2)}) collective-permute-start(bf16[2,128,128]{2,1,0:T(8,128)(2,1)S(1)} %slice_bitcast_fusion), channel_id=1, source_target_pairs={{0,8},{8,0},{16,24},{24,16},{1,9},{9,1},{17,25},{25,17},{2,10},{10... | collective-permute-start | bytes 196616 | tf_op jit(solution)/shard_map/ppermute | solution.py:369
  21.6 9.9 %collective-permute-start.10 = (bf16[2,2,2,128,128]{4,3,2,1,0:T(8,128)(2,1)S(1)}, bf16[2,2,2,128,128]{4,3,2,1,0:T(8,128)(2,1)S(1)}, u32[]{:S(2)}, u32[]{:S(2)}) collective-permute-start(bf16[2,2,2,128,128]{4,3,2,1,0:T(8,128)(2,1)S(1)} %shard_map.59), channel_id=1, source_target_pairs={{0,8},{8,0},{16,24},{24,16},{1,9},{9,1},{17,25},{25,17},{2,10},{10... | collective-permute-start | bytes 786440 | tf_op jit(solution)/shard_map/ppermute | solution.py:369
  26.1 8.8 %collective-permute-start.11 = (bf16[2,2,2,128,128]{4,3,2,1,0:T(8,128)(2,1)S(1)}, bf16[2,2,2,128,128]{4,3,2,1,0:T(8,128)(2,1)S(1)}, u32[]{:S(2)}, u32[]{:S(2)}) collective-permute-start(bf16[2,2,2,128,128]{4,3,2,1,0:T(8,128)(2,1)S(1)} %get-tuple-element.60), channel_id=1, source_target_pairs={{0,16},{8,24},{16,0},{24,8},{1,17},{9,25},{17,1},{25,9},{2,18},{10... | collective-permute-start | bytes 786440 | tf_op jit(solution)/shard_map/ppermute | solution.py:372
  27.3 7.7 %copy-start.1 = (f32[2,2,2,128,128]{4,3,2,1,0:T(8,128)S(1)}, f32[2,2,2,128,128]{4,3,2,1,0:T(8,128)}, u32[]{:S(2)}) copy-start(f32[2,2,2,128,128]{4,3,2,1,0:T(8,128)} %get-tuple-element.57.mine_1) | copy-start | bytes 1572868
  27.3 8.8 %collective-permute-start.9 = (bf16[2,2,2,128,128]{4,3,2,1,0:T(8,128)(2,1)S(1)}, bf16[2,2,2,128,128]{4,3,2,1,0:T(8,128)(2,1)S(1)}, u32[]{:S(2)}, u32[]{:S(2)}) collective-permute-start(bf16[2,2,2,128,128]{4,3,2,1,0:T(8,128)(2,1)S(1)} %shard_map.62), channel_id=1, source_target_pairs={{0,8},{8,0},{16,24},{24,16},{1,9},{9,1},{17,25},{25,17},{2,10},{10... | collective-permute-start | bytes 786440 | tf_op jit(solution)/shard_map/ppermute | solution.py:369
